TPU v7x, 32 devices: a whole 2x2x4 slice. The times are simulated.
32 devices in a mesh: shot: 4 (over x, core), depth: 8 (over z, y).
Axes of the slice: x: 2, y: 2, z: 4, core: 2. Of those that a mesh axis runs over, the one named last changes fastest.
Arguments:
- field_prev: float32 [4, 256, 64, 128], P('shot', 'depth'), may hold values from -6 to 6
- field_now: float32 [4, 256, 64, 128], P('shot', 'depth'), may hold values from -6 to 6
- adjoint_next: float32 [4, 256, 64, 128], P('shot', 'depth'), may hold values from -6 to 6
- adjoint_after: float32 [4, 256, 64, 128], P('shot', 'depth'), may hold values from -6 to 6
- courant: float32 [256, 64, 128], P('depth'), may hold values from 0.05 to 0.2
- wavelet: float32 [4, 4], P('shot'), may hold values from -18 to 18
- source_cell: int32 [4], P('shot'), may hold values from 0 to 2097151
- receiver_cell: int32 [4, 128], P('shot'), may hold values from 0 to 2097151
- observed: float32 [4, 4, 128], P('shot'), may hold values from -6 to 6
- damping_table: float32 [64], replicated, may hold values from 0.1 to 10
- plan_step: int32 [1], replicated, may hold values from 0 to 63
Outputs:
- updated: float32 [256, 64, 128], P('depth')
All inputs are finite; a program needn't handle non-finite values.
Results may differ from a plain program's by a relative error of at most 0.00002.
Values sent between devices are 32-bit elements; how exact they have to be, the bound alone decides.
No kernel may reach another device: no remote copies, remote signals or barrier semaphores. Data moves between devices by JAX's collectives and lax.ppermute only.
A program may use at most 128 MiB of HBM per device.

v0:
```python
import jax
import jax.numpy as jnp
from jax import lax
from jax.experimental import pallas as pl
from jax.experimental.pallas import tpu as pltpu
from jax.sharding import PartitionSpec as P

STEPS = 4
HALO = 4
ROWS = 8
PAD = HALO * ROWS

coeffs = (-205.0 / 72.0, 8.0 / 5.0, -1.0 / 5.0, 8.0 / 315.0, -1.0 / 560.0)

VMEM = pl.BlockSpec(memory_space=pltpu.VMEM)
SMEM = pl.BlockSpec(memory_space=pltpu.SMEM)
HBM = pl.BlockSpec(memory_space=pltpu.HBM)


def f32(*shape):
    return jax.ShapeDtypeStruct(shape, jnp.float32)


def params():
    return pltpu.CompilerParams(vmem_limit_bytes=6 * 2**20)


def cost(planes):
    return pl.CostEstimate(
        flops=planes * 10**4, bytes_accessed=planes * 2**10, transcendentals=0
    )


def split(value, size):
    if size & (size - 1) == 0:
        return value >> (size.bit_length() - 1), value & (size - 1)
    return value // size, value % size


def spread(x, width):
    s, g = split(x, width // ROWS)
    return g * ROWS + s


def interleave(put, get, width):
    for g in range(width // ROWS):
        put(g * ROWS, get(pl.ds(g, ROWS, stride=width // ROWS)))


def margins(pad, first, count, width):
    length = pad.shape[2]
    place = lax.broadcasted_iota(jnp.int32, (ROWS, length), 0)

    def body(i, _):
        p = first + i
        for j in range(HALO):
            at = j * ROWS
            low = pltpu.roll(pad[p, width + at : width + at + ROWS, :], 1, 0)
            pad[p, at : at + ROWS, :] = jnp.where(place == 0, 0.0, low)
            top = pltpu.roll(pad[p, PAD + at : PAD + at + ROWS, :], ROWS - 1, 0)
            beyond = PAD + width + at
            pad[p, beyond : beyond + ROWS, :] = jnp.where(place == ROWS - 1, 0.0, top)

    march(count, body)


def high(side):
    odd = lax.axis_index("depth") % 2
    return odd if side else 1 - odd


def fill_edge(pad, side, halo, halo_at, field, slab, width):
    up = high(side)
    rows = slice(PAD, PAD + width)
    if len(field) == 1:
        for i in range(HALO):

            def put(at, value, i=i):
                pad[up * (2 * HALO) + i, PAD + at : PAD + at + ROWS, :] = value

            interleave(put, lambda spot, i=i: halo[halo_at + i, spot, :], width)
    else:
        pad[pl.ds(up * (2 * HALO), HALO), rows, :] = halo[halo_at : halo_at + HALO]
    inner = pl.ds((1 - up) * (2 * HALO), HALO)
    own = slice(HALO, 2 * HALO)
    if len(field) == 1:
        (ref,) = field
        slab = ref.shape[0]
        pad[own, rows, :] = ref[pl.ds(up * (slab - HALO), HALO)]
        pad[inner, rows, :] = ref[pl.ds(HALO + up * (slab - 3 * HALO), HALO)]
    else:
        core = field[2]
        pad[own, rows, :] = field[side][...]
        pad[inner, rows, :] = core[pl.ds(up * (core.shape[0] - HALO), HALO)]
    margins(pad, HALO, HALO, width)


def fill_core(pad, field, width):
    slab = pad.shape[0]
    rows = slice(PAD, PAD + width)
    if len(field) == 1:
        pad[:, rows, :] = field[0][...]
    else:
        for side in (0, 1):
            pad[pl.ds(high(side) * (slab - HALO), HALO), rows, :] = field[side][...]
        pad[HALO : slab - HALO, rows, :] = field[2][...]
    margins(pad, HALO, slab - 2 * HALO, width)


def place_of(side, field, slab):
    if len(field) == 1:
        return field[0], HALO if side == 2 else high(side) * (slab - HALO)
    return field[side], 0


def columns(pad, along_ref, width):
    planes, _, length = along_ref.shape
    apart = lax.broadcasted_iota(jnp.int32, (length, length), 0)
    apart = jnp.abs(apart - lax.broadcasted_iota(jnp.int32, (length, length), 1))
    band = jnp.where(apart == 0, 3.0 * coeffs[0], 0.0)
    for k in range(1, 5):
        band = jnp.where(apart == k, coeffs[k], band)
    size = HALO if planes % (2 * HALO) else 2 * HALO
    for begin in range(0, planes, size):
        block = pad[HALO + begin : HALO + begin + size, PAD : PAD + width, :]
        product = jnp.dot(
            block.reshape(size * width, length),
            band,
            precision=lax.Precision.HIGHEST,
            preferred_element_type=jnp.float32,
        )
        along_ref[begin : begin + size] = product.reshape(size, width, length)


def stencil(pad, p, width, result):
    rows = slice(PAD, PAD + width)
    plane = pad[p]
    for k in range(1, 5):
        along = pad[p + k, rows, :] + pad[p - k, rows, :]
        along = along + plane[PAD + k * ROWS : PAD + k * ROWS + width]
        along = along + plane[PAD - k * ROWS : PAD - k * ROWS + width]
        result = result + coeffs[k] * along
    return plane[rows], result


def fold(values):
    width, length = values.shape
    return jnp.sum(values.reshape(width // 8, 8, length), axis=0)


def march(count, body, carry=None):
    return lax.fori_loop(0, count, body, carry, unroll=4 if count % 4 == 0 else 2)


def kernel_call(kernel, small, arrays, outs, scratch, planes):
    return pl.pallas_call(
        kernel,
        out_shape=tuple(outs),
        in_specs=[SMEM] * len(small) + [VMEM] * len(arrays),
        out_specs=tuple([VMEM] * len(outs)),
        scratch_shapes=scratch,
        compiler_params=params(),
        cost_estimate=cost(planes),
    )(*small, *arrays)


def grouped(refs, sizes):
    found = []
    for size in sizes:
        found.append(refs[:size])
        refs = refs[size:]
    return found, list(refs)


def sizes_of(side, slab, width, length):
    planes = slab - 2 * HALO if side == 2 else HALO
    depth = slab if side == 2 else 3 * HALO
    return planes, [
        pltpu.VMEM((planes, width, length), jnp.float32),
        pltpu.VMEM((depth, width + 2 * PAD, length), jnp.float32),
    ]


def step_planes(side, along_ref, pad, halo, halo_at, cur, old, c_ref, next_ref, lap_ref):
    slab, width, length = c_ref.shape
    if side == 2:
        fill_core(pad, cur, width)
        plane = HALO
    else:
        fill_edge(pad, side, halo[0], halo_at, cur, slab, width)
        plane = high(side) * (slab - HALO)
    columns(pad, along_ref, width)
    old_ref, old_at = place_of(side, old, slab)

    def body(i, _):
        center, lap = stencil(pad, HALO + i, width, along_ref[i])
        if lap_ref is not None:
            lap_ref[i] = lap
        next_ref[i] = 2.0 * center - old_ref[old_at + i] + c_ref[plane + i] * lap

    march(next_ref.shape[0], body)


def forward(side, step, halo, cur, old, courant, after, wavelet, source):
    slab, width, length = courant.shape
    planes, pad_scratch = sizes_of(side, slab, width, length)
    groups = [list(halo), list(cur), list(old), [courant], list(after)]
    sizes = [len(g) for g in groups]

    def kernel(wave_ref, source_ref, *refs):
        (halo_refs, cur_refs, old_refs, (c_ref,), _), refs = grouped(refs, sizes)
        next_ref, lap_ref, along, pad = refs
        step_planes(side, along, pad, halo_refs, 0, cur_refs, old_refs, c_ref, next_ref, lap_ref)
        plane = HALO if side == 2 else high(side) * (slab - HALO)
        base = (lax.axis_index("depth") * slab + plane) * (width * length)
        local = source_ref[0] - base

        @pl.when((local >= 0) & (local < planes * width * length))
        def _():
            row, y = split(local, length)
            at, x = split(row, width)
            x = spread(x, width)
            spot = lax.broadcasted_iota(jnp.int32, (1, length), 1) == y
            add = jnp.where(spot, wave_ref[0, step], 0.0)
            next_ref[at, pl.ds(x, 1), :] = next_ref[at, pl.ds(x, 1), :] + add

    outs = [f32(planes, width, length)] * 2
    arrays = sum(groups, [])
    return kernel_call(kernel, [wavelet, source], arrays, outs, pad_scratch, planes)


def adjoint_step(
    side, step, along, pad, halo, halo_at, cur, old, c_ref, field_ref, list_ref, obs_ref, next_ref
):
    slab, width, length = c_ref.shape
    step_planes(side, along, pad, halo, halo_at, cur, old, c_ref, next_ref, None)
    column = lax.broadcasted_iota(jnp.int32, (1, length), 1)

    def inject(k, _):
        row, y = split(list_ref[2 * side, k], length)
        at, x = split(row, width)
        x = spread(x, width)
        pred = field_ref[at, pl.ds(x, 1), :]
        res = jnp.where(column == y, pred - obs_ref[step, list_ref[2 * side + 1, k]], 0.0)
        next_ref[at, pl.ds(x, 1), :] = next_ref[at, pl.ds(x, 1), :] + res

    lax.fori_loop(0, list_ref[6, side], inject, None)


def adjoint(side, step, halo, halo_at, cur, old, courant, field, after, listing, observed):
    slab, width, length = courant.shape
    planes, pad_scratch = sizes_of(side, slab, width, length)
    groups = [list(halo), list(cur), list(old), [courant, field], list(after)]
    sizes = [len(g) for g in groups]

    def kernel(list_ref, obs_ref, *refs):
        (halo_refs, cur_refs, old_refs, (c_ref, field_ref), _), refs = grouped(refs, sizes)
        next_ref, along, pad = refs
        adjoint_step(
            side, step, along, pad, halo_refs, halo_at, cur_refs, old_refs, c_ref, field_ref,
            list_ref, obs_ref, next_ref,
        )

    outs = [f32(planes, width, length)]
    arrays = sum(groups, [])
    return kernel_call(kernel, [listing, observed], arrays, outs, pad_scratch, planes)[0]


def adjoint_last(
    side, halo, cur, old, courant, field, laps, adjoints, tile, other, after, listing, observed
):
    slab, width, length = courant.shape
    planes, pad_scratch = sizes_of(side, slab, width, length)
    groups = [list(halo), list(cur), list(old), [courant, field], list(laps)]
    groups += [list(adjoints), list(tile) + list(other), list(after)]
    sizes = [len(g) for g in groups]

    def kernel(list_ref, obs_ref, *refs):
        found, refs = grouped(refs, sizes)
        halo_refs, cur_refs, old_refs, (c_ref, field_ref), lap_refs, adj_refs, more, _ = found
        next_ref, along, pad = refs[-3:]
        adjoint_step(
            side, 0, along, pad, halo_refs, 0, cur_refs, old_refs, c_ref, field_ref,
            list_ref, obs_ref, next_ref,
        )
        core = lax.axis_index("shot") % 2

        def product(i):
            value = next_ref[i] * lap_refs[0][i]
            for lap_ref, adj_ref in zip(lap_refs[1:], adj_refs):
                value = value + adj_ref[i] * lap_ref[i]
            return value

        if side == 2:
            keep_ref, send_ref = refs[:2]
            half = planes // 2

            def body(i, _):
                keep_ref[i] = product(core * half + i)
                send_ref[i] = product((1 - core) * half + i)

            march(half, body)
        elif side == 0:
            for i in range(HALO):
                refs[0][i] = product(i)
        else:
            tile_ref, tiles_ref, other_ref = more

            def write(own_ref, far_ref):
                for i in range(HALO):
                    rows = slice(i * width, (i + 1) * width)
                    own_ref[rows, :] = other_ref[i]
                    far_ref[rows, :] = product(i)

            @pl.when(core == 0)
            def _():
                write(refs[0], refs[1])

            @pl.when(core == 1)
            def _():
                write(refs[1], refs[0])

            for ref in refs[:2]:
                ref[HALO * width : HALO * width + 8, :] = tile_ref[...] + tiles_ref[...]

    if side == 2:
        outs = [f32(planes // 2, width, length)] * 2
    elif side == 0:
        outs = [f32(planes, width, length)]
    else:
        outs = [f32(HALO * width + 8, length)] * 2
    arrays = sum(groups, [])
    scratch = [pltpu.VMEM((planes, width, length), jnp.float32)] + pad_scratch
    return kernel_call(kernel, [listing, observed], arrays, outs, scratch, planes)


def curvature(laps, after):
    number = len(laps)
    inner, width, length = laps[0][2].shape
    half = inner // 2
    size = half + HALO

    def kernel(*refs):
        sides = [refs[n * number : (n + 1) * number] for n in range(3)]
        keep_ref, send_ref, tile_ref = refs[3 * number + 1 :]
        core = lax.axis_index("shot") % 2

        def squares(lap_refs, at):
            value = lap_refs[0][at] * lap_refs[0][at]
            for ref in lap_refs[1:]:
                value = value + ref[at] * ref[at]
            return value

        def body(i, total):
            for ref, start in ((keep_ref, core * half), (send_ref, (1 - core) * half)):
                value = squares(sides[2], start + i)
                ref[i] = value
                total = total + fold(value)
            return total

        tile_ref[...] = march(half, body, jnp.zeros((8, length), jnp.float32))

        def outer(first_ref, second_ref):
            total = jnp.zeros((8, length), jnp.float32)
            for i in range(HALO):
                for ref, lap_refs in ((first_ref, sides[0]), (second_ref, sides[1])):
                    value = squares(lap_refs, i)
                    ref[half + i] = value
                    total = total + fold(value)
            tile_ref[...] = tile_ref[...] + total

        @pl.when(core == 0)
        def _():
            outer(keep_ref, send_ref)

        @pl.when(core == 1)
        def _():
            outer(send_ref, keep_ref)

    outs = [f32(size, width, length)] * 2 + [f32(8, length)]
    arrays = [lap[n] for n in range(3) for lap in laps] + [after]
    return kernel_call(kernel, [], arrays, outs, [], 8)


def list_receivers(cells, slab, width, length):
    count = cells.shape[0]
    area = width * length

    def kernel(cell_ref, out_ref):
        offset = lax.axis_index("depth") * (slab * area)
        starts = [high(0) * ((slab - HALO) * area), high(1) * ((slab - HALO) * area), HALO * area]
        lengths = [HALO * area, HALO * area, (slab - 2 * HALO) * area]

        def body(r, counts):
            cell = cell_ref[r] - offset
            found = []
            for n in range(3):
                local = cell - starts[n]
                inside = (local >= 0) & (local < lengths[n])
                out_ref[2 * n, counts[n]] = local
                out_ref[2 * n + 1, counts[n]] = r
                found.append(counts[n] + inside.astype(jnp.int32))
            return tuple(found)

        counts = lax.fori_loop(0, count, body, (jnp.int32(0),) * 3, unroll=8)
        for n in range(3):
            out_ref[6, n] = counts[n]

    return pl.pallas_call(
        kernel,
        out_shape=jax.ShapeDtypeStruct((7, 2 * count), jnp.int32),
        in_specs=[SMEM],
        out_specs=SMEM,
        compiler_params=params(),
        cost_estimate=cost(8),
    )(cells)


def interleaved(*arrays):
    number = len(arrays)
    slab, width, length = arrays[0].shape

    def kernel(*refs):
        def body(i, _):
            for ref, out_ref in zip(refs[:number], refs[number:]):

                def put(at, value, out_ref=out_ref):
                    out_ref[i, at : at + ROWS, :] = value

                interleave(put, lambda spot, ref=ref: ref[i, spot, :], width)

        march(slab, body)

    outs = [f32(slab, width, length)] * number
    return kernel_call(kernel, [], list(arrays), outs, [], 8)


def pack(field, adjoint_field):
    odd = lax.axis_index("depth") % 2
    far = field.shape[0] - HALO
    found = []
    for start in ((1 - odd) * far, odd * far):
        planes = [lax.dynamic_slice_in_dim(v, start, HALO, 0) for v in (field, adjoint_field)]
        found.append(jnp.concatenate(planes, axis=0))
    return found


def refresh(courant, inner_parts, outer_parts, curv, table, plan):
    slab, width, length = courant.shape
    half = inner_parts[0].shape[0]
    number = len(inner_parts)
    cells = slab * width * length * lax.axis_size("depth")

    def kernel(table_ref, plan_ref, c_ref, curv_ref, *rest):
        inner_refs = rest[:number]
        outer_refs = rest[number : 2 * number]
        out_ref = rest[2 * number]
        tail = slice(HALO * width, HALO * width + 8)
        tile = outer_refs[0][tail, :]
        for ref in outer_refs[1:]:
            tile = tile + ref[tail, :]
        level = jnp.sum(tile) / cells + 1e-06
        extra = table_ref[plan_ref[0]] * level
        core = lax.axis_index("shot") % 2
        start = HALO + core * half

        def store(i, value):
            for g in range(width // ROWS):
                spot = pl.ds(g, ROWS, stride=width // ROWS)
                out_ref[i, spot, :] = value[g * ROWS : (g + 1) * ROWS]

        def body(i, _):
            grad = inner_refs[0][i]
            for ref in inner_refs[1:]:
                grad = grad + ref[i]
            store(i, c_ref[start + i] - grad / (curv_ref[i] + extra))

        march(half, body)
        odd = lax.axis_index("depth") % 2
        up = core + odd == 0
        up = (up | (core + odd == 2)).astype(jnp.int32)
        for i in range(HALO):
            rows = slice(i * width, (i + 1) * width)
            grad = outer_refs[0][rows, :]
            for ref in outer_refs[1:]:
                grad = grad + ref[rows, :]
            model = c_ref[up * (slab - HALO) + i]
            store(half + i, model - grad / (curv_ref[half + i] + extra))

    arrays = [courant, curv, *inner_parts, *outer_parts]
    outs = [f32(half + HALO, width, length)]
    return kernel_call(kernel, [table, plan], arrays, outs, [], half)[0]


def assemble(own, other, slab):
    size, width, length = own.shape
    inner = size - HALO

    def kernel(own_ref, other_ref, out_ref, sems):
        core = lax.axis_index("shot") % 2
        up = (lax.axis_index("depth") + core + 1) % 2
        copies = []
        for n, (ref, c, u) in enumerate([(own_ref, core, up), (other_ref, 1 - core, 1 - up)]):
            for m, (first, count, start) in enumerate(
                [(0, inner, HALO + c * inner), (inner, HALO, u * (slab - HALO))]
            ):
                copies.append(
                    pltpu.make_async_copy(
                        ref.at[pl.ds(first, count)],
                        out_ref.at[pl.ds(start, count)],
                        sems.at[2 * n + m],
                    )
                )
        for copy in copies:
            copy.start()
        for copy in copies:
            copy.wait()

    return pl.pallas_call(
        kernel,
        out_shape=f32(slab, width, length),
        in_specs=[VMEM] * 2,
        out_specs=HBM,
        scratch_shapes=[pltpu.SemaphoreType.DMA((4,))],
        compiler_params=params(),
        cost_estimate=cost(8),
    )(own, other)


def exchange(values, side):
    links = []
    for i in range(side, lax.axis_size("depth") - 1, 2):
        links += [(i, i + 1), (i + 1, i)]
    return lax.ppermute(values, "depth", links)


def swap(values, axis, bit):
    count = lax.axis_size(axis)
    return lax.ppermute(values, axis, [(i, i ^ bit) for i in range(count)])


def sum_of(values, other, after):
    def kernel(values_ref, other_ref, _, out_ref):
        def body(i, _):
            out_ref[i] = values_ref[i] + other_ref[i]

        march(values.shape[0], body)

    return kernel_call(kernel, [], [values, other, after], [f32(*values.shape)], [], 8)[0]


def total_parts(keep, send, after=None):
    parts = [keep, swap(send, "shot", 1)]
    bit = 2
    while bit < lax.axis_size("shot"):
        if after is not None and bit == 2:
            here = sum_of(*parts, after)
        else:
            here = parts[0] + parts[1]
        parts = [here, swap(here, "shot", bit)]
        bit *= 2
    return parts


def on_device(
    field_prev,
    field_now,
    adjoint_next,
    adjoint_after,
    courant,
    wavelet,
    source_cell,
    receiver_cell,
    observed,
    damping_table,
    plan_step,
):
    slab, width, length = courant.shape
    halos = [exchange(v, side) for side, v in enumerate(pack(field_now[0], adjoint_next[0]))]
    first_halos = halos
    start, before, courant = interleaved(field_now[0], field_prev[0], courant)
    first, second = interleaved(adjoint_next[0], adjoint_after[0])
    listing = list_receivers(receiver_cell[0], slab, width, length)
    traces = observed[0]
    old, cur = (before,), (start,)
    laps, fields = [], []
    after = [listing]
    for step in range(STEPS):
        core = forward(2, step, (), cur, old, courant, (), wavelet, source_cell)
        after = after + [core[0]]
        if step == STEPS - 1:
            core_adj = adjoint(
                2, step, (), 0, (first,), (second,), courant, core[0], (), listing, traces
            )
            after = after + [core_adj]
        parts, coming = [], []
        for side in (0, 1):
            edge = forward(
                side, step, halos[side : side + 1], cur, old, courant, after, wavelet, source_cell
            )
            parts.append(edge)
            if step < STEPS - 1:
                coming.append(exchange(edge[0], side))
                after = [edge[0]]
        laps.append((parts[0][1], parts[1][1], core[1]))
        fields.append((parts[0][0], parts[1][0], core[0]))
        old, cur = cur, fields[-1]
        halos, after = coming, []
    old, cur = (second,), (first,)
    halos, halo_at = first_halos, HALO
    adjoints = []
    bit = 1
    extra = []
    for step in range(STEPS - 1, 0, -1):
        field = fields[step]
        if step < STEPS - 1:
            core_adj = adjoint(2, step, (), 0, cur, old, courant, field[2], (), listing, traces)
        after = extra + [core_adj]
        edges, coming = [], []
        for side in (0, 1):
            edge = adjoint(
                side, step, halos[side : side + 1], halo_at, cur, old, courant, field[side], after,
                listing, traces,
            )
            edges.append(edge)
            coming.append(exchange(edge, side))
            after = [edge]
        adjoints.insert(0, (edges[0], edges[1], core_adj))
        old, cur = cur, adjoints[0]
        halos, halo_at = coming, 0
        if step == STEPS - 1:
            keep, send, tile = curvature(laps, edges[1])
        else:
            tile = tile + tiles
        if step == STEPS - 2:
            curv = sum(total_parts(keep, send, edges[1]))
        tiles = swap(tile, "depth", bit)
        bit *= 2
        extra = [tiles]
    while bit < lax.axis_size("depth"):
        tile = tile + tiles
        tiles = swap(tile, "depth", bit)
        bit *= 2
    found = []
    for side, both, other in ((2, [], 0), (0, [], 0), (1, [tile, tiles], 1)):
        found.append(
            adjoint_last(
                side, halos[side : side + 1], cur, old, courant, fields[0][side],
                [lap[side] for lap in laps], [a[side] for a in adjoints], both,
                found[1] if other else [], [curv] if side == 2 else found[0][:1], listing, traces,
            )
        )
    inner_parts = total_parts(*found[0])
    outer_parts = total_parts(*found[2])
    own = refresh(courant, inner_parts, outer_parts, curv, damping_table, plan_step)
    return assemble(own, swap(own, "shot", 1), slab)


def solution(mesh):
    in_specs = (
        P("shot", "depth", None, None),
        P("shot", "depth", None, None),
        P("shot", "depth", None, None),
        P("shot", "depth", None, None),
        P("depth", None, None),
        P("shot", None),
        P("shot"),
        P("shot", None),
        P("shot", None, None),
        P(),
        P(),
    )
    out_specs = P("depth", None, None)
    return jax.shard_map(
        on_device, mesh=mesh, in_specs=in_specs, out_specs=out_specs, check_vma=False
    )
```

profile of v0, /device:TPU:0, one launch (start us, length us, event | category | flops | bytes accessed | tf_op | source)
XLA Modules:
  0.0 101.1 jit_solution(1913435258346033683)
XLA Ops:
  0.0 1.3 %dynamic-slice_bitcast_fusion = (f32[4,64,128]{2,1,0:T(8,128)S(1)}, f32[4,64,128]{2,1,0:T(8,128)S(1)}, f32[4,64,128]{2,1,0:T(8,128)S(1)}, f32[4,64,128]{2,1,0:T(8,128)S(1)}) fusion(f32[1,32,64,128]{3,2,1,0:T(8,128)} %param.13, s32[]{:T(128)S(6)} %select_n.17, s32[]{:T(128)S(6)} %select_n.16, f32[1,32,64,128]{3,2,1,0:T(8,128)} %param.12), kind=kLoop, calls=%fused_computation.2 | loop fusion | bytes 1048584 | tf_op jit(solution)/shard_map/dynamic_slice | solution.py:443
  1.3 3.0 %collective-permute-start = (f32[8,64,128]{2,1,0:T(8,128)S(1)}, f32[8,64,128]{2,1,0:T(8,128)S(1)}, u32[]{:S(2)}, u32[]{:S(2)}) collective-permute-start(f32[8,64,128]{2,1,0:T(8,128)S(1)} %pad_maximum_fusion), channel_id=1, source_target_pairs={{0,1},{1,0},{2,3},{3,2},{4,5},{5,4},{6,7},{7,6},{8,9},{9,8},{10,11... | collective-permute-start | bytes 786440 | tf_op jit(solution)/shard_map/ppermute | solution.py:534
  4.4 0.7 collective-permute-start.2
  5.1 3.0 %shard_map.110.refs_4_.list_ref = s32[7,256]{1,0:T(8,128)S(1)} custom-call(s32[128]{0:T(128)S(1)} %bitcast.30), custom_call_target="tpu_custom_call" | custom-call | flops 80000 | bytes 8192 | tf_op jit(solution)/shard_map/pallas_call | solution.py:409
  8.1 1.2 %copy-done.3 = f32[32,64,128]{2,1,0:T(8,128)S(1)} copy-done((f32[32,64,128]{2,1,0:T(8,128)S(1)}, f32[32,64,128]{2,1,0:T(8,128)}, u32[]{:S(2)}) %copy-start.3) | copy-done | bytes 1048600
  9.3 0.6 shard_map.109
  10.6 0.6 copy-done.6
  11.3 2.2 %shard_map.111 = (f32[24,64,128]{2,1,0:T(8,128)S(1)}, f32[24,64,128]{2,1,0:T(8,128)S(1)}) custom-call(f32[1,4]{1,0:T(1,128)S(1)} %copy-done.6, s32[1]{0:T(128)S(6)} %copy.12.source_ref, f32[32,64,128]{2,1,0:T(8,128)S(1)} %get-tuple-element.42.refs_0_.refs_1_.refs_3_.refs_4_, f32[32,64,128]{2,1,0:T(8,128)S(1)} %get-tuple-element.43.refs_1_.refs_2_, ...), custom_call_target="tpu_custom_call" | custom-call | flops 240000 | bytes 24576 | tf_op jit(solution)/shard_map/pallas_call | solution.py:156
  13.4 2.1 %collective-permute-done.refs_0_ = f32[8,64,128]{2,1,0:T(8,128)S(1)} collective-permute-done((f32[8,64,128]{2,1,0:T(8,128)S(1)}, f32[8,64,128]{2,1,0:T(8,128)S(1)}, u32[]{:S(2)}, u32[]{:S(2)}) %collective-permute-start) | collective-permute-done | bytes 262176 | tf_op jit(solution)/shard_map/ppermute | solution.py:534
  15.5 0.9 shard_map.112
  16.5 2.5 %collective-permute-start.1 = (f32[4,64,128]{2,1,0:T(8,128)S(1)}, f32[4,64,128]{2,1,0:T(8,128)S(1)}, u32[]{:S(2)}, u32[]{:S(2)}) collective-permute-start(f32[4,64,128]{2,1,0:T(8,128)S(1)} %get-tuple-element.46.refs_4_.refs_0_.refs_1_.refs_3_.refs_8_), channel_id=1, source_target_pairs={{0,1},{1,0},{2,3},{3,2},{4,5},{5,4},{6,7},{7,6},{8,9},{9,8},{10,11... | collective-permute-start | bytes 393224 | tf_op jit(solution)/shard_map/ppermute | solution.py:534
  19.0 0.9 shard_map.113
  20.0 0.7 collective-permute-start.4
  20.6 2.2 %shard_map.114 = (f32[24,64,128]{2,1,0:T(8,128)S(1)}, f32[24,64,128]{2,1,0:T(8,128)S(1)}) custom-call(f32[1,4]{1,0:T(1,128)S(1)} %copy-done.6, s32[1]{0:T(128)S(6)} %copy.12.source_ref, f32[4,64,128]{2,1,0:T(8,128)S(1)} %get-tuple-element.46.refs_4_.refs_0_.refs_1_.refs_3_.refs_8_, ...), custom_call_target="tpu_custom_call" | custom-call | flops 240000 | bytes 24576 | tf_op jit(solution)/shard_map/pallas_call | solution.py:156
  22.8 0.9 shard_map.115
  23.8 4.3 %collective-permute-start.3 = (f32[4,64,128]{2,1,0:T(8,128)S(1)}, f32[4,64,128]{2,1,0:T(8,128)S(1)}, u32[]{:S(2)}, u32[]{:S(2)}) collective-permute-start(f32[4,64,128]{2,1,0:T(8,128)S(1)} %get-tuple-element.50.refs_6_.refs_0_.refs_1_.refs_3_.refs_4_.refs_8_), channel_id=1, source_target_pairs={{0,1},{1,0},{2,3},{3,2},{4,5},{5,4},{6,7},{7,6},{8,9},{9,8},{10,11... | collective-permute-start | bytes 393224 | tf_op jit(solution)/shard_map/ppermute | solution.py:534
  28.1 0.9 shard_map.116
  29.0 0.7 collective-permute-start.6
  29.7 2.2 %shard_map.117 = (f32[24,64,128]{2,1,0:T(8,128)S(1)}, f32[24,64,128]{2,1,0:T(8,128)S(1)}) custom-call(f32[1,4]{1,0:T(1,128)S(1)} %copy-done.6, s32[1]{0:T(128)S(6)} %copy.12.source_ref, f32[4,64,128]{2,1,0:T(8,128)S(1)} %get-tuple-element.50.refs_6_.refs_0_.refs_1_.refs_3_.refs_4_.refs_8_, ...), custom_call_target="tpu_custom_call" | custom-call | flops 240000 | bytes 24576 | tf_op jit(solution)/shard_map/pallas_call | solution.py:156
  31.9 0.9 shard_map.118
  32.9 4.3 %collective-permute-start.5 = (f32[4,64,128]{2,1,0:T(8,128)S(1)}, f32[4,64,128]{2,1,0:T(8,128)S(1)}, u32[]{:S(2)}, u32[]{:S(2)}) collective-permute-start(f32[4,64,128]{2,1,0:T(8,128)S(1)} %get-tuple-element.54.refs_8_.refs_0_.refs_1_.refs_6_), channel_id=1, source_target_pairs={{0,1},{1,0},{2,3},{3,2},{4,5},{5,4},{6,7},{7,6},{8,9},{9,8},{10,11... | collective-permute-start | bytes 393224 | tf_op jit(solution)/shard_map/ppermute | solution.py:534
  37.2 0.9 shard_map.119
  38.1 0.7 collective-permute-start.7
  38.8 0.4 shard_map.121
  39.2 2.2 %shard_map.120 = (f32[24,64,128]{2,1,0:T(8,128)S(1)}, f32[24,64,128]{2,1,0:T(8,128)S(1)}) custom-call(f32[1,4]{1,0:T(1,128)S(1)} %copy-done.6, s32[1]{0:T(128)S(6)} %copy.12.source_ref, f32[4,64,128]{2,1,0:T(8,128)S(1)} %get-tuple-element.54.refs_8_.refs_0_.refs_1_.refs_6_, f32[4,64,128]{2,1,0:T(8,128)S(1)} %get-tuple-element.55.refs_1_.refs_2_.refs_6_, ...), custom_call_target="tpu_custom_call" | custom-call | flops 240000 | bytes 24576 | tf_op jit(solution)/shard_map/pallas_call | solution.py:156
  41.4 0.7 copy-done.5
  42.1 2.6 %shard_map.122.refs_9_.refs_5_.refs_2_.refs_3_.refs_6_.refs_14_ = f32[24,64,128]{2,1,0:T(8,128)S(1)} custom-call(s32[7,256]{1,0:T(8,128)S(1)} %shard_map.110.refs_4_.list_ref, f32[4,128]{1,0:T(4,128)S(1)} %bitcast.18, f32[32,64,128]{2,1,0:T(8,128)S(1)} %get-tuple-element.57.refs_0_.refs_1_.refs_3_.refs_4_, ...), custom_call_target="tpu_custom_call" | custom-call | flops 240000 | bytes 24576 | tf_op jit(solution)/shard_map/pallas_call | solution.py:156
  44.8 0.9 shard_map.123
  45.7 1.1 %shard_map.125.refs_5_.refs_0_.refs_1_.refs_3_.refs_4_.refs_15_ = f32[4,64,128]{2,1,0:T(8,128)S(1)} custom-call(s32[7,256]{1,0:T(8,128)S(1)} %shard_map.110.refs_4_.list_ref, f32[4,128]{1,0:T(4,128)S(1)} %bitcast.19, f32[8,64,128]{2,1,0:T(8,128)S(1)} %collective-permute-done.refs_0_, f32[32,64,128]{2,1,0:T(8,128)S(1)} %get-tuple-element.57.refs_0_.refs_1_.refs_3_.refs_4_, ...), custom_call_target="tpu_custom_call" | custom-call | flops 40000 | bytes 4096 | tf_op jit(solution)/shard_map/pallas_call | solution.py:156
  46.8 0.9 shard_map.124
  47.7 1.1 %shard_map.126.refs_12_.refs_1_.refs_2_.refs_4_.refs_5_.refs_15_ = f32[4,64,128]{2,1,0:T(8,128)S(1)} custom-call(s32[7,256]{1,0:T(8,128)S(1)} %shard_map.110.refs_4_.list_ref, f32[4,128]{1,0:T(4,128)S(1)} %bitcast.20, f32[8,64,128]{2,1,0:T(8,128)S(1)} %collective-permute-done.2.refs_0_, f32[32,64,128]{2,1,0:T(8,128)S(1)} %get-tuple-element.57.refs_0_.refs_1_.refs_3_.refs_4_, ...), custom_call_target="tpu_custom_call" | custom-call | flops 40000 | bytes 4096 | tf_op jit(solution)/shard_map/pallas_call | solution.py:156
  48.8 0.3 shard_map.127
  49.2 0.1 collective-permute-start.8
  49.3 4.0 %collective-permute-start.10 = (f32[4,64,128]{2,1,0:T(8,128)S(1)}, f32[4,64,128]{2,1,0:T(8,128)S(1)}, u32[]{:S(2)}, u32[]{:S(2)}) collective-permute-start(f32[4,64,128]{2,1,0:T(8,128)S(1)} %shard_map.125.refs_5_.refs_0_.refs_1_.refs_3_.refs_4_.refs_15_), channel_id=1, source_target_pairs={{0,1},{1,0},{2,3},{3,2},{4,5},{5,4},{6,7},{7,6},{8,9},{9,8},{10,11... | collective-permute-start | bytes 393224 | tf_op jit(solution)/shard_map/ppermute | solution.py:534
  53.3 0.7 collective-permute-start.9
  53.9 4.1 %collective-permute-start.11 = (f32[8,128]{1,0:T(8,128)S(1)}, f32[8,128]{1,0:T(8,128)S(1)}, u32[]{:S(2)}, u32[]{:S(2)}) collective-permute-start(f32[8,128]{1,0:T(8,128)S(1)} %get-tuple-element.72), channel_id=1, source_target_pairs={{0,1},{1,0},{2,3},{3,2},{4,5},{5,4},{6,7},{7,6},{8,9},{9,8},{10,11... | collective-permute-start | bytes 12296 | tf_op jit(solution)/shard_map/ppermute | solution.py:539
  58.0 2.6 %shard_map.128.refs_8_.refs_2_.refs_3_.refs_5_.refs_13_.refs_6_ = f32[24,64,128]{2,1,0:T(8,128)S(1)} custom-call(s32[7,256]{1,0:T(8,128)S(1)} %shard_map.110.refs_4_.list_ref, f32[4,128]{1,0:T(4,128)S(1)} %bitcast.21, f32[4,64,128]{2,1,0:T(8,128)S(1)} %shard_map.125.refs_5_.refs_0_.refs_1_.refs_3_.refs_4_.refs_15_, ...), custom_call_target="tpu_custom_call" | custom-call | flops 240000 | bytes 24576 | tf_op jit(solution)/shard_map/pallas_call | solution.py:156
  60.7 1.1 %shard_map.129.refs_7_.refs_0_.refs_1_.refs_3_.refs_4_.refs_14_ = f32[4,64,128]{2,1,0:T(8,128)S(1)} custom-call(s32[7,256]{1,0:T(8,128)S(1)} %shard_map.110.refs_4_.list_ref, f32[4,128]{1,0:T(4,128)S(1)} %bitcast.22, f32[4,64,128]{2,1,0:T(8,128)S(1)} %collective-permute-done.10.refs_0_, ...), custom_call_target="tpu_custom_call" | custom-call | flops 40000 | bytes 4096 | tf_op jit(solution)/shard_map/pallas_call | solution.py:156
  61.8 1.1 %shard_map.130._.refs_1_.refs_2_.refs_4_.refs_5_.refs_14_ = f32[4,64,128]{2,1,0:T(8,128)S(1)} custom-call(s32[7,256]{1,0:T(8,128)S(1)} %shard_map.110.refs_4_.list_ref, f32[4,128]{1,0:T(4,128)S(1)} %bitcast.23, f32[4,64,128]{2,1,0:T(8,128)S(1)} %collective-permute-done.9.refs_0_, ...), custom_call_target="tpu_custom_call" | custom-call | flops 40000 | bytes 4096 | tf_op jit(solution)/shard_map/pallas_call | solution.py:156
  63.0 1.4 %collective-permute-start.12 = (f32[16,64,128]{2,1,0:T(8,128)S(1)}, f32[16,64,128]{2,1,0:T(8,128)S(1)}, u32[]{:S(2)}, u32[]{:S(2)}) collective-permute-start(f32[16,64,128]{2,1,0:T(8,128)S(1)} %shard_map.131), channel_id=1, source_target_pairs={{0,16},{8,24},{16,0},{24,8},{1,17},{9,25},{17,1},{25,9},{2,18},{10... | collective-permute-start | bytes 1572872 | tf_op jit(solution)/shard_map/ppermute | solution.py:539
  64.3 1.5 %collective-permute-start.13 = (f32[4,64,128]{2,1,0:T(8,128)S(1)}, f32[4,64,128]{2,1,0:T(8,128)S(1)}, u32[]{:S(2)}, u32[]{:S(2)}) collective-permute-start(f32[4,64,128]{2,1,0:T(8,128)S(1)} %shard_map.129.refs_7_.refs_0_.refs_1_.refs_3_.refs_4_.refs_14_), channel_id=1, source_target_pairs={{0,1},{1,0},{2,3},{3,2},{4,5},{5,4},{6,7},{7,6},{8,9},{9,8},{10,11... | collective-permute-start | bytes 393224 | tf_op jit(solution)/shard_map/ppermute | solution.py:534
  65.9 0.8 collective-permute-start.15
  66.7 3.2 %collective-permute-start.14 = (f32[8,128]{1,0:T(8,128)S(1)}, f32[8,128]{1,0:T(8,128)S(1)}, u32[]{:S(2)}, u32[]{:S(2)}) collective-permute-start(f32[8,128]{1,0:T(8,128)S(1)} %add.31), channel_id=1, source_target_pairs={{0,2},{1,3},{2,0},{3,1},{4,6},{5,7},{6,4},{7,5},{8,10},{9,11},{10,... | collective-permute-start | bytes 12296 | tf_op jit(solution)/shard_map/ppermute | solution.py:539
  70.0 2.6 %shard_map.132.refs_10_.refs_2_.refs_12_.refs_3_ = f32[24,64,128]{2,1,0:T(8,128)S(1)} custom-call(s32[7,256]{1,0:T(8,128)S(1)} %shard_map.110.refs_4_.list_ref, f32[4,128]{1,0:T(4,128)S(1)} %bitcast.24, f32[4,64,128]{2,1,0:T(8,128)S(1)} %shard_map.129.refs_7_.refs_0_.refs_1_.refs_3_.refs_4_.refs_14_, ...), custom_call_target="tpu_custom_call" | custom-call | flops 240000 | bytes 24576 | tf_op jit(solution)/shard_map/pallas_call | solution.py:156
  72.6 0.1 collective-permute-done.14.refs_9_
  72.7 1.1 %shard_map.133.refs_9_.refs_0_.refs_1_.refs_13_ = f32[4,64,128]{2,1,0:T(8,128)S(1)} custom-call(s32[7,256]{1,0:T(8,128)S(1)} %shard_map.110.refs_4_.list_ref, f32[4,128]{1,0:T(4,128)S(1)} %bitcast.25, f32[4,64,128]{2,1,0:T(8,128)S(1)} %collective-permute-done.13.refs_0_, f32[4,64,128]{2,1,0:T(8,128)S(1)} %shard_map.129.refs_7_.refs_0_.refs_1_.refs_3_.refs_4_.refs_14_, ...), custom_call_target="tpu_custom_call" | custom-call | flops 40000 | bytes 4096 | tf_op jit(solution)/shard_map/pallas_call | solution.py:156
  73.8 1.1 %shard_map.134.refs_1_.refs_2_.refs_13_ = f32[4,64,128]{2,1,0:T(8,128)S(1)} custom-call(s32[7,256]{1,0:T(8,128)S(1)} %shard_map.110.refs_4_.list_ref, f32[4,128]{1,0:T(4,128)S(1)} %bitcast.26, f32[4,64,128]{2,1,0:T(8,128)S(1)} %collective-permute-done.15.refs_0_, f32[4,64,128]{2,1,0:T(8,128)S(1)} %shard_map.129.refs_7_.refs_0_.refs_1_.refs_3_.refs_4_.refs_14_, ...), custom_call_target="tpu_custom_call" | custom-call | flops 40000 | bytes 4096 | tf_op jit(solution)/shard_map/pallas_call | solution.py:156
  74.9 1.5 %collective-permute-done.12 = f32[16,64,128]{2,1,0:T(8,128)S(1)} collective-permute-done((f32[16,64,128]{2,1,0:T(8,128)S(1)}, f32[16,64,128]{2,1,0:T(8,128)S(1)}, u32[]{:S(2)}, u32[]{:S(2)}) %collective-permute-start.12) | collective-permute-done | bytes 524320 | tf_op jit(solution)/shard_map/ppermute | solution.py:539
  76.4 2.9 %shard_map.135 = (f32[12,64,128]{2,1,0:T(8,128)S(1)}, f32[12,64,128]{2,1,0:T(8,128)S(1)}) custom-call(s32[7,256]{1,0:T(8,128)S(1)} %shard_map.110.refs_4_.list_ref, f32[4,128]{1,0:T(4,128)S(1)} %bitcast.27, f32[4,64,128]{2,1,0:T(8,128)S(1)} %shard_map.133.refs_9_.refs_0_.refs_1_.refs_13_, f32[4,64,128]{2,1,0:T(8,128)S(1)} %shard_map.134.refs_1_.refs_2_.refs_13_, ...), custom_call_target="tpu_custom_call" | custom-call | flops 240000 | bytes 24576 | tf_op jit(solution)/shard_map/pallas_call | solution.py:156
  79.3 0.1 collective-permute-start.16
  79.4 0.9 collective-permute-start.20
  80.3 0.7 collective-permute-start.18
  81.0 0.1 collective-permute-done.16
  81.2 1.4 %collective-permute-start.17 = (f32[12,64,128]{2,1,0:T(8,128)S(1)}, f32[12,64,128]{2,1,0:T(8,128)S(1)}, u32[]{:S(2)}, u32[]{:S(2)}) collective-permute-start(f32[12,64,128]{2,1,0:T(8,128)S(1)} %add.32.rest_0_), channel_id=1, source_target_pairs={{0,16},{8,24},{16,0},{24,8},{1,17},{9,25},{17,1},{25,9},{2,18},{10... | collective-permute-start | bytes 1179656 | tf_op jit(solution)/shard_map/ppermute | solution.py:539
  82.5 4.2 %collective-permute-start.19 = (f32[8,128]{1,0:T(8,128)S(1)}, f32[8,128]{1,0:T(8,128)S(1)}, u32[]{:S(2)}, u32[]{:S(2)}) collective-permute-start(f32[8,128]{1,0:T(8,128)S(1)} %add.33.refs_16_), channel_id=1, source_target_pairs={{0,4},{1,5},{2,6},{3,7},{4,0},{5,1},{6,2},{7,3},{8,12},{9,13},{10,... | collective-permute-start | bytes 12296 | tf_op jit(solution)/shard_map/ppermute | solution.py:539
  86.8 1.2 %shard_map.136.refs_18_ = f32[4,64,128]{2,1,0:T(8,128)S(1)} custom-call(s32[7,256]{1,0:T(8,128)S(1)} %shard_map.110.refs_4_.list_ref, f32[4,128]{1,0:T(4,128)S(1)} %bitcast.28, f32[4,64,128]{2,1,0:T(8,128)S(1)} %collective-permute-done.20.refs_0_, f32[4,64,128]{2,1,0:T(8,128)S(1)} %shard_map.133.refs_9_.refs_0_.refs_1_.refs_13_, ...), custom_call_target="tpu_custom_call" | custom-call | flops 40000 | bytes 4096 | tf_op jit(solution)/shard_map/pallas_call | solution.py:156
  87.9 0.9 collective-permute-done.19.refs_17_
  88.8 1.2 %shard_map.137 = (f32[264,128]{1,0:T(8,128)S(1)}, f32[264,128]{1,0:T(8,128)S(1)}) custom-call(s32[7,256]{1,0:T(8,128)S(1)} %shard_map.110.refs_4_.list_ref, f32[4,128]{1,0:T(4,128)S(1)} %bitcast.29, f32[4,64,128]{2,1,0:T(8,128)S(1)} %collective-permute-done.18.refs_0_, f32[4,64,128]{2,1,0:T(8,128)S(1)} %shard_map.133.refs_9_.refs_0_.refs_1_.refs_13_, ...), custom_call_target="tpu_custom_call" | custom-call | flops 40000 | bytes 4096 | tf_op jit(solution)/shard_map/pallas_call | solution.py:156
  90.1 1.3 %collective-permute-done.21 = f32[264,128]{1,0:T(8,128)S(1)} collective-permute-done((f32[264,128]{1,0:T(8,128)S(1)}, f32[264,128]{1,0:T(8,128)S(1)}, u32[]{:S(2)}, u32[]{:S(2)}) %collective-permute-start.21) | collective-permute-done | bytes 135200 | tf_op jit(solution)/shard_map/ppermute | solution.py:539
  91.4 1.5 %collective-permute-start.22 = (f32[264,128]{1,0:T(8,128)S(1)}, f32[264,128]{1,0:T(8,128)S(1)}, u32[]{:S(2)}, u32[]{:S(2)}) collective-permute-start(f32[264,128]{1,0:T(8,128)S(1)} %add.34.rest_2_), channel_id=1, source_target_pairs={{0,16},{8,24},{16,0},{24,8},{1,17},{9,25},{17,1},{25,9},{2,18},{10... | collective-permute-start | bytes 405512 | tf_op jit(solution)/shard_map/ppermute | solution.py:539
  93.6 3.5 %collective-permute-done.22.rest_3_ = f32[264,128]{1,0:T(8,128)S(1)} collective-permute-done((f32[264,128]{1,0:T(8,128)S(1)}, f32[264,128]{1,0:T(8,128)S(1)}, u32[]{:S(2)}, u32[]{:S(2)}) %collective-permute-start.22) | collective-permute-done | bytes 135200 | tf_op jit(solution)/shard_map/ppermute | solution.py:539
  97.1 0.8 shard_map.138.own_ref
  98.0 1.9 %collective-permute-done.23.other_ref = f32[16,64,128]{2,1,0:T(8,128)S(1)} collective-permute-done((f32[16,64,128]{2,1,0:T(8,128)S(1)}, f32[16,64,128]{2,1,0:T(8,128)S(1)}, u32[]{:S(2)}, u32[]{:S(2)}) %collective-permute-start.23) | collective-permute-done | bytes 524320 | tf_op jit(solution)/shard_map/ppermute | solution.py:539
  99.9 1.0 shard_map.139
  (41 shorter events, 0.5 us)
Async XLA Ops:
  0.0 8.1 %copy-start = (f32[1,32,64,128]{3,2,1,0:T(8,128)S(1)}, f32[1,32,64,128]{3,2,1,0:T(8,128)}, u32[]{:S(2)}) copy-start(f32[1,32,64,128]{3,2,1,0:T(8,128)} %param.12) | copy-start | bytes 3145732
  0.0 8.1 %copy-start.2 = (f32[1,32,64,128]{3,2,1,0:T(8,128)S(1)}, f32[1,32,64,128]{3,2,1,0:T(8,128)}, u32[]{:S(2)}) copy-start(f32[1,32,64,128]{3,2,1,0:T(8,128)} %param.11) | copy-start | bytes 3145732
  1.3 14.2 %collective-permute-start = (f32[8,64,128]{2,1,0:T(8,128)S(1)}, f32[8,64,128]{2,1,0:T(8,128)S(1)}, u32[]{:S(2)}, u32[]{:S(2)}) collective-permute-start(f32[8,64,128]{2,1,0:T(8,128)S(1)} %pad_maximum_fusion), channel_id=1, source_target_pairs={{0,1},{1,0},{2,3},{3,2},{4,5},{5,4},{6,7},{7,6},{8,9},{9,8},{10,11... | collective-permute-start | bytes 786440 | tf_op jit(solution)/shard_map/ppermute | solution.py:534
  4.4 0.7 copy-start.8
  4.4 14.6 %collective-permute-start.2 = (f32[8,64,128]{2,1,0:T(8,128)S(1)}, f32[8,64,128]{2,1,0:T(8,128)S(1)}, u32[]{:S(2)}, u32[]{:S(2)}) collective-permute-start(f32[8,64,128]{2,1,0:T(8,128)S(1)} %pad_maximum_fusion.1), channel_id=1, source_target_pairs={{1,2},{2,1},{3,4},{4,3},{5,6},{6,5},{9,10},{10,9},{11,12},{12,11},... | collective-permute-start | bytes 786440 | tf_op jit(solution)/shard_map/ppermute | solution.py:534
  8.1 1.2 %copy-start.3 = (f32[32,64,128]{2,1,0:T(8,128)S(1)}, f32[32,64,128]{2,1,0:T(8,128)}, u32[]{:S(2)}) copy-start(f32[32,64,128]{2,1,0:T(8,128)} %refs_2_.1) | copy-start | bytes 3145732
  10.6 0.7 copy-start.6
  16.5 6.4 %collective-permute-start.1 = (f32[4,64,128]{2,1,0:T(8,128)S(1)}, f32[4,64,128]{2,1,0:T(8,128)S(1)}, u32[]{:S(2)}, u32[]{:S(2)}) collective-permute-start(f32[4,64,128]{2,1,0:T(8,128)S(1)} %get-tuple-element.46.refs_4_.refs_0_.refs_1_.refs_3_.refs_8_), channel_id=1, source_target_pairs={{0,1},{1,0},{2,3},{3,2},{4,5},{5,4},{6,7},{7,6},{8,9},{9,8},{10,11... | collective-permute-start | bytes 393224 | tf_op jit(solution)/shard_map/ppermute | solution.py:534
  20.0 8.1 %collective-permute-start.4 = (f32[4,64,128]{2,1,0:T(8,128)S(1)}, f32[4,64,128]{2,1,0:T(8,128)S(1)}, u32[]{:S(2)}, u32[]{:S(2)}) collective-permute-start(f32[4,64,128]{2,1,0:T(8,128)S(1)} %get-tuple-element.47.refs_1_.refs_2_.refs_4_.refs_5_.refs_8_), channel_id=1, source_target_pairs={{1,2},{2,1},{3,4},{4,3},{5,6},{6,5},{9,10},{10,9},{11,12},{12,11},... | collective-permute-start | bytes 393224 | tf_op jit(solution)/shard_map/ppermute | solution.py:534
  23.8 8.1 %collective-permute-start.3 = (f32[4,64,128]{2,1,0:T(8,128)S(1)}, f32[4,64,128]{2,1,0:T(8,128)S(1)}, u32[]{:S(2)}, u32[]{:S(2)}) collective-permute-start(f32[4,64,128]{2,1,0:T(8,128)S(1)} %get-tuple-element.50.refs_6_.refs_0_.refs_1_.refs_3_.refs_4_.refs_8_), channel_id=1, source_target_pairs={{0,1},{1,0},{2,3},{3,2},{4,5},{5,4},{6,7},{7,6},{8,9},{9,8},{10,11... | collective-permute-start | bytes 393224 | tf_op jit(solution)/shard_map/ppermute | solution.py:534
  29.0 8.2 %collective-permute-start.6 = (f32[4,64,128]{2,1,0:T(8,128)S(1)}, f32[4,64,128]{2,1,0:T(8,128)S(1)}, u32[]{:S(2)}, u32[]{:S(2)}) collective-permute-start(f32[4,64,128]{2,1,0:T(8,128)S(1)} %get-tuple-element.51.refs_1_.refs_2_.refs_4_.refs_5_.refs_8_), channel_id=1, source_target_pairs={{1,2},{2,1},{3,4},{4,3},{5,6},{6,5},{9,10},{10,9},{11,12},{12,11},... | collective-permute-start | bytes 393224 | tf_op jit(solution)/shard_map/ppermute | solution.py:534
  32.8 6.0 %copy-start.1 = (f32[1,32,64,128]{3,2,1,0:T(8,128)S(1)}, f32[1,32,64,128]{3,2,1,0:T(8,128)}, u32[]{:S(2)}) copy-start(f32[1,32,64,128]{3,2,1,0:T(8,128)} %param.13) | copy-start | bytes 3145732
  32.8 6.0 %copy-start.4 = (f32[1,32,64,128]{3,2,1,0:T(8,128)S(1)}, f32[1,32,64,128]{3,2,1,0:T(8,128)}, u32[]{:S(2)}) copy-start(f32[1,32,64,128]{3,2,1,0:T(8,128)} %param.14) | copy-start | bytes 3145732
  32.9 11.9 %collective-permute-start.5 = (f32[4,64,128]{2,1,0:T(8,128)S(1)}, f32[4,64,128]{2,1,0:T(8,128)S(1)}, u32[]{:S(2)}, u32[]{:S(2)}) collective-permute-start(f32[4,64,128]{2,1,0:T(8,128)S(1)} %get-tuple-element.54.refs_8_.refs_0_.refs_1_.refs_6_), channel_id=1, source_target_pairs={{0,1},{1,0},{2,3},{3,2},{4,5},{5,4},{6,7},{7,6},{8,9},{9,8},{10,11... | collective-permute-start | bytes 393224 | tf_op jit(solution)/shard_map/ppermute | solution.py:534
  38.1 8.7 %collective-permute-start.7 = (f32[4,64,128]{2,1,0:T(8,128)S(1)}, f32[4,64,128]{2,1,0:T(8,128)S(1)}, u32[]{:S(2)}, u32[]{:S(2)}) collective-permute-start(f32[4,64,128]{2,1,0:T(8,128)S(1)} %get-tuple-element.55.refs_1_.refs_2_.refs_6_), channel_id=1, source_target_pairs={{1,2},{2,1},{3,4},{4,3},{5,6},{6,5},{9,10},{10,9},{11,12},{12,11},... | collective-permute-start | bytes 393224 | tf_op jit(solution)/shard_map/ppermute | solution.py:534
  41.4 0.7 copy-start.5
  49.2 13.7 %collective-permute-start.8 = (f32[16,64,128]{2,1,0:T(8,128)S(1)}, f32[16,64,128]{2,1,0:T(8,128)S(1)}, u32[]{:S(2)}, u32[]{:S(2)}) collective-permute-start(f32[16,64,128]{2,1,0:T(8,128)S(1)} %get-tuple-element.71), channel_id=1, source_target_pairs={{0,8},{8,0},{16,24},{24,16},{1,9},{9,1},{17,25},{25,17},{2,10},{10... | collective-permute-start | bytes 1572872 | tf_op jit(solution)/shard_map/ppermute | solution.py:539
  49.3 11.4 %collective-permute-start.10 = (f32[4,64,128]{2,1,0:T(8,128)S(1)}, f32[4,64,128]{2,1,0:T(8,128)S(1)}, u32[]{:S(2)}, u32[]{:S(2)}) collective-permute-start(f32[4,64,128]{2,1,0:T(8,128)S(1)} %shard_map.125.refs_5_.refs_0_.refs_1_.refs_3_.refs_4_.refs_15_), channel_id=1, source_target_pairs={{0,1},{1,0},{2,3},{3,2},{4,5},{5,4},{6,7},{7,6},{8,9},{9,8},{10,11... | collective-permute-start | bytes 393224 | tf_op jit(solution)/shard_map/ppermute | solution.py:534
  53.3 8.5 %collective-permute-start.9 = (f32[4,64,128]{2,1,0:T(8,128)S(1)}, f32[4,64,128]{2,1,0:T(8,128)S(1)}, u32[]{:S(2)}, u32[]{:S(2)}) collective-permute-start(f32[4,64,128]{2,1,0:T(8,128)S(1)} %shard_map.126.refs_12_.refs_1_.refs_2_.refs_4_.refs_5_.refs_15_), channel_id=1, source_target_pairs={{1,2},{2,1},{3,4},{4,3},{5,6},{6,5},{9,10},{10,9},{11,12},{12,11},... | collective-permute-start | bytes 393224 | tf_op jit(solution)/shard_map/ppermute | solution.py:534
  53.9 6.7 %collective-permute-start.11 = (f32[8,128]{1,0:T(8,128)S(1)}, f32[8,128]{1,0:T(8,128)S(1)}, u32[]{:S(2)}, u32[]{:S(2)}) collective-permute-start(f32[8,128]{1,0:T(8,128)S(1)} %get-tuple-element.72), channel_id=1, source_target_pairs={{0,1},{1,0},{2,3},{3,2},{4,5},{5,4},{6,7},{7,6},{8,9},{9,8},{10,11... | collective-permute-start | bytes 12296 | tf_op jit(solution)/shard_map/ppermute | solution.py:539
  63.0 13.4 %collective-permute-start.12 = (f32[16,64,128]{2,1,0:T(8,128)S(1)}, f32[16,64,128]{2,1,0:T(8,128)S(1)}, u32[]{:S(2)}, u32[]{:S(2)}) collective-permute-start(f32[16,64,128]{2,1,0:T(8,128)S(1)} %shard_map.131), channel_id=1, source_target_pairs={{0,16},{8,24},{16,0},{24,8},{1,17},{9,25},{17,1},{25,9},{2,18},{10... | collective-permute-start | bytes 1572872 | tf_op jit(solution)/shard_map/ppermute | solution.py:539
  64.3 8.4 %collective-permute-start.13 = (f32[4,64,128]{2,1,0:T(8,128)S(1)}, f32[4,64,128]{2,1,0:T(8,128)S(1)}, u32[]{:S(2)}, u32[]{:S(2)}) collective-permute-start(f32[4,64,128]{2,1,0:T(8,128)S(1)} %shard_map.129.refs_7_.refs_0_.refs_1_.refs_3_.refs_4_.refs_14_), channel_id=1, source_target_pairs={{0,1},{1,0},{2,3},{3,2},{4,5},{5,4},{6,7},{7,6},{8,9},{9,8},{10,11... | collective-permute-start | bytes 393224 | tf_op jit(solution)/shard_map/ppermute | solution.py:534
  65.9 7.9 %collective-permute-start.15 = (f32[4,64,128]{2,1,0:T(8,128)S(1)}, f32[4,64,128]{2,1,0:T(8,128)S(1)}, u32[]{:S(2)}, u32[]{:S(2)}) collective-permute-start(f32[4,64,128]{2,1,0:T(8,128)S(1)} %shard_map.130._.refs_1_.refs_2_.refs_4_.refs_5_.refs_14_), channel_id=1, source_target_pairs={{1,2},{2,1},{3,4},{4,3},{5,6},{6,5},{9,10},{10,9},{11,12},{12,11},... | collective-permute-start | bytes 393224 | tf_op jit(solution)/shard_map/ppermute | solution.py:534
  66.7 6.0 %collective-permute-start.14 = (f32[8,128]{1,0:T(8,128)S(1)}, f32[8,128]{1,0:T(8,128)S(1)}, u32[]{:S(2)}, u32[]{:S(2)}) collective-permute-start(f32[8,128]{1,0:T(8,128)S(1)} %add.31), channel_id=1, source_target_pairs={{0,2},{1,3},{2,0},{3,1},{4,6},{5,7},{6,4},{7,5},{8,10},{9,11},{10,... | collective-permute-start | bytes 12296 | tf_op jit(solution)/shard_map/ppermute | solution.py:539
  79.3 1.8 %collective-permute-start.16 = (f32[12,64,128]{2,1,0:T(8,128)S(1)}, f32[12,64,128]{2,1,0:T(8,128)S(1)}, u32[]{:S(2)}, u32[]{:S(2)}) collective-permute-start(f32[12,64,128]{2,1,0:T(8,128)S(1)} %get-tuple-element.74), channel_id=1, source_target_pairs={{0,8},{8,0},{16,24},{24,16},{1,9},{9,1},{17,25},{25,17},{2,10},{10... | collective-permute-start | bytes 1179656 | tf_op jit(solution)/shard_map/ppermute | solution.py:539
  79.4 7.3 %collective-permute-start.20 = (f32[4,64,128]{2,1,0:T(8,128)S(1)}, f32[4,64,128]{2,1,0:T(8,128)S(1)}, u32[]{:S(2)}, u32[]{:S(2)}) collective-permute-start(f32[4,64,128]{2,1,0:T(8,128)S(1)} %shard_map.133.refs_9_.refs_0_.refs_1_.refs_13_), channel_id=1, source_target_pairs={{0,1},{1,0},{2,3},{3,2},{4,5},{5,4},{6,7},{7,6},{8,9},{9,8},{10,11... | collective-permute-start | bytes 393224 | tf_op jit(solution)/shard_map/ppermute | solution.py:534
  80.3 8.5 %collective-permute-start.18 = (f32[4,64,128]{2,1,0:T(8,128)S(1)}, f32[4,64,128]{2,1,0:T(8,128)S(1)}, u32[]{:S(2)}, u32[]{:S(2)}) collective-permute-start(f32[4,64,128]{2,1,0:T(8,128)S(1)} %shard_map.134.refs_1_.refs_2_.refs_13_), channel_id=1, source_target_pairs={{1,2},{2,1},{3,4},{4,3},{5,6},{6,5},{9,10},{10,9},{11,12},{12,11},... | collective-permute-start | bytes 393224 | tf_op jit(solution)/shard_map/ppermute | solution.py:534
  81.2 16.0 %collective-permute-start.17 = (f32[12,64,128]{2,1,0:T(8,128)S(1)}, f32[12,64,128]{2,1,0:T(8,128)S(1)}, u32[]{:S(2)}, u32[]{:S(2)}) collective-permute-start(f32[12,64,128]{2,1,0:T(8,128)S(1)} %add.32.rest_0_), channel_id=1, source_target_pairs={{0,16},{8,24},{16,0},{24,8},{1,17},{9,25},{17,1},{25,9},{2,18},{10... | collective-permute-start | bytes 1179656 | tf_op jit(solution)/shard_map/ppermute | solution.py:539
  82.5 6.2 %collective-permute-start.19 = (f32[8,128]{1,0:T(8,128)S(1)}, f32[8,128]{1,0:T(8,128)S(1)}, u32[]{:S(2)}, u32[]{:S(2)}) collective-permute-start(f32[8,128]{1,0:T(8,128)S(1)} %add.33.refs_16_), channel_id=1, source_target_pairs={{0,4},{1,5},{2,6},{3,7},{4,0},{5,1},{6,2},{7,3},{8,12},{9,13},{10,... | collective-permute-start | bytes 12296 | tf_op jit(solution)/shard_map/ppermute | solution.py:539
  90.0 1.4 %collective-permute-start.21 = (f32[264,128]{1,0:T(8,128)S(1)}, f32[264,128]{1,0:T(8,128)S(1)}, u32[]{:S(2)}, u32[]{:S(2)}) collective-permute-start(f32[264,128]{1,0:T(8,128)S(1)} %get-tuple-element.76), channel_id=1, source_target_pairs={{0,8},{8,0},{16,24},{24,16},{1,9},{9,1},{17,25},{25,17},{2,10},{10... | collective-permute-start | bytes 405512 | tf_op jit(solution)/shard_map/ppermute | solution.py:539
  91.4 5.7 %copy-start.7 = (f32[64]{0:T(128)S(1)}, f32[64]{0:T(128)}, u32[]{:S(2)}) copy-start(f32[64]{0:T(128)} %table_ref.1) | copy-start | bytes 772
  91.4 5.7 %collective-permute-start.22 = (f32[264,128]{1,0:T(8,128)S(1)}, f32[264,128]{1,0:T(8,128)S(1)}, u32[]{:S(2)}, u32[]{:S(2)}) collective-permute-start(f32[264,128]{1,0:T(8,128)S(1)} %add.34.rest_2_), channel_id=1, source_target_pairs={{0,16},{8,24},{16,0},{24,8},{1,17},{9,25},{17,1},{25,9},{2,18},{10... | collective-permute-start | bytes 405512 | tf_op jit(solution)/shard_map/ppermute | solution.py:539
  98.0 2.0 %collective-permute-start.23 = (f32[16,64,128]{2,1,0:T(8,128)S(1)}, f32[16,64,128]{2,1,0:T(8,128)S(1)}, u32[]{:S(2)}, u32[]{:S(2)}) collective-permute-start(f32[16,64,128]{2,1,0:T(8,128)S(1)} %shard_map.138.own_ref), channel_id=1, source_target_pairs={{0,8},{8,0},{16,24},{24,16},{1,9},{9,1},{17,25},{25,17},{2,10},{10... | collective-permute-start | bytes 1572872 | tf_op jit(solution)/shard_map/ppermute | solution.py:539
where the time goes:
time: 101 us
  Pallas kernels  41.9 us (41%)
  starting transfers between devices  41.7 us (41%)
  waiting for transfers between devices  11.5 us (11%)
  local copies, waits for them, and re-layouts  3.86 us (4%)
  between operations  1.97 us (2%)
    pallas_call x29, Pallas kernels, kernel_call(): pl.pallas_call(kernel, out_shape=tuple(outs), in_specs=[SMEM] * len(small...  37.9 us
    ppermute x14, starting transfers between devices, exchange(): return lax.ppermute(values, 'depth', links)  25.5 us
    ppermute x10, starting transfers between devices, swap(): return lax.ppermute(values, axis, [(i, i ^ bit) for i in range(count)])  16.1 us
    ppermute x10, waiting for transfers between devices, swap(): return lax.ppermute(values, axis, [(i, i ^ bit) for i in range(count)])  9.36 us
    pallas_call x1, Pallas kernels, list_receivers(): pl.pallas_call(kernel, out_shape=jax.ShapeDtypeStruct((7, 2 * count), jnp...  3.01 us
    unnamed x18, local copies, waits for them, and re-layouts  2.58 us
    ppermute x14, waiting for transfers between devices, exchange(): return lax.ppermute(values, 'depth', links)  2.13 us
  transfers between devices with their start and end apart: 24, of which 8 were waited for; matrix products, arithmetic and copies ran while one was open for 0% of the time, Pallas kernels for 34%

commit v1 on v0

v1 whole, which is shorter than its diff:
```python
import jax
import jax.numpy as jnp
from jax import lax
from jax.experimental import pallas as pl
from jax.experimental.pallas import tpu as pltpu
from jax.sharding import PartitionSpec as P

STEPS = 4
HALO = 4
ROWS = 8
PAD = HALO * ROWS

coeffs = (-205.0 / 72.0, 8.0 / 5.0, -1.0 / 5.0, 8.0 / 315.0, -1.0 / 560.0)

VMEM = pl.BlockSpec(memory_space=pltpu.VMEM)
SMEM = pl.BlockSpec(memory_space=pltpu.SMEM)
HBM = pl.BlockSpec(memory_space=pltpu.HBM)


def f32(*shape):
    return jax.ShapeDtypeStruct(shape, jnp.float32)


def params():
    return pltpu.CompilerParams(vmem_limit_bytes=6 * 2**20)


def cost(planes):
    return pl.CostEstimate(
        flops=planes * 10**4, bytes_accessed=planes * 2**10, transcendentals=0
    )


def split(value, size):
    if size & (size - 1) == 0:
        return value >> (size.bit_length() - 1), value & (size - 1)
    return value // size, value % size


def spread(x, width):
    s, g = split(x, width // ROWS)
    return g * ROWS + s


def interleave(put, get, width):
    for g in range(width // ROWS):
        put(g * ROWS, get(pl.ds(g, ROWS, stride=width // ROWS)))


def margins(pad, first, count, width):
    length = pad.shape[2]
    place = lax.broadcasted_iota(jnp.int32, (ROWS, length), 0)

    def body(i, _):
        p = first + i
        for j in range(HALO):
            at = j * ROWS
            low = pltpu.roll(pad[p, width + at : width + at + ROWS, :], 1, 0)
            pad[p, at : at + ROWS, :] = jnp.where(place == 0, 0.0, low)
            top = pltpu.roll(pad[p, PAD + at : PAD + at + ROWS, :], ROWS - 1, 0)
            beyond = PAD + width + at
            pad[p, beyond : beyond + ROWS, :] = jnp.where(place == ROWS - 1, 0.0, top)

    march(count, body)


def fill(pad, base, pieces, width):
    top = base + pad.shape[0]
    for ref, origin in pieces:
        begin = max(base, origin)
        end = min(top, origin + ref.shape[0])
        if end > begin:
            pad[begin - base : end - base, PAD : PAD + width, :] = ref[begin - origin : end - origin]


def fill_halo(pad, at, ref, ref_at, natural, width):
    odd = lax.axis_index("depth") % 2
    for i in range(HALO):
        if natural:

            def put(row, value, i=i):
                pad[at + i, PAD + row : PAD + row + ROWS, :] = value

            source = ref_at + jnp.where(odd == 1, i, HALO - 1 - i)
            interleave(put, lambda spot, source=source: ref[source, spot, :], width)
        else:
            pad[at + i, PAD : PAD + width, :] = ref[HALO - 1 - i]


def find(pieces, plane):
    for ref, origin in pieces:
        if origin <= plane < origin + ref.shape[0]:
            return ref, plane - origin


def columns(pad, along_ref, width):
    planes, _, length = along_ref.shape
    apart = lax.broadcasted_iota(jnp.int32, (length, length), 0)
    apart = jnp.abs(apart - lax.broadcasted_iota(jnp.int32, (length, length), 1))
    band = jnp.where(apart == 0, 3.0 * coeffs[0], 0.0)
    for k in range(1, 5):
        band = jnp.where(apart == k, coeffs[k], band)
    size = HALO if planes % (2 * HALO) else 2 * HALO
    for begin in range(0, planes, size):
        block = pad[HALO + begin : HALO + begin + size, PAD : PAD + width, :]
        product = jnp.dot(
            block.reshape(size * width, length),
            band,
            precision=lax.Precision.HIGHEST,
            preferred_element_type=jnp.float32,
        )
        along_ref[begin : begin + size] = product.reshape(size, width, length)


def stencil(pad, p, width, result):
    rows = slice(PAD, PAD + width)
    plane = pad[p]
    for k in range(1, 5):
        along = pad[p + k, rows, :] + pad[p - k, rows, :]
        along = along + plane[PAD + k * ROWS : PAD + k * ROWS + width]
        along = along + plane[PAD - k * ROWS : PAD - k * ROWS + width]
        result = result + coeffs[k] * along
    return plane[rows], result


def fold(values):
    width, length = values.shape
    return jnp.sum(values.reshape(width // 8, 8, length), axis=0)


def march(count, body, carry=None):
    return lax.fori_loop(0, count, body, carry, unroll=4 if count % 4 == 0 else 2)


def kernel_call(kernel, small, arrays, outs, scratch, planes):
    return pl.pallas_call(
        kernel,
        out_shape=tuple(outs),
        in_specs=[SMEM] * len(small) + [VMEM] * len(arrays),
        out_specs=tuple([VMEM] * len(outs)),
        scratch_shapes=scratch,
        compiler_params=params(),
        cost_estimate=cost(planes),
    )(*small, *arrays)


def grouped(refs, sizes):
    found = []
    for size in sizes:
        found.append(refs[:size])
        refs = refs[size:]
    return found, list(refs)


def ranges(slab):
    half = slab // 2 - HALO
    return [(0, HALO), (HALO, half), (HALO + half, half), (slab - HALO, HALO)]


def scratch_of(count, width, length):
    return [
        pltpu.VMEM((count, width, length), jnp.float32),
        pltpu.VMEM((count + 2 * HALO, width + 2 * PAD, length), jnp.float32),
    ]


def origins(field):
    return [at for _, at in field]


def arrays_of(field):
    return [values for values, _ in field]


def prepare(first, pad, along_ref, halo, cur, slab, width):
    count = along_ref.shape[0]
    fill(pad, first - HALO, cur, width)
    if halo is not None:
        fill_halo(pad, 0 if first == 0 else HALO + count, *halo, width)
    margins(pad, HALO, count, width)
    columns(pad, along_ref, width)


def forward(place, halo, cur, old, courant, source, wave, after):
    slab, width, length = courant.shape
    first, count = place
    groups = [[halo[0]] if halo else [], arrays_of(cur), arrays_of(old)]
    groups += [[courant, source, wave], list(after)]
    sizes = [len(g) for g in groups]

    def kernel(*refs):
        (halo_ref, cur_refs, old_refs, (c_ref, source_ref, wave_ref), _), refs = grouped(refs, sizes)
        next_ref, lap_ref, along_ref, pad = refs
        coming = (halo_ref[0], *halo[1:]) if halo else None
        prepare(first, pad, along_ref, coming, list(zip(cur_refs, origins(cur))), slab, width)
        old_ref, old_at = find(list(zip(old_refs, origins(old))), first)
        amplitude = wave_ref[0:1, :]

        def body(i, _):
            center, lap = stencil(pad, HALO + i, width, along_ref[i])
            lap_ref[i] = lap
            value = 2.0 * center - old_ref[old_at + i] + c_ref[first + i] * lap
            next_ref[i] = value + source_ref[first + i] * amplitude

        march(count, body)

    outs = [f32(count, width, length)] * 2
    return kernel_call(kernel, [], sum(groups, []), outs, scratch_of(count, width, length), count)


def adjoint(place, halo, cur, old, courant, field, number, observed, after):
    slab, width, length = courant.shape
    first, count = place
    groups = [[halo[0]] if halo else [], arrays_of(cur), arrays_of(old), arrays_of(field)]
    groups += [[courant, number, observed], list(after)]
    sizes = [len(g) for g in groups]

    def kernel(*refs):
        found, refs = grouped(refs, sizes)
        next_ref, along_ref, pad = refs
        adjoint_step(place, halo, cur, old, field, found, next_ref, along_ref, pad)

    outs = [f32(count, width, length)]
    scratch = scratch_of(count, width, length)
    return kernel_call(kernel, [], sum(groups, []), outs, scratch, count)[0]


def adjoint_step(place, halo, cur, old, field, found, next_ref, along_ref, pad):
    halo_ref, cur_refs, old_refs, field_refs, (c_ref, number_ref, observed_ref) = found[:5]
    slab, width, length = c_ref.shape
    first, count = place
    coming = (halo_ref[0], *halo[1:]) if halo else None
    prepare(first, pad, along_ref, coming, list(zip(cur_refs, origins(cur))), slab, width)
    for field_ref, field_at in zip(field_refs, origins(field)):
        begin, end = max(first, field_at), min(first + count, field_at + field_ref.shape[0])
        if end <= begin:
            continue
        old_ref, old_at = find(list(zip(old_refs, origins(old))), begin)

        def body(i, _, field_ref=field_ref, field_at=field_at, begin=begin, old_ref=old_ref, old_at=old_at):
            q = begin + i
            center, lap = stencil(pad, begin - first + HALO + i, width, along_ref[begin - first + i])
            value = 2.0 * center - old_ref[old_at + i] + c_ref[q] * lap
            miss = number_ref[q] * field_ref[begin - field_at + i] - observed_ref[q]
            next_ref[begin - first + i] = value + miss

        march(end - begin, body)


def adjoint_last(
    place, halo, cur, old, courant, field, number, observed, laps, adjoints, tile, other, after
):
    slab, width, length = courant.shape
    first, count = place
    inner = count > HALO
    groups = [[halo[0]] if halo else [], arrays_of(cur), arrays_of(old), arrays_of(field)]
    groups += [[courant, number, observed], sum(laps, []), sum(adjoints, [])]
    groups += [list(tile) + list(other), list(after)]
    sizes = [len(g) for g in groups]
    steps, parts = len(laps), len(laps[0])

    def kernel(*refs):
        found, refs = grouped(refs, sizes)
        next_ref, along_ref, pad = refs[-3:]
        adjoint_step(place, halo, cur, old, field, found, next_ref, along_ref, pad)
        lap_refs, adj_refs, more = found[5:8]
        core = lax.axis_index("shot") % 2

        def product(part, i):
            value = next_ref[part * (count // parts) + i] * lap_refs[part][i]
            for n in range(1, steps):
                value = value + adj_refs[(n - 1) * parts + part][i] * lap_refs[n * parts + part][i]
            return value

        def either(write):
            @pl.when(core == 0)
            def _():
                write(refs[0], refs[1])

            @pl.when(core == 1)
            def _():
                write(refs[1], refs[0])

        if inner:

            def write(first_ref, second_ref):
                def body(i, _):
                    first_ref[i] = product(0, i)
                    second_ref[i] = product(1, i)

                march(count // 2, body)

            either(write)
        elif not other:
            for i in range(HALO):
                refs[0][i] = product(0, i)
        else:
            tile_ref, tiles_ref, other_ref = more

            def write(first_ref, second_ref):
                for i in range(HALO):
                    rows = slice(i * width, (i + 1) * width)
                    first_ref[rows, :] = other_ref[i]
                    second_ref[rows, :] = product(0, i)

            either(write)
            for ref in refs[:2]:
                ref[HALO * width : HALO * width + 8, :] = tile_ref[...] + tiles_ref[...]

    if inner:
        outs = [f32(count // 2, width, length)] * 2
    elif not other:
        outs = [f32(count, width, length)]
    else:
        outs = [f32(HALO * width + 8, length)] * 2
    scratch = [pltpu.VMEM((count, width, length), jnp.float32)] + scratch_of(count, width, length)
    return kernel_call(kernel, [], sum(groups, []), outs, scratch, count)


def curvature(laps, after):
    number = len(laps)
    half, width, length = laps[0][1].shape
    size = half + HALO

    def kernel(*refs):
        ranged = [refs[n * number : (n + 1) * number] for n in range(4)]
        keep_ref, send_ref, tile_ref = refs[4 * number + 1 :]
        core = lax.axis_index("shot") % 2

        def squares(lap_refs, at):
            value = lap_refs[0][at] * lap_refs[0][at]
            for ref in lap_refs[1:]:
                value = value + ref[at] * ref[at]
            return value

        def write(first_ref, second_ref):
            def body(i, total):
                for ref, lap_refs in ((first_ref, ranged[1]), (second_ref, ranged[2])):
                    value = squares(lap_refs, i)
                    ref[i] = value
                    total = total + fold(value)
                return total

            total = march(half, body, jnp.zeros((8, length), jnp.float32))
            for i in range(HALO):
                for ref, lap_refs in ((first_ref, ranged[0]), (second_ref, ranged[3])):
                    value = squares(lap_refs, i)
                    ref[half + i] = value
                    total = total + fold(value)
            tile_ref[...] = total

        @pl.when(core == 0)
        def _():
            write(keep_ref, send_ref)

        @pl.when(core == 1)
        def _():
            write(send_ref, keep_ref)

    outs = [f32(size, width, length)] * 2 + [f32(8, length)]
    arrays = [lap[n] for n in range(4) for lap in laps] + [after]
    return kernel_call(kernel, [], arrays, outs, [], 8)


def points(wavelet, source, cells, observed, slab, width, length):
    receivers = cells.shape[0]
    steps = observed.shape[0]
    area = width * length

    def kernel(wave_ref, source_ref, cell_ref, obs_ref, spot_ref, number_ref, *refs):
        row_refs, sum_refs = refs[:steps], refs[steps:]
        blank = jnp.zeros((width, length), jnp.float32)

        def clear(i, _):
            for ref in (spot_ref, number_ref) + sum_refs:
                ref[i] = blank

        march(slab, clear)
        depth = lax.axis_index("depth")
        offset = depth * (slab * area)
        odd = depth % 2
        column = lax.broadcasted_iota(jnp.int32, (1, length), 1)

        def add(local, terms):
            @pl.when((local >= 0) & (local < slab * area))
            def _():
                row, y = split(local, length)
                plane, x = split(row, width)
                q = jnp.where(odd == 1, plane, slab - 1 - plane)
                at = pl.ds(spread(x, width), 1)
                for ref, term in terms():
                    ref[q, at, :] = ref[q, at, :] + jnp.where(column == y, term, 0.0)

        add(source_ref[0] - offset, lambda: [(spot_ref, 1.0)])
        for n in range(steps):
            row_refs[n][...] = jnp.full((8, length), wave_ref[0, n], jnp.float32)

        def body(r, _):
            def terms():
                found = [(number_ref, 1.0)]
                for n in range(steps):
                    found.append((sum_refs[n], obs_ref[n, r]))
                return found

            add(cell_ref[r] - offset, terms)

        lax.fori_loop(0, receivers, body, None)

    volume = f32(slab, width, length)
    outs = [volume, volume] + [f32(8, length)] * steps + [volume] * steps
    small = [wavelet, source, cells, observed]
    found = kernel_call(kernel, small, [], outs, [], 8)
    return found[0], found[1], found[2 : 2 + steps], found[2 + steps :]


def interleaved(*arrays):
    number = len(arrays)
    slab, width, length = arrays[0].shape

    def kernel(*refs):
        odd = lax.axis_index("depth") % 2

        def body(i, _):
            plane = jnp.where(odd == 1, i, slab - 1 - i)
            for ref, out_ref in zip(refs[:number], refs[number:]):

                def put(at, value, out_ref=out_ref):
                    out_ref[i, at : at + ROWS, :] = value

                interleave(put, lambda spot, ref=ref: ref[plane, spot, :], width)

        march(slab, body)

    outs = [f32(slab, width, length)] * number
    return kernel_call(kernel, [], list(arrays), outs, [], 8)


def pack(field, adjoint_field):
    odd = lax.axis_index("depth") % 2
    far = field.shape[0] - HALO
    found = []
    for start in ((1 - odd) * far, odd * far):
        planes = [lax.dynamic_slice_in_dim(v, start, HALO, 0) for v in (field, adjoint_field)]
        found.append(jnp.concatenate(planes, axis=0))
    return found


def refresh(courant, inner_parts, outer_parts, curv, table, plan):
    slab, width, length = courant.shape
    half = inner_parts[0].shape[0]
    number = len(inner_parts)
    cells = slab * width * length * lax.axis_size("depth")

    def kernel(table_ref, plan_ref, c_ref, curv_ref, *rest):
        inner_refs = rest[:number]
        outer_refs = rest[number : 2 * number]
        out_ref = rest[2 * number]
        tail = slice(HALO * width, HALO * width + 8)
        tile = outer_refs[0][tail, :]
        for ref in outer_refs[1:]:
            tile = tile + ref[tail, :]
        level = jnp.sum(tile) / cells + 1e-06
        extra = table_ref[plan_ref[0]] * level
        core = lax.axis_index("shot") % 2
        odd = lax.axis_index("depth") % 2
        size = half + HALO

        def store(q, value):
            plane = jnp.where(odd == 1, q, size - 1 - q)
            for g in range(width // ROWS):
                spot = pl.ds(g, ROWS, stride=width // ROWS)
                out_ref[plane, spot, :] = value[g * ROWS : (g + 1) * ROWS]

        def body(i, _):
            grad = inner_refs[0][i]
            for ref in inner_refs[1:]:
                grad = grad + ref[i]
            model = c_ref[HALO + core * half + i]
            store((1 - core) * HALO + i, model - grad / (curv_ref[i] + extra))

        march(half, body)
        for i in range(HALO):
            rows = slice(i * width, (i + 1) * width)
            grad = outer_refs[0][rows, :]
            for ref in outer_refs[1:]:
                grad = grad + ref[rows, :]
            model = c_ref[core * (slab - HALO) + i]
            store(core * half + i, model - grad / (curv_ref[half + i] + extra))

    arrays = [courant, curv, *inner_parts, *outer_parts]
    outs = [f32(half + HALO, width, length)]
    return kernel_call(kernel, [table, plan], arrays, outs, [], half)[0]


def assemble(own, other):
    half, width, length = own.shape

    def kernel(own_ref, other_ref, out_ref, sems):
        core = lax.axis_index("shot") % 2
        upper = (lax.axis_index("depth") + core + 1) % 2
        copies = []
        for n, (ref, place) in enumerate([(own_ref, upper), (other_ref, 1 - upper)]):
            spot = out_ref.at[pl.ds(place * half, half)]
            copies.append(pltpu.make_async_copy(ref, spot, sems.at[n]))
        for copy in copies:
            copy.start()
        for copy in copies:
            copy.wait()

    return pl.pallas_call(
        kernel,
        out_shape=f32(2 * half, width, length),
        in_specs=[VMEM] * 2,
        out_specs=HBM,
        scratch_shapes=[pltpu.SemaphoreType.DMA((2,))],
        compiler_params=params(),
        cost_estimate=cost(8),
    )(own, other)


def exchange(values, side):
    links = []
    for i in range(side, lax.axis_size("depth") - 1, 2):
        links += [(i, i + 1), (i + 1, i)]
    return lax.ppermute(values, "depth", links)


def swap(values, axis, bit):
    count = lax.axis_size(axis)
    return lax.ppermute(values, axis, [(i, i ^ bit) for i in range(count)])


def sum_of(values, other, after):
    def kernel(values_ref, other_ref, _, out_ref):
        def body(i, _):
            out_ref[i] = values_ref[i] + other_ref[i]

        march(values.shape[0], body)

    return kernel_call(kernel, [], [values, other, after], [f32(*values.shape)], [], 8)[0]


def total_parts(keep, send, after=None):
    parts = [keep, swap(send, "shot", 1)]
    bit = 2
    while bit < lax.axis_size("shot"):
        if after is not None and bit == 2:
            here = sum_of(*parts, after)
        else:
            here = parts[0] + parts[1]
        parts = [here, swap(here, "shot", bit)]
        bit *= 2
    return parts


def on_device(
    field_prev,
    field_now,
    adjoint_next,
    adjoint_after,
    courant,
    wavelet,
    source_cell,
    receiver_cell,
    observed,
    damping_table,
    plan_step,
):
    slab, width, length = courant.shape
    halos = [exchange(v, side) for side, v in enumerate(pack(field_now[0], adjoint_next[0]))]
    places = ranges(slab)
    starts = [first for first, _ in places]
    spot, number, waves, sums = points(
        wavelet, source_cell, receiver_cell[0], observed[0], slab, width, length
    )
    start, before, courant = interleaved(field_now[0], field_prev[0], courant)
    first, second = interleaved(adjoint_next[0], adjoint_after[0])
    old, cur = [(before, 0)], [(start, 0)]
    coming = [(halos[0], 0, True), (halos[1], 0, True)]

    def ahead(step, side, halo, cur, old, after):
        return forward(
            places[side], halo, cur, old, courant, spot, waves[step], after
        )

    def back(step, side, halo, cur, old, field, after):
        return adjoint(
            places[side], halo, cur, old, courant, [field], number, sums[step], after
        )

    laps, fields = [], []
    near = ahead(0, 1, None, cur, old, ())
    far = ahead(0, 2, None, cur, old, ())
    for step in range(STEPS):
        last = step == STEPS - 1
        after = [near[0], far[0]]
        if last:
            rest, more = [(second, 0)], [(first, 0)]
            near_adj = back(step, 1, None, more, rest, (near[0], starts[1]), ())
            far_adj = back(step, 2, None, more, rest, (far[0], starts[2]), ())
            after += [near_adj, far_adj]
        one = ahead(step, 0, coming[0], cur, old, after)
        if last:
            edge = (halos[0], HALO, True)
            one_adj = back(step, 0, edge, more, rest, (one[0], starts[0]), after)
            message = exchange(one_adj, 0)
            newer = [(one_adj, starts[0]), (near_adj, starts[1]), (far_adj, starts[2])]
            near_next = back(step - 1, 1, None, newer, more, (fields[-1][1], starts[1]), ())
            two = ahead(step, 3, coming[1], cur, old, [near_next])
            edge = (halos[1], HALO, True)
            two_adj = back(step, 3, edge, more, rest, (two[0], starts[3]), [near_next])
            newer.append((two_adj, starts[3]))
        else:
            message = exchange(one[0], 0)
            newer = [(one[0], starts[0]), (near[0], starts[1]), (far[0], starts[2])]
            near_next = ahead(step + 1, 1, None, newer, cur, ())
            two = ahead(step, 3, coming[1], cur, old, [near_next[0]])
            newer.append((two[0], starts[3]))
        laps.append((one[1], near[1], far[1], two[1]))
        fields.append((one[0], near[0], far[0], two[0]))
        if not last:
            coming = [(message, 0, False), (exchange(two[0], 1), 0, False)]
            far = ahead(step + 1, 2, None, newer, cur, ())
            near, old, cur = near_next, cur, newer
    coming = [(message, 0, False), (exchange(two_adj, 1), 0, False)]
    keep, send, tile = curvature(laps, two_adj)
    tiles = swap(tile, "depth", 1)
    bit = 2
    old, cur, near = more, newer, near_next
    adjoints = [arrays_of(cur)]
    for step in range(STEPS - 2, 0, -1):
        far = back(step, 2, None, cur, old, (fields[step][2], starts[2]), ())
        after = [near, far, tiles]
        one = back(step, 0, coming[0], cur, old, (fields[step][0], starts[0]), after)
        message = exchange(one, 0)
        newer = [(one, starts[0]), (near, starts[1]), (far, starts[2])]
        if step > 1:
            near_next = back(step - 1, 1, None, newer, cur, (fields[step - 1][1], starts[1]), ())
            after = [near_next]
        else:
            after = [one]
        two = back(step, 3, coming[1], cur, old, (fields[step][3], starts[3]), after)
        newer.append((two, starts[3]))
        coming = [(message, 0, False), (exchange(two, 1), 0, False)]
        near, old, cur = near_next, cur, newer
        adjoints.insert(0, arrays_of(cur))
        if step == STEPS - 2:
            curv = sum(total_parts(keep, send, two))
        tile = tile + tiles
        if bit < lax.axis_size("depth"):
            tiles = swap(tile, "depth", bit)
            bit *= 2
    while bit < lax.axis_size("depth"):
        tile = tile + tiles
        tiles = swap(tile, "depth", bit)
        bit *= 2
    pieces = [(values, at) for values, at in zip(fields[0], starts)]
    inner = (starts[1], 2 * places[1][1])

    def finish(place, halo, sides, both, other, after):
        return adjoint_last(
            place, halo, cur, old, courant, [pieces[n] for n in sides], number, sums[0],
            [[lap[n] for n in sides] for lap in laps],
            [[a[n] for n in sides] for a in adjoints], both, other, after,
        )

    inside = finish(inner, None, (1, 2), [], [], [curv])
    one = finish(places[0], coming[0], (0,), [], [], inside[:1])
    outside = finish(places[3], coming[1], (3,), [tile, tiles], one, [])
    inner_parts = total_parts(*inside)
    outer_parts = total_parts(*outside)
    own = refresh(courant, inner_parts, outer_parts, curv, damping_table, plan_step)
    return assemble(own, swap(own, "shot", 1))


def solution(mesh):
    in_specs = (
        P("shot", "depth", None, None),
        P("shot", "depth", None, None),
        P("shot", "depth", None, None),
        P("shot", "depth", None, None),
        P("depth", None, None),
        P("shot", None),
        P("shot"),
        P("shot", None),
        P("shot", None, None),
        P(),
        P(),
    )
    out_specs = P("depth", None, None)
    return jax.shard_map(
        on_device, mesh=mesh, in_specs=in_specs, out_specs=out_specs, check_vma=False
    )
```

time: 101 us -> 93.3 us (0.924)
  Pallas kernels: 41.9 us -> 26.5 us
  waiting for transfers between devices: 11.5 us -> 15.8 us
  starting transfers between devices: 41.7 us -> 44.8 us
    pallas_call x29 -> x37, Pallas kernels: 37.9 us -> 25.5 us  [kernel_call(): pl.pallas_call(kernel, out_shape=tuple(outs), in_specs=[SMEM] * len(small...]
    ppermute x10, waiting for transfers between devices: 9.36 us -> 13.2 us  [swap(): return lax.ppermute(values, axis, [(i, i ^ bit) for i in range(count)])]
    ppermute x14, starting transfers between devices: 25.5 us -> 28.8 us  [exchange(): return lax.ppermute(values, 'depth', links)]
    pallas_call x2 -> x1, Pallas kernels: 4 us -> 0.98 us  [assemble(): pl.pallas_call(kernel, out_shape=f32(2 * half, width, length), in_specs=[...]
  transfers between devices with their start and end apart: 24 -> 24, of which waited for: 8 -> 10; matrix products, arithmetic and copies ran while one was open for 0% -> 0% of each run, Pallas kernels for 34% -> 23%
where the time goes in v1:
time: 93.3 us; the launch traced here: 92.9 us
  starting transfers between devices  44.8 us (48%)
  Pallas kernels  26.5 us (28%)
  waiting for transfers between devices  15.8 us (17%)
  local copies, waits for them, and re-layouts  3.57 us (4%)
  between operations  2.01 us (2%)
    ppermute x14, starting transfers between devices, exchange(): return lax.ppermute(values, 'depth', links)  28.8 us
    pallas_call x37, Pallas kernels, kernel_call(): pl.pallas_call(kernel, out_shape=tuple(outs), in_specs=[SMEM] * len(small...  25.5 us
    ppermute x10, starting transfers between devices, swap(): return lax.ppermute(values, axis, [(i, i ^ bit) for i in range(count)])  16 us
    ppermute x10, waiting for transfers between devices, swap(): return lax.ppermute(values, axis, [(i, i ^ bit) for i in range(count)])  13.2 us
    ppermute x14, waiting for transfers between devices, exchange(): return lax.ppermute(values, 'depth', links)  2.59 us
    unnamed x18, local copies, waits for them, and re-layouts  2.29 us
  transfers between devices with their start and end apart: 24, of which 10 were waited for; matrix products, arithmetic and copies ran while one was open for 0% of the time, Pallas kernels for 23%

profile of v1, /device:TPU:0, one launch (start us, length us, event | category | flops | bytes accessed | tf_op | source)
XLA Modules:
  0.0 92.9 jit_solution(50692692997236182)
XLA Ops:
  0.0 1.3 %dynamic-slice_bitcast_fusion = (f32[4,64,128]{2,1,0:T(8,128)S(1)}, f32[4,64,128]{2,1,0:T(8,128)S(1)}, f32[4,64,128]{2,1,0:T(8,128)S(1)}, f32[4,64,128]{2,1,0:T(8,128)S(1)}) fusion(f32[1,32,64,128]{3,2,1,0:T(8,128)} %param.13, s32[]{:T(128)S(6)} %select_n.17, s32[]{:T(128)S(6)} %select_n.16, f32[1,32,64,128]{3,2,1,0:T(8,128)} %param.12), kind=kLoop, calls=%fused_computation.2 | loop fusion | bytes 1048584 | tf_op jit(solution)/shard_map/dynamic_slice | solution.py:443
  1.3 3.0 %collective-permute-start = (f32[8,64,128]{2,1,0:T(8,128)S(1)}, f32[8,64,128]{2,1,0:T(8,128)S(1)}, u32[]{:S(2)}, u32[]{:S(2)}) collective-permute-start(f32[8,64,128]{2,1,0:T(8,128)S(1)} %pad_maximum_fusion), channel_id=1, source_target_pairs={{0,1},{1,0},{2,3},{3,2},{4,5},{5,4},{6,7},{7,6},{8,9},{9,8},{10,11... | collective-permute-start | bytes 786440 | tf_op jit(solution)/shard_map/ppermute | solution.py:525
  4.4 0.7 collective-permute-start.2
  5.1 1.2 %copy-done.3 = f32[32,64,128]{2,1,0:T(8,128)S(1)} copy-done((f32[32,64,128]{2,1,0:T(8,128)S(1)}, f32[32,64,128]{2,1,0:T(8,128)}, u32[]{:S(2)}) %copy-start.3) | copy-done | bytes 1048600
  6.3 0.6 shard_map.109
  7.6 0.6 copy-done.5
  8.3 3.0 %shard_map.110 = (f32[32,64,128]{2,1,0:T(8,128)S(1)}, f32[32,64,128]{2,1,0:T(8,128)S(1)}, f32[8,128]{1,0:T(8,128)S(1)}, f32[8,128]{1,0:T(8,128)S(1)}, f32[8,128]...) custom-call(f32[1,4]{1,0:T(1,128)S(1)} %copy-done.7, ...), custom_call_target="tpu_custom_call" | custom-call | flops 80000 | bytes 8192 | tf_op jit(solution)/shard_map/pallas_call | solution.py:136
  11.3 0.9 shard_map.112
  12.2 0.9 shard_map.111
  13.2 2.4 %collective-permute-done.refs_0_ = f32[8,64,128]{2,1,0:T(8,128)S(1)} collective-permute-done((f32[8,64,128]{2,1,0:T(8,128)S(1)}, f32[8,64,128]{2,1,0:T(8,128)S(1)}, u32[]{:S(2)}, u32[]{:S(2)}) %collective-permute-start) | collective-permute-done | bytes 262176 | tf_op jit(solution)/shard_map/ppermute | solution.py:525
  15.9 2.5 %collective-permute-start.1 = (f32[4,64,128]{2,1,0:T(8,128)S(1)}, f32[4,64,128]{2,1,0:T(8,128)S(1)}, u32[]{:S(2)}, u32[]{:S(2)}) collective-permute-start(f32[4,64,128]{2,1,0:T(8,128)S(1)} %get-tuple-element.67.refs_0_.refs_1_.refs_3_.refs_4_.refs_5_.refs_9_), channel_id=1, source_target_pairs={{0,1},{1,0},{2,3},{3,2},{4,5},{5,4},{6,7},{7,6},{8,9},{9,8},{10,11... | collective-permute-start | bytes 393224 | tf_op jit(solution)/shard_map/ppermute | solution.py:525
  18.4 0.9 shard_map.114
  19.7 0.7 collective-permute-start.4
  20.3 0.9 shard_map.116
  21.7 4.3 %collective-permute-start.3 = (f32[4,64,128]{2,1,0:T(8,128)S(1)}, f32[4,64,128]{2,1,0:T(8,128)S(1)}, u32[]{:S(2)}, u32[]{:S(2)}) collective-permute-start(f32[4,64,128]{2,1,0:T(8,128)S(1)} %get-tuple-element.73.refs_0_.refs_1_.refs_3_.refs_4_.refs_5_.refs_9_), channel_id=1, source_target_pairs={{0,1},{1,0},{2,3},{3,2},{4,5},{5,4},{6,7},{7,6},{8,9},{9,8},{10,11... | collective-permute-start | bytes 393224 | tf_op jit(solution)/shard_map/ppermute | solution.py:525
  25.9 0.9 shard_map.118
  26.9 0.3 shard_map.119
  27.2 0.7 collective-permute-start.6
  27.9 0.9 shard_map.120
  28.9 0.3 shard_map.121
  29.2 4.9 %collective-permute-start.5 = (f32[4,64,128]{2,1,0:T(8,128)S(1)}, f32[4,64,128]{2,1,0:T(8,128)S(1)}, u32[]{:S(2)}, u32[]{:S(2)}) collective-permute-start(f32[4,64,128]{2,1,0:T(8,128)S(1)} %get-tuple-element.79.refs_0_.refs_1_.refs_6_), channel_id=1, source_target_pairs={{0,1},{1,0},{2,3},{3,2},{4,5},{5,4},{6,7},{7,6},{8,9},{9,8},{10,11... | collective-permute-start | bytes 393224 | tf_op jit(solution)/shard_map/ppermute | solution.py:525
  34.1 0.9 shard_map.122
  35.1 0.3 shard_map.123
  35.4 0.8 collective-permute-start.7
  36.6 0.4 shard_map.125
  37.1 0.9 shard_map.124
  38.0 0.9 %shard_map.126.refs_14_.refs_9_.refs_1_.refs_2_.refs_4_.refs_5_.refs_6_.refs_25_ = f32[12,64,128]{2,1,0:T(8,128)S(1)} custom-call(f32[32,64,128]{2,1,0:T(8,128)S(1)} %get-tuple-element.84.refs_0_.refs_1_.refs_3_.refs_4_.refs_5_, f32[32,64,128]{2,1,0:T(8,128)S(1)} %get-tuple-element.85.refs_1_.refs_2_, ...), custom_call_target="tpu_custom_call" | custom-call | flops 120000 | bytes 12288 | tf_op jit(solution)/shard_map/pallas_call | solution.py:136
  38.9 0.9 %shard_map.127.refs_15_.refs_10_.refs_2_.refs_3_.refs_5_.refs_6_.refs_7_.refs_26_ = f32[12,64,128]{2,1,0:T(8,128)S(1)} custom-call(f32[32,64,128]{2,1,0:T(8,128)S(1)} %get-tuple-element.84.refs_0_.refs_1_.refs_3_.refs_4_.refs_5_, f32[32,64,128]{2,1,0:T(8,128)S(1)} %get-tuple-element.85.refs_1_.refs_2_, ...), custom_call_target="tpu_custom_call" | custom-call | flops 120000 | bytes 12288 | tf_op jit(solution)/shard_map/pallas_call | solution.py:136
  39.9 0.3 shard_map.128
  40.2 0.3 shard_map.129.refs_0_.refs_1_.refs_3_.refs_4_.refs_5_.refs_19_
  40.6 0.9 %shard_map.130.refs_12_.refs_7_.refs_10_.refs_1_.refs_2_.refs_5_.refs_23_.refs_6_ = f32[12,64,128]{2,1,0:T(8,128)S(1)} custom-call(f32[4,64,128]{2,1,0:T(8,128)S(1)} %shard_map.129.refs_0_.refs_1_.refs_3_.refs_4_.refs_5_.refs_19_, f32[12,64,128]{2,1,0:T(8,128)S(1)} %shard_map.126.refs_14_.refs_9_.refs_1_.refs_2_.refs_4_.refs_5_.refs_6_.refs_25_, ...), custom_call_target="tpu_custom_call" | custom-call | flops 120000 | bytes 12288 | tf_op jit(solution)/shard_map/pallas_call | solution.py:136
  41.5 0.3 shard_map.131
  41.8 0.3 shard_map.132.refs_16_.refs_3_.refs_4_.refs_6_.refs_7_.refs_8_.refs_19_
  42.6 4.5 %collective-permute-start.10 = (f32[4,64,128]{2,1,0:T(8,128)S(1)}, f32[4,64,128]{2,1,0:T(8,128)S(1)}, u32[]{:S(2)}, u32[]{:S(2)}) collective-permute-start(f32[4,64,128]{2,1,0:T(8,128)S(1)} %shard_map.129.refs_0_.refs_1_.refs_3_.refs_4_.refs_5_.refs_19_), channel_id=1, source_target_pairs={{0,1},{1,0},{2,3},{3,2},{4,5},{5,4},{6,7},{7,6},{8,9},{9,8},{10,11... | collective-permute-start | bytes 393224 | tf_op jit(solution)/shard_map/ppermute | solution.py:525
  47.1 0.8 collective-permute-start.9
  47.9 4.4 %collective-permute-start.11 = (f32[8,128]{1,0:T(8,128)S(1)}, f32[8,128]{1,0:T(8,128)S(1)}, u32[]{:S(2)}, u32[]{:S(2)}) collective-permute-start(f32[8,128]{1,0:T(8,128)S(1)} %get-tuple-element.106), channel_id=1, source_target_pairs={{0,1},{1,0},{2,3},{3,2},{4,5},{5,4},{6,7},{7,6},{8,9},{9,8},{10,11... | collective-permute-start | bytes 12296 | tf_op jit(solution)/shard_map/ppermute | solution.py:530
  52.3 0.9 %shard_map.134.refs_11_.refs_2_.refs_3_.refs_6_.refs_24_.refs_7_ = f32[12,64,128]{2,1,0:T(8,128)S(1)} custom-call(f32[4,64,128]{2,1,0:T(8,128)S(1)} %shard_map.129.refs_0_.refs_1_.refs_3_.refs_4_.refs_5_.refs_19_, f32[12,64,128]{2,1,0:T(8,128)S(1)} %shard_map.126.refs_14_.refs_9_.refs_1_.refs_2_.refs_4_.refs_5_.refs_6_.refs_25_, ...), custom_call_target="tpu_custom_call" | custom-call | flops 120000 | bytes 12288 | tf_op jit(solution)/shard_map/pallas_call | solution.py:136
  53.3 0.6 collective-permute-done.11.refs_12_
  53.9 0.3 shard_map.135.refs_0_.refs_1_.refs_4_.refs_5_.refs_18_
  54.3 1.0 %shard_map.136.refs_10_.refs_13_.refs_1_.refs_21_.refs_2_ = f32[12,64,128]{2,1,0:T(8,128)S(1)} custom-call(f32[4,64,128]{2,1,0:T(8,128)S(1)} %shard_map.135.refs_0_.refs_1_.refs_4_.refs_5_.refs_18_, f32[12,64,128]{2,1,0:T(8,128)S(1)} %shard_map.130.refs_12_.refs_7_.refs_10_.refs_1_.refs_2_.refs_5_.refs_23_.refs_6_, ...), custom_call_target="tpu_custom_call" | custom-call | flops 120000 | bytes 12288 | tf_op jit(solution)/shard_map/pallas_call | solution.py:136
  55.2 0.3 shard_map.137._.refs_3_.refs_4_.refs_7_.refs_8_.refs_18_
  55.7 1.6 %collective-permute-start.12 = (f32[16,64,128]{2,1,0:T(8,128)S(1)}, f32[16,64,128]{2,1,0:T(8,128)S(1)}, u32[]{:S(2)}, u32[]{:S(2)}) collective-permute-start(f32[16,64,128]{2,1,0:T(8,128)S(1)} %shard_map.138), channel_id=1, source_target_pairs={{0,16},{8,24},{16,0},{24,8},{1,17},{9,25},{17,1},{25,9},{2,18},{10... | collective-permute-start | bytes 1572872 | tf_op jit(solution)/shard_map/ppermute | solution.py:530
  57.2 2.1 %collective-permute-start.13 = (f32[4,64,128]{2,1,0:T(8,128)S(1)}, f32[4,64,128]{2,1,0:T(8,128)S(1)}, u32[]{:S(2)}, u32[]{:S(2)}) collective-permute-start(f32[4,64,128]{2,1,0:T(8,128)S(1)} %shard_map.135.refs_0_.refs_1_.refs_4_.refs_5_.refs_18_), channel_id=1, source_target_pairs={{0,1},{1,0},{2,3},{3,2},{4,5},{5,4},{6,7},{7,6},{8,9},{9,8},{10,11... | collective-permute-start | bytes 393224 | tf_op jit(solution)/shard_map/ppermute | solution.py:525
  59.3 0.7 collective-permute-start.15
  60.0 2.8 %collective-permute-start.14 = (f32[8,128]{1,0:T(8,128)S(1)}, f32[8,128]{1,0:T(8,128)S(1)}, u32[]{:S(2)}, u32[]{:S(2)}) collective-permute-start(f32[8,128]{1,0:T(8,128)S(1)} %add.31), channel_id=1, source_target_pairs={{0,2},{1,3},{2,0},{3,1},{4,6},{5,7},{6,4},{7,5},{8,10},{9,11},{10,... | collective-permute-start | bytes 12296 | tf_op jit(solution)/shard_map/ppermute | solution.py:530
  62.8 0.9 %shard_map.139.refs_14_.refs_2_.refs_22_.refs_3_ = f32[12,64,128]{2,1,0:T(8,128)S(1)} custom-call(f32[4,64,128]{2,1,0:T(8,128)S(1)} %shard_map.135.refs_0_.refs_1_.refs_4_.refs_5_.refs_18_, f32[12,64,128]{2,1,0:T(8,128)S(1)} %shard_map.130.refs_12_.refs_7_.refs_10_.refs_1_.refs_2_.refs_5_.refs_23_.refs_6_, ...), custom_call_target="tpu_custom_call" | custom-call | flops 120000 | bytes 12288 | tf_op jit(solution)/shard_map/pallas_call | solution.py:136
  63.7 1.9 %collective-permute-done.14.refs_15_ = f32[8,128]{1,0:T(8,128)S(1)} collective-permute-done((f32[8,128]{1,0:T(8,128)S(1)}, f32[8,128]{1,0:T(8,128)S(1)}, u32[]{:S(2)}, u32[]{:S(2)}) %collective-permute-start.14) | collective-permute-done | bytes 4128 | tf_op jit(solution)/shard_map/ppermute | solution.py:530
  65.6 0.3 shard_map.140.refs_13_.refs_0_.refs_1_.refs_17_
  66.0 0.3 shard_map.141.refs_3_.refs_4_.refs_17_
  66.3 2.3 %collective-permute-done.12 = f32[16,64,128]{2,1,0:T(8,128)S(1)} collective-permute-done((f32[16,64,128]{2,1,0:T(8,128)S(1)}, f32[16,64,128]{2,1,0:T(8,128)S(1)}, u32[]{:S(2)}, u32[]{:S(2)}) %collective-permute-start.12) | collective-permute-done | bytes 524320 | tf_op jit(solution)/shard_map/ppermute | solution.py:530
  68.6 2.0 %shard_map.142 = (f32[12,64,128]{2,1,0:T(8,128)S(1)}, f32[12,64,128]{2,1,0:T(8,128)S(1)}) custom-call(f32[4,64,128]{2,1,0:T(8,128)S(1)} %shard_map.140.refs_13_.refs_0_.refs_1_.refs_17_, f32[12,64,128]{2,1,0:T(8,128)S(1)} %shard_map.136.refs_10_.refs_13_.refs_1_.refs_21_.refs_2_, f32[12,64,128]{2,1,0:T(8,128)S(1)} %shard_map.139.refs_14_.refs_2_.refs_22_.refs_3_, ...), custom_call_target="tpu_custom_call" | custom-call | flops 240000 | bytes 24576 | tf_op jit(solution)/shard_map/pallas_call | solution.py:136
  70.7 2.5 %collective-permute-start.20 = (f32[4,64,128]{2,1,0:T(8,128)S(1)}, f32[4,64,128]{2,1,0:T(8,128)S(1)}, u32[]{:S(2)}, u32[]{:S(2)}) collective-permute-start(f32[4,64,128]{2,1,0:T(8,128)S(1)} %shard_map.140.refs_13_.refs_0_.refs_1_.refs_17_), channel_id=1, source_target_pairs={{0,1},{1,0},{2,3},{3,2},{4,5},{5,4},{6,7},{7,6},{8,9},{9,8},{10,11... | collective-permute-start | bytes 393224 | tf_op jit(solution)/shard_map/ppermute | solution.py:525
  73.2 0.7 collective-permute-start.18
  74.0 1.6 %collective-permute-start.17 = (f32[12,64,128]{2,1,0:T(8,128)S(1)}, f32[12,64,128]{2,1,0:T(8,128)S(1)}, u32[]{:S(2)}, u32[]{:S(2)}) collective-permute-start(f32[12,64,128]{2,1,0:T(8,128)S(1)} %add.32.rest_0_), channel_id=1, source_target_pairs={{0,16},{8,24},{16,0},{24,8},{1,17},{9,25},{17,1},{25,9},{2,18},{10... | collective-permute-start | bytes 1179656 | tf_op jit(solution)/shard_map/ppermute | solution.py:530
  75.5 3.9 %collective-permute-start.19 = (f32[8,128]{1,0:T(8,128)S(1)}, f32[8,128]{1,0:T(8,128)S(1)}, u32[]{:S(2)}, u32[]{:S(2)}) collective-permute-start(f32[8,128]{1,0:T(8,128)S(1)} %add.33.refs_20_), channel_id=1, source_target_pairs={{0,4},{1,5},{2,6},{3,7},{4,0},{5,1},{6,2},{7,3},{8,12},{9,13},{10,... | collective-permute-start | bytes 12296 | tf_op jit(solution)/shard_map/ppermute | solution.py:530
  79.4 0.4 shard_map.143.refs_22_
  79.8 1.7 %collective-permute-done.19.refs_21_ = f32[8,128]{1,0:T(8,128)S(1)} collective-permute-done((f32[8,128]{1,0:T(8,128)S(1)}, f32[8,128]{1,0:T(8,128)S(1)}, u32[]{:S(2)}, u32[]{:S(2)}) %collective-permute-start.19) | collective-permute-done | bytes 4128 | tf_op jit(solution)/shard_map/ppermute | solution.py:530
  81.4 0.4 shard_map.144
  81.9 1.3 %collective-permute-done.21 = f32[264,128]{1,0:T(8,128)S(1)} collective-permute-done((f32[264,128]{1,0:T(8,128)S(1)}, f32[264,128]{1,0:T(8,128)S(1)}, u32[]{:S(2)}, u32[]{:S(2)}) %collective-permute-start.21) | collective-permute-done | bytes 135200 | tf_op jit(solution)/shard_map/ppermute | solution.py:530
  83.3 1.6 %collective-permute-start.22 = (f32[264,128]{1,0:T(8,128)S(1)}, f32[264,128]{1,0:T(8,128)S(1)}, u32[]{:S(2)}, u32[]{:S(2)}) collective-permute-start(f32[264,128]{1,0:T(8,128)S(1)} %add.34.rest_2_), channel_id=1, source_target_pairs={{0,16},{8,24},{16,0},{24,8},{1,17},{9,25},{17,1},{25,9},{2,18},{10... | collective-permute-start | bytes 405512 | tf_op jit(solution)/shard_map/ppermute | solution.py:530
  85.5 3.5 %collective-permute-done.22.rest_3_ = f32[264,128]{1,0:T(8,128)S(1)} collective-permute-done((f32[264,128]{1,0:T(8,128)S(1)}, f32[264,128]{1,0:T(8,128)S(1)}, u32[]{:S(2)}, u32[]{:S(2)}) %collective-permute-start.22) | collective-permute-done | bytes 135200 | tf_op jit(solution)/shard_map/ppermute | solution.py:530
  89.0 0.8 shard_map.145.own_ref
  89.9 1.9 %collective-permute-done.23.other_ref = f32[16,64,128]{2,1,0:T(8,128)S(1)} collective-permute-done((f32[16,64,128]{2,1,0:T(8,128)S(1)}, f32[16,64,128]{2,1,0:T(8,128)S(1)}, u32[]{:S(2)}, u32[]{:S(2)}) %collective-permute-start.23) | collective-permute-done | bytes 524320 | tf_op jit(solution)/shard_map/ppermute | solution.py:530
  91.8 1.0 %shard_map.146 = f32[32,64,128]{2,1,0:T(8,128)} custom-call(f32[16,64,128]{2,1,0:T(8,128)S(1)} %shard_map.145.own_ref, f32[16,64,128]{2,1,0:T(8,128)S(1)} %collective-permute-done.23.other_ref), custom_call_target="tpu_custom_call" | custom-call | flops 80000 | bytes 8192 | tf_op jit(solution)/shard_map/pallas_call | solution.py:510
  (48 shorter events, 2.4 us)
Async XLA Ops:
  0.0 5.1 %copy-start = (f32[1,32,64,128]{3,2,1,0:T(8,128)S(1)}, f32[1,32,64,128]{3,2,1,0:T(8,128)}, u32[]{:S(2)}) copy-start(f32[1,32,64,128]{3,2,1,0:T(8,128)} %param.12) | copy-start | bytes 3145732
  0.0 5.1 %copy-start.2 = (f32[1,32,64,128]{3,2,1,0:T(8,128)S(1)}, f32[1,32,64,128]{3,2,1,0:T(8,128)}, u32[]{:S(2)}) copy-start(f32[1,32,64,128]{3,2,1,0:T(8,128)} %param.11) | copy-start | bytes 3145732
  1.3 14.2 %collective-permute-start = (f32[8,64,128]{2,1,0:T(8,128)S(1)}, f32[8,64,128]{2,1,0:T(8,128)S(1)}, u32[]{:S(2)}, u32[]{:S(2)}) collective-permute-start(f32[8,64,128]{2,1,0:T(8,128)S(1)} %pad_maximum_fusion), channel_id=1, source_target_pairs={{0,1},{1,0},{2,3},{3,2},{4,5},{5,4},{6,7},{7,6},{8,9},{9,8},{10,11... | collective-permute-start | bytes 786440 | tf_op jit(solution)/shard_map/ppermute | solution.py:525
  4.4 14.9 %collective-permute-start.2 = (f32[8,64,128]{2,1,0:T(8,128)S(1)}, f32[8,64,128]{2,1,0:T(8,128)S(1)}, u32[]{:S(2)}, u32[]{:S(2)}) collective-permute-start(f32[8,64,128]{2,1,0:T(8,128)S(1)} %pad_maximum_fusion.1), channel_id=1, source_target_pairs={{1,2},{2,1},{3,4},{4,3},{5,6},{6,5},{9,10},{10,9},{11,12},{12,11},... | collective-permute-start | bytes 786440 | tf_op jit(solution)/shard_map/ppermute | solution.py:525
  5.1 1.2 %copy-start.3 = (f32[32,64,128]{2,1,0:T(8,128)S(1)}, f32[32,64,128]{2,1,0:T(8,128)}, u32[]{:S(2)}) copy-start(f32[32,64,128]{2,1,0:T(8,128)} %refs_2_.1) | copy-start | bytes 3145732
  7.6 0.7 copy-start.5
  7.6 0.7 copy-start.7
  7.6 0.7 copy-start.8
  15.9 5.5 %collective-permute-start.1 = (f32[4,64,128]{2,1,0:T(8,128)S(1)}, f32[4,64,128]{2,1,0:T(8,128)S(1)}, u32[]{:S(2)}, u32[]{:S(2)}) collective-permute-start(f32[4,64,128]{2,1,0:T(8,128)S(1)} %get-tuple-element.67.refs_0_.refs_1_.refs_3_.refs_4_.refs_5_.refs_9_), channel_id=1, source_target_pairs={{0,1},{1,0},{2,3},{3,2},{4,5},{5,4},{6,7},{7,6},{8,9},{9,8},{10,11... | collective-permute-start | bytes 393224 | tf_op jit(solution)/shard_map/ppermute | solution.py:525
  19.7 7.2 %collective-permute-start.4 = (f32[4,64,128]{2,1,0:T(8,128)S(1)}, f32[4,64,128]{2,1,0:T(8,128)S(1)}, u32[]{:S(2)}, u32[]{:S(2)}) collective-permute-start(f32[4,64,128]{2,1,0:T(8,128)S(1)} %get-tuple-element.70.refs_3_.refs_4_.refs_6_.refs_7_.refs_8_.refs_9_), channel_id=1, source_target_pairs={{1,2},{2,1},{3,4},{4,3},{5,6},{6,5},{9,10},{10,9},{11,12},{12,11},... | collective-permute-start | bytes 393224 | tf_op jit(solution)/shard_map/ppermute | solution.py:525
  21.7 7.2 %collective-permute-start.3 = (f32[4,64,128]{2,1,0:T(8,128)S(1)}, f32[4,64,128]{2,1,0:T(8,128)S(1)}, u32[]{:S(2)}, u32[]{:S(2)}) collective-permute-start(f32[4,64,128]{2,1,0:T(8,128)S(1)} %get-tuple-element.73.refs_0_.refs_1_.refs_3_.refs_4_.refs_5_.refs_9_), channel_id=1, source_target_pairs={{0,1},{1,0},{2,3},{3,2},{4,5},{5,4},{6,7},{7,6},{8,9},{9,8},{10,11... | collective-permute-start | bytes 393224 | tf_op jit(solution)/shard_map/ppermute | solution.py:525
  27.2 7.9 %collective-permute-start.6 = (f32[4,64,128]{2,1,0:T(8,128)S(1)}, f32[4,64,128]{2,1,0:T(8,128)S(1)}, u32[]{:S(2)}, u32[]{:S(2)}) collective-permute-start(f32[4,64,128]{2,1,0:T(8,128)S(1)} %get-tuple-element.76.refs_3_.refs_4_.refs_6_.refs_7_.refs_8_.refs_9_), channel_id=1, source_target_pairs={{1,2},{2,1},{3,4},{4,3},{5,6},{6,5},{9,10},{10,9},{11,12},{12,11},... | collective-permute-start | bytes 393224 | tf_op jit(solution)/shard_map/ppermute | solution.py:525
  29.2 10.7 %collective-permute-start.5 = (f32[4,64,128]{2,1,0:T(8,128)S(1)}, f32[4,64,128]{2,1,0:T(8,128)S(1)}, u32[]{:S(2)}, u32[]{:S(2)}) collective-permute-start(f32[4,64,128]{2,1,0:T(8,128)S(1)} %get-tuple-element.79.refs_0_.refs_1_.refs_6_), channel_id=1, source_target_pairs={{0,1},{1,0},{2,3},{3,2},{4,5},{5,4},{6,7},{7,6},{8,9},{9,8},{10,11... | collective-permute-start | bytes 393224 | tf_op jit(solution)/shard_map/ppermute | solution.py:525
  35.1 1.2 %copy-start.1 = (f32[1,32,64,128]{3,2,1,0:T(8,128)S(1)}, f32[1,32,64,128]{3,2,1,0:T(8,128)}, u32[]{:S(2)}) copy-start(f32[1,32,64,128]{3,2,1,0:T(8,128)} %param.13) | copy-start | bytes 3145732
  35.1 1.5 %copy-start.4 = (f32[1,32,64,128]{3,2,1,0:T(8,128)S(1)}, f32[1,32,64,128]{3,2,1,0:T(8,128)}, u32[]{:S(2)}) copy-start(f32[1,32,64,128]{3,2,1,0:T(8,128)} %param.14) | copy-start | bytes 3145732
  35.4 6.1 %collective-permute-start.7 = (f32[4,64,128]{2,1,0:T(8,128)S(1)}, f32[4,64,128]{2,1,0:T(8,128)S(1)}, u32[]{:S(2)}, u32[]{:S(2)}) collective-permute-start(f32[4,64,128]{2,1,0:T(8,128)S(1)} %get-tuple-element.82.refs_3_.refs_4_.refs_6_), channel_id=1, source_target_pairs={{1,2},{2,1},{3,4},{4,3},{5,6},{6,5},{9,10},{10,9},{11,12},{12,11},... | collective-permute-start | bytes 393224 | tf_op jit(solution)/shard_map/ppermute | solution.py:525
  42.5 13.1 %collective-permute-start.8 = (f32[16,64,128]{2,1,0:T(8,128)S(1)}, f32[16,64,128]{2,1,0:T(8,128)S(1)}, u32[]{:S(2)}, u32[]{:S(2)}) collective-permute-start(f32[16,64,128]{2,1,0:T(8,128)S(1)} %get-tuple-element.105), channel_id=1, source_target_pairs={{0,8},{8,0},{16,24},{24,16},{1,9},{9,1},{17,25},{25,17},{2,10},{10... | collective-permute-start | bytes 1572872 | tf_op jit(solution)/shard_map/ppermute | solution.py:530
  42.6 11.3 %collective-permute-start.10 = (f32[4,64,128]{2,1,0:T(8,128)S(1)}, f32[4,64,128]{2,1,0:T(8,128)S(1)}, u32[]{:S(2)}, u32[]{:S(2)}) collective-permute-start(f32[4,64,128]{2,1,0:T(8,128)S(1)} %shard_map.129.refs_0_.refs_1_.refs_3_.refs_4_.refs_5_.refs_19_), channel_id=1, source_target_pairs={{0,1},{1,0},{2,3},{3,2},{4,5},{5,4},{6,7},{7,6},{8,9},{9,8},{10,11... | collective-permute-start | bytes 393224 | tf_op jit(solution)/shard_map/ppermute | solution.py:525
  47.1 8.1 %collective-permute-start.9 = (f32[4,64,128]{2,1,0:T(8,128)S(1)}, f32[4,64,128]{2,1,0:T(8,128)S(1)}, u32[]{:S(2)}, u32[]{:S(2)}) collective-permute-start(f32[4,64,128]{2,1,0:T(8,128)S(1)} %shard_map.132.refs_16_.refs_3_.refs_4_.refs_6_.refs_7_.refs_8_.refs_19_), channel_id=1, source_target_pairs={{1,2},{2,1},{3,4},{4,3},{5,6},{6,5},{9,10},{10,9},{11,12},{12,11},... | collective-permute-start | bytes 393224 | tf_op jit(solution)/shard_map/ppermute | solution.py:525
  47.9 6.0 %collective-permute-start.11 = (f32[8,128]{1,0:T(8,128)S(1)}, f32[8,128]{1,0:T(8,128)S(1)}, u32[]{:S(2)}, u32[]{:S(2)}) collective-permute-start(f32[8,128]{1,0:T(8,128)S(1)} %get-tuple-element.106), channel_id=1, source_target_pairs={{0,1},{1,0},{2,3},{3,2},{4,5},{5,4},{6,7},{7,6},{8,9},{9,8},{10,11... | collective-permute-start | bytes 12296 | tf_op jit(solution)/shard_map/ppermute | solution.py:530
  55.7 12.9 %collective-permute-start.12 = (f32[16,64,128]{2,1,0:T(8,128)S(1)}, f32[16,64,128]{2,1,0:T(8,128)S(1)}, u32[]{:S(2)}, u32[]{:S(2)}) collective-permute-start(f32[16,64,128]{2,1,0:T(8,128)S(1)} %shard_map.138), channel_id=1, source_target_pairs={{0,16},{8,24},{16,0},{24,8},{1,17},{9,25},{17,1},{25,9},{2,18},{10... | collective-permute-start | bytes 1572872 | tf_op jit(solution)/shard_map/ppermute | solution.py:530
  57.2 8.4 %collective-permute-start.13 = (f32[4,64,128]{2,1,0:T(8,128)S(1)}, f32[4,64,128]{2,1,0:T(8,128)S(1)}, u32[]{:S(2)}, u32[]{:S(2)}) collective-permute-start(f32[4,64,128]{2,1,0:T(8,128)S(1)} %shard_map.135.refs_0_.refs_1_.refs_4_.refs_5_.refs_18_), channel_id=1, source_target_pairs={{0,1},{1,0},{2,3},{3,2},{4,5},{5,4},{6,7},{7,6},{8,9},{9,8},{10,11... | collective-permute-start | bytes 393224 | tf_op jit(solution)/shard_map/ppermute | solution.py:525
  59.3 6.7 %collective-permute-start.15 = (f32[4,64,128]{2,1,0:T(8,128)S(1)}, f32[4,64,128]{2,1,0:T(8,128)S(1)}, u32[]{:S(2)}, u32[]{:S(2)}) collective-permute-start(f32[4,64,128]{2,1,0:T(8,128)S(1)} %shard_map.137._.refs_3_.refs_4_.refs_7_.refs_8_.refs_18_), channel_id=1, source_target_pairs={{1,2},{2,1},{3,4},{4,3},{5,6},{6,5},{9,10},{10,9},{11,12},{12,11},... | collective-permute-start | bytes 393224 | tf_op jit(solution)/shard_map/ppermute | solution.py:525
  60.0 5.7 %collective-permute-start.14 = (f32[8,128]{1,0:T(8,128)S(1)}, f32[8,128]{1,0:T(8,128)S(1)}, u32[]{:S(2)}, u32[]{:S(2)}) collective-permute-start(f32[8,128]{1,0:T(8,128)S(1)} %add.31), channel_id=1, source_target_pairs={{0,2},{1,3},{2,0},{3,1},{4,6},{5,7},{6,4},{7,5},{8,10},{9,11},{10,... | collective-permute-start | bytes 12296 | tf_op jit(solution)/shard_map/ppermute | solution.py:530
  70.7 3.2 %collective-permute-start.16 = (f32[12,64,128]{2,1,0:T(8,128)S(1)}, f32[12,64,128]{2,1,0:T(8,128)S(1)}, u32[]{:S(2)}, u32[]{:S(2)}) collective-permute-start(f32[12,64,128]{2,1,0:T(8,128)S(1)} %get-tuple-element.110), channel_id=1, source_target_pairs={{0,8},{8,0},{16,24},{24,16},{1,9},{9,1},{17,25},{25,17},{2,10},{10... | collective-permute-start | bytes 1179656 | tf_op jit(solution)/shard_map/ppermute | solution.py:530
  70.7 8.7 %collective-permute-start.20 = (f32[4,64,128]{2,1,0:T(8,128)S(1)}, f32[4,64,128]{2,1,0:T(8,128)S(1)}, u32[]{:S(2)}, u32[]{:S(2)}) collective-permute-start(f32[4,64,128]{2,1,0:T(8,128)S(1)} %shard_map.140.refs_13_.refs_0_.refs_1_.refs_17_), channel_id=1, source_target_pairs={{0,1},{1,0},{2,3},{3,2},{4,5},{5,4},{6,7},{7,6},{8,9},{9,8},{10,11... | collective-permute-start | bytes 393224 | tf_op jit(solution)/shard_map/ppermute | solution.py:525
  73.2 8.2 %collective-permute-start.18 = (f32[4,64,128]{2,1,0:T(8,128)S(1)}, f32[4,64,128]{2,1,0:T(8,128)S(1)}, u32[]{:S(2)}, u32[]{:S(2)}) collective-permute-start(f32[4,64,128]{2,1,0:T(8,128)S(1)} %shard_map.141.refs_3_.refs_4_.refs_17_), channel_id=1, source_target_pairs={{1,2},{2,1},{3,4},{4,3},{5,6},{6,5},{9,10},{10,9},{11,12},{12,11},... | collective-permute-start | bytes 393224 | tf_op jit(solution)/shard_map/ppermute | solution.py:525
  74.0 15.0 %collective-permute-start.17 = (f32[12,64,128]{2,1,0:T(8,128)S(1)}, f32[12,64,128]{2,1,0:T(8,128)S(1)}, u32[]{:S(2)}, u32[]{:S(2)}) collective-permute-start(f32[12,64,128]{2,1,0:T(8,128)S(1)} %add.32.rest_0_), channel_id=1, source_target_pairs={{0,16},{8,24},{16,0},{24,8},{1,17},{9,25},{17,1},{25,9},{2,18},{10... | collective-permute-start | bytes 1179656 | tf_op jit(solution)/shard_map/ppermute | solution.py:530
  75.5 5.9 %collective-permute-start.19 = (f32[8,128]{1,0:T(8,128)S(1)}, f32[8,128]{1,0:T(8,128)S(1)}, u32[]{:S(2)}, u32[]{:S(2)}) collective-permute-start(f32[8,128]{1,0:T(8,128)S(1)} %add.33.refs_20_), channel_id=1, source_target_pairs={{0,4},{1,5},{2,6},{3,7},{4,0},{5,1},{6,2},{7,3},{8,12},{9,13},{10,... | collective-permute-start | bytes 12296 | tf_op jit(solution)/shard_map/ppermute | solution.py:530
  81.8 1.4 %collective-permute-start.21 = (f32[264,128]{1,0:T(8,128)S(1)}, f32[264,128]{1,0:T(8,128)S(1)}, u32[]{:S(2)}, u32[]{:S(2)}) collective-permute-start(f32[264,128]{1,0:T(8,128)S(1)} %get-tuple-element.112), channel_id=1, source_target_pairs={{0,8},{8,0},{16,24},{24,16},{1,9},{9,1},{17,25},{25,17},{2,10},{10... | collective-permute-start | bytes 405512 | tf_op jit(solution)/shard_map/ppermute | solution.py:530
  83.3 5.7 %copy-start.6 = (f32[64]{0:T(128)S(1)}, f32[64]{0:T(128)}, u32[]{:S(2)}) copy-start(f32[64]{0:T(128)} %table_ref.1) | copy-start | bytes 772
  83.3 5.7 %collective-permute-start.22 = (f32[264,128]{1,0:T(8,128)S(1)}, f32[264,128]{1,0:T(8,128)S(1)}, u32[]{:S(2)}, u32[]{:S(2)}) collective-permute-start(f32[264,128]{1,0:T(8,128)S(1)} %add.34.rest_2_), channel_id=1, source_target_pairs={{0,16},{8,24},{16,0},{24,8},{1,17},{9,25},{17,1},{25,9},{2,18},{10... | collective-permute-start | bytes 405512 | tf_op jit(solution)/shard_map/ppermute | solution.py:530
  89.8 2.0 %collective-permute-start.23 = (f32[16,64,128]{2,1,0:T(8,128)S(1)}, f32[16,64,128]{2,1,0:T(8,128)S(1)}, u32[]{:S(2)}, u32[]{:S(2)}) collective-permute-start(f32[16,64,128]{2,1,0:T(8,128)S(1)} %shard_map.145.own_ref), channel_id=1, source_target_pairs={{0,8},{8,0},{16,24},{24,16},{1,9},{9,1},{17,25},{25,17},{2,10},{10... | collective-permute-start | bytes 1572872 | tf_op jit(solution)/shard_map/ppermute | solution.py:530

commit v2 on v1

--- a/solution.py
+++ b/solution.py
@@ -282,15 +282,14 @@
                 write(refs[1], refs[0])
 
         if inner:
-
-            def write(first_ref, second_ref):
-                def body(i, _):
-                    first_ref[i] = product(0, i)
-                    second_ref[i] = product(1, i)
-
-                march(count // 2, body)
-
-            either(write)
+            for part in (0, 1):
+
+                @pl.when(core == part)
+                def _(part=part):
+                    for i in range(count // 2):
+                        refs[0][i] = product(part, i)
+                        write_piece(refs[1:-3], i, product(1 - part, i))
+
         elif not other:
             for i in range(HALO):
                 refs[0][i] = product(0, i)
@@ -308,7 +307,8 @@
                 ref[HALO * width : HALO * width + 8, :] = tile_ref[...] + tiles_ref[...]
 
     if inner:
-        outs = [f32(count // 2, width, length)] * 2
+        outs = [f32(count // 2, width, length)]
+        outs += [f32(count // 2 // 1, width, length)] * 1
     elif not other:
         outs = [f32(count, width, length)]
     else:
@@ -324,7 +324,7 @@
 
     def kernel(*refs):
         ranged = [refs[n * number : (n + 1) * number] for n in range(4)]
-        keep_ref, send_ref, tile_ref = refs[4 * number + 1 :]
+        keep_ref, *send_refs, tile_ref = refs[4 * number + 1 :]
         core = lax.axis_index("shot") % 2
 
         def squares(lap_refs, at):
@@ -333,31 +333,25 @@
                 value = value + ref[at] * ref[at]
             return value
 
-        def write(first_ref, second_ref):
-            def body(i, total):
-                for ref, lap_refs in ((first_ref, ranged[1]), (second_ref, ranged[2])):
-                    value = squares(lap_refs, i)
-                    ref[i] = value
+        for part in (0, 1):
+
+            @pl.when(core == part)
+            def _(part=part):
+                total = jnp.zeros((8, length), jnp.float32)
+                own, far = (0, 1) if part == 0 else (3, 2)
+                other = (3, 2) if part == 0 else (0, 1)
+                for i in range(size):
+                    outer = i >= half
+                    value = squares(ranged[own if outer else far], i % half)
+                    keep_ref[i] = value
                     total = total + fold(value)
-                return total
-
-            total = march(half, body, jnp.zeros((8, length), jnp.float32))
-            for i in range(HALO):
-                for ref, lap_refs in ((first_ref, ranged[0]), (second_ref, ranged[3])):
-                    value = squares(lap_refs, i)
-                    ref[half + i] = value
+                    value = squares(ranged[other[0] if outer else other[1]], i % half)
+                    write_piece(send_refs, i, value)
                     total = total + fold(value)
-            tile_ref[...] = total
-
-        @pl.when(core == 0)
-        def _():
-            write(keep_ref, send_ref)
-
-        @pl.when(core == 1)
-        def _():
-            write(send_ref, keep_ref)
-
-    outs = [f32(size, width, length)] * 2 + [f32(8, length)]
+                tile_ref[...] = total
+
+    outs = [f32(size, width, length)]
+    outs += [f32(size // 1, width, length)] * 1 + [f32(8, length)]
     arrays = [lap[n] for n in range(4) for lap in laps] + [after]
     return kernel_call(kernel, [], arrays, outs, [], 8)
 
@@ -530,27 +524,36 @@
     return lax.ppermute(values, axis, [(i, i ^ bit) for i in range(count)])
 
 
-def sum_of(values, other, after):
-    def kernel(values_ref, other_ref, _, out_ref):
-        def body(i, _):
-            out_ref[i] = values_ref[i] + other_ref[i]
-
-        march(values.shape[0], body)
-
-    return kernel_call(kernel, [], [values, other, after], [f32(*values.shape)], [], 8)[0]
-
-
-def total_parts(keep, send, after=None):
-    parts = [keep, swap(send, "shot", 1)]
+def sum_of(values, pieces, after):
+    size = pieces[0].shape[0]
+
+    def kernel(values_ref, *refs):
+        for i in range(values.shape[0]):
+            refs[-1][i] = values_ref[i] + refs[i // size][i % size]
+
+    arrays = [values, *pieces, *after]
+    return kernel_call(kernel, [], arrays, [f32(*values.shape)], [], 8)[0]
+
+
+def total_parts(keep, send, after=()):
+    if isinstance(send, (list, tuple)):
+        parts = [keep, [swap(piece, "shot", 1) for piece in send]]
+    else:
+        parts = [keep, swap(send, "shot", 1)]
     bit = 2
     while bit < lax.axis_size("shot"):
-        if after is not None and bit == 2:
+        if isinstance(parts[1], list):
             here = sum_of(*parts, after)
         else:
             here = parts[0] + parts[1]
         parts = [here, swap(here, "shot", bit)]
         bit *= 2
     return parts
+
+
+def write_piece(refs, i, value):
+    size = refs[0].shape[0]
+    refs[i // size][i % size] = value
 
 
 def on_device(
@@ -623,29 +626,29 @@
             far = ahead(step + 1, 2, None, newer, cur, ())
             near, old, cur = near_next, cur, newer
     coming = [(message, 0, False), (exchange(two_adj, 1), 0, False)]
-    keep, send, tile = curvature(laps, two_adj)
+    keep, *send, tile = curvature(laps, two_adj)
     tiles = swap(tile, "depth", 1)
     bit = 2
     old, cur, near = more, newer, near_next
     adjoints = [arrays_of(cur)]
     for step in range(STEPS - 2, 0, -1):
         far = back(step, 2, None, cur, old, (fields[step][2], starts[2]), ())
-        after = [near, far, tiles]
+        after = [near, far]
         one = back(step, 0, coming[0], cur, old, (fields[step][0], starts[0]), after)
         message = exchange(one, 0)
         newer = [(one, starts[0]), (near, starts[1]), (far, starts[2])]
         if step > 1:
             near_next = back(step - 1, 1, None, newer, cur, (fields[step - 1][1], starts[1]), ())
-            after = [near_next]
+            after = [near_next, tiles]
         else:
-            after = [one]
+            after = [one, tiles]
         two = back(step, 3, coming[1], cur, old, (fields[step][3], starts[3]), after)
         newer.append((two, starts[3]))
         coming = [(message, 0, False), (exchange(two, 1), 0, False)]
         near, old, cur = near_next, cur, newer
         adjoints.insert(0, arrays_of(cur))
         if step == STEPS - 2:
-            curv = sum(total_parts(keep, send, two))
+            curv = sum(total_parts(keep, send, [two]))
         tile = tile + tiles
         if bit < lax.axis_size("depth"):
             tiles = swap(tile, "depth", bit)
@@ -664,10 +667,10 @@
             [[a[n] for n in sides] for a in adjoints], both, other, after,
         )
 
-    inside = finish(inner, None, (1, 2), [], [], [curv])
+    inside = finish(inner, None, (1, 2), [], [], [])
     one = finish(places[0], coming[0], (0,), [], [], inside[:1])
-    outside = finish(places[3], coming[1], (3,), [tile, tiles], one, [])
-    inner_parts = total_parts(*inside)
+    outside = finish(places[3], coming[1], (3,), [tile, tiles], one, [curv])
+    inner_parts = total_parts(inside[0], inside[1:])
     outer_parts = total_parts(*outside)
     own = refresh(courant, inner_parts, outer_parts, curv, damping_table, plan_step)
     return assemble(own, swap(own, "shot", 1))

time: 93.3 us -> 88.4 us (0.947)
  waiting for transfers between devices: 15.8 us -> 11.9 us
    ppermute x10, waiting for transfers between devices: 13.2 us -> 9.35 us  [swap(): return lax.ppermute(values, axis, [(i, i ^ bit) for i in range(count)])]
    ppermute x14, starting transfers between devices: 28.8 us -> 26.9 us  [exchange(): return lax.ppermute(values, 'depth', links)]
    ppermute x10, starting transfers between devices: 16 us -> 17 us  [swap(): return lax.ppermute(values, axis, [(i, i ^ bit) for i in range(count)])]
    pallas_call x37 -> x38, Pallas kernels: 25.5 us -> 25.4 us  [kernel_call(): pl.pallas_call(kernel, out_shape=tuple(outs), in_specs=[SMEM] * len(small...]
  transfers between devices with their start and end apart: 24 -> 24, of which waited for: 10 -> 9; matrix products, arithmetic and copies ran while one was open for 0% -> 0% of each run, Pallas kernels for 23% -> 27%
where the time goes in v2:
time: 88.4 us; the launch traced here: 88 us
  starting transfers between devices  43.9 us (50%)
  Pallas kernels  26.4 us (30%)
  waiting for transfers between devices  11.9 us (13%)
  local copies, waits for them, and re-layouts  3.58 us (4%)
  between operations  2.03 us (2%)
    ppermute x14, starting transfers between devices, exchange(): return lax.ppermute(values, 'depth', links)  26.9 us
    pallas_call x38, Pallas kernels, kernel_call(): pl.pallas_call(kernel, out_shape=tuple(outs), in_specs=[SMEM] * len(small...  25.4 us
    ppermute x10, starting transfers between devices, swap(): return lax.ppermute(values, axis, [(i, i ^ bit) for i in range(count)])  17 us
    ppermute x10, waiting for transfers between devices, swap(): return lax.ppermute(values, axis, [(i, i ^ bit) for i in range(count)])  9.35 us
    ppermute x14, waiting for transfers between devices, exchange(): return lax.ppermute(values, 'depth', links)  2.59 us
    unnamed x18, local copies, waits for them, and re-layouts  2.3 us
  transfers between devices with their start and end apart: 24, of which 9 were waited for; matrix products, arithmetic and copies ran while one was open for 0% of the time, Pallas kernels for 27%

profile of v2, /device:TPU:0, one launch (start us, length us, event | category | flops | bytes accessed | tf_op | source)
XLA Modules:
  0.0 88.0 jit_solution(10002943642706207814)
XLA Ops:
  0.0 1.3 %dynamic-slice_bitcast_fusion = (f32[4,64,128]{2,1,0:T(8,128)S(1)}, f32[4,64,128]{2,1,0:T(8,128)S(1)}, f32[4,64,128]{2,1,0:T(8,128)S(1)}, f32[4,64,128]{2,1,0:T(8,128)S(1)}) fusion(f32[1,32,64,128]{3,2,1,0:T(8,128)} %param.13, s32[]{:T(128)S(6)} %select_n.17, s32[]{:T(128)S(6)} %select_n.16, f32[1,32,64,128]{3,2,1,0:T(8,128)} %param.12), kind=kLoop, calls=%fused_computation.2 | loop fusion | bytes 1048584 | tf_op jit(solution)/shard_map/dynamic_slice | solution.py:437
  1.3 3.0 %collective-permute-start = (f32[8,64,128]{2,1,0:T(8,128)S(1)}, f32[8,64,128]{2,1,0:T(8,128)S(1)}, u32[]{:S(2)}, u32[]{:S(2)}) collective-permute-start(f32[8,64,128]{2,1,0:T(8,128)S(1)} %pad_maximum_fusion), channel_id=1, source_target_pairs={{0,1},{1,0},{2,3},{3,2},{4,5},{5,4},{6,7},{7,6},{8,9},{9,8},{10,11... | collective-permute-start | bytes 786440 | tf_op jit(solution)/shard_map/ppermute | solution.py:519
  4.4 0.7 collective-permute-start.2
  5.1 1.2 %copy-done.3 = f32[32,64,128]{2,1,0:T(8,128)S(1)} copy-done((f32[32,64,128]{2,1,0:T(8,128)S(1)}, f32[32,64,128]{2,1,0:T(8,128)}, u32[]{:S(2)}) %copy-start.3) | copy-done | bytes 1048600
  6.3 0.6 shard_map.109
  7.6 0.6 copy-done.5
  8.3 3.0 %shard_map.110 = (f32[32,64,128]{2,1,0:T(8,128)S(1)}, f32[32,64,128]{2,1,0:T(8,128)S(1)}, f32[8,128]{1,0:T(8,128)S(1)}, f32[8,128]{1,0:T(8,128)S(1)}, f32[8,128]...) custom-call(f32[1,4]{1,0:T(1,128)S(1)} %copy-done.7, ...), custom_call_target="tpu_custom_call" | custom-call | flops 80000 | bytes 8192 | tf_op jit(solution)/shard_map/pallas_call | solution.py:136
  11.3 0.9 %shard_map.112 = (f32[12,64,128]{2,1,0:T(8,128)S(1)}, f32[12,64,128]{2,1,0:T(8,128)S(1)}) custom-call(f32[32,64,128]{2,1,0:T(8,128)S(1)} %get-tuple-element.60.refs_0_.refs_1_.refs_3_.refs_4_.refs_5_, f32[32,64,128]{2,1,0:T(8,128)S(1)} %get-tuple-element.61.refs_1_.refs_2_, ...), custom_call_target="tpu_custom_call" | custom-call | flops 120000 | bytes 12288 | tf_op jit(solution)/shard_map/pallas_call | solution.py:136
  12.2 0.9 %shard_map.111 = (f32[12,64,128]{2,1,0:T(8,128)S(1)}, f32[12,64,128]{2,1,0:T(8,128)S(1)}) custom-call(f32[32,64,128]{2,1,0:T(8,128)S(1)} %get-tuple-element.60.refs_0_.refs_1_.refs_3_.refs_4_.refs_5_, f32[32,64,128]{2,1,0:T(8,128)S(1)} %get-tuple-element.61.refs_1_.refs_2_, ...), custom_call_target="tpu_custom_call" | custom-call | flops 120000 | bytes 12288 | tf_op jit(solution)/shard_map/pallas_call | solution.py:136
  13.1 2.4 %collective-permute-done.refs_0_ = f32[8,64,128]{2,1,0:T(8,128)S(1)} collective-permute-done((f32[8,64,128]{2,1,0:T(8,128)S(1)}, f32[8,64,128]{2,1,0:T(8,128)S(1)}, u32[]{:S(2)}, u32[]{:S(2)}) %collective-permute-start) | collective-permute-done | bytes 262176 | tf_op jit(solution)/shard_map/ppermute | solution.py:519
  15.5 0.3 shard_map.113
  15.9 2.5 %collective-permute-start.1 = (f32[4,64,128]{2,1,0:T(8,128)S(1)}, f32[4,64,128]{2,1,0:T(8,128)S(1)}, u32[]{:S(2)}, u32[]{:S(2)}) collective-permute-start(f32[4,64,128]{2,1,0:T(8,128)S(1)} %get-tuple-element.67.refs_0_.refs_1_.refs_3_.refs_4_.refs_5_.refs_9_), channel_id=1, source_target_pairs={{0,1},{1,0},{2,3},{3,2},{4,5},{5,4},{6,7},{7,6},{8,9},{9,8},{10,11... | collective-permute-start | bytes 393224 | tf_op jit(solution)/shard_map/ppermute | solution.py:519
  18.4 0.9 %shard_map.114 = (f32[12,64,128]{2,1,0:T(8,128)S(1)}, f32[12,64,128]{2,1,0:T(8,128)S(1)}) custom-call(f32[4,64,128]{2,1,0:T(8,128)S(1)} %get-tuple-element.67.refs_0_.refs_1_.refs_3_.refs_4_.refs_5_.refs_9_, f32[12,64,128]{2,1,0:T(8,128)S(1)} %get-tuple-element.64.refs_6_.refs_1_.refs_2_.refs_4_.refs_5_.refs_8_, ...), custom_call_target="tpu_custom_call" | custom-call | flops 120000 | bytes 12288 | tf_op jit(solution)/shard_map/pallas_call | solution.py:136
  19.3 0.3 shard_map.115
  19.7 0.7 collective-permute-start.4
  20.3 0.9 %shard_map.116 = (f32[12,64,128]{2,1,0:T(8,128)S(1)}, f32[12,64,128]{2,1,0:T(8,128)S(1)}) custom-call(f32[4,64,128]{2,1,0:T(8,128)S(1)} %get-tuple-element.67.refs_0_.refs_1_.refs_3_.refs_4_.refs_5_.refs_9_, f32[12,64,128]{2,1,0:T(8,128)S(1)} %get-tuple-element.64.refs_6_.refs_1_.refs_2_.refs_4_.refs_5_.refs_8_, ...), custom_call_target="tpu_custom_call" | custom-call | flops 120000 | bytes 12288 | tf_op jit(solution)/shard_map/pallas_call | solution.py:136
  21.4 0.3 shard_map.117
  21.7 4.3 %collective-permute-start.3 = (f32[4,64,128]{2,1,0:T(8,128)S(1)}, f32[4,64,128]{2,1,0:T(8,128)S(1)}, u32[]{:S(2)}, u32[]{:S(2)}) collective-permute-start(f32[4,64,128]{2,1,0:T(8,128)S(1)} %get-tuple-element.73.refs_0_.refs_1_.refs_3_.refs_4_.refs_5_.refs_9_), channel_id=1, source_target_pairs={{0,1},{1,0},{2,3},{3,2},{4,5},{5,4},{6,7},{7,6},{8,9},{9,8},{10,11... | collective-permute-start | bytes 393224 | tf_op jit(solution)/shard_map/ppermute | solution.py:519
  25.9 0.9 %shard_map.118 = (f32[12,64,128]{2,1,0:T(8,128)S(1)}, f32[12,64,128]{2,1,0:T(8,128)S(1)}) custom-call(f32[4,64,128]{2,1,0:T(8,128)S(1)} %get-tuple-element.73.refs_0_.refs_1_.refs_3_.refs_4_.refs_5_.refs_9_, f32[12,64,128]{2,1,0:T(8,128)S(1)} %get-tuple-element.69.refs_6_.refs_9_.refs_1_.refs_2_.refs_4_.refs_5_.refs_7_, ...), custom_call_target="tpu_custom_call" | custom-call | flops 120000 | bytes 12288 | tf_op jit(solution)/shard_map/pallas_call | solution.py:136
  26.9 0.3 shard_map.119
  27.2 0.7 collective-permute-start.6
  27.9 0.9 %shard_map.120 = (f32[12,64,128]{2,1,0:T(8,128)S(1)}, f32[12,64,128]{2,1,0:T(8,128)S(1)}) custom-call(f32[4,64,128]{2,1,0:T(8,128)S(1)} %get-tuple-element.73.refs_0_.refs_1_.refs_3_.refs_4_.refs_5_.refs_9_, f32[12,64,128]{2,1,0:T(8,128)S(1)} %get-tuple-element.69.refs_6_.refs_9_.refs_1_.refs_2_.refs_4_.refs_5_.refs_7_, ...), custom_call_target="tpu_custom_call" | custom-call | flops 120000 | bytes 12288 | tf_op jit(solution)/shard_map/pallas_call | solution.py:136
  29.2 4.9 %collective-permute-start.5 = (f32[4,64,128]{2,1,0:T(8,128)S(1)}, f32[4,64,128]{2,1,0:T(8,128)S(1)}, u32[]{:S(2)}, u32[]{:S(2)}) collective-permute-start(f32[4,64,128]{2,1,0:T(8,128)S(1)} %get-tuple-element.79.refs_0_.refs_1_.refs_6_), channel_id=1, source_target_pairs={{0,1},{1,0},{2,3},{3,2},{4,5},{5,4},{6,7},{7,6},{8,9},{9,8},{10,11... | collective-permute-start | bytes 393224 | tf_op jit(solution)/shard_map/ppermute | solution.py:519
  34.1 0.9 %shard_map.122 = (f32[12,64,128]{2,1,0:T(8,128)S(1)}, f32[12,64,128]{2,1,0:T(8,128)S(1)}) custom-call(f32[4,64,128]{2,1,0:T(8,128)S(1)} %get-tuple-element.79.refs_0_.refs_1_.refs_6_, f32[12,64,128]{2,1,0:T(8,128)S(1)} %get-tuple-element.75.refs_9_.refs_12_.refs_1_.refs_2_.refs_4_, f32[12,64,128]{2,1,0:T(8,128)S(1)} %get-tuple-element.77.refs_13_.refs_2_.refs_3_.refs_5_, ...), custom_call_target="tpu_custom_call" | custom-call | flops 120000 | bytes 12288 | tf_op jit(solution)/shard_map/pallas_call | solution.py:136
  35.1 0.3 shard_map.123
  35.4 0.8 collective-permute-start.7
  36.3 0.3 copy-done.4
  36.6 0.4 shard_map.125
  37.0 0.9 %shard_map.124 = (f32[12,64,128]{2,1,0:T(8,128)S(1)}, f32[12,64,128]{2,1,0:T(8,128)S(1)}) custom-call(f32[4,64,128]{2,1,0:T(8,128)S(1)} %get-tuple-element.79.refs_0_.refs_1_.refs_6_, f32[12,64,128]{2,1,0:T(8,128)S(1)} %get-tuple-element.75.refs_9_.refs_12_.refs_1_.refs_2_.refs_4_, f32[12,64,128]{2,1,0:T(8,128)S(1)} %get-tuple-element.77.refs_13_.refs_2_.refs_3_.refs_5_, ...), custom_call_target="tpu_custom_call" | custom-call | flops 120000 | bytes 12288 | tf_op jit(solution)/shard_map/pallas_call | solution.py:136
  38.0 0.9 %shard_map.126.refs_14_.refs_9_.refs_1_.refs_2_.refs_4_.refs_5_.refs_6_.refs_25_ = f32[12,64,128]{2,1,0:T(8,128)S(1)} custom-call(f32[32,64,128]{2,1,0:T(8,128)S(1)} %get-tuple-element.84.refs_0_.refs_1_.refs_3_.refs_4_.refs_5_, f32[32,64,128]{2,1,0:T(8,128)S(1)} %get-tuple-element.85.refs_1_.refs_2_, ...), custom_call_target="tpu_custom_call" | custom-call | flops 120000 | bytes 12288 | tf_op jit(solution)/shard_map/pallas_call | solution.py:136
  38.9 0.9 %shard_map.127.refs_15_.refs_10_.refs_2_.refs_3_.refs_5_.refs_6_.refs_7_.refs_26_ = f32[12,64,128]{2,1,0:T(8,128)S(1)} custom-call(f32[32,64,128]{2,1,0:T(8,128)S(1)} %get-tuple-element.84.refs_0_.refs_1_.refs_3_.refs_4_.refs_5_, f32[32,64,128]{2,1,0:T(8,128)S(1)} %get-tuple-element.85.refs_1_.refs_2_, ...), custom_call_target="tpu_custom_call" | custom-call | flops 120000 | bytes 12288 | tf_op jit(solution)/shard_map/pallas_call | solution.py:136
  39.9 0.3 shard_map.128
  40.2 0.3 shard_map.129.refs_0_.refs_1_.refs_3_.refs_4_.refs_5_.refs_19_
  40.5 0.9 %shard_map.130.refs_12_.refs_7_.refs_10_.refs_1_.refs_2_.refs_5_.refs_23_.refs_6_ = f32[12,64,128]{2,1,0:T(8,128)S(1)} custom-call(f32[4,64,128]{2,1,0:T(8,128)S(1)} %shard_map.129.refs_0_.refs_1_.refs_3_.refs_4_.refs_5_.refs_19_, f32[12,64,128]{2,1,0:T(8,128)S(1)} %shard_map.126.refs_14_.refs_9_.refs_1_.refs_2_.refs_4_.refs_5_.refs_6_.refs_25_, ...), custom_call_target="tpu_custom_call" | custom-call | flops 120000 | bytes 12288 | tf_op jit(solution)/shard_map/pallas_call | solution.py:136
  41.5 0.3 shard_map.131
  41.8 0.3 shard_map.132.refs_16_.refs_3_.refs_4_.refs_6_.refs_7_.refs_8_.refs_19_
  42.5 4.5 %collective-permute-start.10 = (f32[4,64,128]{2,1,0:T(8,128)S(1)}, f32[4,64,128]{2,1,0:T(8,128)S(1)}, u32[]{:S(2)}, u32[]{:S(2)}) collective-permute-start(f32[4,64,128]{2,1,0:T(8,128)S(1)} %shard_map.129.refs_0_.refs_1_.refs_3_.refs_4_.refs_5_.refs_19_), channel_id=1, source_target_pairs={{0,1},{1,0},{2,3},{3,2},{4,5},{5,4},{6,7},{7,6},{8,9},{9,8},{10,11... | collective-permute-start | bytes 393224 | tf_op jit(solution)/shard_map/ppermute | solution.py:519
  47.1 0.8 collective-permute-start.9
  47.9 4.4 %collective-permute-start.11 = (f32[8,128]{1,0:T(8,128)S(1)}, f32[8,128]{1,0:T(8,128)S(1)}, u32[]{:S(2)}, u32[]{:S(2)}) collective-permute-start(f32[8,128]{1,0:T(8,128)S(1)} %get-tuple-element.107), channel_id=1, source_target_pairs={{0,1},{1,0},{2,3},{3,2},{4,5},{5,4},{6,7},{7,6},{8,9},{9,8},{10,11... | collective-permute-start | bytes 12296 | tf_op jit(solution)/shard_map/ppermute | solution.py:524
  52.3 0.9 %shard_map.134.refs_11_.refs_2_.refs_3_.refs_6_.refs_24_.refs_7_ = f32[12,64,128]{2,1,0:T(8,128)S(1)} custom-call(f32[4,64,128]{2,1,0:T(8,128)S(1)} %shard_map.129.refs_0_.refs_1_.refs_3_.refs_4_.refs_5_.refs_19_, f32[12,64,128]{2,1,0:T(8,128)S(1)} %shard_map.126.refs_14_.refs_9_.refs_1_.refs_2_.refs_4_.refs_5_.refs_6_.refs_25_, ...), custom_call_target="tpu_custom_call" | custom-call | flops 120000 | bytes 12288 | tf_op jit(solution)/shard_map/pallas_call | solution.py:136
  53.2 0.3 shard_map.135.refs_0_.refs_1_.refs_4_.refs_5_.refs_18_
  53.7 0.9 %shard_map.136.refs_10_.refs_13_.refs_1_.refs_21_.refs_2_ = f32[12,64,128]{2,1,0:T(8,128)S(1)} custom-call(f32[4,64,128]{2,1,0:T(8,128)S(1)} %shard_map.135.refs_0_.refs_1_.refs_4_.refs_5_.refs_18_, f32[12,64,128]{2,1,0:T(8,128)S(1)} %shard_map.130.refs_12_.refs_7_.refs_10_.refs_1_.refs_2_.refs_5_.refs_23_.refs_6_, ...), custom_call_target="tpu_custom_call" | custom-call | flops 120000 | bytes 12288 | tf_op jit(solution)/shard_map/pallas_call | solution.py:136
  54.6 0.3 shard_map.137.refs_1_.refs_3_.refs_4_.refs_7_.refs_8_.refs_18_
  55.0 0.7 collective-permute-start.14
  55.7 1.6 %collective-permute-start.12 = (f32[16,64,128]{2,1,0:T(8,128)S(1)}, f32[16,64,128]{2,1,0:T(8,128)S(1)}, u32[]{:S(2)}, u32[]{:S(2)}) collective-permute-start(f32[16,64,128]{2,1,0:T(8,128)S(1)} %shard_map.138), channel_id=1, source_target_pairs={{0,16},{8,24},{16,0},{24,8},{1,17},{9,25},{17,1},{25,9},{2,18},{10... | collective-permute-start | bytes 1572872 | tf_op jit(solution)/shard_map/ppermute | solution.py:524
  57.3 4.7 %collective-permute-start.15 = (f32[8,128]{1,0:T(8,128)S(1)}, f32[8,128]{1,0:T(8,128)S(1)}, u32[]{:S(2)}, u32[]{:S(2)}) collective-permute-start(f32[8,128]{1,0:T(8,128)S(1)} %add.28), channel_id=1, source_target_pairs={{0,2},{1,3},{2,0},{3,1},{4,6},{5,7},{6,4},{7,5},{8,10},{9,11},{10,... | collective-permute-start | bytes 12296 | tf_op jit(solution)/shard_map/ppermute | solution.py:524
  62.0 0.9 %shard_map.139.refs_14_.refs_2_.refs_22_.refs_3_ = f32[12,64,128]{2,1,0:T(8,128)S(1)} custom-call(f32[4,64,128]{2,1,0:T(8,128)S(1)} %shard_map.135.refs_0_.refs_1_.refs_4_.refs_5_.refs_18_, f32[12,64,128]{2,1,0:T(8,128)S(1)} %shard_map.130.refs_12_.refs_7_.refs_10_.refs_1_.refs_2_.refs_5_.refs_23_.refs_6_, ...), custom_call_target="tpu_custom_call" | custom-call | flops 120000 | bytes 12288 | tf_op jit(solution)/shard_map/pallas_call | solution.py:136
  62.9 0.3 shard_map.140.refs_13_.refs_0_.refs_1_.refs_17_
  63.6 0.3 shard_map.141.refs_3_.refs_4_.refs_17_
  63.9 2.0 %shard_map.142 = (f32[12,64,128]{2,1,0:T(8,128)S(1)}, f32[12,64,128]{2,1,0:T(8,128)S(1)}) custom-call(f32[4,64,128]{2,1,0:T(8,128)S(1)} %shard_map.140.refs_13_.refs_0_.refs_1_.refs_17_, f32[12,64,128]{2,1,0:T(8,128)S(1)} %shard_map.136.refs_10_.refs_13_.refs_1_.refs_21_.refs_2_, f32[12,64,128]{2,1,0:T(8,128)S(1)} %shard_map.139.refs_14_.refs_2_.refs_22_.refs_3_, ...), custom_call_target="tpu_custom_call" | custom-call | flops 240000 | bytes 24576 | tf_op jit(solution)/shard_map/pallas_call | solution.py:136
  66.0 2.6 %collective-permute-start.20 = (f32[4,64,128]{2,1,0:T(8,128)S(1)}, f32[4,64,128]{2,1,0:T(8,128)S(1)}, u32[]{:S(2)}, u32[]{:S(2)}) collective-permute-start(f32[4,64,128]{2,1,0:T(8,128)S(1)} %shard_map.140.refs_13_.refs_0_.refs_1_.refs_17_), channel_id=1, source_target_pairs={{0,1},{1,0},{2,3},{3,2},{4,5},{5,4},{6,7},{7,6},{8,9},{9,8},{10,11... | collective-permute-start | bytes 393224 | tf_op jit(solution)/shard_map/ppermute | solution.py:519
  68.6 0.7 collective-permute-start.18
  69.3 0.6 collective-permute-start.17
  69.9 4.3 %collective-permute-start.19 = (f32[8,128]{1,0:T(8,128)S(1)}, f32[8,128]{1,0:T(8,128)S(1)}, u32[]{:S(2)}, u32[]{:S(2)}) collective-permute-start(f32[8,128]{1,0:T(8,128)S(1)} %add.29.refs_20_), channel_id=1, source_target_pairs={{0,4},{1,5},{2,6},{3,7},{4,0},{5,1},{6,2},{7,3},{8,12},{9,13},{10,... | collective-permute-start | bytes 12296 | tf_op jit(solution)/shard_map/ppermute | solution.py:524
  74.1 0.4 shard_map.144.refs_22_
  74.6 1.9 %collective-permute-done.19.refs_21_ = f32[8,128]{1,0:T(8,128)S(1)} collective-permute-done((f32[8,128]{1,0:T(8,128)S(1)}, f32[8,128]{1,0:T(8,128)S(1)}, u32[]{:S(2)}, u32[]{:S(2)}) %collective-permute-start.19) | collective-permute-done | bytes 4128 | tf_op jit(solution)/shard_map/ppermute | solution.py:524
  76.5 0.4 shard_map.145
  77.0 1.3 %collective-permute-done.21 = f32[264,128]{1,0:T(8,128)S(1)} collective-permute-done((f32[264,128]{1,0:T(8,128)S(1)}, f32[264,128]{1,0:T(8,128)S(1)}, u32[]{:S(2)}, u32[]{:S(2)}) %collective-permute-start.21) | collective-permute-done | bytes 135200 | tf_op jit(solution)/shard_map/ppermute | solution.py:524
  78.4 1.2 %collective-permute-start.22 = (f32[264,128]{1,0:T(8,128)S(1)}, f32[264,128]{1,0:T(8,128)S(1)}, u32[]{:S(2)}, u32[]{:S(2)}) collective-permute-start(f32[264,128]{1,0:T(8,128)S(1)} %add.30.rest_2_), channel_id=1, source_target_pairs={{0,16},{8,24},{16,0},{24,8},{1,17},{9,25},{17,1},{25,9},{2,18},{10... | collective-permute-start | bytes 405512 | tf_op jit(solution)/shard_map/ppermute | solution.py:524
  80.2 0.3 collective-permute-done.17.rest_1_
  80.5 3.5 %collective-permute-done.22.rest_3_ = f32[264,128]{1,0:T(8,128)S(1)} collective-permute-done((f32[264,128]{1,0:T(8,128)S(1)}, f32[264,128]{1,0:T(8,128)S(1)}, u32[]{:S(2)}, u32[]{:S(2)}) %collective-permute-start.22) | collective-permute-done | bytes 135200 | tf_op jit(solution)/shard_map/ppermute | solution.py:524
  84.1 0.8 shard_map.146.own_ref
  85.0 1.9 %collective-permute-done.23.other_ref = f32[16,64,128]{2,1,0:T(8,128)S(1)} collective-permute-done((f32[16,64,128]{2,1,0:T(8,128)S(1)}, f32[16,64,128]{2,1,0:T(8,128)S(1)}, u32[]{:S(2)}, u32[]{:S(2)}) %collective-permute-start.23) | collective-permute-done | bytes 524320 | tf_op jit(solution)/shard_map/ppermute | solution.py:524
  86.9 1.0 %shard_map.147 = f32[32,64,128]{2,1,0:T(8,128)} custom-call(f32[16,64,128]{2,1,0:T(8,128)S(1)} %shard_map.146.own_ref, f32[16,64,128]{2,1,0:T(8,128)S(1)} %collective-permute-done.23.other_ref), custom_call_target="tpu_custom_call" | custom-call | flops 80000 | bytes 8192 | tf_op jit(solution)/shard_map/pallas_call | solution.py:504
  (48 shorter events, 1.8 us)
Async XLA Ops:
  0.0 5.1 %copy-start = (f32[1,32,64,128]{3,2,1,0:T(8,128)S(1)}, f32[1,32,64,128]{3,2,1,0:T(8,128)}, u32[]{:S(2)}) copy-start(f32[1,32,64,128]{3,2,1,0:T(8,128)} %param.12) | copy-start | bytes 3145732
  0.0 5.1 %copy-start.2 = (f32[1,32,64,128]{3,2,1,0:T(8,128)S(1)}, f32[1,32,64,128]{3,2,1,0:T(8,128)}, u32[]{:S(2)}) copy-start(f32[1,32,64,128]{3,2,1,0:T(8,128)} %param.11) | copy-start | bytes 3145732
  1.3 14.2 %collective-permute-start = (f32[8,64,128]{2,1,0:T(8,128)S(1)}, f32[8,64,128]{2,1,0:T(8,128)S(1)}, u32[]{:S(2)}, u32[]{:S(2)}) collective-permute-start(f32[8,64,128]{2,1,0:T(8,128)S(1)} %pad_maximum_fusion), channel_id=1, source_target_pairs={{0,1},{1,0},{2,3},{3,2},{4,5},{5,4},{6,7},{7,6},{8,9},{9,8},{10,11... | collective-permute-start | bytes 786440 | tf_op jit(solution)/shard_map/ppermute | solution.py:519
  4.4 14.9 %collective-permute-start.2 = (f32[8,64,128]{2,1,0:T(8,128)S(1)}, f32[8,64,128]{2,1,0:T(8,128)S(1)}, u32[]{:S(2)}, u32[]{:S(2)}) collective-permute-start(f32[8,64,128]{2,1,0:T(8,128)S(1)} %pad_maximum_fusion.1), channel_id=1, source_target_pairs={{1,2},{2,1},{3,4},{4,3},{5,6},{6,5},{9,10},{10,9},{11,12},{12,11},... | collective-permute-start | bytes 786440 | tf_op jit(solution)/shard_map/ppermute | solution.py:519
  5.1 1.2 %copy-start.3 = (f32[32,64,128]{2,1,0:T(8,128)S(1)}, f32[32,64,128]{2,1,0:T(8,128)}, u32[]{:S(2)}) copy-start(f32[32,64,128]{2,1,0:T(8,128)} %refs_2_.1) | copy-start | bytes 3145732
  7.6 0.7 copy-start.5
  7.6 0.7 copy-start.7
  7.6 0.7 copy-start.8
  15.9 5.5 %collective-permute-start.1 = (f32[4,64,128]{2,1,0:T(8,128)S(1)}, f32[4,64,128]{2,1,0:T(8,128)S(1)}, u32[]{:S(2)}, u32[]{:S(2)}) collective-permute-start(f32[4,64,128]{2,1,0:T(8,128)S(1)} %get-tuple-element.67.refs_0_.refs_1_.refs_3_.refs_4_.refs_5_.refs_9_), channel_id=1, source_target_pairs={{0,1},{1,0},{2,3},{3,2},{4,5},{5,4},{6,7},{7,6},{8,9},{9,8},{10,11... | collective-permute-start | bytes 393224 | tf_op jit(solution)/shard_map/ppermute | solution.py:519
  19.7 7.2 %collective-permute-start.4 = (f32[4,64,128]{2,1,0:T(8,128)S(1)}, f32[4,64,128]{2,1,0:T(8,128)S(1)}, u32[]{:S(2)}, u32[]{:S(2)}) collective-permute-start(f32[4,64,128]{2,1,0:T(8,128)S(1)} %get-tuple-element.70.refs_3_.refs_4_.refs_6_.refs_7_.refs_8_.refs_9_), channel_id=1, source_target_pairs={{1,2},{2,1},{3,4},{4,3},{5,6},{6,5},{9,10},{10,9},{11,12},{12,11},... | collective-permute-start | bytes 393224 | tf_op jit(solution)/shard_map/ppermute | solution.py:519
  21.7 7.2 %collective-permute-start.3 = (f32[4,64,128]{2,1,0:T(8,128)S(1)}, f32[4,64,128]{2,1,0:T(8,128)S(1)}, u32[]{:S(2)}, u32[]{:S(2)}) collective-permute-start(f32[4,64,128]{2,1,0:T(8,128)S(1)} %get-tuple-element.73.refs_0_.refs_1_.refs_3_.refs_4_.refs_5_.refs_9_), channel_id=1, source_target_pairs={{0,1},{1,0},{2,3},{3,2},{4,5},{5,4},{6,7},{7,6},{8,9},{9,8},{10,11... | collective-permute-start | bytes 393224 | tf_op jit(solution)/shard_map/ppermute | solution.py:519
  27.2 7.8 %collective-permute-start.6 = (f32[4,64,128]{2,1,0:T(8,128)S(1)}, f32[4,64,128]{2,1,0:T(8,128)S(1)}, u32[]{:S(2)}, u32[]{:S(2)}) collective-permute-start(f32[4,64,128]{2,1,0:T(8,128)S(1)} %get-tuple-element.76.refs_3_.refs_4_.refs_6_.refs_7_.refs_8_.refs_9_), channel_id=1, source_target_pairs={{1,2},{2,1},{3,4},{4,3},{5,6},{6,5},{9,10},{10,9},{11,12},{12,11},... | collective-permute-start | bytes 393224 | tf_op jit(solution)/shard_map/ppermute | solution.py:519
  29.2 10.7 %collective-permute-start.5 = (f32[4,64,128]{2,1,0:T(8,128)S(1)}, f32[4,64,128]{2,1,0:T(8,128)S(1)}, u32[]{:S(2)}, u32[]{:S(2)}) collective-permute-start(f32[4,64,128]{2,1,0:T(8,128)S(1)} %get-tuple-element.79.refs_0_.refs_1_.refs_6_), channel_id=1, source_target_pairs={{0,1},{1,0},{2,3},{3,2},{4,5},{5,4},{6,7},{7,6},{8,9},{9,8},{10,11... | collective-permute-start | bytes 393224 | tf_op jit(solution)/shard_map/ppermute | solution.py:519
  35.1 1.2 %copy-start.1 = (f32[1,32,64,128]{3,2,1,0:T(8,128)S(1)}, f32[1,32,64,128]{3,2,1,0:T(8,128)}, u32[]{:S(2)}) copy-start(f32[1,32,64,128]{3,2,1,0:T(8,128)} %param.13) | copy-start | bytes 3145732
  35.1 1.5 %copy-start.4 = (f32[1,32,64,128]{3,2,1,0:T(8,128)S(1)}, f32[1,32,64,128]{3,2,1,0:T(8,128)}, u32[]{:S(2)}) copy-start(f32[1,32,64,128]{3,2,1,0:T(8,128)} %param.14) | copy-start | bytes 3145732
  35.4 6.1 %collective-permute-start.7 = (f32[4,64,128]{2,1,0:T(8,128)S(1)}, f32[4,64,128]{2,1,0:T(8,128)S(1)}, u32[]{:S(2)}, u32[]{:S(2)}) collective-permute-start(f32[4,64,128]{2,1,0:T(8,128)S(1)} %get-tuple-element.82.refs_3_.refs_4_.refs_6_), channel_id=1, source_target_pairs={{1,2},{2,1},{3,4},{4,3},{5,6},{6,5},{9,10},{10,9},{11,12},{12,11},... | collective-permute-start | bytes 393224 | tf_op jit(solution)/shard_map/ppermute | solution.py:519
  42.5 13.2 %collective-permute-start.8 = (f32[16,64,128]{2,1,0:T(8,128)S(1)}, f32[16,64,128]{2,1,0:T(8,128)S(1)}, u32[]{:S(2)}, u32[]{:S(2)}) collective-permute-start(f32[16,64,128]{2,1,0:T(8,128)S(1)} %get-tuple-element.105), channel_id=1, source_target_pairs={{0,8},{8,0},{16,24},{24,16},{1,9},{9,1},{17,25},{25,17},{2,10},{10... | collective-permute-start | bytes 1572872 | tf_op jit(solution)/shard_map/ppermute | solution.py:524
  42.5 10.7 %collective-permute-start.10 = (f32[4,64,128]{2,1,0:T(8,128)S(1)}, f32[4,64,128]{2,1,0:T(8,128)S(1)}, u32[]{:S(2)}, u32[]{:S(2)}) collective-permute-start(f32[4,64,128]{2,1,0:T(8,128)S(1)} %shard_map.129.refs_0_.refs_1_.refs_3_.refs_4_.refs_5_.refs_19_), channel_id=1, source_target_pairs={{0,1},{1,0},{2,3},{3,2},{4,5},{5,4},{6,7},{7,6},{8,9},{9,8},{10,11... | collective-permute-start | bytes 393224 | tf_op jit(solution)/shard_map/ppermute | solution.py:519
  47.1 7.6 %collective-permute-start.9 = (f32[4,64,128]{2,1,0:T(8,128)S(1)}, f32[4,64,128]{2,1,0:T(8,128)S(1)}, u32[]{:S(2)}, u32[]{:S(2)}) collective-permute-start(f32[4,64,128]{2,1,0:T(8,128)S(1)} %shard_map.132.refs_16_.refs_3_.refs_4_.refs_6_.refs_7_.refs_8_.refs_19_), channel_id=1, source_target_pairs={{1,2},{2,1},{3,4},{4,3},{5,6},{6,5},{9,10},{10,9},{11,12},{12,11},... | collective-permute-start | bytes 393224 | tf_op jit(solution)/shard_map/ppermute | solution.py:519
  47.9 6.7 %collective-permute-start.11 = (f32[8,128]{1,0:T(8,128)S(1)}, f32[8,128]{1,0:T(8,128)S(1)}, u32[]{:S(2)}, u32[]{:S(2)}) collective-permute-start(f32[8,128]{1,0:T(8,128)S(1)} %get-tuple-element.107), channel_id=1, source_target_pairs={{0,1},{1,0},{2,3},{3,2},{4,5},{5,4},{6,7},{7,6},{8,9},{9,8},{10,11... | collective-permute-start | bytes 12296 | tf_op jit(solution)/shard_map/ppermute | solution.py:524
  53.6 9.3 %collective-permute-start.13 = (f32[4,64,128]{2,1,0:T(8,128)S(1)}, f32[4,64,128]{2,1,0:T(8,128)S(1)}, u32[]{:S(2)}, u32[]{:S(2)}) collective-permute-start(f32[4,64,128]{2,1,0:T(8,128)S(1)} %shard_map.135.refs_0_.refs_1_.refs_4_.refs_5_.refs_18_), channel_id=1, source_target_pairs={{0,1},{1,0},{2,3},{3,2},{4,5},{5,4},{6,7},{7,6},{8,9},{9,8},{10,11... | collective-permute-start | bytes 393224 | tf_op jit(solution)/shard_map/ppermute | solution.py:519
  55.0 8.6 %collective-permute-start.14 = (f32[4,64,128]{2,1,0:T(8,128)S(1)}, f32[4,64,128]{2,1,0:T(8,128)S(1)}, u32[]{:S(2)}, u32[]{:S(2)}) collective-permute-start(f32[4,64,128]{2,1,0:T(8,128)S(1)} %shard_map.137.refs_1_.refs_3_.refs_4_.refs_7_.refs_8_.refs_18_), channel_id=1, source_target_pairs={{1,2},{2,1},{3,4},{4,3},{5,6},{6,5},{9,10},{10,9},{11,12},{12,11},... | collective-permute-start | bytes 393224 | tf_op jit(solution)/shard_map/ppermute | solution.py:519
  55.7 18.8 %collective-permute-start.12 = (f32[16,64,128]{2,1,0:T(8,128)S(1)}, f32[16,64,128]{2,1,0:T(8,128)S(1)}, u32[]{:S(2)}, u32[]{:S(2)}) collective-permute-start(f32[16,64,128]{2,1,0:T(8,128)S(1)} %shard_map.138), channel_id=1, source_target_pairs={{0,16},{8,24},{16,0},{24,8},{1,17},{9,25},{17,1},{25,9},{2,18},{10... | collective-permute-start | bytes 1572872 | tf_op jit(solution)/shard_map/ppermute | solution.py:524
  57.3 6.3 %collective-permute-start.15 = (f32[8,128]{1,0:T(8,128)S(1)}, f32[8,128]{1,0:T(8,128)S(1)}, u32[]{:S(2)}, u32[]{:S(2)}) collective-permute-start(f32[8,128]{1,0:T(8,128)S(1)} %add.28), channel_id=1, source_target_pairs={{0,2},{1,3},{2,0},{3,1},{4,6},{5,7},{6,4},{7,5},{8,10},{9,11},{10,... | collective-permute-start | bytes 12296 | tf_op jit(solution)/shard_map/ppermute | solution.py:524
  65.9 3.3 %collective-permute-start.16 = (f32[12,64,128]{2,1,0:T(8,128)S(1)}, f32[12,64,128]{2,1,0:T(8,128)S(1)}, u32[]{:S(2)}, u32[]{:S(2)}) collective-permute-start(f32[12,64,128]{2,1,0:T(8,128)S(1)} %get-tuple-element.110), channel_id=1, source_target_pairs={{0,8},{8,0},{16,24},{24,16},{1,9},{9,1},{17,25},{25,17},{2,10},{10... | collective-permute-start | bytes 1179656 | tf_op jit(solution)/shard_map/ppermute | solution.py:524
  66.0 8.2 %collective-permute-start.20 = (f32[4,64,128]{2,1,0:T(8,128)S(1)}, f32[4,64,128]{2,1,0:T(8,128)S(1)}, u32[]{:S(2)}, u32[]{:S(2)}) collective-permute-start(f32[4,64,128]{2,1,0:T(8,128)S(1)} %shard_map.140.refs_13_.refs_0_.refs_1_.refs_17_), channel_id=1, source_target_pairs={{0,1},{1,0},{2,3},{3,2},{4,5},{5,4},{6,7},{7,6},{8,9},{9,8},{10,11... | collective-permute-start | bytes 393224 | tf_op jit(solution)/shard_map/ppermute | solution.py:519
  68.6 8.0 %collective-permute-start.18 = (f32[4,64,128]{2,1,0:T(8,128)S(1)}, f32[4,64,128]{2,1,0:T(8,128)S(1)}, u32[]{:S(2)}, u32[]{:S(2)}) collective-permute-start(f32[4,64,128]{2,1,0:T(8,128)S(1)} %shard_map.141.refs_3_.refs_4_.refs_17_), channel_id=1, source_target_pairs={{1,2},{2,1},{3,4},{4,3},{5,6},{6,5},{9,10},{10,9},{11,12},{12,11},... | collective-permute-start | bytes 393224 | tf_op jit(solution)/shard_map/ppermute | solution.py:519
  69.3 11.3 %collective-permute-start.17 = (f32[12,64,128]{2,1,0:T(8,128)S(1)}, f32[12,64,128]{2,1,0:T(8,128)S(1)}, u32[]{:S(2)}, u32[]{:S(2)}) collective-permute-start(f32[12,64,128]{2,1,0:T(8,128)S(1)} %shard_map.143.rest_0_), channel_id=1, source_target_pairs={{0,16},{8,24},{16,0},{24,8},{1,17},{9,25},{17,1},{25,9},{2,18},{10... | collective-permute-start | bytes 1179656 | tf_op jit(solution)/shard_map/ppermute | solution.py:524
  69.9 6.7 %collective-permute-start.19 = (f32[8,128]{1,0:T(8,128)S(1)}, f32[8,128]{1,0:T(8,128)S(1)}, u32[]{:S(2)}, u32[]{:S(2)}) collective-permute-start(f32[8,128]{1,0:T(8,128)S(1)} %add.29.refs_20_), channel_id=1, source_target_pairs={{0,4},{1,5},{2,6},{3,7},{4,0},{5,1},{6,2},{7,3},{8,12},{9,13},{10,... | collective-permute-start | bytes 12296 | tf_op jit(solution)/shard_map/ppermute | solution.py:524
  76.9 1.4 %collective-permute-start.21 = (f32[264,128]{1,0:T(8,128)S(1)}, f32[264,128]{1,0:T(8,128)S(1)}, u32[]{:S(2)}, u32[]{:S(2)}) collective-permute-start(f32[264,128]{1,0:T(8,128)S(1)} %get-tuple-element.112), channel_id=1, source_target_pairs={{0,8},{8,0},{16,24},{24,16},{1,9},{9,1},{17,25},{25,17},{2,10},{10... | collective-permute-start | bytes 405512 | tf_op jit(solution)/shard_map/ppermute | solution.py:524
  78.4 5.7 %copy-start.6 = (f32[64]{0:T(128)S(1)}, f32[64]{0:T(128)}, u32[]{:S(2)}) copy-start(f32[64]{0:T(128)} %table_ref.1) | copy-start | bytes 772
  78.4 5.7 %collective-permute-start.22 = (f32[264,128]{1,0:T(8,128)S(1)}, f32[264,128]{1,0:T(8,128)S(1)}, u32[]{:S(2)}, u32[]{:S(2)}) collective-permute-start(f32[264,128]{1,0:T(8,128)S(1)} %add.30.rest_2_), channel_id=1, source_target_pairs={{0,16},{8,24},{16,0},{24,8},{1,17},{9,25},{17,1},{25,9},{2,18},{10... | collective-permute-start | bytes 405512 | tf_op jit(solution)/shard_map/ppermute | solution.py:524
  84.9 2.0 %collective-permute-start.23 = (f32[16,64,128]{2,1,0:T(8,128)S(1)}, f32[16,64,128]{2,1,0:T(8,128)S(1)}, u32[]{:S(2)}, u32[]{:S(2)}) collective-permute-start(f32[16,64,128]{2,1,0:T(8,128)S(1)} %shard_map.146.own_ref), channel_id=1, source_target_pairs={{0,8},{8,0},{16,24},{24,16},{1,9},{9,1},{17,25},{25,17},{2,10},{10... | collective-permute-start | bytes 1572872 | tf_op jit(solution)/shard_map/ppermute | solution.py:524

commit v3 on v2

--- a/solution.py
+++ b/solution.py
@@ -83,6 +83,9 @@
 
             source = ref_at + jnp.where(odd == 1, i, HALO - 1 - i)
             interleave(put, lambda spot, source=source: ref[source, spot, :], width)
+        elif len(ref.shape) == 2:
+            rows = slice((HALO - 1 - i) * width, (HALO - i) * width)
+            pad[at + i, PAD : PAD + width, :] = ref[rows, :]
         else:
             pad[at + i, PAD : PAD + width, :] = ref[HALO - 1 - i]
 
@@ -317,14 +320,17 @@
     return kernel_call(kernel, [], sum(groups, []), outs, scratch, count)
 
 
-def curvature(laps, after):
+def curvature(laps, message, after):
     number = len(laps)
     half, width, length = laps[0][1].shape
     size = half + HALO
 
     def kernel(*refs):
         ranged = [refs[n * number : (n + 1) * number] for n in range(4)]
-        keep_ref, *send_refs, tile_ref = refs[4 * number + 1 :]
+        planes_ref = refs[4 * number]
+        keep_ref, *send_refs, tile_ref, message_ref = refs[4 * number + 2 :]
+        for i in range(HALO):
+            message_ref[i * width : (i + 1) * width, :] = planes_ref[i]
         core = lax.axis_index("shot") % 2
 
         def squares(lap_refs, at):
@@ -349,10 +355,11 @@
                     write_piece(send_refs, i, value)
                     total = total + fold(value)
                 tile_ref[...] = total
+                message_ref[HALO * width : HALO * width + 8, :] = total
 
     outs = [f32(size, width, length)]
-    outs += [f32(size // 1, width, length)] * 1 + [f32(8, length)]
-    arrays = [lap[n] for n in range(4) for lap in laps] + [after]
+    outs += [f32(size // 1, width, length)] * 1 + [f32(8, length), f32(HALO * width + 8, length)]
+    arrays = [lap[n] for n in range(4) for lap in laps] + [message, after]
     return kernel_call(kernel, [], arrays, outs, [], 8)
 
 
@@ -606,7 +613,6 @@
         if last:
             edge = (halos[0], HALO, True)
             one_adj = back(step, 0, edge, more, rest, (one[0], starts[0]), after)
-            message = exchange(one_adj, 0)
             newer = [(one_adj, starts[0]), (near_adj, starts[1]), (far_adj, starts[2])]
             near_next = back(step - 1, 1, None, newer, more, (fields[-1][1], starts[1]), ())
             two = ahead(step, 3, coming[1], cur, old, [near_next])
@@ -625,9 +631,10 @@
             coming = [(message, 0, False), (exchange(two[0], 1), 0, False)]
             far = ahead(step + 1, 2, None, newer, cur, ())
             near, old, cur = near_next, cur, newer
+    keep, *send, tile, message = curvature(laps, one_adj, two_adj)
+    message = exchange(message, 0)
     coming = [(message, 0, False), (exchange(two_adj, 1), 0, False)]
-    keep, *send, tile = curvature(laps, two_adj)
-    tiles = swap(tile, "depth", 1)
+    tiles = message[HALO * width :, :]
     bit = 2
     old, cur, near = more, newer, near_next
     adjoints = [arrays_of(cur)]
@@ -636,6 +643,10 @@
         after = [near, far]
         one = back(step, 0, coming[0], cur, old, (fields[step][0], starts[0]), after)
         message = exchange(one, 0)
+        if bit < lax.axis_size("depth"):
+            tile = tile + tiles
+            tiles = swap(tile, "depth", bit)
+            bit *= 2
         newer = [(one, starts[0]), (near, starts[1]), (far, starts[2])]
         if step > 1:
             near_next = back(step - 1, 1, None, newer, cur, (fields[step - 1][1], starts[1]), ())
@@ -649,10 +660,6 @@
         adjoints.insert(0, arrays_of(cur))
         if step == STEPS - 2:
             curv = sum(total_parts(keep, send, [two]))
-        tile = tile + tiles
-        if bit < lax.axis_size("depth"):
-            tiles = swap(tile, "depth", bit)
-            bit *= 2
     while bit < lax.axis_size("depth"):
         tile = tile + tiles
         tiles = swap(tile, "depth", bit)

time: 88.4 us -> 91.5 us (1.035)
  waiting for transfers between devices: 11.9 us -> 19.1 us
  starting transfers between devices: 43.9 us -> 39.5 us
    ppermute x10 -> x9, starting transfers between devices: 17 us -> 8.31 us  [swap(): return lax.ppermute(values, axis, [(i, i ^ bit) for i in range(count)])]
    ppermute x14, waiting for transfers between devices: 2.59 us -> 8.54 us  [exchange(): return lax.ppermute(values, 'depth', links)]
    ppermute x14, starting transfers between devices: 26.9 us -> 31.2 us  [exchange(): return lax.ppermute(values, 'depth', links)]
    ppermute x10 -> x9, waiting for transfers between devices: 9.35 us -> 10.6 us  [swap(): return lax.ppermute(values, axis, [(i, i ^ bit) for i in range(count)])]
  transfers between devices with their start and end apart: 24 -> 23, of which waited for: 9 -> 10; matrix products, arithmetic and copies ran while one was open for 0% -> 0% of each run, Pallas kernels for 27% -> 26%
where the time goes in v3:
time: 91.5 us; the launch traced here: 90.9 us
  starting transfers between devices  39.5 us (43%)
  Pallas kernels  26.6 us (29%)
  waiting for transfers between devices  19.1 us (21%)
  local copies, waits for them, and re-layouts  3.57 us (4%)
  between operations  2.02 us (2%)
    ppermute x14, starting transfers between devices, exchange(): return lax.ppermute(values, 'depth', links)  31.2 us
    pallas_call x38, Pallas kernels, kernel_call(): pl.pallas_call(kernel, out_shape=tuple(outs), in_specs=[SMEM] * len(small...  25.7 us
    ppermute x9, waiting for transfers between devices, swap(): return lax.ppermute(values, axis, [(i, i ^ bit) for i in range(count)])  10.6 us
    ppermute x14, waiting for transfers between devices, exchange(): return lax.ppermute(values, 'depth', links)  8.54 us
    ppermute x9, starting transfers between devices, swap(): return lax.ppermute(values, axis, [(i, i ^ bit) for i in range(count)])  8.31 us
    unnamed x18, local copies, waits for them, and re-layouts  2.29 us
  transfers between devices with their start and end apart: 23, of which 10 were waited for; matrix products, arithmetic and copies ran while one was open for 0% of the time, Pallas kernels for 26%

profile of v3, /device:TPU:0, one launch (start us, length us, event | category | flops | bytes accessed | tf_op | source)
XLA Modules:
  0.0 90.9 jit_solution(5143577928030012303)
XLA Ops:
  0.0 1.3 %dynamic-slice_bitcast_fusion = (f32[4,64,128]{2,1,0:T(8,128)S(1)}, f32[4,64,128]{2,1,0:T(8,128)S(1)}, f32[4,64,128]{2,1,0:T(8,128)S(1)}, f32[4,64,128]{2,1,0:T(8,128)S(1)}) fusion(f32[1,32,64,128]{3,2,1,0:T(8,128)} %param.13, s32[]{:T(128)S(6)} %select_n.17, s32[]{:T(128)S(6)} %select_n.16, f32[1,32,64,128]{3,2,1,0:T(8,128)} %param.12), kind=kLoop, calls=%fused_computation.2 | loop fusion | bytes 1048584 | tf_op jit(solution)/shard_map/dynamic_slice | solution.py:444
  1.3 3.0 %collective-permute-start = (f32[8,64,128]{2,1,0:T(8,128)S(1)}, f32[8,64,128]{2,1,0:T(8,128)S(1)}, u32[]{:S(2)}, u32[]{:S(2)}) collective-permute-start(f32[8,64,128]{2,1,0:T(8,128)S(1)} %pad_maximum_fusion), channel_id=1, source_target_pairs={{0,1},{1,0},{2,3},{3,2},{4,5},{5,4},{6,7},{7,6},{8,9},{9,8},{10,11... | collective-permute-start | bytes 786440 | tf_op jit(solution)/shard_map/ppermute | solution.py:526
  4.4 0.7 collective-permute-start.2
  5.1 1.2 %copy-done.3 = f32[32,64,128]{2,1,0:T(8,128)S(1)} copy-done((f32[32,64,128]{2,1,0:T(8,128)S(1)}, f32[32,64,128]{2,1,0:T(8,128)}, u32[]{:S(2)}) %copy-start.3) | copy-done | bytes 1048600
  6.3 0.6 shard_map.109
  7.6 0.6 copy-done.5
  8.3 3.1 %shard_map.110 = (f32[32,64,128]{2,1,0:T(8,128)S(1)}, f32[32,64,128]{2,1,0:T(8,128)S(1)}, f32[8,128]{1,0:T(8,128)S(1)}, f32[8,128]{1,0:T(8,128)S(1)}, f32[8,128]...) custom-call(f32[1,4]{1,0:T(1,128)S(1)} %copy-done.7, ...), custom_call_target="tpu_custom_call" | custom-call | flops 80000 | bytes 8192 | tf_op jit(solution)/shard_map/pallas_call | solution.py:139
  11.4 0.9 %shard_map.112 = (f32[12,64,128]{2,1,0:T(8,128)S(1)}, f32[12,64,128]{2,1,0:T(8,128)S(1)}) custom-call(f32[32,64,128]{2,1,0:T(8,128)S(1)} %get-tuple-element.61.refs_0_.refs_1_.refs_3_.refs_4_.refs_5_, f32[32,64,128]{2,1,0:T(8,128)S(1)} %get-tuple-element.62.refs_1_.refs_2_, ...), custom_call_target="tpu_custom_call" | custom-call | flops 120000 | bytes 12288 | tf_op jit(solution)/shard_map/pallas_call | solution.py:139
  12.4 0.9 %shard_map.111 = (f32[12,64,128]{2,1,0:T(8,128)S(1)}, f32[12,64,128]{2,1,0:T(8,128)S(1)}) custom-call(f32[32,64,128]{2,1,0:T(8,128)S(1)} %get-tuple-element.61.refs_0_.refs_1_.refs_3_.refs_4_.refs_5_, f32[32,64,128]{2,1,0:T(8,128)S(1)} %get-tuple-element.62.refs_1_.refs_2_, ...), custom_call_target="tpu_custom_call" | custom-call | flops 120000 | bytes 12288 | tf_op jit(solution)/shard_map/pallas_call | solution.py:139
  13.3 2.3 %collective-permute-done.refs_0_ = f32[8,64,128]{2,1,0:T(8,128)S(1)} collective-permute-done((f32[8,64,128]{2,1,0:T(8,128)S(1)}, f32[8,64,128]{2,1,0:T(8,128)S(1)}, u32[]{:S(2)}, u32[]{:S(2)}) %collective-permute-start) | collective-permute-done | bytes 262176 | tf_op jit(solution)/shard_map/ppermute | solution.py:526
  15.9 2.5 %collective-permute-start.1 = (f32[4,64,128]{2,1,0:T(8,128)S(1)}, f32[4,64,128]{2,1,0:T(8,128)S(1)}, u32[]{:S(2)}, u32[]{:S(2)}) collective-permute-start(f32[4,64,128]{2,1,0:T(8,128)S(1)} %get-tuple-element.68.refs_0_.refs_1_.refs_3_.refs_4_.refs_5_.refs_9_), channel_id=1, source_target_pairs={{0,1},{1,0},{2,3},{3,2},{4,5},{5,4},{6,7},{7,6},{8,9},{9,8},{10,11... | collective-permute-start | bytes 393224 | tf_op jit(solution)/shard_map/ppermute | solution.py:526
  18.4 0.9 %shard_map.114 = (f32[12,64,128]{2,1,0:T(8,128)S(1)}, f32[12,64,128]{2,1,0:T(8,128)S(1)}) custom-call(f32[4,64,128]{2,1,0:T(8,128)S(1)} %get-tuple-element.68.refs_0_.refs_1_.refs_3_.refs_4_.refs_5_.refs_9_, f32[12,64,128]{2,1,0:T(8,128)S(1)} %get-tuple-element.65.refs_6_.refs_1_.refs_2_.refs_4_.refs_5_.refs_8_, ...), custom_call_target="tpu_custom_call" | custom-call | flops 120000 | bytes 12288 | tf_op jit(solution)/shard_map/pallas_call | solution.py:139
  19.3 0.3 shard_map.115
  19.7 0.7 collective-permute-start.4
  20.3 0.9 %shard_map.116 = (f32[12,64,128]{2,1,0:T(8,128)S(1)}, f32[12,64,128]{2,1,0:T(8,128)S(1)}) custom-call(f32[4,64,128]{2,1,0:T(8,128)S(1)} %get-tuple-element.68.refs_0_.refs_1_.refs_3_.refs_4_.refs_5_.refs_9_, f32[12,64,128]{2,1,0:T(8,128)S(1)} %get-tuple-element.65.refs_6_.refs_1_.refs_2_.refs_4_.refs_5_.refs_8_, ...), custom_call_target="tpu_custom_call" | custom-call | flops 120000 | bytes 12288 | tf_op jit(solution)/shard_map/pallas_call | solution.py:139
  21.7 4.3 %collective-permute-start.3 = (f32[4,64,128]{2,1,0:T(8,128)S(1)}, f32[4,64,128]{2,1,0:T(8,128)S(1)}, u32[]{:S(2)}, u32[]{:S(2)}) collective-permute-start(f32[4,64,128]{2,1,0:T(8,128)S(1)} %get-tuple-element.74.refs_0_.refs_1_.refs_3_.refs_4_.refs_5_.refs_9_), channel_id=1, source_target_pairs={{0,1},{1,0},{2,3},{3,2},{4,5},{5,4},{6,7},{7,6},{8,9},{9,8},{10,11... | collective-permute-start | bytes 393224 | tf_op jit(solution)/shard_map/ppermute | solution.py:526
  25.9 0.9 %shard_map.118 = (f32[12,64,128]{2,1,0:T(8,128)S(1)}, f32[12,64,128]{2,1,0:T(8,128)S(1)}) custom-call(f32[4,64,128]{2,1,0:T(8,128)S(1)} %get-tuple-element.74.refs_0_.refs_1_.refs_3_.refs_4_.refs_5_.refs_9_, f32[12,64,128]{2,1,0:T(8,128)S(1)} %get-tuple-element.70.refs_6_.refs_9_.refs_1_.refs_2_.refs_4_.refs_5_.refs_7_, ...), custom_call_target="tpu_custom_call" | custom-call | flops 120000 | bytes 12288 | tf_op jit(solution)/shard_map/pallas_call | solution.py:139
  26.9 0.3 shard_map.119
  27.2 0.7 collective-permute-start.6
  27.9 0.9 %shard_map.120 = (f32[12,64,128]{2,1,0:T(8,128)S(1)}, f32[12,64,128]{2,1,0:T(8,128)S(1)}) custom-call(f32[4,64,128]{2,1,0:T(8,128)S(1)} %get-tuple-element.74.refs_0_.refs_1_.refs_3_.refs_4_.refs_5_.refs_9_, f32[12,64,128]{2,1,0:T(8,128)S(1)} %get-tuple-element.70.refs_6_.refs_9_.refs_1_.refs_2_.refs_4_.refs_5_.refs_7_, ...), custom_call_target="tpu_custom_call" | custom-call | flops 120000 | bytes 12288 | tf_op jit(solution)/shard_map/pallas_call | solution.py:139
  28.9 0.3 shard_map.121
  29.2 4.9 %collective-permute-start.5 = (f32[4,64,128]{2,1,0:T(8,128)S(1)}, f32[4,64,128]{2,1,0:T(8,128)S(1)}, u32[]{:S(2)}, u32[]{:S(2)}) collective-permute-start(f32[4,64,128]{2,1,0:T(8,128)S(1)} %get-tuple-element.80.refs_0_.refs_1_.refs_6_), channel_id=1, source_target_pairs={{0,1},{1,0},{2,3},{3,2},{4,5},{5,4},{6,7},{7,6},{8,9},{9,8},{10,11... | collective-permute-start | bytes 393224 | tf_op jit(solution)/shard_map/ppermute | solution.py:526
  34.1 0.9 %shard_map.122 = (f32[12,64,128]{2,1,0:T(8,128)S(1)}, f32[12,64,128]{2,1,0:T(8,128)S(1)}) custom-call(f32[4,64,128]{2,1,0:T(8,128)S(1)} %get-tuple-element.80.refs_0_.refs_1_.refs_6_, f32[12,64,128]{2,1,0:T(8,128)S(1)} %get-tuple-element.76.refs_9_.refs_12_.refs_1_.refs_2_.refs_4_, f32[12,64,128]{2,1,0:T(8,128)S(1)} %get-tuple-element.78.refs_13_.refs_2_.refs_3_.refs_5_, ...), custom_call_target="tpu_custom_call" | custom-call | flops 120000 | bytes 12288 | tf_op jit(solution)/shard_map/pallas_call | solution.py:139
  35.1 0.3 shard_map.123
  35.4 0.8 collective-permute-start.7
  36.3 0.3 copy-done.4
  36.6 0.4 shard_map.125
  37.1 0.9 %shard_map.124 = (f32[12,64,128]{2,1,0:T(8,128)S(1)}, f32[12,64,128]{2,1,0:T(8,128)S(1)}) custom-call(f32[4,64,128]{2,1,0:T(8,128)S(1)} %get-tuple-element.80.refs_0_.refs_1_.refs_6_, f32[12,64,128]{2,1,0:T(8,128)S(1)} %get-tuple-element.76.refs_9_.refs_12_.refs_1_.refs_2_.refs_4_, f32[12,64,128]{2,1,0:T(8,128)S(1)} %get-tuple-element.78.refs_13_.refs_2_.refs_3_.refs_5_, ...), custom_call_target="tpu_custom_call" | custom-call | flops 120000 | bytes 12288 | tf_op jit(solution)/shard_map/pallas_call | solution.py:139
  38.0 0.9 %shard_map.126.refs_14_.refs_9_.refs_1_.refs_2_.refs_4_.refs_5_.refs_6_.refs_25_ = f32[12,64,128]{2,1,0:T(8,128)S(1)} custom-call(f32[32,64,128]{2,1,0:T(8,128)S(1)} %get-tuple-element.85.refs_0_.refs_1_.refs_3_.refs_4_.refs_5_, f32[32,64,128]{2,1,0:T(8,128)S(1)} %get-tuple-element.86.refs_1_.refs_2_, ...), custom_call_target="tpu_custom_call" | custom-call | flops 120000 | bytes 12288 | tf_op jit(solution)/shard_map/pallas_call | solution.py:139
  38.9 0.9 %shard_map.127.refs_15_.refs_10_.refs_2_.refs_3_.refs_5_.refs_6_.refs_7_.refs_26_ = f32[12,64,128]{2,1,0:T(8,128)S(1)} custom-call(f32[32,64,128]{2,1,0:T(8,128)S(1)} %get-tuple-element.85.refs_0_.refs_1_.refs_3_.refs_4_.refs_5_, f32[32,64,128]{2,1,0:T(8,128)S(1)} %get-tuple-element.86.refs_1_.refs_2_, ...), custom_call_target="tpu_custom_call" | custom-call | flops 120000 | bytes 12288 | tf_op jit(solution)/shard_map/pallas_call | solution.py:139
  39.9 0.3 shard_map.128
  40.2 0.3 shard_map.129.refs_0_.refs_16_.refs_1_.refs_3_.refs_4_.refs_5_.refs_19_
  40.6 0.9 %shard_map.130.refs_12_.refs_7_.refs_10_.refs_1_.refs_2_.refs_5_.refs_23_.refs_6_ = f32[12,64,128]{2,1,0:T(8,128)S(1)} custom-call(f32[4,64,128]{2,1,0:T(8,128)S(1)} %shard_map.129.refs_0_.refs_16_.refs_1_.refs_3_.refs_4_.refs_5_.refs_19_, f32[12,64,128]{2,1,0:T(8,128)S(1)} %shard_map.126.refs_14_.refs_9_.refs_1_.refs_2_.refs_4_.refs_5_.refs_6_.refs_25_, ...), custom_call_target="tpu_custom_call" | custom-call | flops 120000 | bytes 12288 | tf_op jit(solution)/shard_map/pallas_call | solution.py:139
  41.5 0.3 shard_map.131
  41.8 0.3 shard_map.132.refs_17_.refs_3_.refs_4_.refs_6_.refs_7_.refs_8_.refs_19_
  42.6 4.5 %collective-permute-start.10 = (f32[264,128]{1,0:T(8,128)S(1)}, f32[264,128]{1,0:T(8,128)S(1)}, u32[]{:S(2)}, u32[]{:S(2)}) collective-permute-start(f32[264,128]{1,0:T(8,128)S(1)} %get-tuple-element.107), channel_id=1, source_target_pairs={{0,1},{1,0},{2,3},{3,2},{4,5},{5,4},{6,7},{7,6},{8,9},{9,8},{10,11... | collective-permute-start | bytes 405512 | tf_op jit(solution)/shard_map/ppermute | solution.py:526
  47.1 0.8 collective-permute-start.9
  47.9 3.3 %collective-permute-done.10.refs_0_ = f32[264,128]{1,0:T(8,128)S(1)} collective-permute-done((f32[264,128]{1,0:T(8,128)S(1)}, f32[264,128]{1,0:T(8,128)S(1)}, u32[]{:S(2)}, u32[]{:S(2)}) %collective-permute-start.10) | collective-permute-done | bytes 135200 | tf_op jit(solution)/shard_map/ppermute | solution.py:526
  51.3 1.6 %collective-permute-start.11 = (f32[8,128]{1,0:T(8,128)S(1)}, f32[8,128]{1,0:T(8,128)S(1)}, u32[]{:S(2)}, u32[]{:S(2)}) collective-permute-start(f32[8,128]{1,0:T(8,128)S(1)} %slice_add_fusion), channel_id=1, source_target_pairs={{0,2},{1,3},{2,0},{3,1},{4,6},{5,7},{6,4},{7,5},{8,10},{9,11},{10,... | collective-permute-start | bytes 12296 | tf_op jit(solution)/shard_map/ppermute | solution.py:531
  52.9 0.9 %shard_map.134.refs_11_.refs_2_.refs_3_.refs_6_.refs_24_.refs_7_ = f32[12,64,128]{2,1,0:T(8,128)S(1)} custom-call(f32[4,64,128]{2,1,0:T(8,128)S(1)} %shard_map.129.refs_0_.refs_16_.refs_1_.refs_3_.refs_4_.refs_5_.refs_19_, f32[12,64,128]{2,1,0:T(8,128)S(1)} %shard_map.126.refs_14_.refs_9_.refs_1_.refs_2_.refs_4_.refs_5_.refs_6_.refs_25_, ...), custom_call_target="tpu_custom_call" | custom-call | flops 120000 | bytes 12288 | tf_op jit(solution)/shard_map/pallas_call | solution.py:139
  53.8 0.3 shard_map.135.refs_0_.refs_1_.refs_4_.refs_5_.refs_18_
  54.2 4.6 %collective-permute-start.13 = (f32[4,64,128]{2,1,0:T(8,128)S(1)}, f32[4,64,128]{2,1,0:T(8,128)S(1)}, u32[]{:S(2)}, u32[]{:S(2)}) collective-permute-start(f32[4,64,128]{2,1,0:T(8,128)S(1)} %shard_map.135.refs_0_.refs_1_.refs_4_.refs_5_.refs_18_), channel_id=1, source_target_pairs={{0,1},{1,0},{2,3},{3,2},{4,5},{5,4},{6,7},{7,6},{8,9},{9,8},{10,11... | collective-permute-start | bytes 393224 | tf_op jit(solution)/shard_map/ppermute | solution.py:526
  58.8 1.0 %shard_map.136.refs_10_.refs_13_.refs_1_.refs_21_.refs_2_ = f32[12,64,128]{2,1,0:T(8,128)S(1)} custom-call(f32[4,64,128]{2,1,0:T(8,128)S(1)} %shard_map.135.refs_0_.refs_1_.refs_4_.refs_5_.refs_18_, f32[12,64,128]{2,1,0:T(8,128)S(1)} %shard_map.130.refs_12_.refs_7_.refs_10_.refs_1_.refs_2_.refs_5_.refs_23_.refs_6_, ...), custom_call_target="tpu_custom_call" | custom-call | flops 120000 | bytes 12288 | tf_op jit(solution)/shard_map/pallas_call | solution.py:139
  59.8 0.3 shard_map.137.refs_1_.refs_3_.refs_4_.refs_7_.refs_8_.refs_18_
  60.1 0.7 collective-permute-start.14
  60.9 1.6 %collective-permute-start.12 = (f32[16,64,128]{2,1,0:T(8,128)S(1)}, f32[16,64,128]{2,1,0:T(8,128)S(1)}, u32[]{:S(2)}, u32[]{:S(2)}) collective-permute-start(f32[16,64,128]{2,1,0:T(8,128)S(1)} %shard_map.138), channel_id=1, source_target_pairs={{0,16},{8,24},{16,0},{24,8},{1,17},{9,25},{17,1},{25,9},{2,18},{10... | collective-permute-start | bytes 1572872 | tf_op jit(solution)/shard_map/ppermute | solution.py:531
  62.4 3.4 %collective-permute-start.15 = (f32[8,128]{1,0:T(8,128)S(1)}, f32[8,128]{1,0:T(8,128)S(1)}, u32[]{:S(2)}, u32[]{:S(2)}) collective-permute-start(f32[8,128]{1,0:T(8,128)S(1)} %add.29.refs_20_), channel_id=1, source_target_pairs={{0,4},{1,5},{2,6},{3,7},{4,0},{5,1},{6,2},{7,3},{8,12},{9,13},{10,... | collective-permute-start | bytes 12296 | tf_op jit(solution)/shard_map/ppermute | solution.py:531
  65.9 0.9 %shard_map.139.refs_14_.refs_2_.refs_22_.refs_3_ = f32[12,64,128]{2,1,0:T(8,128)S(1)} custom-call(f32[4,64,128]{2,1,0:T(8,128)S(1)} %shard_map.135.refs_0_.refs_1_.refs_4_.refs_5_.refs_18_, f32[12,64,128]{2,1,0:T(8,128)S(1)} %shard_map.130.refs_12_.refs_7_.refs_10_.refs_1_.refs_2_.refs_5_.refs_23_.refs_6_, ...), custom_call_target="tpu_custom_call" | custom-call | flops 120000 | bytes 12288 | tf_op jit(solution)/shard_map/pallas_call | solution.py:139
  66.8 0.3 shard_map.140.refs_13_.refs_0_.refs_1_.refs_17_
  67.4 0.3 shard_map.141.refs_3_.refs_4_.refs_17_
  67.8 2.0 %shard_map.142 = (f32[12,64,128]{2,1,0:T(8,128)S(1)}, f32[12,64,128]{2,1,0:T(8,128)S(1)}) custom-call(f32[4,64,128]{2,1,0:T(8,128)S(1)} %shard_map.140.refs_13_.refs_0_.refs_1_.refs_17_, f32[12,64,128]{2,1,0:T(8,128)S(1)} %shard_map.136.refs_10_.refs_13_.refs_1_.refs_21_.refs_2_, f32[12,64,128]{2,1,0:T(8,128)S(1)} %shard_map.139.refs_14_.refs_2_.refs_22_.refs_3_, ...), custom_call_target="tpu_custom_call" | custom-call | flops 240000 | bytes 24576 | tf_op jit(solution)/shard_map/pallas_call | solution.py:139
  69.8 2.3 %collective-permute-start.19 = (f32[4,64,128]{2,1,0:T(8,128)S(1)}, f32[4,64,128]{2,1,0:T(8,128)S(1)}, u32[]{:S(2)}, u32[]{:S(2)}) collective-permute-start(f32[4,64,128]{2,1,0:T(8,128)S(1)} %shard_map.140.refs_13_.refs_0_.refs_1_.refs_17_), channel_id=1, source_target_pairs={{0,1},{1,0},{2,3},{3,2},{4,5},{5,4},{6,7},{7,6},{8,9},{9,8},{10,11... | collective-permute-start | bytes 393224 | tf_op jit(solution)/shard_map/ppermute | solution.py:526
  72.1 0.7 collective-permute-start.18
  72.8 0.6 collective-permute-start.17
  73.5 2.8 %collective-permute-done.19.refs_0_ = f32[4,64,128]{2,1,0:T(8,128)S(1)} collective-permute-done((f32[4,64,128]{2,1,0:T(8,128)S(1)}, f32[4,64,128]{2,1,0:T(8,128)S(1)}, u32[]{:S(2)}, u32[]{:S(2)}) %collective-permute-start.19) | collective-permute-done | bytes 131104 | tf_op jit(solution)/shard_map/ppermute | solution.py:526
  76.2 0.4 shard_map.144.refs_22_
  76.7 0.4 shard_map.145
  77.1 1.3 %collective-permute-done.20 = f32[264,128]{1,0:T(8,128)S(1)} collective-permute-done((f32[264,128]{1,0:T(8,128)S(1)}, f32[264,128]{1,0:T(8,128)S(1)}, u32[]{:S(2)}, u32[]{:S(2)}) %collective-permute-start.20) | collective-permute-done | bytes 135200 | tf_op jit(solution)/shard_map/ppermute | solution.py:531
  78.5 0.8 collective-permute-start.21
  80.0 4.9 %collective-permute-done.17.rest_1_ = f32[12,64,128]{2,1,0:T(8,128)S(1)} collective-permute-done((f32[12,64,128]{2,1,0:T(8,128)S(1)}, f32[12,64,128]{2,1,0:T(8,128)S(1)}, u32[]{:S(2)}, u32[]{:S(2)}) %collective-permute-start.17) | collective-permute-done | bytes 393248 | tf_op jit(solution)/shard_map/ppermute | solution.py:531
  84.9 2.1 %collective-permute-done.21.rest_3_ = f32[264,128]{1,0:T(8,128)S(1)} collective-permute-done((f32[264,128]{1,0:T(8,128)S(1)}, f32[264,128]{1,0:T(8,128)S(1)}, u32[]{:S(2)}, u32[]{:S(2)}) %collective-permute-start.21) | collective-permute-done | bytes 135200 | tf_op jit(solution)/shard_map/ppermute | solution.py:531
  87.0 0.8 shard_map.146.own_ref
  87.9 1.9 %collective-permute-done.22.other_ref = f32[16,64,128]{2,1,0:T(8,128)S(1)} collective-permute-done((f32[16,64,128]{2,1,0:T(8,128)S(1)}, f32[16,64,128]{2,1,0:T(8,128)S(1)}, u32[]{:S(2)}, u32[]{:S(2)}) %collective-permute-start.22) | collective-permute-done | bytes 524320 | tf_op jit(solution)/shard_map/ppermute | solution.py:531
  89.8 1.0 %shard_map.147 = f32[32,64,128]{2,1,0:T(8,128)} custom-call(f32[16,64,128]{2,1,0:T(8,128)S(1)} %shard_map.146.own_ref, f32[16,64,128]{2,1,0:T(8,128)S(1)} %collective-permute-done.22.other_ref), custom_call_target="tpu_custom_call" | custom-call | flops 80000 | bytes 8192 | tf_op jit(solution)/shard_map/pallas_call | solution.py:511
  (46 shorter events, 2.1 us)
Async XLA Ops:
  0.0 5.1 %copy-start = (f32[1,32,64,128]{3,2,1,0:T(8,128)S(1)}, f32[1,32,64,128]{3,2,1,0:T(8,128)}, u32[]{:S(2)}) copy-start(f32[1,32,64,128]{3,2,1,0:T(8,128)} %param.12) | copy-start | bytes 3145732
  0.0 5.1 %copy-start.2 = (f32[1,32,64,128]{3,2,1,0:T(8,128)S(1)}, f32[1,32,64,128]{3,2,1,0:T(8,128)}, u32[]{:S(2)}) copy-start(f32[1,32,64,128]{3,2,1,0:T(8,128)} %param.11) | copy-start | bytes 3145732
  1.3 14.2 %collective-permute-start = (f32[8,64,128]{2,1,0:T(8,128)S(1)}, f32[8,64,128]{2,1,0:T(8,128)S(1)}, u32[]{:S(2)}, u32[]{:S(2)}) collective-permute-start(f32[8,64,128]{2,1,0:T(8,128)S(1)} %pad_maximum_fusion), channel_id=1, source_target_pairs={{0,1},{1,0},{2,3},{3,2},{4,5},{5,4},{6,7},{7,6},{8,9},{9,8},{10,11... | collective-permute-start | bytes 786440 | tf_op jit(solution)/shard_map/ppermute | solution.py:526
  4.4 14.9 %collective-permute-start.2 = (f32[8,64,128]{2,1,0:T(8,128)S(1)}, f32[8,64,128]{2,1,0:T(8,128)S(1)}, u32[]{:S(2)}, u32[]{:S(2)}) collective-permute-start(f32[8,64,128]{2,1,0:T(8,128)S(1)} %pad_maximum_fusion.1), channel_id=1, source_target_pairs={{1,2},{2,1},{3,4},{4,3},{5,6},{6,5},{9,10},{10,9},{11,12},{12,11},... | collective-permute-start | bytes 786440 | tf_op jit(solution)/shard_map/ppermute | solution.py:526
  5.1 1.2 %copy-start.3 = (f32[32,64,128]{2,1,0:T(8,128)S(1)}, f32[32,64,128]{2,1,0:T(8,128)}, u32[]{:S(2)}) copy-start(f32[32,64,128]{2,1,0:T(8,128)} %refs_2_.1) | copy-start | bytes 3145732
  7.6 0.7 copy-start.5
  7.6 0.7 copy-start.7
  7.6 0.7 copy-start.8
  15.9 5.5 %collective-permute-start.1 = (f32[4,64,128]{2,1,0:T(8,128)S(1)}, f32[4,64,128]{2,1,0:T(8,128)S(1)}, u32[]{:S(2)}, u32[]{:S(2)}) collective-permute-start(f32[4,64,128]{2,1,0:T(8,128)S(1)} %get-tuple-element.68.refs_0_.refs_1_.refs_3_.refs_4_.refs_5_.refs_9_), channel_id=1, source_target_pairs={{0,1},{1,0},{2,3},{3,2},{4,5},{5,4},{6,7},{7,6},{8,9},{9,8},{10,11... | collective-permute-start | bytes 393224 | tf_op jit(solution)/shard_map/ppermute | solution.py:526
  19.7 7.2 %collective-permute-start.4 = (f32[4,64,128]{2,1,0:T(8,128)S(1)}, f32[4,64,128]{2,1,0:T(8,128)S(1)}, u32[]{:S(2)}, u32[]{:S(2)}) collective-permute-start(f32[4,64,128]{2,1,0:T(8,128)S(1)} %get-tuple-element.71.refs_3_.refs_4_.refs_6_.refs_7_.refs_8_.refs_9_), channel_id=1, source_target_pairs={{1,2},{2,1},{3,4},{4,3},{5,6},{6,5},{9,10},{10,9},{11,12},{12,11},... | collective-permute-start | bytes 393224 | tf_op jit(solution)/shard_map/ppermute | solution.py:526
  21.7 7.2 %collective-permute-start.3 = (f32[4,64,128]{2,1,0:T(8,128)S(1)}, f32[4,64,128]{2,1,0:T(8,128)S(1)}, u32[]{:S(2)}, u32[]{:S(2)}) collective-permute-start(f32[4,64,128]{2,1,0:T(8,128)S(1)} %get-tuple-element.74.refs_0_.refs_1_.refs_3_.refs_4_.refs_5_.refs_9_), channel_id=1, source_target_pairs={{0,1},{1,0},{2,3},{3,2},{4,5},{5,4},{6,7},{7,6},{8,9},{9,8},{10,11... | collective-permute-start | bytes 393224 | tf_op jit(solution)/shard_map/ppermute | solution.py:526
  27.2 7.9 %collective-permute-start.6 = (f32[4,64,128]{2,1,0:T(8,128)S(1)}, f32[4,64,128]{2,1,0:T(8,128)S(1)}, u32[]{:S(2)}, u32[]{:S(2)}) collective-permute-start(f32[4,64,128]{2,1,0:T(8,128)S(1)} %get-tuple-element.77.refs_3_.refs_4_.refs_6_.refs_7_.refs_8_.refs_9_), channel_id=1, source_target_pairs={{1,2},{2,1},{3,4},{4,3},{5,6},{6,5},{9,10},{10,9},{11,12},{12,11},... | collective-permute-start | bytes 393224 | tf_op jit(solution)/shard_map/ppermute | solution.py:526
  29.2 10.7 %collective-permute-start.5 = (f32[4,64,128]{2,1,0:T(8,128)S(1)}, f32[4,64,128]{2,1,0:T(8,128)S(1)}, u32[]{:S(2)}, u32[]{:S(2)}) collective-permute-start(f32[4,64,128]{2,1,0:T(8,128)S(1)} %get-tuple-element.80.refs_0_.refs_1_.refs_6_), channel_id=1, source_target_pairs={{0,1},{1,0},{2,3},{3,2},{4,5},{5,4},{6,7},{7,6},{8,9},{9,8},{10,11... | collective-permute-start | bytes 393224 | tf_op jit(solution)/shard_map/ppermute | solution.py:526
  35.1 1.2 %copy-start.1 = (f32[1,32,64,128]{3,2,1,0:T(8,128)S(1)}, f32[1,32,64,128]{3,2,1,0:T(8,128)}, u32[]{:S(2)}) copy-start(f32[1,32,64,128]{3,2,1,0:T(8,128)} %param.13) | copy-start | bytes 3145732
  35.1 1.5 %copy-start.4 = (f32[1,32,64,128]{3,2,1,0:T(8,128)S(1)}, f32[1,32,64,128]{3,2,1,0:T(8,128)}, u32[]{:S(2)}) copy-start(f32[1,32,64,128]{3,2,1,0:T(8,128)} %param.14) | copy-start | bytes 3145732
  35.4 6.1 %collective-permute-start.7 = (f32[4,64,128]{2,1,0:T(8,128)S(1)}, f32[4,64,128]{2,1,0:T(8,128)S(1)}, u32[]{:S(2)}, u32[]{:S(2)}) collective-permute-start(f32[4,64,128]{2,1,0:T(8,128)S(1)} %get-tuple-element.83.refs_3_.refs_4_.refs_6_), channel_id=1, source_target_pairs={{1,2},{2,1},{3,4},{4,3},{5,6},{6,5},{9,10},{10,9},{11,12},{12,11},... | collective-permute-start | bytes 393224 | tf_op jit(solution)/shard_map/ppermute | solution.py:526
  42.5 18.3 %collective-permute-start.8 = (f32[16,64,128]{2,1,0:T(8,128)S(1)}, f32[16,64,128]{2,1,0:T(8,128)S(1)}, u32[]{:S(2)}, u32[]{:S(2)}) collective-permute-start(f32[16,64,128]{2,1,0:T(8,128)S(1)} %get-tuple-element.106), channel_id=1, source_target_pairs={{0,8},{8,0},{16,24},{24,16},{1,9},{9,1},{17,25},{25,17},{2,10},{10... | collective-permute-start | bytes 1572872 | tf_op jit(solution)/shard_map/ppermute | solution.py:531
  42.6 8.7 %collective-permute-start.10 = (f32[264,128]{1,0:T(8,128)S(1)}, f32[264,128]{1,0:T(8,128)S(1)}, u32[]{:S(2)}, u32[]{:S(2)}) collective-permute-start(f32[264,128]{1,0:T(8,128)S(1)} %get-tuple-element.107), channel_id=1, source_target_pairs={{0,1},{1,0},{2,3},{3,2},{4,5},{5,4},{6,7},{7,6},{8,9},{9,8},{10,11... | collective-permute-start | bytes 405512 | tf_op jit(solution)/shard_map/ppermute | solution.py:526
  47.1 12.7 %collective-permute-start.9 = (f32[4,64,128]{2,1,0:T(8,128)S(1)}, f32[4,64,128]{2,1,0:T(8,128)S(1)}, u32[]{:S(2)}, u32[]{:S(2)}) collective-permute-start(f32[4,64,128]{2,1,0:T(8,128)S(1)} %shard_map.132.refs_17_.refs_3_.refs_4_.refs_6_.refs_7_.refs_8_.refs_19_), channel_id=1, source_target_pairs={{1,2},{2,1},{3,4},{4,3},{5,6},{6,5},{9,10},{10,9},{11,12},{12,11},... | collective-permute-start | bytes 393224 | tf_op jit(solution)/shard_map/ppermute | solution.py:526
  51.3 8.5 %collective-permute-start.11 = (f32[8,128]{1,0:T(8,128)S(1)}, f32[8,128]{1,0:T(8,128)S(1)}, u32[]{:S(2)}, u32[]{:S(2)}) collective-permute-start(f32[8,128]{1,0:T(8,128)S(1)} %slice_add_fusion), channel_id=1, source_target_pairs={{0,2},{1,3},{2,0},{3,1},{4,6},{5,7},{6,4},{7,5},{8,10},{9,11},{10,... | collective-permute-start | bytes 12296 | tf_op jit(solution)/shard_map/ppermute | solution.py:531
  54.2 12.6 %collective-permute-start.13 = (f32[4,64,128]{2,1,0:T(8,128)S(1)}, f32[4,64,128]{2,1,0:T(8,128)S(1)}, u32[]{:S(2)}, u32[]{:S(2)}) collective-permute-start(f32[4,64,128]{2,1,0:T(8,128)S(1)} %shard_map.135.refs_0_.refs_1_.refs_4_.refs_5_.refs_18_), channel_id=1, source_target_pairs={{0,1},{1,0},{2,3},{3,2},{4,5},{5,4},{6,7},{7,6},{8,9},{9,8},{10,11... | collective-permute-start | bytes 393224 | tf_op jit(solution)/shard_map/ppermute | solution.py:526
  60.1 7.3 %collective-permute-start.14 = (f32[4,64,128]{2,1,0:T(8,128)S(1)}, f32[4,64,128]{2,1,0:T(8,128)S(1)}, u32[]{:S(2)}, u32[]{:S(2)}) collective-permute-start(f32[4,64,128]{2,1,0:T(8,128)S(1)} %shard_map.137.refs_1_.refs_3_.refs_4_.refs_7_.refs_8_.refs_18_), channel_id=1, source_target_pairs={{1,2},{2,1},{3,4},{4,3},{5,6},{6,5},{9,10},{10,9},{11,12},{12,11},... | collective-permute-start | bytes 393224 | tf_op jit(solution)/shard_map/ppermute | solution.py:526
  60.9 15.7 %collective-permute-start.12 = (f32[16,64,128]{2,1,0:T(8,128)S(1)}, f32[16,64,128]{2,1,0:T(8,128)S(1)}, u32[]{:S(2)}, u32[]{:S(2)}) collective-permute-start(f32[16,64,128]{2,1,0:T(8,128)S(1)} %shard_map.138), channel_id=1, source_target_pairs={{0,16},{8,24},{16,0},{24,8},{1,17},{9,25},{17,1},{25,9},{2,18},{10... | collective-permute-start | bytes 1572872 | tf_op jit(solution)/shard_map/ppermute | solution.py:531
  62.4 5.0 %collective-permute-start.15 = (f32[8,128]{1,0:T(8,128)S(1)}, f32[8,128]{1,0:T(8,128)S(1)}, u32[]{:S(2)}, u32[]{:S(2)}) collective-permute-start(f32[8,128]{1,0:T(8,128)S(1)} %add.29.refs_20_), channel_id=1, source_target_pairs={{0,4},{1,5},{2,6},{3,7},{4,0},{5,1},{6,2},{7,3},{8,12},{9,13},{10,... | collective-permute-start | bytes 12296 | tf_op jit(solution)/shard_map/ppermute | solution.py:531
  69.8 3.0 %collective-permute-start.16 = (f32[12,64,128]{2,1,0:T(8,128)S(1)}, f32[12,64,128]{2,1,0:T(8,128)S(1)}, u32[]{:S(2)}, u32[]{:S(2)}) collective-permute-start(f32[12,64,128]{2,1,0:T(8,128)S(1)} %get-tuple-element.112), channel_id=1, source_target_pairs={{0,8},{8,0},{16,24},{24,16},{1,9},{9,1},{17,25},{25,17},{2,10},{10... | collective-permute-start | bytes 1179656 | tf_op jit(solution)/shard_map/ppermute | solution.py:531
  69.8 6.4 %collective-permute-start.19 = (f32[4,64,128]{2,1,0:T(8,128)S(1)}, f32[4,64,128]{2,1,0:T(8,128)S(1)}, u32[]{:S(2)}, u32[]{:S(2)}) collective-permute-start(f32[4,64,128]{2,1,0:T(8,128)S(1)} %shard_map.140.refs_13_.refs_0_.refs_1_.refs_17_), channel_id=1, source_target_pairs={{0,1},{1,0},{2,3},{3,2},{4,5},{5,4},{6,7},{7,6},{8,9},{9,8},{10,11... | collective-permute-start | bytes 393224 | tf_op jit(solution)/shard_map/ppermute | solution.py:526
  72.1 4.5 %collective-permute-start.18 = (f32[4,64,128]{2,1,0:T(8,128)S(1)}, f32[4,64,128]{2,1,0:T(8,128)S(1)}, u32[]{:S(2)}, u32[]{:S(2)}) collective-permute-start(f32[4,64,128]{2,1,0:T(8,128)S(1)} %shard_map.141.refs_3_.refs_4_.refs_17_), channel_id=1, source_target_pairs={{1,2},{2,1},{3,4},{4,3},{5,6},{6,5},{9,10},{10,9},{11,12},{12,11},... | collective-permute-start | bytes 393224 | tf_op jit(solution)/shard_map/ppermute | solution.py:526
  72.8 12.0 %collective-permute-start.17 = (f32[12,64,128]{2,1,0:T(8,128)S(1)}, f32[12,64,128]{2,1,0:T(8,128)S(1)}, u32[]{:S(2)}, u32[]{:S(2)}) collective-permute-start(f32[12,64,128]{2,1,0:T(8,128)S(1)} %shard_map.143.rest_0_), channel_id=1, source_target_pairs={{0,16},{8,24},{16,0},{24,8},{1,17},{9,25},{17,1},{25,9},{2,18},{10... | collective-permute-start | bytes 1179656 | tf_op jit(solution)/shard_map/ppermute | solution.py:531
  77.1 1.4 %collective-permute-start.20 = (f32[264,128]{1,0:T(8,128)S(1)}, f32[264,128]{1,0:T(8,128)S(1)}, u32[]{:S(2)}, u32[]{:S(2)}) collective-permute-start(f32[264,128]{1,0:T(8,128)S(1)} %get-tuple-element.114), channel_id=1, source_target_pairs={{0,8},{8,0},{16,24},{24,16},{1,9},{9,1},{17,25},{25,17},{2,10},{10... | collective-permute-start | bytes 405512 | tf_op jit(solution)/shard_map/ppermute | solution.py:531
  78.5 8.5 %copy-start.6 = (f32[64]{0:T(128)S(1)}, f32[64]{0:T(128)}, u32[]{:S(2)}) copy-start(f32[64]{0:T(128)} %table_ref.1) | copy-start | bytes 772
  78.5 8.5 %collective-permute-start.21 = (f32[264,128]{1,0:T(8,128)S(1)}, f32[264,128]{1,0:T(8,128)S(1)}, u32[]{:S(2)}, u32[]{:S(2)}) collective-permute-start(f32[264,128]{1,0:T(8,128)S(1)} %add.30.rest_2_), channel_id=1, source_target_pairs={{0,16},{8,24},{16,0},{24,8},{1,17},{9,25},{17,1},{25,9},{2,18},{10... | collective-permute-start | bytes 405512 | tf_op jit(solution)/shard_map/ppermute | solution.py:531
  87.8 2.0 %collective-permute-start.22 = (f32[16,64,128]{2,1,0:T(8,128)S(1)}, f32[16,64,128]{2,1,0:T(8,128)S(1)}, u32[]{:S(2)}, u32[]{:S(2)}) collective-permute-start(f32[16,64,128]{2,1,0:T(8,128)S(1)} %shard_map.146.own_ref), channel_id=1, source_target_pairs={{0,8},{8,0},{16,24},{24,16},{1,9},{9,1},{17,25},{25,17},{2,10},{10... | collective-permute-start | bytes 1572872 | tf_op jit(solution)/shard_map/ppermute | solution.py:531

commit v4 on v3

--- a/solution.py
+++ b/solution.py
@@ -493,30 +493,28 @@
     return kernel_call(kernel, [table, plan], arrays, outs, [], half)[0]
 
 
-def assemble(own, other):
-    half, width, length = own.shape
-
-    def kernel(own_ref, other_ref, out_ref, sems):
+def place_half(values, own, result=None):
+    half, width, length = values.shape
+
+    def kernel(values_ref, *refs):
+        out_ref, sem = refs[-2:]
         core = lax.axis_index("shot") % 2
         upper = (lax.axis_index("depth") + core + 1) % 2
-        copies = []
-        for n, (ref, place) in enumerate([(own_ref, upper), (other_ref, 1 - upper)]):
-            spot = out_ref.at[pl.ds(place * half, half)]
-            copies.append(pltpu.make_async_copy(ref, spot, sems.at[n]))
-        for copy in copies:
-            copy.start()
-        for copy in copies:
-            copy.wait()
+        place = upper if own else 1 - upper
+        copy = pltpu.make_async_copy(values_ref, out_ref.at[pl.ds(place * half, half)], sem)
+        copy.start()
+        copy.wait()
 
     return pl.pallas_call(
         kernel,
         out_shape=f32(2 * half, width, length),
-        in_specs=[VMEM] * 2,
+        in_specs=[VMEM] if own else [VMEM, HBM],
         out_specs=HBM,
-        scratch_shapes=[pltpu.SemaphoreType.DMA((2,))],
+        input_output_aliases={} if own else {1: 0},
+        scratch_shapes=[pltpu.SemaphoreType.DMA],
         compiler_params=params(),
         cost_estimate=cost(8),
-    )(own, other)
+    )(*([values] if own else [values, result]))
 
 
 def exchange(values, side):
@@ -615,9 +613,9 @@
             one_adj = back(step, 0, edge, more, rest, (one[0], starts[0]), after)
             newer = [(one_adj, starts[0]), (near_adj, starts[1]), (far_adj, starts[2])]
             near_next = back(step - 1, 1, None, newer, more, (fields[-1][1], starts[1]), ())
-            two = ahead(step, 3, coming[1], cur, old, [near_next])
+            two = ahead(step, 3, coming[1], cur, old, [one_adj])
             edge = (halos[1], HALO, True)
-            two_adj = back(step, 3, edge, more, rest, (two[0], starts[3]), [near_next])
+            two_adj = back(step, 3, edge, more, rest, (two[0], starts[3]), [one_adj])
             newer.append((two_adj, starts[3]))
         else:
             message = exchange(one[0], 0)
@@ -643,10 +641,6 @@
         after = [near, far]
         one = back(step, 0, coming[0], cur, old, (fields[step][0], starts[0]), after)
         message = exchange(one, 0)
-        if bit < lax.axis_size("depth"):
-            tile = tile + tiles
-            tiles = swap(tile, "depth", bit)
-            bit *= 2
         newer = [(one, starts[0]), (near, starts[1]), (far, starts[2])]
         if step > 1:
             near_next = back(step - 1, 1, None, newer, cur, (fields[step - 1][1], starts[1]), ())
@@ -660,6 +654,10 @@
         adjoints.insert(0, arrays_of(cur))
         if step == STEPS - 2:
             curv = sum(total_parts(keep, send, [two]))
+        if bit < lax.axis_size("depth"):
+            tile = tile + tiles
+            tiles = swap(tile, "depth", bit)
+            bit *= 2
     while bit < lax.axis_size("depth"):
         tile = tile + tiles
         tiles = swap(tile, "depth", bit)
@@ -680,7 +678,8 @@
     inner_parts = total_parts(inside[0], inside[1:])
     outer_parts = total_parts(*outside)
     own = refresh(courant, inner_parts, outer_parts, curv, damping_table, plan_step)
-    return assemble(own, swap(own, "shot", 1))
+    other = swap(own, "shot", 1)
+    return place_half(other, False, place_half(own, True))
 
 
 def solution(mesh):

time: 91.5 us -> 89.3 us (0.976)
  waiting for transfers between devices: 19.1 us -> 12 us
  starting transfers between devices: 39.5 us -> 43.6 us
    ppermute x9, starting transfers between devices: 8.31 us -> 13.4 us  [swap(): return lax.ppermute(values, axis, [(i, i ^ bit) for i in range(count)])]
    ppermute x14, waiting for transfers between devices: 8.54 us -> 4.12 us  [exchange(): return lax.ppermute(values, 'depth', links)]
    ppermute x9, waiting for transfers between devices: 10.6 us -> 7.85 us  [swap(): return lax.ppermute(values, axis, [(i, i ^ bit) for i in range(count)])]
    ppermute x14, starting transfers between devices: 31.2 us -> 30.2 us  [exchange(): return lax.ppermute(values, 'depth', links)]
  transfers between devices with their start and end apart: 23 -> 23, of which waited for: 10 -> 10; matrix products, arithmetic and copies ran while one was open for 0% -> 0% of each run, Pallas kernels for 26% -> 28%
where the time goes in v4:
time: 89.3 us; the launch traced here: 88.6 us
  starting transfers between devices  43.6 us (49%)
  Pallas kernels  27.4 us (31%)
  waiting for transfers between devices  12 us (13%)
  local copies, waits for them, and re-layouts  3.56 us (4%)
  between operations  2.01 us (2%)
    ppermute x14, starting transfers between devices, exchange(): return lax.ppermute(values, 'depth', links)  30.2 us
    pallas_call x38, Pallas kernels, kernel_call(): pl.pallas_call(kernel, out_shape=tuple(outs), in_specs=[SMEM] * len(small...  25.8 us
    ppermute x9, starting transfers between devices, swap(): return lax.ppermute(values, axis, [(i, i ^ bit) for i in range(count)])  13.4 us
    ppermute x9, waiting for transfers between devices, swap(): return lax.ppermute(values, axis, [(i, i ^ bit) for i in range(count)])  7.85 us
    ppermute x14, waiting for transfers between devices, exchange(): return lax.ppermute(values, 'depth', links)  4.12 us
    unnamed x18, local copies, waits for them, and re-layouts  2.29 us
  transfers between devices with their start and end apart: 23, of which 10 were waited for; matrix products, arithmetic and copies ran while one was open for 0% of the time, Pallas kernels for 28%

profile of v4, /device:TPU:0, one launch (start us, length us, event | category | flops | bytes accessed | tf_op | source)
XLA Modules:
  0.0 88.6 jit_solution(11702943314489894069)
XLA Ops:
  0.0 1.3 %dynamic-slice_bitcast_fusion = (f32[4,64,128]{2,1,0:T(8,128)S(1)}, f32[4,64,128]{2,1,0:T(8,128)S(1)}, f32[4,64,128]{2,1,0:T(8,128)S(1)}, f32[4,64,128]{2,1,0:T(8,128)S(1)}) fusion(f32[1,32,64,128]{3,2,1,0:T(8,128)} %param.13, s32[]{:T(128)S(6)} %select_n.17, s32[]{:T(128)S(6)} %select_n.16, f32[1,32,64,128]{3,2,1,0:T(8,128)} %param.12), kind=kLoop, calls=%fused_computation.2 | loop fusion | bytes 1048584 | tf_op jit(solution)/shard_map/dynamic_slice | solution.py:444
  1.3 3.0 %collective-permute-start = (f32[8,64,128]{2,1,0:T(8,128)S(1)}, f32[8,64,128]{2,1,0:T(8,128)S(1)}, u32[]{:S(2)}, u32[]{:S(2)}) collective-permute-start(f32[8,64,128]{2,1,0:T(8,128)S(1)} %pad_maximum_fusion), channel_id=1, source_target_pairs={{0,1},{1,0},{2,3},{3,2},{4,5},{5,4},{6,7},{7,6},{8,9},{9,8},{10,11... | collective-permute-start | bytes 786440 | tf_op jit(solution)/shard_map/ppermute | solution.py:524
  4.4 0.7 collective-permute-start.2
  5.1 1.2 %copy-done.3 = f32[32,64,128]{2,1,0:T(8,128)S(1)} copy-done((f32[32,64,128]{2,1,0:T(8,128)S(1)}, f32[32,64,128]{2,1,0:T(8,128)}, u32[]{:S(2)}) %copy-start.3) | copy-done | bytes 1048600
  6.3 0.6 shard_map.109
  7.6 0.6 copy-done.5
  8.3 3.1 %shard_map.110 = (f32[32,64,128]{2,1,0:T(8,128)S(1)}, f32[32,64,128]{2,1,0:T(8,128)S(1)}, f32[8,128]{1,0:T(8,128)S(1)}, f32[8,128]{1,0:T(8,128)S(1)}, f32[8,128]...) custom-call(f32[1,4]{1,0:T(1,128)S(1)} %copy-done.7, ...), custom_call_target="tpu_custom_call" | custom-call | flops 80000 | bytes 8192 | tf_op jit(solution)/shard_map/pallas_call | solution.py:139
  11.3 0.9 %shard_map.112 = (f32[12,64,128]{2,1,0:T(8,128)S(1)}, f32[12,64,128]{2,1,0:T(8,128)S(1)}) custom-call(f32[32,64,128]{2,1,0:T(8,128)S(1)} %get-tuple-element.61.refs_0_.refs_1_.refs_3_.refs_4_.refs_5_, f32[32,64,128]{2,1,0:T(8,128)S(1)} %get-tuple-element.62.refs_1_.refs_2_, ...), custom_call_target="tpu_custom_call" | custom-call | flops 120000 | bytes 12288 | tf_op jit(solution)/shard_map/pallas_call | solution.py:139
  12.3 0.9 %shard_map.111 = (f32[12,64,128]{2,1,0:T(8,128)S(1)}, f32[12,64,128]{2,1,0:T(8,128)S(1)}) custom-call(f32[32,64,128]{2,1,0:T(8,128)S(1)} %get-tuple-element.61.refs_0_.refs_1_.refs_3_.refs_4_.refs_5_, f32[32,64,128]{2,1,0:T(8,128)S(1)} %get-tuple-element.62.refs_1_.refs_2_, ...), custom_call_target="tpu_custom_call" | custom-call | flops 120000 | bytes 12288 | tf_op jit(solution)/shard_map/pallas_call | solution.py:139
  13.2 2.3 %collective-permute-done.refs_0_ = f32[8,64,128]{2,1,0:T(8,128)S(1)} collective-permute-done((f32[8,64,128]{2,1,0:T(8,128)S(1)}, f32[8,64,128]{2,1,0:T(8,128)S(1)}, u32[]{:S(2)}, u32[]{:S(2)}) %collective-permute-start) | collective-permute-done | bytes 262176 | tf_op jit(solution)/shard_map/ppermute | solution.py:524
  15.8 2.5 %collective-permute-start.1 = (f32[4,64,128]{2,1,0:T(8,128)S(1)}, f32[4,64,128]{2,1,0:T(8,128)S(1)}, u32[]{:S(2)}, u32[]{:S(2)}) collective-permute-start(f32[4,64,128]{2,1,0:T(8,128)S(1)} %get-tuple-element.68.refs_0_.refs_1_.refs_3_.refs_4_.refs_5_.refs_9_), channel_id=1, source_target_pairs={{0,1},{1,0},{2,3},{3,2},{4,5},{5,4},{6,7},{7,6},{8,9},{9,8},{10,11... | collective-permute-start | bytes 393224 | tf_op jit(solution)/shard_map/ppermute | solution.py:524
  18.4 0.9 %shard_map.114 = (f32[12,64,128]{2,1,0:T(8,128)S(1)}, f32[12,64,128]{2,1,0:T(8,128)S(1)}) custom-call(f32[4,64,128]{2,1,0:T(8,128)S(1)} %get-tuple-element.68.refs_0_.refs_1_.refs_3_.refs_4_.refs_5_.refs_9_, f32[12,64,128]{2,1,0:T(8,128)S(1)} %get-tuple-element.65.refs_6_.refs_1_.refs_2_.refs_4_.refs_5_.refs_8_, ...), custom_call_target="tpu_custom_call" | custom-call | flops 120000 | bytes 12288 | tf_op jit(solution)/shard_map/pallas_call | solution.py:139
  19.6 0.7 collective-permute-start.4
  20.3 0.9 %shard_map.116 = (f32[12,64,128]{2,1,0:T(8,128)S(1)}, f32[12,64,128]{2,1,0:T(8,128)S(1)}) custom-call(f32[4,64,128]{2,1,0:T(8,128)S(1)} %get-tuple-element.68.refs_0_.refs_1_.refs_3_.refs_4_.refs_5_.refs_9_, f32[12,64,128]{2,1,0:T(8,128)S(1)} %get-tuple-element.65.refs_6_.refs_1_.refs_2_.refs_4_.refs_5_.refs_8_, ...), custom_call_target="tpu_custom_call" | custom-call | flops 120000 | bytes 12288 | tf_op jit(solution)/shard_map/pallas_call | solution.py:139
  21.7 4.3 %collective-permute-start.3 = (f32[4,64,128]{2,1,0:T(8,128)S(1)}, f32[4,64,128]{2,1,0:T(8,128)S(1)}, u32[]{:S(2)}, u32[]{:S(2)}) collective-permute-start(f32[4,64,128]{2,1,0:T(8,128)S(1)} %get-tuple-element.74.refs_0_.refs_1_.refs_3_.refs_4_.refs_5_.refs_9_), channel_id=1, source_target_pairs={{0,1},{1,0},{2,3},{3,2},{4,5},{5,4},{6,7},{7,6},{8,9},{9,8},{10,11... | collective-permute-start | bytes 393224 | tf_op jit(solution)/shard_map/ppermute | solution.py:524
  25.9 0.9 %shard_map.118 = (f32[12,64,128]{2,1,0:T(8,128)S(1)}, f32[12,64,128]{2,1,0:T(8,128)S(1)}) custom-call(f32[4,64,128]{2,1,0:T(8,128)S(1)} %get-tuple-element.74.refs_0_.refs_1_.refs_3_.refs_4_.refs_5_.refs_9_, f32[12,64,128]{2,1,0:T(8,128)S(1)} %get-tuple-element.70.refs_6_.refs_9_.refs_1_.refs_2_.refs_4_.refs_5_.refs_7_, ...), custom_call_target="tpu_custom_call" | custom-call | flops 120000 | bytes 12288 | tf_op jit(solution)/shard_map/pallas_call | solution.py:139
  26.9 0.3 shard_map.119
  27.2 0.7 collective-permute-start.6
  27.9 0.9 %shard_map.120 = (f32[12,64,128]{2,1,0:T(8,128)S(1)}, f32[12,64,128]{2,1,0:T(8,128)S(1)}) custom-call(f32[4,64,128]{2,1,0:T(8,128)S(1)} %get-tuple-element.74.refs_0_.refs_1_.refs_3_.refs_4_.refs_5_.refs_9_, f32[12,64,128]{2,1,0:T(8,128)S(1)} %get-tuple-element.70.refs_6_.refs_9_.refs_1_.refs_2_.refs_4_.refs_5_.refs_7_, ...), custom_call_target="tpu_custom_call" | custom-call | flops 120000 | bytes 12288 | tf_op jit(solution)/shard_map/pallas_call | solution.py:139
  28.9 0.3 shard_map.121
  29.2 4.9 %collective-permute-start.5 = (f32[4,64,128]{2,1,0:T(8,128)S(1)}, f32[4,64,128]{2,1,0:T(8,128)S(1)}, u32[]{:S(2)}, u32[]{:S(2)}) collective-permute-start(f32[4,64,128]{2,1,0:T(8,128)S(1)} %get-tuple-element.80.refs_0_.refs_1_.refs_6_), channel_id=1, source_target_pairs={{0,1},{1,0},{2,3},{3,2},{4,5},{5,4},{6,7},{7,6},{8,9},{9,8},{10,11... | collective-permute-start | bytes 393224 | tf_op jit(solution)/shard_map/ppermute | solution.py:524
  34.1 0.9 %shard_map.122 = (f32[12,64,128]{2,1,0:T(8,128)S(1)}, f32[12,64,128]{2,1,0:T(8,128)S(1)}) custom-call(f32[4,64,128]{2,1,0:T(8,128)S(1)} %get-tuple-element.80.refs_0_.refs_1_.refs_6_, f32[12,64,128]{2,1,0:T(8,128)S(1)} %get-tuple-element.76.refs_9_.refs_12_.refs_1_.refs_2_.refs_4_, f32[12,64,128]{2,1,0:T(8,128)S(1)} %get-tuple-element.78.refs_13_.refs_2_.refs_3_.refs_5_, ...), custom_call_target="tpu_custom_call" | custom-call | flops 120000 | bytes 12288 | tf_op jit(solution)/shard_map/pallas_call | solution.py:139
  35.1 0.3 shard_map.123
  35.4 0.8 collective-permute-start.7
  36.6 0.4 shard_map.125
  37.1 0.9 %shard_map.124 = (f32[12,64,128]{2,1,0:T(8,128)S(1)}, f32[12,64,128]{2,1,0:T(8,128)S(1)}) custom-call(f32[4,64,128]{2,1,0:T(8,128)S(1)} %get-tuple-element.80.refs_0_.refs_1_.refs_6_, f32[12,64,128]{2,1,0:T(8,128)S(1)} %get-tuple-element.76.refs_9_.refs_12_.refs_1_.refs_2_.refs_4_, f32[12,64,128]{2,1,0:T(8,128)S(1)} %get-tuple-element.78.refs_13_.refs_2_.refs_3_.refs_5_, ...), custom_call_target="tpu_custom_call" | custom-call | flops 120000 | bytes 12288 | tf_op jit(solution)/shard_map/pallas_call | solution.py:139
  38.0 0.9 %shard_map.126.refs_14_.refs_9_.refs_1_.refs_2_.refs_4_.refs_5_.refs_6_.refs_25_ = f32[12,64,128]{2,1,0:T(8,128)S(1)} custom-call(f32[32,64,128]{2,1,0:T(8,128)S(1)} %get-tuple-element.85.refs_0_.refs_1_.refs_3_.refs_4_.refs_5_, f32[32,64,128]{2,1,0:T(8,128)S(1)} %get-tuple-element.86.refs_1_.refs_2_, ...), custom_call_target="tpu_custom_call" | custom-call | flops 120000 | bytes 12288 | tf_op jit(solution)/shard_map/pallas_call | solution.py:139
  38.9 0.9 %shard_map.127.refs_15_.refs_10_.refs_2_.refs_3_.refs_5_.refs_6_.refs_7_.refs_26_ = f32[12,64,128]{2,1,0:T(8,128)S(1)} custom-call(f32[32,64,128]{2,1,0:T(8,128)S(1)} %get-tuple-element.85.refs_0_.refs_1_.refs_3_.refs_4_.refs_5_, f32[32,64,128]{2,1,0:T(8,128)S(1)} %get-tuple-element.86.refs_1_.refs_2_, ...), custom_call_target="tpu_custom_call" | custom-call | flops 120000 | bytes 12288 | tf_op jit(solution)/shard_map/pallas_call | solution.py:139
  39.9 0.3 shard_map.128
  40.2 0.3 shard_map.129.refs_12_.refs_7_.refs_16_.refs_0_.refs_1_.refs_3_.refs_4_.refs_5_.refs_19_
  40.6 0.3 shard_map.130
  40.9 0.3 shard_map.131.refs_17_.refs_3_.refs_4_.refs_6_.refs_7_.refs_8_.refs_19_
  41.2 0.5 shard_map.132
  41.8 4.5 %collective-permute-start.10 = (f32[264,128]{1,0:T(8,128)S(1)}, f32[264,128]{1,0:T(8,128)S(1)}, u32[]{:S(2)}, u32[]{:S(2)}) collective-permute-start(f32[264,128]{1,0:T(8,128)S(1)} %get-tuple-element.107), channel_id=1, source_target_pairs={{0,1},{1,0},{2,3},{3,2},{4,5},{5,4},{6,7},{7,6},{8,9},{9,8},{10,11... | collective-permute-start | bytes 405512 | tf_op jit(solution)/shard_map/ppermute | solution.py:524
  46.3 0.9 %shard_map.134.refs_11_.refs_2_.refs_3_.refs_6_.refs_24_.refs_7_ = f32[12,64,128]{2,1,0:T(8,128)S(1)} custom-call(f32[4,64,128]{2,1,0:T(8,128)S(1)} %shard_map.129.refs_12_.refs_7_.refs_16_.refs_0_.refs_1_.refs_3_.refs_4_.refs_5_.refs_19_, f32[12,64,128]{2,1,0:T(8,128)S(1)} %shard_map.126.refs_14_.refs_9_.refs_1_.refs_2_.refs_4_.refs_5_.refs_6_.refs_25_, ...), custom_call_target="tpu_custom_call" | custom-call | flops 120000 | bytes 12288 | tf_op jit(solution)/shard_map/pallas_call | solution.py:139
  47.2 0.9 %shard_map.133.refs_10_.refs_1_.refs_2_.refs_5_.refs_23_.refs_6_ = f32[12,64,128]{2,1,0:T(8,128)S(1)} custom-call(f32[4,64,128]{2,1,0:T(8,128)S(1)} %shard_map.129.refs_12_.refs_7_.refs_16_.refs_0_.refs_1_.refs_3_.refs_4_.refs_5_.refs_19_, f32[12,64,128]{2,1,0:T(8,128)S(1)} %shard_map.126.refs_14_.refs_9_.refs_1_.refs_2_.refs_4_.refs_5_.refs_6_.refs_25_, ...), custom_call_target="tpu_custom_call" | custom-call | flops 120000 | bytes 12288 | tf_op jit(solution)/shard_map/pallas_call | solution.py:139
  48.2 0.7 collective-permute-start.9
  48.9 1.6 %collective-permute-done.10.refs_0_ = f32[264,128]{1,0:T(8,128)S(1)} collective-permute-done((f32[264,128]{1,0:T(8,128)S(1)}, f32[264,128]{1,0:T(8,128)S(1)}, u32[]{:S(2)}, u32[]{:S(2)}) %collective-permute-start.10) | collective-permute-done | bytes 135200 | tf_op jit(solution)/shard_map/ppermute | solution.py:524
  50.5 0.3 shard_map.135.refs_0_.refs_1_.refs_4_.refs_5_.refs_18_
  50.8 2.8 %collective-permute-start.12 = (f32[4,64,128]{2,1,0:T(8,128)S(1)}, f32[4,64,128]{2,1,0:T(8,128)S(1)}, u32[]{:S(2)}, u32[]{:S(2)}) collective-permute-start(f32[4,64,128]{2,1,0:T(8,128)S(1)} %shard_map.135.refs_0_.refs_1_.refs_4_.refs_5_.refs_18_), channel_id=1, source_target_pairs={{0,1},{1,0},{2,3},{3,2},{4,5},{5,4},{6,7},{7,6},{8,9},{9,8},{10,11... | collective-permute-start | bytes 393224 | tf_op jit(solution)/shard_map/ppermute | solution.py:524
  53.6 1.0 %shard_map.136.refs_10_.refs_13_.refs_1_.refs_21_.refs_2_ = f32[12,64,128]{2,1,0:T(8,128)S(1)} custom-call(f32[4,64,128]{2,1,0:T(8,128)S(1)} %shard_map.135.refs_0_.refs_1_.refs_4_.refs_5_.refs_18_, f32[12,64,128]{2,1,0:T(8,128)S(1)} %shard_map.133.refs_10_.refs_1_.refs_2_.refs_5_.refs_23_.refs_6_, ...), custom_call_target="tpu_custom_call" | custom-call | flops 120000 | bytes 12288 | tf_op jit(solution)/shard_map/pallas_call | solution.py:139
  54.6 0.3 shard_map.137.refs_1_.refs_3_.refs_4_.refs_7_.refs_8_.refs_18_
  54.9 0.7 collective-permute-start.13
  55.7 1.5 %collective-permute-start.11 = (f32[16,64,128]{2,1,0:T(8,128)S(1)}, f32[16,64,128]{2,1,0:T(8,128)S(1)}, u32[]{:S(2)}, u32[]{:S(2)}) collective-permute-start(f32[16,64,128]{2,1,0:T(8,128)S(1)} %shard_map.138), channel_id=1, source_target_pairs={{0,16},{8,24},{16,0},{24,8},{1,17},{9,25},{17,1},{25,9},{2,18},{10... | collective-permute-start | bytes 1572872 | tf_op jit(solution)/shard_map/ppermute | solution.py:529
  57.2 5.2 %collective-permute-start.14 = (f32[8,128]{1,0:T(8,128)S(1)}, f32[8,128]{1,0:T(8,128)S(1)}, u32[]{:S(2)}, u32[]{:S(2)}) collective-permute-start(f32[8,128]{1,0:T(8,128)S(1)} %get-tuple-element.119), channel_id=1, source_target_pairs={{0,2},{1,3},{2,0},{3,1},{4,6},{5,7},{6,4},{7,5},{8,10},{9,11},{10,... | collective-permute-start | bytes 12296 | tf_op jit(solution)/shard_map/ppermute | solution.py:529
  62.5 0.9 %shard_map.139.refs_14_.refs_2_.refs_22_.refs_3_ = f32[12,64,128]{2,1,0:T(8,128)S(1)} custom-call(f32[4,64,128]{2,1,0:T(8,128)S(1)} %shard_map.135.refs_0_.refs_1_.refs_4_.refs_5_.refs_18_, f32[12,64,128]{2,1,0:T(8,128)S(1)} %shard_map.133.refs_10_.refs_1_.refs_2_.refs_5_.refs_23_.refs_6_, ...), custom_call_target="tpu_custom_call" | custom-call | flops 120000 | bytes 12288 | tf_op jit(solution)/shard_map/pallas_call | solution.py:139
  63.4 0.3 shard_map.140.refs_13_.refs_0_.refs_1_.refs_17_
  64.0 0.3 shard_map.141.refs_3_.refs_4_.refs_17_
  64.4 2.0 %shard_map.142 = (f32[12,64,128]{2,1,0:T(8,128)S(1)}, f32[12,64,128]{2,1,0:T(8,128)S(1)}) custom-call(f32[4,64,128]{2,1,0:T(8,128)S(1)} %shard_map.140.refs_13_.refs_0_.refs_1_.refs_17_, f32[12,64,128]{2,1,0:T(8,128)S(1)} %shard_map.136.refs_10_.refs_13_.refs_1_.refs_21_.refs_2_, f32[12,64,128]{2,1,0:T(8,128)S(1)} %shard_map.139.refs_14_.refs_2_.refs_22_.refs_3_, ...), custom_call_target="tpu_custom_call" | custom-call | flops 240000 | bytes 24576 | tf_op jit(solution)/shard_map/pallas_call | solution.py:139
  66.4 3.3 %collective-permute-start.19 = (f32[4,64,128]{2,1,0:T(8,128)S(1)}, f32[4,64,128]{2,1,0:T(8,128)S(1)}, u32[]{:S(2)}, u32[]{:S(2)}) collective-permute-start(f32[4,64,128]{2,1,0:T(8,128)S(1)} %shard_map.140.refs_13_.refs_0_.refs_1_.refs_17_), channel_id=1, source_target_pairs={{0,1},{1,0},{2,3},{3,2},{4,5},{5,4},{6,7},{7,6},{8,9},{9,8},{10,11... | collective-permute-start | bytes 393224 | tf_op jit(solution)/shard_map/ppermute | solution.py:524
  69.7 0.7 collective-permute-start.17
  70.4 0.6 collective-permute-start.16
  71.1 4.2 %collective-permute-start.18 = (f32[8,128]{1,0:T(8,128)S(1)}, f32[8,128]{1,0:T(8,128)S(1)}, u32[]{:S(2)}, u32[]{:S(2)}) collective-permute-start(f32[8,128]{1,0:T(8,128)S(1)} %add.29.refs_20_), channel_id=1, source_target_pairs={{0,4},{1,5},{2,6},{3,7},{4,0},{5,1},{6,2},{7,3},{8,12},{9,13},{10,... | collective-permute-start | bytes 12296 | tf_op jit(solution)/shard_map/ppermute | solution.py:529
  75.3 0.4 shard_map.144.refs_22_
  75.7 1.6 %collective-permute-done.18.refs_21_ = f32[8,128]{1,0:T(8,128)S(1)} collective-permute-done((f32[8,128]{1,0:T(8,128)S(1)}, f32[8,128]{1,0:T(8,128)S(1)}, u32[]{:S(2)}, u32[]{:S(2)}) %collective-permute-start.18) | collective-permute-done | bytes 4128 | tf_op jit(solution)/shard_map/ppermute | solution.py:529
  77.4 0.4 shard_map.145
  77.8 1.3 %collective-permute-done.20 = f32[264,128]{1,0:T(8,128)S(1)} collective-permute-done((f32[264,128]{1,0:T(8,128)S(1)}, f32[264,128]{1,0:T(8,128)S(1)}, u32[]{:S(2)}, u32[]{:S(2)}) %collective-permute-start.20) | collective-permute-done | bytes 135200 | tf_op jit(solution)/shard_map/ppermute | solution.py:529
  79.2 1.5 %collective-permute-start.21 = (f32[264,128]{1,0:T(8,128)S(1)}, f32[264,128]{1,0:T(8,128)S(1)}, u32[]{:S(2)}, u32[]{:S(2)}) collective-permute-start(f32[264,128]{1,0:T(8,128)S(1)} %add.30.rest_2_), channel_id=1, source_target_pairs={{0,16},{8,24},{16,0},{24,8},{1,17},{9,25},{17,1},{25,9},{2,18},{10... | collective-permute-start | bytes 405512 | tf_op jit(solution)/shard_map/ppermute | solution.py:529
  81.4 0.3 collective-permute-done.16.rest_1_
  81.7 3.2 %collective-permute-done.21.rest_3_ = f32[264,128]{1,0:T(8,128)S(1)} collective-permute-done((f32[264,128]{1,0:T(8,128)S(1)}, f32[264,128]{1,0:T(8,128)S(1)}, u32[]{:S(2)}, u32[]{:S(2)}) %collective-permute-start.21) | collective-permute-done | bytes 135200 | tf_op jit(solution)/shard_map/ppermute | solution.py:529
  84.9 0.8 shard_map.146.values_ref
  85.8 0.8 shard_map.147.refs_0_
  86.6 1.1 %collective-permute-done.22.values_ref = f32[16,64,128]{2,1,0:T(8,128)S(1)} collective-permute-done((f32[16,64,128]{2,1,0:T(8,128)S(1)}, f32[16,64,128]{2,1,0:T(8,128)S(1)}, u32[]{:S(2)}, u32[]{:S(2)}) %collective-permute-start.22) | collective-permute-done | bytes 524320 | tf_op jit(solution)/shard_map/ppermute | solution.py:529
  87.7 0.8 shard_map.148
  (47 shorter events, 2.4 us)
Async XLA Ops:
  0.0 5.1 %copy-start = (f32[1,32,64,128]{3,2,1,0:T(8,128)S(1)}, f32[1,32,64,128]{3,2,1,0:T(8,128)}, u32[]{:S(2)}) copy-start(f32[1,32,64,128]{3,2,1,0:T(8,128)} %param.12) | copy-start | bytes 3145732
  0.0 5.1 %copy-start.2 = (f32[1,32,64,128]{3,2,1,0:T(8,128)S(1)}, f32[1,32,64,128]{3,2,1,0:T(8,128)}, u32[]{:S(2)}) copy-start(f32[1,32,64,128]{3,2,1,0:T(8,128)} %param.11) | copy-start | bytes 3145732
  1.3 14.2 %collective-permute-start = (f32[8,64,128]{2,1,0:T(8,128)S(1)}, f32[8,64,128]{2,1,0:T(8,128)S(1)}, u32[]{:S(2)}, u32[]{:S(2)}) collective-permute-start(f32[8,64,128]{2,1,0:T(8,128)S(1)} %pad_maximum_fusion), channel_id=1, source_target_pairs={{0,1},{1,0},{2,3},{3,2},{4,5},{5,4},{6,7},{7,6},{8,9},{9,8},{10,11... | collective-permute-start | bytes 786440 | tf_op jit(solution)/shard_map/ppermute | solution.py:524
  4.4 14.9 %collective-permute-start.2 = (f32[8,64,128]{2,1,0:T(8,128)S(1)}, f32[8,64,128]{2,1,0:T(8,128)S(1)}, u32[]{:S(2)}, u32[]{:S(2)}) collective-permute-start(f32[8,64,128]{2,1,0:T(8,128)S(1)} %pad_maximum_fusion.1), channel_id=1, source_target_pairs={{1,2},{2,1},{3,4},{4,3},{5,6},{6,5},{9,10},{10,9},{11,12},{12,11},... | collective-permute-start | bytes 786440 | tf_op jit(solution)/shard_map/ppermute | solution.py:524
  5.1 1.2 %copy-start.3 = (f32[32,64,128]{2,1,0:T(8,128)S(1)}, f32[32,64,128]{2,1,0:T(8,128)}, u32[]{:S(2)}) copy-start(f32[32,64,128]{2,1,0:T(8,128)} %refs_2_.1) | copy-start | bytes 3145732
  7.6 0.7 copy-start.5
  7.6 0.7 copy-start.7
  7.6 0.7 copy-start.8
  15.8 5.5 %collective-permute-start.1 = (f32[4,64,128]{2,1,0:T(8,128)S(1)}, f32[4,64,128]{2,1,0:T(8,128)S(1)}, u32[]{:S(2)}, u32[]{:S(2)}) collective-permute-start(f32[4,64,128]{2,1,0:T(8,128)S(1)} %get-tuple-element.68.refs_0_.refs_1_.refs_3_.refs_4_.refs_5_.refs_9_), channel_id=1, source_target_pairs={{0,1},{1,0},{2,3},{3,2},{4,5},{5,4},{6,7},{7,6},{8,9},{9,8},{10,11... | collective-permute-start | bytes 393224 | tf_op jit(solution)/shard_map/ppermute | solution.py:524
  19.6 7.2 %collective-permute-start.4 = (f32[4,64,128]{2,1,0:T(8,128)S(1)}, f32[4,64,128]{2,1,0:T(8,128)S(1)}, u32[]{:S(2)}, u32[]{:S(2)}) collective-permute-start(f32[4,64,128]{2,1,0:T(8,128)S(1)} %get-tuple-element.71.refs_3_.refs_4_.refs_6_.refs_7_.refs_8_.refs_9_), channel_id=1, source_target_pairs={{1,2},{2,1},{3,4},{4,3},{5,6},{6,5},{9,10},{10,9},{11,12},{12,11},... | collective-permute-start | bytes 393224 | tf_op jit(solution)/shard_map/ppermute | solution.py:524
  21.7 7.2 %collective-permute-start.3 = (f32[4,64,128]{2,1,0:T(8,128)S(1)}, f32[4,64,128]{2,1,0:T(8,128)S(1)}, u32[]{:S(2)}, u32[]{:S(2)}) collective-permute-start(f32[4,64,128]{2,1,0:T(8,128)S(1)} %get-tuple-element.74.refs_0_.refs_1_.refs_3_.refs_4_.refs_5_.refs_9_), channel_id=1, source_target_pairs={{0,1},{1,0},{2,3},{3,2},{4,5},{5,4},{6,7},{7,6},{8,9},{9,8},{10,11... | collective-permute-start | bytes 393224 | tf_op jit(solution)/shard_map/ppermute | solution.py:524
  27.2 7.9 %collective-permute-start.6 = (f32[4,64,128]{2,1,0:T(8,128)S(1)}, f32[4,64,128]{2,1,0:T(8,128)S(1)}, u32[]{:S(2)}, u32[]{:S(2)}) collective-permute-start(f32[4,64,128]{2,1,0:T(8,128)S(1)} %get-tuple-element.77.refs_3_.refs_4_.refs_6_.refs_7_.refs_8_.refs_9_), channel_id=1, source_target_pairs={{1,2},{2,1},{3,4},{4,3},{5,6},{6,5},{9,10},{10,9},{11,12},{12,11},... | collective-permute-start | bytes 393224 | tf_op jit(solution)/shard_map/ppermute | solution.py:524
  29.2 10.7 %collective-permute-start.5 = (f32[4,64,128]{2,1,0:T(8,128)S(1)}, f32[4,64,128]{2,1,0:T(8,128)S(1)}, u32[]{:S(2)}, u32[]{:S(2)}) collective-permute-start(f32[4,64,128]{2,1,0:T(8,128)S(1)} %get-tuple-element.80.refs_0_.refs_1_.refs_6_), channel_id=1, source_target_pairs={{0,1},{1,0},{2,3},{3,2},{4,5},{5,4},{6,7},{7,6},{8,9},{9,8},{10,11... | collective-permute-start | bytes 393224 | tf_op jit(solution)/shard_map/ppermute | solution.py:524
  35.1 1.2 %copy-start.1 = (f32[1,32,64,128]{3,2,1,0:T(8,128)S(1)}, f32[1,32,64,128]{3,2,1,0:T(8,128)}, u32[]{:S(2)}) copy-start(f32[1,32,64,128]{3,2,1,0:T(8,128)} %param.13) | copy-start | bytes 3145732
  35.1 1.5 %copy-start.4 = (f32[1,32,64,128]{3,2,1,0:T(8,128)S(1)}, f32[1,32,64,128]{3,2,1,0:T(8,128)}, u32[]{:S(2)}) copy-start(f32[1,32,64,128]{3,2,1,0:T(8,128)} %param.14) | copy-start | bytes 3145732
  35.4 5.1 %collective-permute-start.7 = (f32[4,64,128]{2,1,0:T(8,128)S(1)}, f32[4,64,128]{2,1,0:T(8,128)S(1)}, u32[]{:S(2)}, u32[]{:S(2)}) collective-permute-start(f32[4,64,128]{2,1,0:T(8,128)S(1)} %get-tuple-element.83.refs_3_.refs_4_.refs_6_), channel_id=1, source_target_pairs={{1,2},{2,1},{3,4},{4,3},{5,6},{6,5},{9,10},{10,9},{11,12},{12,11},... | collective-permute-start | bytes 393224 | tf_op jit(solution)/shard_map/ppermute | solution.py:524
  41.7 13.9 %collective-permute-start.8 = (f32[16,64,128]{2,1,0:T(8,128)S(1)}, f32[16,64,128]{2,1,0:T(8,128)S(1)}, u32[]{:S(2)}, u32[]{:S(2)}) collective-permute-start(f32[16,64,128]{2,1,0:T(8,128)S(1)} %get-tuple-element.105), channel_id=1, source_target_pairs={{0,8},{8,0},{16,24},{24,16},{1,9},{9,1},{17,25},{25,17},{2,10},{10... | collective-permute-start | bytes 1572872 | tf_op jit(solution)/shard_map/ppermute | solution.py:529
  41.8 8.7 %collective-permute-start.10 = (f32[264,128]{1,0:T(8,128)S(1)}, f32[264,128]{1,0:T(8,128)S(1)}, u32[]{:S(2)}, u32[]{:S(2)}) collective-permute-start(f32[264,128]{1,0:T(8,128)S(1)} %get-tuple-element.107), channel_id=1, source_target_pairs={{0,1},{1,0},{2,3},{3,2},{4,5},{5,4},{6,7},{7,6},{8,9},{9,8},{10,11... | collective-permute-start | bytes 405512 | tf_op jit(solution)/shard_map/ppermute | solution.py:524
  48.2 6.4 %collective-permute-start.9 = (f32[4,64,128]{2,1,0:T(8,128)S(1)}, f32[4,64,128]{2,1,0:T(8,128)S(1)}, u32[]{:S(2)}, u32[]{:S(2)}) collective-permute-start(f32[4,64,128]{2,1,0:T(8,128)S(1)} %shard_map.131.refs_17_.refs_3_.refs_4_.refs_6_.refs_7_.refs_8_.refs_19_), channel_id=1, source_target_pairs={{1,2},{2,1},{3,4},{4,3},{5,6},{6,5},{9,10},{10,9},{11,12},{12,11},... | collective-permute-start | bytes 393224 | tf_op jit(solution)/shard_map/ppermute | solution.py:524
  50.8 12.6 %collective-permute-start.12 = (f32[4,64,128]{2,1,0:T(8,128)S(1)}, f32[4,64,128]{2,1,0:T(8,128)S(1)}, u32[]{:S(2)}, u32[]{:S(2)}) collective-permute-start(f32[4,64,128]{2,1,0:T(8,128)S(1)} %shard_map.135.refs_0_.refs_1_.refs_4_.refs_5_.refs_18_), channel_id=1, source_target_pairs={{0,1},{1,0},{2,3},{3,2},{4,5},{5,4},{6,7},{7,6},{8,9},{9,8},{10,11... | collective-permute-start | bytes 393224 | tf_op jit(solution)/shard_map/ppermute | solution.py:524
  54.9 9.1 %collective-permute-start.13 = (f32[4,64,128]{2,1,0:T(8,128)S(1)}, f32[4,64,128]{2,1,0:T(8,128)S(1)}, u32[]{:S(2)}, u32[]{:S(2)}) collective-permute-start(f32[4,64,128]{2,1,0:T(8,128)S(1)} %shard_map.137.refs_1_.refs_3_.refs_4_.refs_7_.refs_8_.refs_18_), channel_id=1, source_target_pairs={{1,2},{2,1},{3,4},{4,3},{5,6},{6,5},{9,10},{10,9},{11,12},{12,11},... | collective-permute-start | bytes 393224 | tf_op jit(solution)/shard_map/ppermute | solution.py:524
  55.7 19.9 %collective-permute-start.11 = (f32[16,64,128]{2,1,0:T(8,128)S(1)}, f32[16,64,128]{2,1,0:T(8,128)S(1)}, u32[]{:S(2)}, u32[]{:S(2)}) collective-permute-start(f32[16,64,128]{2,1,0:T(8,128)S(1)} %shard_map.138), channel_id=1, source_target_pairs={{0,16},{8,24},{16,0},{24,8},{1,17},{9,25},{17,1},{25,9},{2,18},{10... | collective-permute-start | bytes 1572872 | tf_op jit(solution)/shard_map/ppermute | solution.py:529
  57.2 6.8 %collective-permute-start.14 = (f32[8,128]{1,0:T(8,128)S(1)}, f32[8,128]{1,0:T(8,128)S(1)}, u32[]{:S(2)}, u32[]{:S(2)}) collective-permute-start(f32[8,128]{1,0:T(8,128)S(1)} %get-tuple-element.119), channel_id=1, source_target_pairs={{0,2},{1,3},{2,0},{3,1},{4,6},{5,7},{6,4},{7,5},{8,10},{9,11},{10,... | collective-permute-start | bytes 12296 | tf_op jit(solution)/shard_map/ppermute | solution.py:529
  66.4 4.0 %collective-permute-start.15 = (f32[12,64,128]{2,1,0:T(8,128)S(1)}, f32[12,64,128]{2,1,0:T(8,128)S(1)}, u32[]{:S(2)}, u32[]{:S(2)}) collective-permute-start(f32[12,64,128]{2,1,0:T(8,128)S(1)} %get-tuple-element.112), channel_id=1, source_target_pairs={{0,8},{8,0},{16,24},{24,16},{1,9},{9,1},{17,25},{25,17},{2,10},{10... | collective-permute-start | bytes 1179656 | tf_op jit(solution)/shard_map/ppermute | solution.py:529
  66.4 8.8 %collective-permute-start.19 = (f32[4,64,128]{2,1,0:T(8,128)S(1)}, f32[4,64,128]{2,1,0:T(8,128)S(1)}, u32[]{:S(2)}, u32[]{:S(2)}) collective-permute-start(f32[4,64,128]{2,1,0:T(8,128)S(1)} %shard_map.140.refs_13_.refs_0_.refs_1_.refs_17_), channel_id=1, source_target_pairs={{0,1},{1,0},{2,3},{3,2},{4,5},{5,4},{6,7},{7,6},{8,9},{9,8},{10,11... | collective-permute-start | bytes 393224 | tf_op jit(solution)/shard_map/ppermute | solution.py:524
  69.7 7.6 %collective-permute-start.17 = (f32[4,64,128]{2,1,0:T(8,128)S(1)}, f32[4,64,128]{2,1,0:T(8,128)S(1)}, u32[]{:S(2)}, u32[]{:S(2)}) collective-permute-start(f32[4,64,128]{2,1,0:T(8,128)S(1)} %shard_map.141.refs_3_.refs_4_.refs_17_), channel_id=1, source_target_pairs={{1,2},{2,1},{3,4},{4,3},{5,6},{6,5},{9,10},{10,9},{11,12},{12,11},... | collective-permute-start | bytes 393224 | tf_op jit(solution)/shard_map/ppermute | solution.py:524
  70.4 11.3 %collective-permute-start.16 = (f32[12,64,128]{2,1,0:T(8,128)S(1)}, f32[12,64,128]{2,1,0:T(8,128)S(1)}, u32[]{:S(2)}, u32[]{:S(2)}) collective-permute-start(f32[12,64,128]{2,1,0:T(8,128)S(1)} %shard_map.143.rest_0_), channel_id=1, source_target_pairs={{0,16},{8,24},{16,0},{24,8},{1,17},{9,25},{17,1},{25,9},{2,18},{10... | collective-permute-start | bytes 1179656 | tf_op jit(solution)/shard_map/ppermute | solution.py:529
  71.1 6.3 %collective-permute-start.18 = (f32[8,128]{1,0:T(8,128)S(1)}, f32[8,128]{1,0:T(8,128)S(1)}, u32[]{:S(2)}, u32[]{:S(2)}) collective-permute-start(f32[8,128]{1,0:T(8,128)S(1)} %add.29.refs_20_), channel_id=1, source_target_pairs={{0,4},{1,5},{2,6},{3,7},{4,0},{5,1},{6,2},{7,3},{8,12},{9,13},{10,... | collective-permute-start | bytes 12296 | tf_op jit(solution)/shard_map/ppermute | solution.py:529
  77.7 1.4 %collective-permute-start.20 = (f32[264,128]{1,0:T(8,128)S(1)}, f32[264,128]{1,0:T(8,128)S(1)}, u32[]{:S(2)}, u32[]{:S(2)}) collective-permute-start(f32[264,128]{1,0:T(8,128)S(1)} %get-tuple-element.114), channel_id=1, source_target_pairs={{0,8},{8,0},{16,24},{24,16},{1,9},{9,1},{17,25},{25,17},{2,10},{10... | collective-permute-start | bytes 405512 | tf_op jit(solution)/shard_map/ppermute | solution.py:529
  79.2 5.7 %copy-start.6 = (f32[64]{0:T(128)S(1)}, f32[64]{0:T(128)}, u32[]{:S(2)}) copy-start(f32[64]{0:T(128)} %table_ref.1) | copy-start | bytes 772
  79.2 5.7 %collective-permute-start.21 = (f32[264,128]{1,0:T(8,128)S(1)}, f32[264,128]{1,0:T(8,128)S(1)}, u32[]{:S(2)}, u32[]{:S(2)}) collective-permute-start(f32[264,128]{1,0:T(8,128)S(1)} %add.30.rest_2_), channel_id=1, source_target_pairs={{0,16},{8,24},{16,0},{24,8},{1,17},{9,25},{17,1},{25,9},{2,18},{10... | collective-permute-start | bytes 405512 | tf_op jit(solution)/shard_map/ppermute | solution.py:529
  85.7 2.0 %collective-permute-start.22 = (f32[16,64,128]{2,1,0:T(8,128)S(1)}, f32[16,64,128]{2,1,0:T(8,128)S(1)}, u32[]{:S(2)}, u32[]{:S(2)}) collective-permute-start(f32[16,64,128]{2,1,0:T(8,128)S(1)} %shard_map.146.values_ref), channel_id=1, source_target_pairs={{0,8},{8,0},{16,24},{24,16},{1,9},{9,1},{17,25},{25,17},{2,10},{10... | collective-permute-start | bytes 1572872 | tf_op jit(solution)/shard_map/ppermute | solution.py:529

commit v5 on v2

--- a/solution.py
+++ b/solution.py
@@ -223,6 +223,48 @@
     outs = [f32(count, width, length)]
     scratch = scratch_of(count, width, length)
     return kernel_call(kernel, [], sum(groups, []), outs, scratch, count)[0]
+
+
+def adjoint_base(place, cur, old, courant):
+    slab, width, length = courant.shape
+    first, count = place
+    groups = [arrays_of(cur), arrays_of(old), [courant]]
+    sizes = [len(g) for g in groups]
+
+    def kernel(*refs):
+        (cur_refs, old_refs, (c_ref,)), refs = grouped(refs, sizes)
+        next_ref, along_ref, pad = refs
+        prepare(first, pad, along_ref, None, list(zip(cur_refs, origins(cur))), slab, width)
+        old_ref, old_at = find(list(zip(old_refs, origins(old))), first)
+
+        def body(i, _):
+            center, lap = stencil(pad, HALO + i, width, along_ref[i])
+            next_ref[i] = 2.0 * center - old_ref[old_at + i] + c_ref[first + i] * lap
+
+        march(count, body)
+
+    outs = [f32(count, width, length)]
+    scratch = scratch_of(count, width, length)
+    return kernel_call(kernel, [], sum(groups, []), outs, scratch, count)[0]
+
+
+def with_points(bases, firsts, fields, number, observed):
+    many = len(bases)
+
+    def kernel(*refs):
+        base_refs, field_refs = refs[:many], refs[many : 2 * many]
+        number_ref, observed_ref = refs[2 * many : 2 * many + 2]
+        for n in range(many):
+
+            def body(i, _, n=n):
+                q = firsts[n] + i
+                miss = number_ref[q] * field_refs[n][i] - observed_ref[q]
+                refs[2 * many + 2 + n][i] = base_refs[n][i] + miss
+
+            march(bases[n].shape[0], body)
+
+    outs = [f32(*base.shape) for base in bases]
+    return kernel_call(kernel, [], [*bases, *fields, number, observed], outs, [], 8)
 
 
 def adjoint_step(place, halo, cur, old, field, found, next_ref, along_ref, pad):
@@ -591,7 +633,7 @@
             places[side], halo, cur, old, courant, [field], number, sums[step], after
         )
 
-    laps, fields = [], []
+    laps, fields, bases = [], [], []
     near = ahead(0, 1, None, cur, old, ())
     far = ahead(0, 2, None, cur, old, ())
     for step in range(STEPS):
@@ -599,8 +641,9 @@
         after = [near[0], far[0]]
         if last:
             rest, more = [(second, 0)], [(first, 0)]
-            near_adj = back(step, 1, None, more, rest, (near[0], starts[1]), ())
-            far_adj = back(step, 2, None, more, rest, (far[0], starts[2]), ())
+            near_adj, far_adj = with_points(
+                bases, starts[1:3], [near[0], far[0]], number, sums[step]
+            )
             after += [near_adj, far_adj]
         one = ahead(step, 0, coming[0], cur, old, after)
         if last:
@@ -617,7 +660,11 @@
             message = exchange(one[0], 0)
             newer = [(one[0], starts[0]), (near[0], starts[1]), (far[0], starts[2])]
             near_next = ahead(step + 1, 1, None, newer, cur, ())
-            two = ahead(step, 3, coming[1], cur, old, [near_next[0]])
+            behind = [near_next[0]]
+            if 0 < step < STEPS - 1:
+                bases.append(adjoint_base(places[step], [(first, 0)], [(second, 0)], courant))
+                behind.append(bases[-1])
+            two = ahead(step, 3, coming[1], cur, old, behind)
             newer.append((two[0], starts[3]))
         laps.append((one[1], near[1], far[1], two[1]))
         fields.append((one[0], near[0], far[0], two[0]))

time: 88.4 us -> 87.7 us (level)
  starting transfers between devices: 43.9 us -> 43 us
    pallas_call x38 -> x39, Pallas kernels: 25.4 us -> 25.5 us  [kernel_call(): pl.pallas_call(kernel, out_shape=tuple(outs), in_specs=[SMEM] * len(small...]
  transfers between devices with their start and end apart: 24 -> 24, of which waited for: 9 -> 7; matrix products, arithmetic and copies ran while one was open for 0% -> 0% of each run, Pallas kernels for 27% -> 27%
where the time goes in v5:
time: 87.7 us; the launch traced here: 86.9 us
  starting transfers between devices  43 us (49%)
  Pallas kernels  26.5 us (30%)
  waiting for transfers between devices  11.7 us (13%)
  local copies, waits for them, and re-layouts  3.58 us (4%)
  between operations  2.05 us (2%)
    ppermute x14, starting transfers between devices, exchange(): return lax.ppermute(values, 'depth', links)  26.2 us
    pallas_call x39, Pallas kernels, kernel_call(): pl.pallas_call(kernel, out_shape=tuple(outs), in_specs=[SMEM] * len(small...  25.5 us
    ppermute x10, starting transfers between devices, swap(): return lax.ppermute(values, axis, [(i, i ^ bit) for i in range(count)])  16.7 us
    ppermute x10, waiting for transfers between devices, swap(): return lax.ppermute(values, axis, [(i, i ^ bit) for i in range(count)])  9.21 us
    ppermute x14, waiting for transfers between devices, exchange(): return lax.ppermute(values, 'depth', links)  2.45 us
    unnamed x18, local copies, waits for them, and re-layouts  2.29 us
  transfers between devices with their start and end apart: 24, of which 7 were waited for; matrix products, arithmetic and copies ran while one was open for 0% of the time, Pallas kernels for 27%

profile of v5, /device:TPU:0, one launch (start us, length us, event | category | flops | bytes accessed | tf_op | source)
XLA Modules:
  0.0 86.9 jit_solution(5559313751396892297)
XLA Ops:
  0.0 1.3 %dynamic-slice_bitcast_fusion = (f32[4,64,128]{2,1,0:T(8,128)S(1)}, f32[4,64,128]{2,1,0:T(8,128)S(1)}, f32[4,64,128]{2,1,0:T(8,128)S(1)}, f32[4,64,128]{2,1,0:T(8,128)S(1)}) fusion(f32[1,32,64,128]{3,2,1,0:T(8,128)} %param.13, s32[]{:T(128)S(6)} %select_n.17, s32[]{:T(128)S(6)} %select_n.16, f32[1,32,64,128]{3,2,1,0:T(8,128)} %param.12), kind=kLoop, calls=%fused_computation.2 | loop fusion | bytes 1048584 | tf_op jit(solution)/shard_map/dynamic_slice | solution.py:479
  1.3 3.0 %collective-permute-start = (f32[8,64,128]{2,1,0:T(8,128)S(1)}, f32[8,64,128]{2,1,0:T(8,128)S(1)}, u32[]{:S(2)}, u32[]{:S(2)}) collective-permute-start(f32[8,64,128]{2,1,0:T(8,128)S(1)} %pad_maximum_fusion), channel_id=1, source_target_pairs={{0,1},{1,0},{2,3},{3,2},{4,5},{5,4},{6,7},{7,6},{8,9},{9,8},{10,11... | collective-permute-start | bytes 786440 | tf_op jit(solution)/shard_map/ppermute | solution.py:561
  4.4 0.7 collective-permute-start.2
  5.1 1.2 %copy-done.3 = f32[32,64,128]{2,1,0:T(8,128)S(1)} copy-done((f32[32,64,128]{2,1,0:T(8,128)S(1)}, f32[32,64,128]{2,1,0:T(8,128)}, u32[]{:S(2)}) %copy-start.3) | copy-done | bytes 1048600
  6.3 0.6 shard_map.109
  7.6 0.6 copy-done.5
  8.3 3.0 %shard_map.110 = (f32[32,64,128]{2,1,0:T(8,128)S(1)}, f32[32,64,128]{2,1,0:T(8,128)S(1)}, f32[8,128]{1,0:T(8,128)S(1)}, f32[8,128]{1,0:T(8,128)S(1)}, f32[8,128]...) custom-call(f32[1,4]{1,0:T(1,128)S(1)} %copy-done.7, ...), custom_call_target="tpu_custom_call" | custom-call | flops 80000 | bytes 8192 | tf_op jit(solution)/shard_map/pallas_call | solution.py:136
  11.3 0.9 %shard_map.112 = (f32[12,64,128]{2,1,0:T(8,128)S(1)}, f32[12,64,128]{2,1,0:T(8,128)S(1)}) custom-call(f32[32,64,128]{2,1,0:T(8,128)S(1)} %get-tuple-element.62.refs_0_.refs_1_.refs_3_.refs_4_.refs_5_, f32[32,64,128]{2,1,0:T(8,128)S(1)} %get-tuple-element.63.refs_1_.refs_2_, ...), custom_call_target="tpu_custom_call" | custom-call | flops 120000 | bytes 12288 | tf_op jit(solution)/shard_map/pallas_call | solution.py:136
  12.2 0.9 %shard_map.111 = (f32[12,64,128]{2,1,0:T(8,128)S(1)}, f32[12,64,128]{2,1,0:T(8,128)S(1)}) custom-call(f32[32,64,128]{2,1,0:T(8,128)S(1)} %get-tuple-element.62.refs_0_.refs_1_.refs_3_.refs_4_.refs_5_, f32[32,64,128]{2,1,0:T(8,128)S(1)} %get-tuple-element.63.refs_1_.refs_2_, ...), custom_call_target="tpu_custom_call" | custom-call | flops 120000 | bytes 12288 | tf_op jit(solution)/shard_map/pallas_call | solution.py:136
  13.1 2.4 %collective-permute-done.refs_0_ = f32[8,64,128]{2,1,0:T(8,128)S(1)} collective-permute-done((f32[8,64,128]{2,1,0:T(8,128)S(1)}, f32[8,64,128]{2,1,0:T(8,128)S(1)}, u32[]{:S(2)}, u32[]{:S(2)}) %collective-permute-start) | collective-permute-done | bytes 262176 | tf_op jit(solution)/shard_map/ppermute | solution.py:561
  15.9 2.5 %collective-permute-start.1 = (f32[4,64,128]{2,1,0:T(8,128)S(1)}, f32[4,64,128]{2,1,0:T(8,128)S(1)}, u32[]{:S(2)}, u32[]{:S(2)}) collective-permute-start(f32[4,64,128]{2,1,0:T(8,128)S(1)} %get-tuple-element.69.refs_0_.refs_1_.refs_3_.refs_4_.refs_5_.refs_9_), channel_id=1, source_target_pairs={{0,1},{1,0},{2,3},{3,2},{4,5},{5,4},{6,7},{7,6},{8,9},{9,8},{10,11... | collective-permute-start | bytes 393224 | tf_op jit(solution)/shard_map/ppermute | solution.py:561
  18.4 0.9 %shard_map.114 = (f32[12,64,128]{2,1,0:T(8,128)S(1)}, f32[12,64,128]{2,1,0:T(8,128)S(1)}) custom-call(f32[4,64,128]{2,1,0:T(8,128)S(1)} %get-tuple-element.69.refs_0_.refs_1_.refs_3_.refs_4_.refs_5_.refs_9_, f32[12,64,128]{2,1,0:T(8,128)S(1)} %get-tuple-element.66.refs_6_.refs_1_.refs_2_.refs_4_.refs_5_.refs_8_, ...), custom_call_target="tpu_custom_call" | custom-call | flops 120000 | bytes 12288 | tf_op jit(solution)/shard_map/pallas_call | solution.py:136
  19.4 0.3 shard_map.115
  19.7 0.8 collective-permute-start.4
  20.6 0.3 copy-done.4
  20.9 0.4 shard_map.119
  21.3 0.9 %shard_map.116 = (f32[12,64,128]{2,1,0:T(8,128)S(1)}, f32[12,64,128]{2,1,0:T(8,128)S(1)}) custom-call(f32[4,64,128]{2,1,0:T(8,128)S(1)} %get-tuple-element.69.refs_0_.refs_1_.refs_3_.refs_4_.refs_5_.refs_9_, f32[12,64,128]{2,1,0:T(8,128)S(1)} %get-tuple-element.66.refs_6_.refs_1_.refs_2_.refs_4_.refs_5_.refs_8_, ...), custom_call_target="tpu_custom_call" | custom-call | flops 120000 | bytes 12288 | tf_op jit(solution)/shard_map/pallas_call | solution.py:136
  22.3 0.3 shard_map.117
  22.6 4.0 %collective-permute-start.3 = (f32[4,64,128]{2,1,0:T(8,128)S(1)}, f32[4,64,128]{2,1,0:T(8,128)S(1)}, u32[]{:S(2)}, u32[]{:S(2)}) collective-permute-start(f32[4,64,128]{2,1,0:T(8,128)S(1)} %get-tuple-element.75.refs_0_.refs_1_.refs_3_.refs_4_.refs_5_.refs_9_), channel_id=1, source_target_pairs={{0,1},{1,0},{2,3},{3,2},{4,5},{5,4},{6,7},{7,6},{8,9},{9,8},{10,11... | collective-permute-start | bytes 393224 | tf_op jit(solution)/shard_map/ppermute | solution.py:561
  26.6 0.9 %shard_map.120.refs_10_.refs_0_ = f32[12,64,128]{2,1,0:T(8,128)S(1)} custom-call(f32[32,64,128]{2,1,0:T(8,128)S(1)} %get-tuple-element.78.refs_0_.refs_1_.refs_3_.refs_4_.refs_5_, f32[32,64,128]{2,1,0:T(8,128)S(1)} %get-tuple-element.79.refs_1_.refs_2_, ...), custom_call_target="tpu_custom_call" | custom-call | flops 120000 | bytes 12288 | tf_op jit(solution)/shard_map/pallas_call | solution.py:136
  27.5 0.9 %shard_map.118 = (f32[12,64,128]{2,1,0:T(8,128)S(1)}, f32[12,64,128]{2,1,0:T(8,128)S(1)}) custom-call(f32[4,64,128]{2,1,0:T(8,128)S(1)} %get-tuple-element.75.refs_0_.refs_1_.refs_3_.refs_4_.refs_5_.refs_9_, f32[12,64,128]{2,1,0:T(8,128)S(1)} %get-tuple-element.71.refs_6_.refs_9_.refs_1_.refs_2_.refs_4_.refs_5_.refs_7_, ...), custom_call_target="tpu_custom_call" | custom-call | flops 120000 | bytes 12288 | tf_op jit(solution)/shard_map/pallas_call | solution.py:136
  28.4 0.3 shard_map.121
  28.7 0.7 collective-permute-start.6
  29.4 0.9 %shard_map.122 = (f32[12,64,128]{2,1,0:T(8,128)S(1)}, f32[12,64,128]{2,1,0:T(8,128)S(1)}) custom-call(f32[4,64,128]{2,1,0:T(8,128)S(1)} %get-tuple-element.75.refs_0_.refs_1_.refs_3_.refs_4_.refs_5_.refs_9_, f32[12,64,128]{2,1,0:T(8,128)S(1)} %get-tuple-element.71.refs_6_.refs_9_.refs_1_.refs_2_.refs_4_.refs_5_.refs_7_, ...), custom_call_target="tpu_custom_call" | custom-call | flops 120000 | bytes 12288 | tf_op jit(solution)/shard_map/pallas_call | solution.py:136
  30.4 0.3 shard_map.123
  30.7 4.3 %collective-permute-start.5 = (f32[4,64,128]{2,1,0:T(8,128)S(1)}, f32[4,64,128]{2,1,0:T(8,128)S(1)}, u32[]{:S(2)}, u32[]{:S(2)}) collective-permute-start(f32[4,64,128]{2,1,0:T(8,128)S(1)} %get-tuple-element.83.refs_0_.refs_1_.refs_6_), channel_id=1, source_target_pairs={{0,1},{1,0},{2,3},{3,2},{4,5},{5,4},{6,7},{7,6},{8,9},{9,8},{10,11... | collective-permute-start | bytes 393224 | tf_op jit(solution)/shard_map/ppermute | solution.py:561
  35.0 0.9 %shard_map.125.refs_13_.refs_1_ = f32[12,64,128]{2,1,0:T(8,128)S(1)} custom-call(f32[32,64,128]{2,1,0:T(8,128)S(1)} %get-tuple-element.78.refs_0_.refs_1_.refs_3_.refs_4_.refs_5_, f32[32,64,128]{2,1,0:T(8,128)S(1)} %get-tuple-element.79.refs_1_.refs_2_, ...), custom_call_target="tpu_custom_call" | custom-call | flops 120000 | bytes 12288 | tf_op jit(solution)/shard_map/pallas_call | solution.py:136
  35.9 0.9 %shard_map.124 = (f32[12,64,128]{2,1,0:T(8,128)S(1)}, f32[12,64,128]{2,1,0:T(8,128)S(1)}) custom-call(f32[4,64,128]{2,1,0:T(8,128)S(1)} %get-tuple-element.83.refs_0_.refs_1_.refs_6_, f32[12,64,128]{2,1,0:T(8,128)S(1)} %get-tuple-element.77.refs_9_.refs_12_.refs_1_.refs_2_.refs_4_, f32[12,64,128]{2,1,0:T(8,128)S(1)} %get-tuple-element.81.refs_13_.refs_2_.refs_3_.refs_5_, ...), custom_call_target="tpu_custom_call" | custom-call | flops 120000 | bytes 12288 | tf_op jit(solution)/shard_map/pallas_call | solution.py:136
  36.9 0.3 shard_map.126
  37.2 0.7 collective-permute-start.7
  37.9 0.9 %shard_map.127 = (f32[12,64,128]{2,1,0:T(8,128)S(1)}, f32[12,64,128]{2,1,0:T(8,128)S(1)}) custom-call(f32[4,64,128]{2,1,0:T(8,128)S(1)} %get-tuple-element.83.refs_0_.refs_1_.refs_6_, f32[12,64,128]{2,1,0:T(8,128)S(1)} %get-tuple-element.77.refs_9_.refs_12_.refs_1_.refs_2_.refs_4_, f32[12,64,128]{2,1,0:T(8,128)S(1)} %get-tuple-element.81.refs_13_.refs_2_.refs_3_.refs_5_, ...), custom_call_target="tpu_custom_call" | custom-call | flops 120000 | bytes 12288 | tf_op jit(solution)/shard_map/pallas_call | solution.py:136
  39.0 0.3 shard_map.129
  39.3 0.3 shard_map.130.refs_0_.refs_1_.refs_3_.refs_4_.refs_5_.refs_19_
  39.6 0.9 %shard_map.131.refs_12_.refs_7_.refs_10_.refs_1_.refs_2_.refs_5_.refs_23_.refs_6_ = f32[12,64,128]{2,1,0:T(8,128)S(1)} custom-call(f32[4,64,128]{2,1,0:T(8,128)S(1)} %shard_map.130.refs_0_.refs_1_.refs_3_.refs_4_.refs_5_.refs_19_, f32[12,64,128]{2,1,0:T(8,128)S(1)} %get-tuple-element.90.refs_14_.refs_9_.refs_1_.refs_2_.refs_4_.refs_5_.refs_6_.refs_25_, ...), custom_call_target="tpu_custom_call" | custom-call | flops 120000 | bytes 12288 | tf_op jit(solution)/shard_map/pallas_call | solution.py:136
  40.6 0.3 shard_map.132
  40.9 0.3 shard_map.133.refs_16_.refs_3_.refs_4_.refs_6_.refs_7_.refs_8_.refs_19_
  41.6 4.4 %collective-permute-start.10 = (f32[4,64,128]{2,1,0:T(8,128)S(1)}, f32[4,64,128]{2,1,0:T(8,128)S(1)}, u32[]{:S(2)}, u32[]{:S(2)}) collective-permute-start(f32[4,64,128]{2,1,0:T(8,128)S(1)} %shard_map.130.refs_0_.refs_1_.refs_3_.refs_4_.refs_5_.refs_19_), channel_id=1, source_target_pairs={{0,1},{1,0},{2,3},{3,2},{4,5},{5,4},{6,7},{7,6},{8,9},{9,8},{10,11... | collective-permute-start | bytes 393224 | tf_op jit(solution)/shard_map/ppermute | solution.py:561
  46.1 0.8 collective-permute-start.9
  46.9 4.1 %collective-permute-start.11 = (f32[8,128]{1,0:T(8,128)S(1)}, f32[8,128]{1,0:T(8,128)S(1)}, u32[]{:S(2)}, u32[]{:S(2)}) collective-permute-start(f32[8,128]{1,0:T(8,128)S(1)} %get-tuple-element.111), channel_id=1, source_target_pairs={{0,1},{1,0},{2,3},{3,2},{4,5},{5,4},{6,7},{7,6},{8,9},{9,8},{10,11... | collective-permute-start | bytes 12296 | tf_op jit(solution)/shard_map/ppermute | solution.py:566
  51.0 0.9 %shard_map.135.refs_11_.refs_2_.refs_3_.refs_6_.refs_24_.refs_7_ = f32[12,64,128]{2,1,0:T(8,128)S(1)} custom-call(f32[4,64,128]{2,1,0:T(8,128)S(1)} %shard_map.130.refs_0_.refs_1_.refs_3_.refs_4_.refs_5_.refs_19_, f32[12,64,128]{2,1,0:T(8,128)S(1)} %get-tuple-element.90.refs_14_.refs_9_.refs_1_.refs_2_.refs_4_.refs_5_.refs_6_.refs_25_, ...), custom_call_target="tpu_custom_call" | custom-call | flops 120000 | bytes 12288 | tf_op jit(solution)/shard_map/pallas_call | solution.py:136
  52.0 0.3 shard_map.136.refs_0_.refs_1_.refs_4_.refs_5_.refs_18_
  52.4 0.9 %shard_map.137.refs_10_.refs_13_.refs_1_.refs_21_.refs_2_ = f32[12,64,128]{2,1,0:T(8,128)S(1)} custom-call(f32[4,64,128]{2,1,0:T(8,128)S(1)} %shard_map.136.refs_0_.refs_1_.refs_4_.refs_5_.refs_18_, f32[12,64,128]{2,1,0:T(8,128)S(1)} %shard_map.131.refs_12_.refs_7_.refs_10_.refs_1_.refs_2_.refs_5_.refs_23_.refs_6_, ...), custom_call_target="tpu_custom_call" | custom-call | flops 120000 | bytes 12288 | tf_op jit(solution)/shard_map/pallas_call | solution.py:136
  53.4 0.3 shard_map.138.refs_1_.refs_3_.refs_4_.refs_7_.refs_8_.refs_18_
  53.7 0.7 collective-permute-start.14
  54.4 1.6 %collective-permute-start.12 = (f32[16,64,128]{2,1,0:T(8,128)S(1)}, f32[16,64,128]{2,1,0:T(8,128)S(1)}, u32[]{:S(2)}, u32[]{:S(2)}) collective-permute-start(f32[16,64,128]{2,1,0:T(8,128)S(1)} %shard_map.139), channel_id=1, source_target_pairs={{0,16},{8,24},{16,0},{24,8},{1,17},{9,25},{17,1},{25,9},{2,18},{10... | collective-permute-start | bytes 1572872 | tf_op jit(solution)/shard_map/ppermute | solution.py:566
  56.0 4.7 %collective-permute-start.15 = (f32[8,128]{1,0:T(8,128)S(1)}, f32[8,128]{1,0:T(8,128)S(1)}, u32[]{:S(2)}, u32[]{:S(2)}) collective-permute-start(f32[8,128]{1,0:T(8,128)S(1)} %add.28), channel_id=1, source_target_pairs={{0,2},{1,3},{2,0},{3,1},{4,6},{5,7},{6,4},{7,5},{8,10},{9,11},{10,... | collective-permute-start | bytes 12296 | tf_op jit(solution)/shard_map/ppermute | solution.py:566
  60.7 0.9 %shard_map.140.refs_14_.refs_2_.refs_22_.refs_3_ = f32[12,64,128]{2,1,0:T(8,128)S(1)} custom-call(f32[4,64,128]{2,1,0:T(8,128)S(1)} %shard_map.136.refs_0_.refs_1_.refs_4_.refs_5_.refs_18_, f32[12,64,128]{2,1,0:T(8,128)S(1)} %shard_map.131.refs_12_.refs_7_.refs_10_.refs_1_.refs_2_.refs_5_.refs_23_.refs_6_, ...), custom_call_target="tpu_custom_call" | custom-call | flops 120000 | bytes 12288 | tf_op jit(solution)/shard_map/pallas_call | solution.py:136
  61.7 0.3 shard_map.141.refs_13_.refs_0_.refs_1_.refs_17_
  62.3 0.3 shard_map.142.refs_3_.refs_4_.refs_17_
  62.6 2.0 %shard_map.143 = (f32[12,64,128]{2,1,0:T(8,128)S(1)}, f32[12,64,128]{2,1,0:T(8,128)S(1)}) custom-call(f32[4,64,128]{2,1,0:T(8,128)S(1)} %shard_map.141.refs_13_.refs_0_.refs_1_.refs_17_, f32[12,64,128]{2,1,0:T(8,128)S(1)} %shard_map.137.refs_10_.refs_13_.refs_1_.refs_21_.refs_2_, f32[12,64,128]{2,1,0:T(8,128)S(1)} %shard_map.140.refs_14_.refs_2_.refs_22_.refs_3_, ...), custom_call_target="tpu_custom_call" | custom-call | flops 240000 | bytes 24576 | tf_op jit(solution)/shard_map/pallas_call | solution.py:136
  64.7 2.8 %collective-permute-start.20 = (f32[4,64,128]{2,1,0:T(8,128)S(1)}, f32[4,64,128]{2,1,0:T(8,128)S(1)}, u32[]{:S(2)}, u32[]{:S(2)}) collective-permute-start(f32[4,64,128]{2,1,0:T(8,128)S(1)} %shard_map.141.refs_13_.refs_0_.refs_1_.refs_17_), channel_id=1, source_target_pairs={{0,1},{1,0},{2,3},{3,2},{4,5},{5,4},{6,7},{7,6},{8,9},{9,8},{10,11... | collective-permute-start | bytes 393224 | tf_op jit(solution)/shard_map/ppermute | solution.py:561
  67.5 0.7 collective-permute-start.18
  68.3 0.6 collective-permute-start.17
  68.9 4.3 %collective-permute-start.19 = (f32[8,128]{1,0:T(8,128)S(1)}, f32[8,128]{1,0:T(8,128)S(1)}, u32[]{:S(2)}, u32[]{:S(2)}) collective-permute-start(f32[8,128]{1,0:T(8,128)S(1)} %add.29.refs_20_), channel_id=1, source_target_pairs={{0,4},{1,5},{2,6},{3,7},{4,0},{5,1},{6,2},{7,3},{8,12},{9,13},{10,... | collective-permute-start | bytes 12296 | tf_op jit(solution)/shard_map/ppermute | solution.py:566
  73.1 0.4 shard_map.145.refs_22_
  73.6 1.9 %collective-permute-done.19.refs_21_ = f32[8,128]{1,0:T(8,128)S(1)} collective-permute-done((f32[8,128]{1,0:T(8,128)S(1)}, f32[8,128]{1,0:T(8,128)S(1)}, u32[]{:S(2)}, u32[]{:S(2)}) %collective-permute-start.19) | collective-permute-done | bytes 4128 | tf_op jit(solution)/shard_map/ppermute | solution.py:566
  75.4 0.4 shard_map.146
  75.9 1.3 %collective-permute-done.21 = f32[264,128]{1,0:T(8,128)S(1)} collective-permute-done((f32[264,128]{1,0:T(8,128)S(1)}, f32[264,128]{1,0:T(8,128)S(1)}, u32[]{:S(2)}, u32[]{:S(2)}) %collective-permute-start.21) | collective-permute-done | bytes 135200 | tf_op jit(solution)/shard_map/ppermute | solution.py:566
  77.3 1.2 %collective-permute-start.22 = (f32[264,128]{1,0:T(8,128)S(1)}, f32[264,128]{1,0:T(8,128)S(1)}, u32[]{:S(2)}, u32[]{:S(2)}) collective-permute-start(f32[264,128]{1,0:T(8,128)S(1)} %add.30.rest_2_), channel_id=1, source_target_pairs={{0,16},{8,24},{16,0},{24,8},{1,17},{9,25},{17,1},{25,9},{2,18},{10... | collective-permute-start | bytes 405512 | tf_op jit(solution)/shard_map/ppermute | solution.py:566
  79.2 0.4 collective-permute-done.17.rest_1_
  79.5 3.4 %collective-permute-done.22.rest_3_ = f32[264,128]{1,0:T(8,128)S(1)} collective-permute-done((f32[264,128]{1,0:T(8,128)S(1)}, f32[264,128]{1,0:T(8,128)S(1)}, u32[]{:S(2)}, u32[]{:S(2)}) %collective-permute-start.22) | collective-permute-done | bytes 135200 | tf_op jit(solution)/shard_map/ppermute | solution.py:566
  83.0 0.8 shard_map.147.own_ref
  83.8 1.9 %collective-permute-done.23.other_ref = f32[16,64,128]{2,1,0:T(8,128)S(1)} collective-permute-done((f32[16,64,128]{2,1,0:T(8,128)S(1)}, f32[16,64,128]{2,1,0:T(8,128)S(1)}, u32[]{:S(2)}, u32[]{:S(2)}) %collective-permute-start.23) | collective-permute-done | bytes 524320 | tf_op jit(solution)/shard_map/ppermute | solution.py:566
  85.7 1.0 %shard_map.148 = f32[32,64,128]{2,1,0:T(8,128)} custom-call(f32[16,64,128]{2,1,0:T(8,128)S(1)} %shard_map.147.own_ref, f32[16,64,128]{2,1,0:T(8,128)S(1)} %collective-permute-done.23.other_ref), custom_call_target="tpu_custom_call" | custom-call | flops 80000 | bytes 8192 | tf_op jit(solution)/shard_map/pallas_call | solution.py:546
  (49 shorter events, 1.8 us)
Async XLA Ops:
  0.0 5.1 %copy-start = (f32[1,32,64,128]{3,2,1,0:T(8,128)S(1)}, f32[1,32,64,128]{3,2,1,0:T(8,128)}, u32[]{:S(2)}) copy-start(f32[1,32,64,128]{3,2,1,0:T(8,128)} %param.12) | copy-start | bytes 3145732
  0.0 5.1 %copy-start.2 = (f32[1,32,64,128]{3,2,1,0:T(8,128)S(1)}, f32[1,32,64,128]{3,2,1,0:T(8,128)}, u32[]{:S(2)}) copy-start(f32[1,32,64,128]{3,2,1,0:T(8,128)} %param.11) | copy-start | bytes 3145732
  1.3 14.2 %collective-permute-start = (f32[8,64,128]{2,1,0:T(8,128)S(1)}, f32[8,64,128]{2,1,0:T(8,128)S(1)}, u32[]{:S(2)}, u32[]{:S(2)}) collective-permute-start(f32[8,64,128]{2,1,0:T(8,128)S(1)} %pad_maximum_fusion), channel_id=1, source_target_pairs={{0,1},{1,0},{2,3},{3,2},{4,5},{5,4},{6,7},{7,6},{8,9},{9,8},{10,11... | collective-permute-start | bytes 786440 | tf_op jit(solution)/shard_map/ppermute | solution.py:561
  4.4 14.9 %collective-permute-start.2 = (f32[8,64,128]{2,1,0:T(8,128)S(1)}, f32[8,64,128]{2,1,0:T(8,128)S(1)}, u32[]{:S(2)}, u32[]{:S(2)}) collective-permute-start(f32[8,64,128]{2,1,0:T(8,128)S(1)} %pad_maximum_fusion.1), channel_id=1, source_target_pairs={{1,2},{2,1},{3,4},{4,3},{5,6},{6,5},{9,10},{10,9},{11,12},{12,11},... | collective-permute-start | bytes 786440 | tf_op jit(solution)/shard_map/ppermute | solution.py:561
  5.1 1.2 %copy-start.3 = (f32[32,64,128]{2,1,0:T(8,128)S(1)}, f32[32,64,128]{2,1,0:T(8,128)}, u32[]{:S(2)}) copy-start(f32[32,64,128]{2,1,0:T(8,128)} %refs_2_.1) | copy-start | bytes 3145732
  7.6 0.7 copy-start.5
  7.6 0.7 copy-start.7
  7.6 0.7 copy-start.8
  15.9 6.4 %collective-permute-start.1 = (f32[4,64,128]{2,1,0:T(8,128)S(1)}, f32[4,64,128]{2,1,0:T(8,128)S(1)}, u32[]{:S(2)}, u32[]{:S(2)}) collective-permute-start(f32[4,64,128]{2,1,0:T(8,128)S(1)} %get-tuple-element.69.refs_0_.refs_1_.refs_3_.refs_4_.refs_5_.refs_9_), channel_id=1, source_target_pairs={{0,1},{1,0},{2,3},{3,2},{4,5},{5,4},{6,7},{7,6},{8,9},{9,8},{10,11... | collective-permute-start | bytes 393224 | tf_op jit(solution)/shard_map/ppermute | solution.py:561
  19.3 1.2 %copy-start.1 = (f32[1,32,64,128]{3,2,1,0:T(8,128)S(1)}, f32[1,32,64,128]{3,2,1,0:T(8,128)}, u32[]{:S(2)}) copy-start(f32[1,32,64,128]{3,2,1,0:T(8,128)} %param.13) | copy-start | bytes 3145732
  19.3 1.5 %copy-start.4 = (f32[1,32,64,128]{3,2,1,0:T(8,128)S(1)}, f32[1,32,64,128]{3,2,1,0:T(8,128)}, u32[]{:S(2)}) copy-start(f32[1,32,64,128]{3,2,1,0:T(8,128)} %param.14) | copy-start | bytes 3145732
  19.7 8.7 %collective-permute-start.4 = (f32[4,64,128]{2,1,0:T(8,128)S(1)}, f32[4,64,128]{2,1,0:T(8,128)S(1)}, u32[]{:S(2)}, u32[]{:S(2)}) collective-permute-start(f32[4,64,128]{2,1,0:T(8,128)S(1)} %get-tuple-element.72.refs_3_.refs_4_.refs_6_.refs_7_.refs_8_.refs_9_), channel_id=1, source_target_pairs={{1,2},{2,1},{3,4},{4,3},{5,6},{6,5},{9,10},{10,9},{11,12},{12,11},... | collective-permute-start | bytes 393224 | tf_op jit(solution)/shard_map/ppermute | solution.py:561
  22.6 7.8 %collective-permute-start.3 = (f32[4,64,128]{2,1,0:T(8,128)S(1)}, f32[4,64,128]{2,1,0:T(8,128)S(1)}, u32[]{:S(2)}, u32[]{:S(2)}) collective-permute-start(f32[4,64,128]{2,1,0:T(8,128)S(1)} %get-tuple-element.75.refs_0_.refs_1_.refs_3_.refs_4_.refs_5_.refs_9_), channel_id=1, source_target_pairs={{0,1},{1,0},{2,3},{3,2},{4,5},{5,4},{6,7},{7,6},{8,9},{9,8},{10,11... | collective-permute-start | bytes 393224 | tf_op jit(solution)/shard_map/ppermute | solution.py:561
  28.7 8.1 %collective-permute-start.6 = (f32[4,64,128]{2,1,0:T(8,128)S(1)}, f32[4,64,128]{2,1,0:T(8,128)S(1)}, u32[]{:S(2)}, u32[]{:S(2)}) collective-permute-start(f32[4,64,128]{2,1,0:T(8,128)S(1)} %get-tuple-element.80.refs_3_.refs_4_.refs_6_.refs_7_.refs_8_.refs_9_), channel_id=1, source_target_pairs={{1,2},{2,1},{3,4},{4,3},{5,6},{6,5},{9,10},{10,9},{11,12},{12,11},... | collective-permute-start | bytes 393224 | tf_op jit(solution)/shard_map/ppermute | solution.py:561
  30.7 8.3 %collective-permute-start.5 = (f32[4,64,128]{2,1,0:T(8,128)S(1)}, f32[4,64,128]{2,1,0:T(8,128)S(1)}, u32[]{:S(2)}, u32[]{:S(2)}) collective-permute-start(f32[4,64,128]{2,1,0:T(8,128)S(1)} %get-tuple-element.83.refs_0_.refs_1_.refs_6_), channel_id=1, source_target_pairs={{0,1},{1,0},{2,3},{3,2},{4,5},{5,4},{6,7},{7,6},{8,9},{9,8},{10,11... | collective-permute-start | bytes 393224 | tf_op jit(solution)/shard_map/ppermute | solution.py:561
  37.2 3.4 %collective-permute-start.7 = (f32[4,64,128]{2,1,0:T(8,128)S(1)}, f32[4,64,128]{2,1,0:T(8,128)S(1)}, u32[]{:S(2)}, u32[]{:S(2)}) collective-permute-start(f32[4,64,128]{2,1,0:T(8,128)S(1)} %get-tuple-element.86.refs_3_.refs_4_.refs_6_), channel_id=1, source_target_pairs={{1,2},{2,1},{3,4},{4,3},{5,6},{6,5},{9,10},{10,9},{11,12},{12,11},... | collective-permute-start | bytes 393224 | tf_op jit(solution)/shard_map/ppermute | solution.py:561
  41.6 12.8 %collective-permute-start.8 = (f32[16,64,128]{2,1,0:T(8,128)S(1)}, f32[16,64,128]{2,1,0:T(8,128)S(1)}, u32[]{:S(2)}, u32[]{:S(2)}) collective-permute-start(f32[16,64,128]{2,1,0:T(8,128)S(1)} %get-tuple-element.109), channel_id=1, source_target_pairs={{0,8},{8,0},{16,24},{24,16},{1,9},{9,1},{17,25},{25,17},{2,10},{10... | collective-permute-start | bytes 1572872 | tf_op jit(solution)/shard_map/ppermute | solution.py:566
  41.6 10.3 %collective-permute-start.10 = (f32[4,64,128]{2,1,0:T(8,128)S(1)}, f32[4,64,128]{2,1,0:T(8,128)S(1)}, u32[]{:S(2)}, u32[]{:S(2)}) collective-permute-start(f32[4,64,128]{2,1,0:T(8,128)S(1)} %shard_map.130.refs_0_.refs_1_.refs_3_.refs_4_.refs_5_.refs_19_), channel_id=1, source_target_pairs={{0,1},{1,0},{2,3},{3,2},{4,5},{5,4},{6,7},{7,6},{8,9},{9,8},{10,11... | collective-permute-start | bytes 393224 | tf_op jit(solution)/shard_map/ppermute | solution.py:561
  46.1 7.3 %collective-permute-start.9 = (f32[4,64,128]{2,1,0:T(8,128)S(1)}, f32[4,64,128]{2,1,0:T(8,128)S(1)}, u32[]{:S(2)}, u32[]{:S(2)}) collective-permute-start(f32[4,64,128]{2,1,0:T(8,128)S(1)} %shard_map.133.refs_16_.refs_3_.refs_4_.refs_6_.refs_7_.refs_8_.refs_19_), channel_id=1, source_target_pairs={{1,2},{2,1},{3,4},{4,3},{5,6},{6,5},{9,10},{10,9},{11,12},{12,11},... | collective-permute-start | bytes 393224 | tf_op jit(solution)/shard_map/ppermute | solution.py:561
  46.9 6.4 %collective-permute-start.11 = (f32[8,128]{1,0:T(8,128)S(1)}, f32[8,128]{1,0:T(8,128)S(1)}, u32[]{:S(2)}, u32[]{:S(2)}) collective-permute-start(f32[8,128]{1,0:T(8,128)S(1)} %get-tuple-element.111), channel_id=1, source_target_pairs={{0,1},{1,0},{2,3},{3,2},{4,5},{5,4},{6,7},{7,6},{8,9},{9,8},{10,11... | collective-permute-start | bytes 12296 | tf_op jit(solution)/shard_map/ppermute | solution.py:566
  52.3 9.4 %collective-permute-start.13 = (f32[4,64,128]{2,1,0:T(8,128)S(1)}, f32[4,64,128]{2,1,0:T(8,128)S(1)}, u32[]{:S(2)}, u32[]{:S(2)}) collective-permute-start(f32[4,64,128]{2,1,0:T(8,128)S(1)} %shard_map.136.refs_0_.refs_1_.refs_4_.refs_5_.refs_18_), channel_id=1, source_target_pairs={{0,1},{1,0},{2,3},{3,2},{4,5},{5,4},{6,7},{7,6},{8,9},{9,8},{10,11... | collective-permute-start | bytes 393224 | tf_op jit(solution)/shard_map/ppermute | solution.py:561
  53.7 8.6 %collective-permute-start.14 = (f32[4,64,128]{2,1,0:T(8,128)S(1)}, f32[4,64,128]{2,1,0:T(8,128)S(1)}, u32[]{:S(2)}, u32[]{:S(2)}) collective-permute-start(f32[4,64,128]{2,1,0:T(8,128)S(1)} %shard_map.138.refs_1_.refs_3_.refs_4_.refs_7_.refs_8_.refs_18_), channel_id=1, source_target_pairs={{1,2},{2,1},{3,4},{4,3},{5,6},{6,5},{9,10},{10,9},{11,12},{12,11},... | collective-permute-start | bytes 393224 | tf_op jit(solution)/shard_map/ppermute | solution.py:561
  54.4 19.1 %collective-permute-start.12 = (f32[16,64,128]{2,1,0:T(8,128)S(1)}, f32[16,64,128]{2,1,0:T(8,128)S(1)}, u32[]{:S(2)}, u32[]{:S(2)}) collective-permute-start(f32[16,64,128]{2,1,0:T(8,128)S(1)} %shard_map.139), channel_id=1, source_target_pairs={{0,16},{8,24},{16,0},{24,8},{1,17},{9,25},{17,1},{25,9},{2,18},{10... | collective-permute-start | bytes 1572872 | tf_op jit(solution)/shard_map/ppermute | solution.py:566
  56.0 6.3 %collective-permute-start.15 = (f32[8,128]{1,0:T(8,128)S(1)}, f32[8,128]{1,0:T(8,128)S(1)}, u32[]{:S(2)}, u32[]{:S(2)}) collective-permute-start(f32[8,128]{1,0:T(8,128)S(1)} %add.28), channel_id=1, source_target_pairs={{0,2},{1,3},{2,0},{3,1},{4,6},{5,7},{6,4},{7,5},{8,10},{9,11},{10,... | collective-permute-start | bytes 12296 | tf_op jit(solution)/shard_map/ppermute | solution.py:566
  64.6 3.6 %collective-permute-start.16 = (f32[12,64,128]{2,1,0:T(8,128)S(1)}, f32[12,64,128]{2,1,0:T(8,128)S(1)}, u32[]{:S(2)}, u32[]{:S(2)}) collective-permute-start(f32[12,64,128]{2,1,0:T(8,128)S(1)} %get-tuple-element.114), channel_id=1, source_target_pairs={{0,8},{8,0},{16,24},{24,16},{1,9},{9,1},{17,25},{25,17},{2,10},{10... | collective-permute-start | bytes 1179656 | tf_op jit(solution)/shard_map/ppermute | solution.py:566
  64.7 8.4 %collective-permute-start.20 = (f32[4,64,128]{2,1,0:T(8,128)S(1)}, f32[4,64,128]{2,1,0:T(8,128)S(1)}, u32[]{:S(2)}, u32[]{:S(2)}) collective-permute-start(f32[4,64,128]{2,1,0:T(8,128)S(1)} %shard_map.141.refs_13_.refs_0_.refs_1_.refs_17_), channel_id=1, source_target_pairs={{0,1},{1,0},{2,3},{3,2},{4,5},{5,4},{6,7},{7,6},{8,9},{9,8},{10,11... | collective-permute-start | bytes 393224 | tf_op jit(solution)/shard_map/ppermute | solution.py:561
  67.5 7.9 %collective-permute-start.18 = (f32[4,64,128]{2,1,0:T(8,128)S(1)}, f32[4,64,128]{2,1,0:T(8,128)S(1)}, u32[]{:S(2)}, u32[]{:S(2)}) collective-permute-start(f32[4,64,128]{2,1,0:T(8,128)S(1)} %shard_map.142.refs_3_.refs_4_.refs_17_), channel_id=1, source_target_pairs={{1,2},{2,1},{3,4},{4,3},{5,6},{6,5},{9,10},{10,9},{11,12},{12,11},... | collective-permute-start | bytes 393224 | tf_op jit(solution)/shard_map/ppermute | solution.py:561
  68.3 11.3 %collective-permute-start.17 = (f32[12,64,128]{2,1,0:T(8,128)S(1)}, f32[12,64,128]{2,1,0:T(8,128)S(1)}, u32[]{:S(2)}, u32[]{:S(2)}) collective-permute-start(f32[12,64,128]{2,1,0:T(8,128)S(1)} %shard_map.144.rest_0_), channel_id=1, source_target_pairs={{0,16},{8,24},{16,0},{24,8},{1,17},{9,25},{17,1},{25,9},{2,18},{10... | collective-permute-start | bytes 1179656 | tf_op jit(solution)/shard_map/ppermute | solution.py:566
  68.9 6.6 %collective-permute-start.19 = (f32[8,128]{1,0:T(8,128)S(1)}, f32[8,128]{1,0:T(8,128)S(1)}, u32[]{:S(2)}, u32[]{:S(2)}) collective-permute-start(f32[8,128]{1,0:T(8,128)S(1)} %add.29.refs_20_), channel_id=1, source_target_pairs={{0,4},{1,5},{2,6},{3,7},{4,0},{5,1},{6,2},{7,3},{8,12},{9,13},{10,... | collective-permute-start | bytes 12296 | tf_op jit(solution)/shard_map/ppermute | solution.py:566
  75.8 1.4 %collective-permute-start.21 = (f32[264,128]{1,0:T(8,128)S(1)}, f32[264,128]{1,0:T(8,128)S(1)}, u32[]{:S(2)}, u32[]{:S(2)}) collective-permute-start(f32[264,128]{1,0:T(8,128)S(1)} %get-tuple-element.116), channel_id=1, source_target_pairs={{0,8},{8,0},{16,24},{24,16},{1,9},{9,1},{17,25},{25,17},{2,10},{10... | collective-permute-start | bytes 405512 | tf_op jit(solution)/shard_map/ppermute | solution.py:566
  77.2 5.7 %copy-start.6 = (f32[64]{0:T(128)S(1)}, f32[64]{0:T(128)}, u32[]{:S(2)}) copy-start(f32[64]{0:T(128)} %table_ref.1) | copy-start | bytes 772
  77.3 5.7 %collective-permute-start.22 = (f32[264,128]{1,0:T(8,128)S(1)}, f32[264,128]{1,0:T(8,128)S(1)}, u32[]{:S(2)}, u32[]{:S(2)}) collective-permute-start(f32[264,128]{1,0:T(8,128)S(1)} %add.30.rest_2_), channel_id=1, source_target_pairs={{0,16},{8,24},{16,0},{24,8},{1,17},{9,25},{17,1},{25,9},{2,18},{10... | collective-permute-start | bytes 405512 | tf_op jit(solution)/shard_map/ppermute | solution.py:566
  83.8 2.0 %collective-permute-start.23 = (f32[16,64,128]{2,1,0:T(8,128)S(1)}, f32[16,64,128]{2,1,0:T(8,128)S(1)}, u32[]{:S(2)}, u32[]{:S(2)}) collective-permute-start(f32[16,64,128]{2,1,0:T(8,128)S(1)} %shard_map.147.own_ref), channel_id=1, source_target_pairs={{0,8},{8,0},{16,24},{24,16},{1,9},{9,1},{17,25},{25,17},{2,10},{10... | collective-permute-start | bytes 1572872 | tf_op jit(solution)/shard_map/ppermute | solution.py:566

commit v6 on v4

--- a/solution.py
+++ b/solution.py
@@ -226,6 +226,48 @@
     outs = [f32(count, width, length)]
     scratch = scratch_of(count, width, length)
     return kernel_call(kernel, [], sum(groups, []), outs, scratch, count)[0]
+
+
+def adjoint_base(place, cur, old, courant):
+    slab, width, length = courant.shape
+    first, count = place
+    groups = [arrays_of(cur), arrays_of(old), [courant]]
+    sizes = [len(g) for g in groups]
+
+    def kernel(*refs):
+        (cur_refs, old_refs, (c_ref,)), refs = grouped(refs, sizes)
+        next_ref, along_ref, pad = refs
+        prepare(first, pad, along_ref, None, list(zip(cur_refs, origins(cur))), slab, width)
+        old_ref, old_at = find(list(zip(old_refs, origins(old))), first)
+
+        def body(i, _):
+            center, lap = stencil(pad, HALO + i, width, along_ref[i])
+            next_ref[i] = 2.0 * center - old_ref[old_at + i] + c_ref[first + i] * lap
+
+        march(count, body)
+
+    outs = [f32(count, width, length)]
+    scratch = scratch_of(count, width, length)
+    return kernel_call(kernel, [], sum(groups, []), outs, scratch, count)[0]
+
+
+def with_points(bases, firsts, fields, number, observed):
+    many = len(bases)
+
+    def kernel(*refs):
+        base_refs, field_refs = refs[:many], refs[many : 2 * many]
+        number_ref, observed_ref = refs[2 * many : 2 * many + 2]
+        for n in range(many):
+
+            def body(i, _, n=n):
+                q = firsts[n] + i
+                miss = number_ref[q] * field_refs[n][i] - observed_ref[q]
+                refs[2 * many + 2 + n][i] = base_refs[n][i] + miss
+
+            march(bases[n].shape[0], body)
+
+    outs = [f32(*base.shape) for base in bases]
+    return kernel_call(kernel, [], [*bases, *fields, number, observed], outs, [], 8)
 
 
 def adjoint_step(place, halo, cur, old, field, found, next_ref, along_ref, pad):
@@ -596,7 +638,7 @@
             places[side], halo, cur, old, courant, [field], number, sums[step], after
         )
 
-    laps, fields = [], []
+    laps, fields, bases = [], [], []
     near = ahead(0, 1, None, cur, old, ())
     far = ahead(0, 2, None, cur, old, ())
     for step in range(STEPS):
@@ -604,8 +646,9 @@
         after = [near[0], far[0]]
         if last:
             rest, more = [(second, 0)], [(first, 0)]
-            near_adj = back(step, 1, None, more, rest, (near[0], starts[1]), ())
-            far_adj = back(step, 2, None, more, rest, (far[0], starts[2]), ())
+            near_adj, far_adj = with_points(
+                bases, starts[1:3], [near[0], far[0]], number, sums[step]
+            )
             after += [near_adj, far_adj]
         one = ahead(step, 0, coming[0], cur, old, after)
         if last:
@@ -613,15 +656,19 @@
             one_adj = back(step, 0, edge, more, rest, (one[0], starts[0]), after)
             newer = [(one_adj, starts[0]), (near_adj, starts[1]), (far_adj, starts[2])]
             near_next = back(step - 1, 1, None, newer, more, (fields[-1][1], starts[1]), ())
-            two = ahead(step, 3, coming[1], cur, old, [one_adj])
+            two = ahead(step, 3, coming[1], cur, old, [near_next])
             edge = (halos[1], HALO, True)
-            two_adj = back(step, 3, edge, more, rest, (two[0], starts[3]), [one_adj])
+            two_adj = back(step, 3, edge, more, rest, (two[0], starts[3]), [near_next])
             newer.append((two_adj, starts[3]))
         else:
             message = exchange(one[0], 0)
             newer = [(one[0], starts[0]), (near[0], starts[1]), (far[0], starts[2])]
             near_next = ahead(step + 1, 1, None, newer, cur, ())
-            two = ahead(step, 3, coming[1], cur, old, [near_next[0]])
+            behind = [near_next[0]]
+            if 0 < step < STEPS - 1:
+                bases.append(adjoint_base(places[step], [(first, 0)], [(second, 0)], courant))
+                behind.append(bases[-1])
+            two = ahead(step, 3, coming[1], cur, old, behind)
             newer.append((two[0], starts[3]))
         laps.append((one[1], near[1], far[1], two[1]))
         fields.append((one[0], near[0], far[0], two[0]))

time: 89.3 us -> 88.4 us (0.990)
  starting transfers between devices: 43.6 us -> 41.5 us
  waiting for transfers between devices: 12 us -> 13 us
    ppermute x14, starting transfers between devices: 30.2 us -> 28.2 us  [exchange(): return lax.ppermute(values, 'depth', links)]
    pallas_call x38 -> x39, Pallas kernels: 25.8 us -> 25.8 us  [kernel_call(): pl.pallas_call(kernel, out_shape=tuple(outs), in_specs=[SMEM] * len(small...]
  transfers between devices with their start and end apart: 23 -> 23, of which waited for: 10 -> 8; matrix products, arithmetic and copies ran while one was open for 0% -> 0% of each run, Pallas kernels for 28% -> 28%
where the time goes in v6:
time: 88.4 us; the launch traced here: 87.6 us
  starting transfers between devices  41.5 us (47%)
  Pallas kernels  27.4 us (31%)
  waiting for transfers between devices  13 us (15%)
  local copies, waits for them, and re-layouts  3.57 us (4%)
  between operations  2.04 us (2%)
    ppermute x14, starting transfers between devices, exchange(): return lax.ppermute(values, 'depth', links)  28.2 us
    pallas_call x39, Pallas kernels, kernel_call(): pl.pallas_call(kernel, out_shape=tuple(outs), in_specs=[SMEM] * len(small...  25.8 us
    ppermute x9, starting transfers between devices, swap(): return lax.ppermute(values, axis, [(i, i ^ bit) for i in range(count)])  13.2 us
    ppermute x9, waiting for transfers between devices, swap(): return lax.ppermute(values, axis, [(i, i ^ bit) for i in range(count)])  8.02 us
    ppermute x14, waiting for transfers between devices, exchange(): return lax.ppermute(values, 'depth', links)  4.97 us
    unnamed x18, local copies, waits for them, and re-layouts  2.29 us
  transfers between devices with their start and end apart: 23, of which 8 were waited for; matrix products, arithmetic and copies ran while one was open for 0% of the time, Pallas kernels for 28%

profile of v6, /device:TPU:0, one launch (start us, length us, event | category | flops | bytes accessed | tf_op | source)
XLA Modules:
  0.0 87.6 jit_solution(10032419575455668780)
XLA Ops:
  0.0 1.3 %dynamic-slice_bitcast_fusion = (f32[4,64,128]{2,1,0:T(8,128)S(1)}, f32[4,64,128]{2,1,0:T(8,128)S(1)}, f32[4,64,128]{2,1,0:T(8,128)S(1)}, f32[4,64,128]{2,1,0:T(8,128)S(1)}) fusion(f32[1,32,64,128]{3,2,1,0:T(8,128)} %param.13, s32[]{:T(128)S(6)} %select_n.17, s32[]{:T(128)S(6)} %select_n.16, f32[1,32,64,128]{3,2,1,0:T(8,128)} %param.12), kind=kLoop, calls=%fused_computation.2 | loop fusion | bytes 1048584 | tf_op jit(solution)/shard_map/dynamic_slice | solution.py:486
  1.3 3.0 %collective-permute-start = (f32[8,64,128]{2,1,0:T(8,128)S(1)}, f32[8,64,128]{2,1,0:T(8,128)S(1)}, u32[]{:S(2)}, u32[]{:S(2)}) collective-permute-start(f32[8,64,128]{2,1,0:T(8,128)S(1)} %pad_maximum_fusion), channel_id=1, source_target_pairs={{0,1},{1,0},{2,3},{3,2},{4,5},{5,4},{6,7},{7,6},{8,9},{9,8},{10,11... | collective-permute-start | bytes 786440 | tf_op jit(solution)/shard_map/ppermute | solution.py:566
  4.4 0.7 collective-permute-start.2
  5.1 1.2 %copy-done.3 = f32[32,64,128]{2,1,0:T(8,128)S(1)} copy-done((f32[32,64,128]{2,1,0:T(8,128)S(1)}, f32[32,64,128]{2,1,0:T(8,128)}, u32[]{:S(2)}) %copy-start.3) | copy-done | bytes 1048600
  6.3 0.6 shard_map.109
  7.6 0.6 copy-done.5
  8.3 3.0 %shard_map.110 = (f32[32,64,128]{2,1,0:T(8,128)S(1)}, f32[32,64,128]{2,1,0:T(8,128)S(1)}, f32[8,128]{1,0:T(8,128)S(1)}, f32[8,128]{1,0:T(8,128)S(1)}, f32[8,128]...) custom-call(f32[1,4]{1,0:T(1,128)S(1)} %copy-done.7, ...), custom_call_target="tpu_custom_call" | custom-call | flops 80000 | bytes 8192 | tf_op jit(solution)/shard_map/pallas_call | solution.py:139
  11.3 0.9 %shard_map.112 = (f32[12,64,128]{2,1,0:T(8,128)S(1)}, f32[12,64,128]{2,1,0:T(8,128)S(1)}) custom-call(f32[32,64,128]{2,1,0:T(8,128)S(1)} %get-tuple-element.63.refs_0_.refs_1_.refs_3_.refs_4_.refs_5_, f32[32,64,128]{2,1,0:T(8,128)S(1)} %get-tuple-element.64.refs_1_.refs_2_, ...), custom_call_target="tpu_custom_call" | custom-call | flops 120000 | bytes 12288 | tf_op jit(solution)/shard_map/pallas_call | solution.py:139
  12.2 0.9 %shard_map.111 = (f32[12,64,128]{2,1,0:T(8,128)S(1)}, f32[12,64,128]{2,1,0:T(8,128)S(1)}) custom-call(f32[32,64,128]{2,1,0:T(8,128)S(1)} %get-tuple-element.63.refs_0_.refs_1_.refs_3_.refs_4_.refs_5_, f32[32,64,128]{2,1,0:T(8,128)S(1)} %get-tuple-element.64.refs_1_.refs_2_, ...), custom_call_target="tpu_custom_call" | custom-call | flops 120000 | bytes 12288 | tf_op jit(solution)/shard_map/pallas_call | solution.py:139
  13.1 2.4 %collective-permute-done.refs_0_ = f32[8,64,128]{2,1,0:T(8,128)S(1)} collective-permute-done((f32[8,64,128]{2,1,0:T(8,128)S(1)}, f32[8,64,128]{2,1,0:T(8,128)S(1)}, u32[]{:S(2)}, u32[]{:S(2)}) %collective-permute-start) | collective-permute-done | bytes 262176 | tf_op jit(solution)/shard_map/ppermute | solution.py:566
  15.8 2.5 %collective-permute-start.1 = (f32[4,64,128]{2,1,0:T(8,128)S(1)}, f32[4,64,128]{2,1,0:T(8,128)S(1)}, u32[]{:S(2)}, u32[]{:S(2)}) collective-permute-start(f32[4,64,128]{2,1,0:T(8,128)S(1)} %get-tuple-element.70.refs_0_.refs_1_.refs_3_.refs_4_.refs_5_.refs_9_), channel_id=1, source_target_pairs={{0,1},{1,0},{2,3},{3,2},{4,5},{5,4},{6,7},{7,6},{8,9},{9,8},{10,11... | collective-permute-start | bytes 393224 | tf_op jit(solution)/shard_map/ppermute | solution.py:566
  18.4 0.9 %shard_map.114 = (f32[12,64,128]{2,1,0:T(8,128)S(1)}, f32[12,64,128]{2,1,0:T(8,128)S(1)}) custom-call(f32[4,64,128]{2,1,0:T(8,128)S(1)} %get-tuple-element.70.refs_0_.refs_1_.refs_3_.refs_4_.refs_5_.refs_9_, f32[12,64,128]{2,1,0:T(8,128)S(1)} %get-tuple-element.67.refs_6_.refs_1_.refs_2_.refs_4_.refs_5_.refs_8_, ...), custom_call_target="tpu_custom_call" | custom-call | flops 120000 | bytes 12288 | tf_op jit(solution)/shard_map/pallas_call | solution.py:139
  19.3 0.3 shard_map.115
  19.7 0.8 collective-permute-start.4
  20.6 0.3 copy-done.4
  20.9 0.4 shard_map.119
  21.3 0.9 %shard_map.116 = (f32[12,64,128]{2,1,0:T(8,128)S(1)}, f32[12,64,128]{2,1,0:T(8,128)S(1)}) custom-call(f32[4,64,128]{2,1,0:T(8,128)S(1)} %get-tuple-element.70.refs_0_.refs_1_.refs_3_.refs_4_.refs_5_.refs_9_, f32[12,64,128]{2,1,0:T(8,128)S(1)} %get-tuple-element.67.refs_6_.refs_1_.refs_2_.refs_4_.refs_5_.refs_8_, ...), custom_call_target="tpu_custom_call" | custom-call | flops 120000 | bytes 12288 | tf_op jit(solution)/shard_map/pallas_call | solution.py:139
  22.6 4.0 %collective-permute-start.3 = (f32[4,64,128]{2,1,0:T(8,128)S(1)}, f32[4,64,128]{2,1,0:T(8,128)S(1)}, u32[]{:S(2)}, u32[]{:S(2)}) collective-permute-start(f32[4,64,128]{2,1,0:T(8,128)S(1)} %get-tuple-element.76.refs_0_.refs_1_.refs_3_.refs_4_.refs_5_.refs_9_), channel_id=1, source_target_pairs={{0,1},{1,0},{2,3},{3,2},{4,5},{5,4},{6,7},{7,6},{8,9},{9,8},{10,11... | collective-permute-start | bytes 393224 | tf_op jit(solution)/shard_map/ppermute | solution.py:566
  26.6 0.9 %shard_map.120.refs_10_.refs_0_ = f32[12,64,128]{2,1,0:T(8,128)S(1)} custom-call(f32[32,64,128]{2,1,0:T(8,128)S(1)} %get-tuple-element.79.refs_0_.refs_1_.refs_3_.refs_4_.refs_5_, f32[32,64,128]{2,1,0:T(8,128)S(1)} %get-tuple-element.80.refs_1_.refs_2_, ...), custom_call_target="tpu_custom_call" | custom-call | flops 120000 | bytes 12288 | tf_op jit(solution)/shard_map/pallas_call | solution.py:139
  27.5 0.9 %shard_map.118 = (f32[12,64,128]{2,1,0:T(8,128)S(1)}, f32[12,64,128]{2,1,0:T(8,128)S(1)}) custom-call(f32[4,64,128]{2,1,0:T(8,128)S(1)} %get-tuple-element.76.refs_0_.refs_1_.refs_3_.refs_4_.refs_5_.refs_9_, f32[12,64,128]{2,1,0:T(8,128)S(1)} %get-tuple-element.72.refs_6_.refs_9_.refs_1_.refs_2_.refs_4_.refs_5_.refs_7_, ...), custom_call_target="tpu_custom_call" | custom-call | flops 120000 | bytes 12288 | tf_op jit(solution)/shard_map/pallas_call | solution.py:139
  28.7 0.7 collective-permute-start.6
  29.4 0.9 %shard_map.122 = (f32[12,64,128]{2,1,0:T(8,128)S(1)}, f32[12,64,128]{2,1,0:T(8,128)S(1)}) custom-call(f32[4,64,128]{2,1,0:T(8,128)S(1)} %get-tuple-element.76.refs_0_.refs_1_.refs_3_.refs_4_.refs_5_.refs_9_, f32[12,64,128]{2,1,0:T(8,128)S(1)} %get-tuple-element.72.refs_6_.refs_9_.refs_1_.refs_2_.refs_4_.refs_5_.refs_7_, ...), custom_call_target="tpu_custom_call" | custom-call | flops 120000 | bytes 12288 | tf_op jit(solution)/shard_map/pallas_call | solution.py:139
  30.3 0.3 shard_map.123
  30.7 4.3 %collective-permute-start.5 = (f32[4,64,128]{2,1,0:T(8,128)S(1)}, f32[4,64,128]{2,1,0:T(8,128)S(1)}, u32[]{:S(2)}, u32[]{:S(2)}) collective-permute-start(f32[4,64,128]{2,1,0:T(8,128)S(1)} %get-tuple-element.84.refs_0_.refs_1_.refs_6_), channel_id=1, source_target_pairs={{0,1},{1,0},{2,3},{3,2},{4,5},{5,4},{6,7},{7,6},{8,9},{9,8},{10,11... | collective-permute-start | bytes 393224 | tf_op jit(solution)/shard_map/ppermute | solution.py:566
  35.0 0.9 %shard_map.125.refs_13_.refs_1_ = f32[12,64,128]{2,1,0:T(8,128)S(1)} custom-call(f32[32,64,128]{2,1,0:T(8,128)S(1)} %get-tuple-element.79.refs_0_.refs_1_.refs_3_.refs_4_.refs_5_, f32[32,64,128]{2,1,0:T(8,128)S(1)} %get-tuple-element.80.refs_1_.refs_2_, ...), custom_call_target="tpu_custom_call" | custom-call | flops 120000 | bytes 12288 | tf_op jit(solution)/shard_map/pallas_call | solution.py:139
  35.9 0.9 %shard_map.124 = (f32[12,64,128]{2,1,0:T(8,128)S(1)}, f32[12,64,128]{2,1,0:T(8,128)S(1)}) custom-call(f32[4,64,128]{2,1,0:T(8,128)S(1)} %get-tuple-element.84.refs_0_.refs_1_.refs_6_, f32[12,64,128]{2,1,0:T(8,128)S(1)} %get-tuple-element.78.refs_9_.refs_12_.refs_1_.refs_2_.refs_4_, f32[12,64,128]{2,1,0:T(8,128)S(1)} %get-tuple-element.82.refs_13_.refs_2_.refs_3_.refs_5_, ...), custom_call_target="tpu_custom_call" | custom-call | flops 120000 | bytes 12288 | tf_op jit(solution)/shard_map/pallas_call | solution.py:139
  37.2 0.7 collective-permute-start.7
  37.9 0.9 %shard_map.127 = (f32[12,64,128]{2,1,0:T(8,128)S(1)}, f32[12,64,128]{2,1,0:T(8,128)S(1)}) custom-call(f32[4,64,128]{2,1,0:T(8,128)S(1)} %get-tuple-element.84.refs_0_.refs_1_.refs_6_, f32[12,64,128]{2,1,0:T(8,128)S(1)} %get-tuple-element.78.refs_9_.refs_12_.refs_1_.refs_2_.refs_4_, f32[12,64,128]{2,1,0:T(8,128)S(1)} %get-tuple-element.82.refs_13_.refs_2_.refs_3_.refs_5_, ...), custom_call_target="tpu_custom_call" | custom-call | flops 120000 | bytes 12288 | tf_op jit(solution)/shard_map/pallas_call | solution.py:139
  39.0 0.3 shard_map.129
  39.3 0.3 shard_map.130.refs_0_.refs_16_.refs_1_.refs_3_.refs_4_.refs_5_.refs_19_
  39.7 0.9 %shard_map.131.refs_12_.refs_7_.refs_10_.refs_1_.refs_2_.refs_5_.refs_23_.refs_6_ = f32[12,64,128]{2,1,0:T(8,128)S(1)} custom-call(f32[4,64,128]{2,1,0:T(8,128)S(1)} %shard_map.130.refs_0_.refs_16_.refs_1_.refs_3_.refs_4_.refs_5_.refs_19_, f32[12,64,128]{2,1,0:T(8,128)S(1)} %get-tuple-element.91.refs_14_.refs_9_.refs_1_.refs_2_.refs_4_.refs_5_.refs_6_.refs_25_, ...), custom_call_target="tpu_custom_call" | custom-call | flops 120000 | bytes 12288 | tf_op jit(solution)/shard_map/pallas_call | solution.py:139
  40.6 0.3 shard_map.132
  41.0 0.3 shard_map.133.refs_17_.refs_3_.refs_4_.refs_6_.refs_7_.refs_8_.refs_19_
  41.3 0.5 shard_map.134
  41.9 4.4 %collective-permute-start.10 = (f32[264,128]{1,0:T(8,128)S(1)}, f32[264,128]{1,0:T(8,128)S(1)}, u32[]{:S(2)}, u32[]{:S(2)}) collective-permute-start(f32[264,128]{1,0:T(8,128)S(1)} %get-tuple-element.111), channel_id=1, source_target_pairs={{0,1},{1,0},{2,3},{3,2},{4,5},{5,4},{6,7},{7,6},{8,9},{9,8},{10,11... | collective-permute-start | bytes 405512 | tf_op jit(solution)/shard_map/ppermute | solution.py:566
  46.3 0.9 %shard_map.135.refs_11_.refs_2_.refs_3_.refs_6_.refs_24_.refs_7_ = f32[12,64,128]{2,1,0:T(8,128)S(1)} custom-call(f32[4,64,128]{2,1,0:T(8,128)S(1)} %shard_map.130.refs_0_.refs_16_.refs_1_.refs_3_.refs_4_.refs_5_.refs_19_, f32[12,64,128]{2,1,0:T(8,128)S(1)} %get-tuple-element.91.refs_14_.refs_9_.refs_1_.refs_2_.refs_4_.refs_5_.refs_6_.refs_25_, ...), custom_call_target="tpu_custom_call" | custom-call | flops 120000 | bytes 12288 | tf_op jit(solution)/shard_map/pallas_call | solution.py:139
  47.2 0.7 collective-permute-start.9
  47.9 2.6 %collective-permute-done.10.refs_0_ = f32[264,128]{1,0:T(8,128)S(1)} collective-permute-done((f32[264,128]{1,0:T(8,128)S(1)}, f32[264,128]{1,0:T(8,128)S(1)}, u32[]{:S(2)}, u32[]{:S(2)}) %collective-permute-start.10) | collective-permute-done | bytes 135200 | tf_op jit(solution)/shard_map/ppermute | solution.py:566
  50.5 0.3 shard_map.136.refs_0_.refs_1_.refs_4_.refs_5_.refs_18_
  50.8 1.8 %collective-permute-start.12 = (f32[4,64,128]{2,1,0:T(8,128)S(1)}, f32[4,64,128]{2,1,0:T(8,128)S(1)}, u32[]{:S(2)}, u32[]{:S(2)}) collective-permute-start(f32[4,64,128]{2,1,0:T(8,128)S(1)} %shard_map.136.refs_0_.refs_1_.refs_4_.refs_5_.refs_18_), channel_id=1, source_target_pairs={{0,1},{1,0},{2,3},{3,2},{4,5},{5,4},{6,7},{7,6},{8,9},{9,8},{10,11... | collective-permute-start | bytes 393224 | tf_op jit(solution)/shard_map/ppermute | solution.py:566
  52.6 1.0 %shard_map.137.refs_10_.refs_13_.refs_1_.refs_21_.refs_2_ = f32[12,64,128]{2,1,0:T(8,128)S(1)} custom-call(f32[4,64,128]{2,1,0:T(8,128)S(1)} %shard_map.136.refs_0_.refs_1_.refs_4_.refs_5_.refs_18_, f32[12,64,128]{2,1,0:T(8,128)S(1)} %shard_map.131.refs_12_.refs_7_.refs_10_.refs_1_.refs_2_.refs_5_.refs_23_.refs_6_, ...), custom_call_target="tpu_custom_call" | custom-call | flops 120000 | bytes 12288 | tf_op jit(solution)/shard_map/pallas_call | solution.py:139
  53.6 0.3 shard_map.138.refs_1_.refs_3_.refs_4_.refs_7_.refs_8_.refs_18_
  53.9 0.7 collective-permute-start.13
  54.7 1.5 %collective-permute-start.11 = (f32[16,64,128]{2,1,0:T(8,128)S(1)}, f32[16,64,128]{2,1,0:T(8,128)S(1)}, u32[]{:S(2)}, u32[]{:S(2)}) collective-permute-start(f32[16,64,128]{2,1,0:T(8,128)S(1)} %shard_map.139), channel_id=1, source_target_pairs={{0,16},{8,24},{16,0},{24,8},{1,17},{9,25},{17,1},{25,9},{2,18},{10... | collective-permute-start | bytes 1572872 | tf_op jit(solution)/shard_map/ppermute | solution.py:571
  56.3 5.1 %collective-permute-start.14 = (f32[8,128]{1,0:T(8,128)S(1)}, f32[8,128]{1,0:T(8,128)S(1)}, u32[]{:S(2)}, u32[]{:S(2)}) collective-permute-start(f32[8,128]{1,0:T(8,128)S(1)} %get-tuple-element.123), channel_id=1, source_target_pairs={{0,2},{1,3},{2,0},{3,1},{4,6},{5,7},{6,4},{7,5},{8,10},{9,11},{10,... | collective-permute-start | bytes 12296 | tf_op jit(solution)/shard_map/ppermute | solution.py:571
  61.4 0.9 %shard_map.140.refs_14_.refs_2_.refs_22_.refs_3_ = f32[12,64,128]{2,1,0:T(8,128)S(1)} custom-call(f32[4,64,128]{2,1,0:T(8,128)S(1)} %shard_map.136.refs_0_.refs_1_.refs_4_.refs_5_.refs_18_, f32[12,64,128]{2,1,0:T(8,128)S(1)} %shard_map.131.refs_12_.refs_7_.refs_10_.refs_1_.refs_2_.refs_5_.refs_23_.refs_6_, ...), custom_call_target="tpu_custom_call" | custom-call | flops 120000 | bytes 12288 | tf_op jit(solution)/shard_map/pallas_call | solution.py:139
  62.3 0.3 shard_map.141.refs_13_.refs_0_.refs_1_.refs_17_
  63.0 0.3 shard_map.142.refs_3_.refs_4_.refs_17_
  63.3 2.0 %shard_map.143 = (f32[12,64,128]{2,1,0:T(8,128)S(1)}, f32[12,64,128]{2,1,0:T(8,128)S(1)}) custom-call(f32[4,64,128]{2,1,0:T(8,128)S(1)} %shard_map.141.refs_13_.refs_0_.refs_1_.refs_17_, f32[12,64,128]{2,1,0:T(8,128)S(1)} %shard_map.137.refs_10_.refs_13_.refs_1_.refs_21_.refs_2_, f32[12,64,128]{2,1,0:T(8,128)S(1)} %shard_map.140.refs_14_.refs_2_.refs_22_.refs_3_, ...), custom_call_target="tpu_custom_call" | custom-call | flops 240000 | bytes 24576 | tf_op jit(solution)/shard_map/pallas_call | solution.py:139
  65.4 3.3 %collective-permute-start.19 = (f32[4,64,128]{2,1,0:T(8,128)S(1)}, f32[4,64,128]{2,1,0:T(8,128)S(1)}, u32[]{:S(2)}, u32[]{:S(2)}) collective-permute-start(f32[4,64,128]{2,1,0:T(8,128)S(1)} %shard_map.141.refs_13_.refs_0_.refs_1_.refs_17_), channel_id=1, source_target_pairs={{0,1},{1,0},{2,3},{3,2},{4,5},{5,4},{6,7},{7,6},{8,9},{9,8},{10,11... | collective-permute-start | bytes 393224 | tf_op jit(solution)/shard_map/ppermute | solution.py:566
  68.6 0.7 collective-permute-start.17
  69.3 0.6 collective-permute-start.16
  70.0 4.2 %collective-permute-start.18 = (f32[8,128]{1,0:T(8,128)S(1)}, f32[8,128]{1,0:T(8,128)S(1)}, u32[]{:S(2)}, u32[]{:S(2)}) collective-permute-start(f32[8,128]{1,0:T(8,128)S(1)} %add.29.refs_20_), channel_id=1, source_target_pairs={{0,4},{1,5},{2,6},{3,7},{4,0},{5,1},{6,2},{7,3},{8,12},{9,13},{10,... | collective-permute-start | bytes 12296 | tf_op jit(solution)/shard_map/ppermute | solution.py:571
  74.2 0.4 shard_map.145.refs_22_
  74.6 1.7 %collective-permute-done.18.refs_21_ = f32[8,128]{1,0:T(8,128)S(1)} collective-permute-done((f32[8,128]{1,0:T(8,128)S(1)}, f32[8,128]{1,0:T(8,128)S(1)}, u32[]{:S(2)}, u32[]{:S(2)}) %collective-permute-start.18) | collective-permute-done | bytes 4128 | tf_op jit(solution)/shard_map/ppermute | solution.py:571
  76.3 0.4 shard_map.146
  76.8 1.3 %collective-permute-done.20 = f32[264,128]{1,0:T(8,128)S(1)} collective-permute-done((f32[264,128]{1,0:T(8,128)S(1)}, f32[264,128]{1,0:T(8,128)S(1)}, u32[]{:S(2)}, u32[]{:S(2)}) %collective-permute-start.20) | collective-permute-done | bytes 135200 | tf_op jit(solution)/shard_map/ppermute | solution.py:571
  78.1 1.4 %collective-permute-start.21 = (f32[264,128]{1,0:T(8,128)S(1)}, f32[264,128]{1,0:T(8,128)S(1)}, u32[]{:S(2)}, u32[]{:S(2)}) collective-permute-start(f32[264,128]{1,0:T(8,128)S(1)} %add.30.rest_2_), channel_id=1, source_target_pairs={{0,16},{8,24},{16,0},{24,8},{1,17},{9,25},{17,1},{25,9},{2,18},{10... | collective-permute-start | bytes 405512 | tf_op jit(solution)/shard_map/ppermute | solution.py:571
  80.2 0.4 collective-permute-done.16.rest_1_
  80.6 3.3 %collective-permute-done.21.rest_3_ = f32[264,128]{1,0:T(8,128)S(1)} collective-permute-done((f32[264,128]{1,0:T(8,128)S(1)}, f32[264,128]{1,0:T(8,128)S(1)}, u32[]{:S(2)}, u32[]{:S(2)}) %collective-permute-start.21) | collective-permute-done | bytes 135200 | tf_op jit(solution)/shard_map/ppermute | solution.py:571
  83.9 0.8 shard_map.147.values_ref
  84.7 0.8 shard_map.148.refs_0_
  85.6 1.1 %collective-permute-done.22.values_ref = f32[16,64,128]{2,1,0:T(8,128)S(1)} collective-permute-done((f32[16,64,128]{2,1,0:T(8,128)S(1)}, f32[16,64,128]{2,1,0:T(8,128)S(1)}, u32[]{:S(2)}, u32[]{:S(2)}) %collective-permute-start.22) | collective-permute-done | bytes 524320 | tf_op jit(solution)/shard_map/ppermute | solution.py:571
  86.6 0.8 shard_map.149
  (48 shorter events, 2.4 us)
Async XLA Ops:
  0.0 5.1 %copy-start = (f32[1,32,64,128]{3,2,1,0:T(8,128)S(1)}, f32[1,32,64,128]{3,2,1,0:T(8,128)}, u32[]{:S(2)}) copy-start(f32[1,32,64,128]{3,2,1,0:T(8,128)} %param.12) | copy-start | bytes 3145732
  0.0 5.1 %copy-start.2 = (f32[1,32,64,128]{3,2,1,0:T(8,128)S(1)}, f32[1,32,64,128]{3,2,1,0:T(8,128)}, u32[]{:S(2)}) copy-start(f32[1,32,64,128]{3,2,1,0:T(8,128)} %param.11) | copy-start | bytes 3145732
  1.3 14.2 %collective-permute-start = (f32[8,64,128]{2,1,0:T(8,128)S(1)}, f32[8,64,128]{2,1,0:T(8,128)S(1)}, u32[]{:S(2)}, u32[]{:S(2)}) collective-permute-start(f32[8,64,128]{2,1,0:T(8,128)S(1)} %pad_maximum_fusion), channel_id=1, source_target_pairs={{0,1},{1,0},{2,3},{3,2},{4,5},{5,4},{6,7},{7,6},{8,9},{9,8},{10,11... | collective-permute-start | bytes 786440 | tf_op jit(solution)/shard_map/ppermute | solution.py:566
  4.4 14.9 %collective-permute-start.2 = (f32[8,64,128]{2,1,0:T(8,128)S(1)}, f32[8,64,128]{2,1,0:T(8,128)S(1)}, u32[]{:S(2)}, u32[]{:S(2)}) collective-permute-start(f32[8,64,128]{2,1,0:T(8,128)S(1)} %pad_maximum_fusion.1), channel_id=1, source_target_pairs={{1,2},{2,1},{3,4},{4,3},{5,6},{6,5},{9,10},{10,9},{11,12},{12,11},... | collective-permute-start | bytes 786440 | tf_op jit(solution)/shard_map/ppermute | solution.py:566
  5.1 1.2 %copy-start.3 = (f32[32,64,128]{2,1,0:T(8,128)S(1)}, f32[32,64,128]{2,1,0:T(8,128)}, u32[]{:S(2)}) copy-start(f32[32,64,128]{2,1,0:T(8,128)} %refs_2_.1) | copy-start | bytes 3145732
  7.6 0.7 copy-start.5
  7.6 0.7 copy-start.7
  7.6 0.7 copy-start.8
  15.8 6.4 %collective-permute-start.1 = (f32[4,64,128]{2,1,0:T(8,128)S(1)}, f32[4,64,128]{2,1,0:T(8,128)S(1)}, u32[]{:S(2)}, u32[]{:S(2)}) collective-permute-start(f32[4,64,128]{2,1,0:T(8,128)S(1)} %get-tuple-element.70.refs_0_.refs_1_.refs_3_.refs_4_.refs_5_.refs_9_), channel_id=1, source_target_pairs={{0,1},{1,0},{2,3},{3,2},{4,5},{5,4},{6,7},{7,6},{8,9},{9,8},{10,11... | collective-permute-start | bytes 393224 | tf_op jit(solution)/shard_map/ppermute | solution.py:566
  19.3 1.2 %copy-start.1 = (f32[1,32,64,128]{3,2,1,0:T(8,128)S(1)}, f32[1,32,64,128]{3,2,1,0:T(8,128)}, u32[]{:S(2)}) copy-start(f32[1,32,64,128]{3,2,1,0:T(8,128)} %param.13) | copy-start | bytes 3145732
  19.3 1.5 %copy-start.4 = (f32[1,32,64,128]{3,2,1,0:T(8,128)S(1)}, f32[1,32,64,128]{3,2,1,0:T(8,128)}, u32[]{:S(2)}) copy-start(f32[1,32,64,128]{3,2,1,0:T(8,128)} %param.14) | copy-start | bytes 3145732
  19.7 8.7 %collective-permute-start.4 = (f32[4,64,128]{2,1,0:T(8,128)S(1)}, f32[4,64,128]{2,1,0:T(8,128)S(1)}, u32[]{:S(2)}, u32[]{:S(2)}) collective-permute-start(f32[4,64,128]{2,1,0:T(8,128)S(1)} %get-tuple-element.73.refs_3_.refs_4_.refs_6_.refs_7_.refs_8_.refs_9_), channel_id=1, source_target_pairs={{1,2},{2,1},{3,4},{4,3},{5,6},{6,5},{9,10},{10,9},{11,12},{12,11},... | collective-permute-start | bytes 393224 | tf_op jit(solution)/shard_map/ppermute | solution.py:566
  22.6 7.8 %collective-permute-start.3 = (f32[4,64,128]{2,1,0:T(8,128)S(1)}, f32[4,64,128]{2,1,0:T(8,128)S(1)}, u32[]{:S(2)}, u32[]{:S(2)}) collective-permute-start(f32[4,64,128]{2,1,0:T(8,128)S(1)} %get-tuple-element.76.refs_0_.refs_1_.refs_3_.refs_4_.refs_5_.refs_9_), channel_id=1, source_target_pairs={{0,1},{1,0},{2,3},{3,2},{4,5},{5,4},{6,7},{7,6},{8,9},{9,8},{10,11... | collective-permute-start | bytes 393224 | tf_op jit(solution)/shard_map/ppermute | solution.py:566
  28.7 8.2 %collective-permute-start.6 = (f32[4,64,128]{2,1,0:T(8,128)S(1)}, f32[4,64,128]{2,1,0:T(8,128)S(1)}, u32[]{:S(2)}, u32[]{:S(2)}) collective-permute-start(f32[4,64,128]{2,1,0:T(8,128)S(1)} %get-tuple-element.81.refs_3_.refs_4_.refs_6_.refs_7_.refs_8_.refs_9_), channel_id=1, source_target_pairs={{1,2},{2,1},{3,4},{4,3},{5,6},{6,5},{9,10},{10,9},{11,12},{12,11},... | collective-permute-start | bytes 393224 | tf_op jit(solution)/shard_map/ppermute | solution.py:566
  30.7 8.3 %collective-permute-start.5 = (f32[4,64,128]{2,1,0:T(8,128)S(1)}, f32[4,64,128]{2,1,0:T(8,128)S(1)}, u32[]{:S(2)}, u32[]{:S(2)}) collective-permute-start(f32[4,64,128]{2,1,0:T(8,128)S(1)} %get-tuple-element.84.refs_0_.refs_1_.refs_6_), channel_id=1, source_target_pairs={{0,1},{1,0},{2,3},{3,2},{4,5},{5,4},{6,7},{7,6},{8,9},{9,8},{10,11... | collective-permute-start | bytes 393224 | tf_op jit(solution)/shard_map/ppermute | solution.py:566
  37.2 3.4 %collective-permute-start.7 = (f32[4,64,128]{2,1,0:T(8,128)S(1)}, f32[4,64,128]{2,1,0:T(8,128)S(1)}, u32[]{:S(2)}, u32[]{:S(2)}) collective-permute-start(f32[4,64,128]{2,1,0:T(8,128)S(1)} %get-tuple-element.87.refs_3_.refs_4_.refs_6_), channel_id=1, source_target_pairs={{1,2},{2,1},{3,4},{4,3},{5,6},{6,5},{9,10},{10,9},{11,12},{12,11},... | collective-permute-start | bytes 393224 | tf_op jit(solution)/shard_map/ppermute | solution.py:566
  41.8 12.8 %collective-permute-start.8 = (f32[16,64,128]{2,1,0:T(8,128)S(1)}, f32[16,64,128]{2,1,0:T(8,128)S(1)}, u32[]{:S(2)}, u32[]{:S(2)}) collective-permute-start(f32[16,64,128]{2,1,0:T(8,128)S(1)} %get-tuple-element.110), channel_id=1, source_target_pairs={{0,8},{8,0},{16,24},{24,16},{1,9},{9,1},{17,25},{25,17},{2,10},{10... | collective-permute-start | bytes 1572872 | tf_op jit(solution)/shard_map/ppermute | solution.py:571
  41.9 8.6 %collective-permute-start.10 = (f32[264,128]{1,0:T(8,128)S(1)}, f32[264,128]{1,0:T(8,128)S(1)}, u32[]{:S(2)}, u32[]{:S(2)}) collective-permute-start(f32[264,128]{1,0:T(8,128)S(1)} %get-tuple-element.111), channel_id=1, source_target_pairs={{0,1},{1,0},{2,3},{3,2},{4,5},{5,4},{6,7},{7,6},{8,9},{9,8},{10,11... | collective-permute-start | bytes 405512 | tf_op jit(solution)/shard_map/ppermute | solution.py:566
  47.2 6.4 %collective-permute-start.9 = (f32[4,64,128]{2,1,0:T(8,128)S(1)}, f32[4,64,128]{2,1,0:T(8,128)S(1)}, u32[]{:S(2)}, u32[]{:S(2)}) collective-permute-start(f32[4,64,128]{2,1,0:T(8,128)S(1)} %shard_map.133.refs_17_.refs_3_.refs_4_.refs_6_.refs_7_.refs_8_.refs_19_), channel_id=1, source_target_pairs={{1,2},{2,1},{3,4},{4,3},{5,6},{6,5},{9,10},{10,9},{11,12},{12,11},... | collective-permute-start | bytes 393224 | tf_op jit(solution)/shard_map/ppermute | solution.py:566
  50.8 11.5 %collective-permute-start.12 = (f32[4,64,128]{2,1,0:T(8,128)S(1)}, f32[4,64,128]{2,1,0:T(8,128)S(1)}, u32[]{:S(2)}, u32[]{:S(2)}) collective-permute-start(f32[4,64,128]{2,1,0:T(8,128)S(1)} %shard_map.136.refs_0_.refs_1_.refs_4_.refs_5_.refs_18_), channel_id=1, source_target_pairs={{0,1},{1,0},{2,3},{3,2},{4,5},{5,4},{6,7},{7,6},{8,9},{9,8},{10,11... | collective-permute-start | bytes 393224 | tf_op jit(solution)/shard_map/ppermute | solution.py:566
  53.9 9.0 %collective-permute-start.13 = (f32[4,64,128]{2,1,0:T(8,128)S(1)}, f32[4,64,128]{2,1,0:T(8,128)S(1)}, u32[]{:S(2)}, u32[]{:S(2)}) collective-permute-start(f32[4,64,128]{2,1,0:T(8,128)S(1)} %shard_map.138.refs_1_.refs_3_.refs_4_.refs_7_.refs_8_.refs_18_), channel_id=1, source_target_pairs={{1,2},{2,1},{3,4},{4,3},{5,6},{6,5},{9,10},{10,9},{11,12},{12,11},... | collective-permute-start | bytes 393224 | tf_op jit(solution)/shard_map/ppermute | solution.py:566
  54.7 19.9 %collective-permute-start.11 = (f32[16,64,128]{2,1,0:T(8,128)S(1)}, f32[16,64,128]{2,1,0:T(8,128)S(1)}, u32[]{:S(2)}, u32[]{:S(2)}) collective-permute-start(f32[16,64,128]{2,1,0:T(8,128)S(1)} %shard_map.139), channel_id=1, source_target_pairs={{0,16},{8,24},{16,0},{24,8},{1,17},{9,25},{17,1},{25,9},{2,18},{10... | collective-permute-start | bytes 1572872 | tf_op jit(solution)/shard_map/ppermute | solution.py:571
  56.3 6.7 %collective-permute-start.14 = (f32[8,128]{1,0:T(8,128)S(1)}, f32[8,128]{1,0:T(8,128)S(1)}, u32[]{:S(2)}, u32[]{:S(2)}) collective-permute-start(f32[8,128]{1,0:T(8,128)S(1)} %get-tuple-element.123), channel_id=1, source_target_pairs={{0,2},{1,3},{2,0},{3,1},{4,6},{5,7},{6,4},{7,5},{8,10},{9,11},{10,... | collective-permute-start | bytes 12296 | tf_op jit(solution)/shard_map/ppermute | solution.py:571
  65.3 4.0 %collective-permute-start.15 = (f32[12,64,128]{2,1,0:T(8,128)S(1)}, f32[12,64,128]{2,1,0:T(8,128)S(1)}, u32[]{:S(2)}, u32[]{:S(2)}) collective-permute-start(f32[12,64,128]{2,1,0:T(8,128)S(1)} %get-tuple-element.116), channel_id=1, source_target_pairs={{0,8},{8,0},{16,24},{24,16},{1,9},{9,1},{17,25},{25,17},{2,10},{10... | collective-permute-start | bytes 1179656 | tf_op jit(solution)/shard_map/ppermute | solution.py:571
  65.4 8.8 %collective-permute-start.19 = (f32[4,64,128]{2,1,0:T(8,128)S(1)}, f32[4,64,128]{2,1,0:T(8,128)S(1)}, u32[]{:S(2)}, u32[]{:S(2)}) collective-permute-start(f32[4,64,128]{2,1,0:T(8,128)S(1)} %shard_map.141.refs_13_.refs_0_.refs_1_.refs_17_), channel_id=1, source_target_pairs={{0,1},{1,0},{2,3},{3,2},{4,5},{5,4},{6,7},{7,6},{8,9},{9,8},{10,11... | collective-permute-start | bytes 393224 | tf_op jit(solution)/shard_map/ppermute | solution.py:566
  68.6 7.7 %collective-permute-start.17 = (f32[4,64,128]{2,1,0:T(8,128)S(1)}, f32[4,64,128]{2,1,0:T(8,128)S(1)}, u32[]{:S(2)}, u32[]{:S(2)}) collective-permute-start(f32[4,64,128]{2,1,0:T(8,128)S(1)} %shard_map.142.refs_3_.refs_4_.refs_17_), channel_id=1, source_target_pairs={{1,2},{2,1},{3,4},{4,3},{5,6},{6,5},{9,10},{10,9},{11,12},{12,11},... | collective-permute-start | bytes 393224 | tf_op jit(solution)/shard_map/ppermute | solution.py:566
  69.3 11.3 %collective-permute-start.16 = (f32[12,64,128]{2,1,0:T(8,128)S(1)}, f32[12,64,128]{2,1,0:T(8,128)S(1)}, u32[]{:S(2)}, u32[]{:S(2)}) collective-permute-start(f32[12,64,128]{2,1,0:T(8,128)S(1)} %shard_map.144.rest_0_), channel_id=1, source_target_pairs={{0,16},{8,24},{16,0},{24,8},{1,17},{9,25},{17,1},{25,9},{2,18},{10... | collective-permute-start | bytes 1179656 | tf_op jit(solution)/shard_map/ppermute | solution.py:571
  70.0 6.4 %collective-permute-start.18 = (f32[8,128]{1,0:T(8,128)S(1)}, f32[8,128]{1,0:T(8,128)S(1)}, u32[]{:S(2)}, u32[]{:S(2)}) collective-permute-start(f32[8,128]{1,0:T(8,128)S(1)} %add.29.refs_20_), channel_id=1, source_target_pairs={{0,4},{1,5},{2,6},{3,7},{4,0},{5,1},{6,2},{7,3},{8,12},{9,13},{10,... | collective-permute-start | bytes 12296 | tf_op jit(solution)/shard_map/ppermute | solution.py:571
  76.7 1.4 %collective-permute-start.20 = (f32[264,128]{1,0:T(8,128)S(1)}, f32[264,128]{1,0:T(8,128)S(1)}, u32[]{:S(2)}, u32[]{:S(2)}) collective-permute-start(f32[264,128]{1,0:T(8,128)S(1)} %get-tuple-element.118), channel_id=1, source_target_pairs={{0,8},{8,0},{16,24},{24,16},{1,9},{9,1},{17,25},{25,17},{2,10},{10... | collective-permute-start | bytes 405512 | tf_op jit(solution)/shard_map/ppermute | solution.py:571
  78.1 5.7 %copy-start.6 = (f32[64]{0:T(128)S(1)}, f32[64]{0:T(128)}, u32[]{:S(2)}) copy-start(f32[64]{0:T(128)} %table_ref.1) | copy-start | bytes 772
  78.1 5.7 %collective-permute-start.21 = (f32[264,128]{1,0:T(8,128)S(1)}, f32[264,128]{1,0:T(8,128)S(1)}, u32[]{:S(2)}, u32[]{:S(2)}) collective-permute-start(f32[264,128]{1,0:T(8,128)S(1)} %add.30.rest_2_), channel_id=1, source_target_pairs={{0,16},{8,24},{16,0},{24,8},{1,17},{9,25},{17,1},{25,9},{2,18},{10... | collective-permute-start | bytes 405512 | tf_op jit(solution)/shard_map/ppermute | solution.py:571
  84.7 2.0 %collective-permute-start.22 = (f32[16,64,128]{2,1,0:T(8,128)S(1)}, f32[16,64,128]{2,1,0:T(8,128)S(1)}, u32[]{:S(2)}, u32[]{:S(2)}) collective-permute-start(f32[16,64,128]{2,1,0:T(8,128)S(1)} %shard_map.147.values_ref), channel_id=1, source_target_pairs={{0,8},{8,0},{16,24},{24,16},{1,9},{9,1},{17,25},{25,17},{2,10},{10... | collective-permute-start | bytes 1572872 | tf_op jit(solution)/shard_map/ppermute | solution.py:571

commit v7 on v6

--- a/solution.py
+++ b/solution.py
@@ -83,9 +83,6 @@
 
             source = ref_at + jnp.where(odd == 1, i, HALO - 1 - i)
             interleave(put, lambda spot, source=source: ref[source, spot, :], width)
-        elif len(ref.shape) == 2:
-            rows = slice((HALO - 1 - i) * width, (HALO - i) * width)
-            pad[at + i, PAD : PAD + width, :] = ref[rows, :]
         else:
             pad[at + i, PAD : PAD + width, :] = ref[HALO - 1 - i]
 
@@ -362,17 +359,14 @@
     return kernel_call(kernel, [], sum(groups, []), outs, scratch, count)
 
 
-def curvature(laps, message, after):
+def curvature(laps, after):
     number = len(laps)
     half, width, length = laps[0][1].shape
     size = half + HALO
 
     def kernel(*refs):
         ranged = [refs[n * number : (n + 1) * number] for n in range(4)]
-        planes_ref = refs[4 * number]
-        keep_ref, *send_refs, tile_ref, message_ref = refs[4 * number + 2 :]
-        for i in range(HALO):
-            message_ref[i * width : (i + 1) * width, :] = planes_ref[i]
+        keep_ref, *send_refs, tile_ref = refs[4 * number + 1 :]
         core = lax.axis_index("shot") % 2
 
         def squares(lap_refs, at):
@@ -397,11 +391,10 @@
                     write_piece(send_refs, i, value)
                     total = total + fold(value)
                 tile_ref[...] = total
-                message_ref[HALO * width : HALO * width + 8, :] = total
 
     outs = [f32(size, width, length)]
-    outs += [f32(size // 1, width, length)] * 1 + [f32(8, length), f32(HALO * width + 8, length)]
-    arrays = [lap[n] for n in range(4) for lap in laps] + [message, after]
+    outs += [f32(size // 1, width, length)] * 1 + [f32(8, length)]
+    arrays = [lap[n] for n in range(4) for lap in laps] + [after]
     return kernel_call(kernel, [], arrays, outs, [], 8)
 
 
@@ -654,6 +647,7 @@
         if last:
             edge = (halos[0], HALO, True)
             one_adj = back(step, 0, edge, more, rest, (one[0], starts[0]), after)
+            message = exchange(one_adj, 0)
             newer = [(one_adj, starts[0]), (near_adj, starts[1]), (far_adj, starts[2])]
             near_next = back(step - 1, 1, None, newer, more, (fields[-1][1], starts[1]), ())
             two = ahead(step, 3, coming[1], cur, old, [near_next])
@@ -676,10 +670,9 @@
             coming = [(message, 0, False), (exchange(two[0], 1), 0, False)]
             far = ahead(step + 1, 2, None, newer, cur, ())
             near, old, cur = near_next, cur, newer
-    keep, *send, tile, message = curvature(laps, one_adj, two_adj)
-    message = exchange(message, 0)
     coming = [(message, 0, False), (exchange(two_adj, 1), 0, False)]
-    tiles = message[HALO * width :, :]
+    keep, *send, tile = curvature(laps, two_adj)
+    tiles = swap(tile, "depth", 1)
     bit = 2
     old, cur, near = more, newer, near_next
     adjoints = [arrays_of(cur)]
@@ -701,8 +694,8 @@
         adjoints.insert(0, arrays_of(cur))
         if step == STEPS - 2:
             curv = sum(total_parts(keep, send, [two]))
+        tile = tile + tiles
         if bit < lax.axis_size("depth"):
-            tile = tile + tiles
             tiles = swap(tile, "depth", bit)
             bit *= 2
     while bit < lax.axis_size("depth"):

time: 88.4 us -> 87.5 us (0.990)
  waiting for transfers between devices: 13 us -> 10.7 us
  starting transfers between devices: 41.5 us -> 43 us
    ppermute x9 -> x10, starting transfers between devices: 13.2 us -> 16.7 us  [swap(): return lax.ppermute(values, axis, [(i, i ^ bit) for i in range(count)])]
    ppermute x14, waiting for transfers between devices: 4.97 us -> 2.36 us  [exchange(): return lax.ppermute(values, 'depth', links)]
    ppermute x14, starting transfers between devices: 28.2 us -> 26.2 us  [exchange(): return lax.ppermute(values, 'depth', links)]
    ppermute x9 -> x10, waiting for transfers between devices: 8.02 us -> 8.39 us  [swap(): return lax.ppermute(values, axis, [(i, i ^ bit) for i in range(count)])]
  transfers between devices with their start and end apart: 23 -> 24, of which waited for: 8 -> 7; matrix products, arithmetic and copies ran while one was open for 0% -> 0% of each run, Pallas kernels for 28% -> 28%
where the time goes in v7:
time: 87.5 us; the launch traced here: 86.7 us
  starting transfers between devices  43 us (49%)
  Pallas kernels  27.2 us (31%)
  waiting for transfers between devices  10.7 us (12%)
  local copies, waits for them, and re-layouts  3.58 us (4%)
  between operations  2.06 us (2%)
    ppermute x14, starting transfers between devices, exchange(): return lax.ppermute(values, 'depth', links)  26.2 us
    pallas_call x39, Pallas kernels, kernel_call(): pl.pallas_call(kernel, out_shape=tuple(outs), in_specs=[SMEM] * len(small...  25.6 us
    ppermute x10, starting transfers between devices, swap(): return lax.ppermute(values, axis, [(i, i ^ bit) for i in range(count)])  16.7 us
    ppermute x10, waiting for transfers between devices, swap(): return lax.ppermute(values, axis, [(i, i ^ bit) for i in range(count)])  8.39 us
    ppermute x14, waiting for transfers between devices, exchange(): return lax.ppermute(values, 'depth', links)  2.36 us
    unnamed x18, local copies, waits for them, and re-layouts  2.29 us
  transfers between devices with their start and end apart: 24, of which 7 were waited for; matrix products, arithmetic and copies ran while one was open for 0% of the time, Pallas kernels for 28%

profile of v7, /device:TPU:0, one launch (start us, length us, event | category | flops | bytes accessed | tf_op | source)
XLA Modules:
  0.0 86.7 jit_solution(5772104663785215354)
XLA Ops:
  0.0 1.3 %dynamic-slice_bitcast_fusion = (f32[4,64,128]{2,1,0:T(8,128)S(1)}, f32[4,64,128]{2,1,0:T(8,128)S(1)}, f32[4,64,128]{2,1,0:T(8,128)S(1)}, f32[4,64,128]{2,1,0:T(8,128)S(1)}) fusion(f32[1,32,64,128]{3,2,1,0:T(8,128)} %param.13, s32[]{:T(128)S(6)} %select_n.17, s32[]{:T(128)S(6)} %select_n.16, f32[1,32,64,128]{3,2,1,0:T(8,128)} %param.12), kind=kLoop, calls=%fused_computation.2 | loop fusion | bytes 1048584 | tf_op jit(solution)/shard_map/dynamic_slice | solution.py:479
  1.3 3.0 %collective-permute-start = (f32[8,64,128]{2,1,0:T(8,128)S(1)}, f32[8,64,128]{2,1,0:T(8,128)S(1)}, u32[]{:S(2)}, u32[]{:S(2)}) collective-permute-start(f32[8,64,128]{2,1,0:T(8,128)S(1)} %pad_maximum_fusion), channel_id=1, source_target_pairs={{0,1},{1,0},{2,3},{3,2},{4,5},{5,4},{6,7},{7,6},{8,9},{9,8},{10,11... | collective-permute-start | bytes 786440 | tf_op jit(solution)/shard_map/ppermute | solution.py:559
  4.4 0.7 collective-permute-start.2
  5.1 1.2 %copy-done.3 = f32[32,64,128]{2,1,0:T(8,128)S(1)} copy-done((f32[32,64,128]{2,1,0:T(8,128)S(1)}, f32[32,64,128]{2,1,0:T(8,128)}, u32[]{:S(2)}) %copy-start.3) | copy-done | bytes 1048600
  6.3 0.6 shard_map.109
  7.6 0.6 copy-done.5
  8.3 3.1 %shard_map.110 = (f32[32,64,128]{2,1,0:T(8,128)S(1)}, f32[32,64,128]{2,1,0:T(8,128)S(1)}, f32[8,128]{1,0:T(8,128)S(1)}, f32[8,128]{1,0:T(8,128)S(1)}, f32[8,128]...) custom-call(f32[1,4]{1,0:T(1,128)S(1)} %copy-done.7, ...), custom_call_target="tpu_custom_call" | custom-call | flops 80000 | bytes 8192 | tf_op jit(solution)/shard_map/pallas_call | solution.py:136
  11.4 0.9 %shard_map.112 = (f32[12,64,128]{2,1,0:T(8,128)S(1)}, f32[12,64,128]{2,1,0:T(8,128)S(1)}) custom-call(f32[32,64,128]{2,1,0:T(8,128)S(1)} %get-tuple-element.62.refs_0_.refs_1_.refs_3_.refs_4_.refs_5_, f32[32,64,128]{2,1,0:T(8,128)S(1)} %get-tuple-element.63.refs_1_.refs_2_, ...), custom_call_target="tpu_custom_call" | custom-call | flops 120000 | bytes 12288 | tf_op jit(solution)/shard_map/pallas_call | solution.py:136
  12.3 0.9 %shard_map.111 = (f32[12,64,128]{2,1,0:T(8,128)S(1)}, f32[12,64,128]{2,1,0:T(8,128)S(1)}) custom-call(f32[32,64,128]{2,1,0:T(8,128)S(1)} %get-tuple-element.62.refs_0_.refs_1_.refs_3_.refs_4_.refs_5_, f32[32,64,128]{2,1,0:T(8,128)S(1)} %get-tuple-element.63.refs_1_.refs_2_, ...), custom_call_target="tpu_custom_call" | custom-call | flops 120000 | bytes 12288 | tf_op jit(solution)/shard_map/pallas_call | solution.py:136
  13.2 2.3 %collective-permute-done.refs_0_ = f32[8,64,128]{2,1,0:T(8,128)S(1)} collective-permute-done((f32[8,64,128]{2,1,0:T(8,128)S(1)}, f32[8,64,128]{2,1,0:T(8,128)S(1)}, u32[]{:S(2)}, u32[]{:S(2)}) %collective-permute-start) | collective-permute-done | bytes 262176 | tf_op jit(solution)/shard_map/ppermute | solution.py:559
  15.9 2.5 %collective-permute-start.1 = (f32[4,64,128]{2,1,0:T(8,128)S(1)}, f32[4,64,128]{2,1,0:T(8,128)S(1)}, u32[]{:S(2)}, u32[]{:S(2)}) collective-permute-start(f32[4,64,128]{2,1,0:T(8,128)S(1)} %get-tuple-element.69.refs_0_.refs_1_.refs_3_.refs_4_.refs_5_.refs_9_), channel_id=1, source_target_pairs={{0,1},{1,0},{2,3},{3,2},{4,5},{5,4},{6,7},{7,6},{8,9},{9,8},{10,11... | collective-permute-start | bytes 393224 | tf_op jit(solution)/shard_map/ppermute | solution.py:559
  18.4 0.9 %shard_map.114 = (f32[12,64,128]{2,1,0:T(8,128)S(1)}, f32[12,64,128]{2,1,0:T(8,128)S(1)}) custom-call(f32[4,64,128]{2,1,0:T(8,128)S(1)} %get-tuple-element.69.refs_0_.refs_1_.refs_3_.refs_4_.refs_5_.refs_9_, f32[12,64,128]{2,1,0:T(8,128)S(1)} %get-tuple-element.66.refs_6_.refs_1_.refs_2_.refs_4_.refs_5_.refs_8_, ...), custom_call_target="tpu_custom_call" | custom-call | flops 120000 | bytes 12288 | tf_op jit(solution)/shard_map/pallas_call | solution.py:136
  19.4 0.3 shard_map.115
  19.7 0.8 collective-permute-start.4
  20.6 0.3 copy-done.4
  20.9 0.4 shard_map.119
  21.3 0.9 %shard_map.116 = (f32[12,64,128]{2,1,0:T(8,128)S(1)}, f32[12,64,128]{2,1,0:T(8,128)S(1)}) custom-call(f32[4,64,128]{2,1,0:T(8,128)S(1)} %get-tuple-element.69.refs_0_.refs_1_.refs_3_.refs_4_.refs_5_.refs_9_, f32[12,64,128]{2,1,0:T(8,128)S(1)} %get-tuple-element.66.refs_6_.refs_1_.refs_2_.refs_4_.refs_5_.refs_8_, ...), custom_call_target="tpu_custom_call" | custom-call | flops 120000 | bytes 12288 | tf_op jit(solution)/shard_map/pallas_call | solution.py:136
  22.6 4.0 %collective-permute-start.3 = (f32[4,64,128]{2,1,0:T(8,128)S(1)}, f32[4,64,128]{2,1,0:T(8,128)S(1)}, u32[]{:S(2)}, u32[]{:S(2)}) collective-permute-start(f32[4,64,128]{2,1,0:T(8,128)S(1)} %get-tuple-element.75.refs_0_.refs_1_.refs_3_.refs_4_.refs_5_.refs_9_), channel_id=1, source_target_pairs={{0,1},{1,0},{2,3},{3,2},{4,5},{5,4},{6,7},{7,6},{8,9},{9,8},{10,11... | collective-permute-start | bytes 393224 | tf_op jit(solution)/shard_map/ppermute | solution.py:559
  26.6 0.9 %shard_map.120.refs_10_.refs_0_ = f32[12,64,128]{2,1,0:T(8,128)S(1)} custom-call(f32[32,64,128]{2,1,0:T(8,128)S(1)} %get-tuple-element.78.refs_0_.refs_1_.refs_3_.refs_4_.refs_5_, f32[32,64,128]{2,1,0:T(8,128)S(1)} %get-tuple-element.79.refs_1_.refs_2_, ...), custom_call_target="tpu_custom_call" | custom-call | flops 120000 | bytes 12288 | tf_op jit(solution)/shard_map/pallas_call | solution.py:136
  27.5 0.9 %shard_map.118 = (f32[12,64,128]{2,1,0:T(8,128)S(1)}, f32[12,64,128]{2,1,0:T(8,128)S(1)}) custom-call(f32[4,64,128]{2,1,0:T(8,128)S(1)} %get-tuple-element.75.refs_0_.refs_1_.refs_3_.refs_4_.refs_5_.refs_9_, f32[12,64,128]{2,1,0:T(8,128)S(1)} %get-tuple-element.71.refs_6_.refs_9_.refs_1_.refs_2_.refs_4_.refs_5_.refs_7_, ...), custom_call_target="tpu_custom_call" | custom-call | flops 120000 | bytes 12288 | tf_op jit(solution)/shard_map/pallas_call | solution.py:136
  28.4 0.3 shard_map.121
  28.7 0.7 collective-permute-start.6
  29.4 0.9 %shard_map.122 = (f32[12,64,128]{2,1,0:T(8,128)S(1)}, f32[12,64,128]{2,1,0:T(8,128)S(1)}) custom-call(f32[4,64,128]{2,1,0:T(8,128)S(1)} %get-tuple-element.75.refs_0_.refs_1_.refs_3_.refs_4_.refs_5_.refs_9_, f32[12,64,128]{2,1,0:T(8,128)S(1)} %get-tuple-element.71.refs_6_.refs_9_.refs_1_.refs_2_.refs_4_.refs_5_.refs_7_, ...), custom_call_target="tpu_custom_call" | custom-call | flops 120000 | bytes 12288 | tf_op jit(solution)/shard_map/pallas_call | solution.py:136
  30.4 0.3 shard_map.123
  30.7 4.3 %collective-permute-start.5 = (f32[4,64,128]{2,1,0:T(8,128)S(1)}, f32[4,64,128]{2,1,0:T(8,128)S(1)}, u32[]{:S(2)}, u32[]{:S(2)}) collective-permute-start(f32[4,64,128]{2,1,0:T(8,128)S(1)} %get-tuple-element.83.refs_0_.refs_1_.refs_6_), channel_id=1, source_target_pairs={{0,1},{1,0},{2,3},{3,2},{4,5},{5,4},{6,7},{7,6},{8,9},{9,8},{10,11... | collective-permute-start | bytes 393224 | tf_op jit(solution)/shard_map/ppermute | solution.py:559
  35.0 0.9 %shard_map.125.refs_13_.refs_1_ = f32[12,64,128]{2,1,0:T(8,128)S(1)} custom-call(f32[32,64,128]{2,1,0:T(8,128)S(1)} %get-tuple-element.78.refs_0_.refs_1_.refs_3_.refs_4_.refs_5_, f32[32,64,128]{2,1,0:T(8,128)S(1)} %get-tuple-element.79.refs_1_.refs_2_, ...), custom_call_target="tpu_custom_call" | custom-call | flops 120000 | bytes 12288 | tf_op jit(solution)/shard_map/pallas_call | solution.py:136
  35.9 0.9 %shard_map.124 = (f32[12,64,128]{2,1,0:T(8,128)S(1)}, f32[12,64,128]{2,1,0:T(8,128)S(1)}) custom-call(f32[4,64,128]{2,1,0:T(8,128)S(1)} %get-tuple-element.83.refs_0_.refs_1_.refs_6_, f32[12,64,128]{2,1,0:T(8,128)S(1)} %get-tuple-element.77.refs_9_.refs_12_.refs_1_.refs_2_.refs_4_, f32[12,64,128]{2,1,0:T(8,128)S(1)} %get-tuple-element.81.refs_13_.refs_2_.refs_3_.refs_5_, ...), custom_call_target="tpu_custom_call" | custom-call | flops 120000 | bytes 12288 | tf_op jit(solution)/shard_map/pallas_call | solution.py:136
  36.9 0.3 shard_map.126
  37.2 0.7 collective-permute-start.7
  37.9 0.9 %shard_map.127 = (f32[12,64,128]{2,1,0:T(8,128)S(1)}, f32[12,64,128]{2,1,0:T(8,128)S(1)}) custom-call(f32[4,64,128]{2,1,0:T(8,128)S(1)} %get-tuple-element.83.refs_0_.refs_1_.refs_6_, f32[12,64,128]{2,1,0:T(8,128)S(1)} %get-tuple-element.77.refs_9_.refs_12_.refs_1_.refs_2_.refs_4_, f32[12,64,128]{2,1,0:T(8,128)S(1)} %get-tuple-element.81.refs_13_.refs_2_.refs_3_.refs_5_, ...), custom_call_target="tpu_custom_call" | custom-call | flops 120000 | bytes 12288 | tf_op jit(solution)/shard_map/pallas_call | solution.py:136
  39.0 0.3 shard_map.129
  39.3 0.3 shard_map.130.refs_0_.refs_1_.refs_3_.refs_4_.refs_5_.refs_19_
  39.6 0.9 %shard_map.131.refs_12_.refs_7_.refs_10_.refs_1_.refs_2_.refs_5_.refs_23_.refs_6_ = f32[12,64,128]{2,1,0:T(8,128)S(1)} custom-call(f32[4,64,128]{2,1,0:T(8,128)S(1)} %shard_map.130.refs_0_.refs_1_.refs_3_.refs_4_.refs_5_.refs_19_, f32[12,64,128]{2,1,0:T(8,128)S(1)} %get-tuple-element.90.refs_14_.refs_9_.refs_1_.refs_2_.refs_4_.refs_5_.refs_6_.refs_25_, ...), custom_call_target="tpu_custom_call" | custom-call | flops 120000 | bytes 12288 | tf_op jit(solution)/shard_map/pallas_call | solution.py:136
  40.6 0.3 shard_map.132
  40.9 0.3 shard_map.133.refs_16_.refs_3_.refs_4_.refs_6_.refs_7_.refs_8_.refs_19_
  41.6 4.4 %collective-permute-start.10 = (f32[4,64,128]{2,1,0:T(8,128)S(1)}, f32[4,64,128]{2,1,0:T(8,128)S(1)}, u32[]{:S(2)}, u32[]{:S(2)}) collective-permute-start(f32[4,64,128]{2,1,0:T(8,128)S(1)} %shard_map.130.refs_0_.refs_1_.refs_3_.refs_4_.refs_5_.refs_19_), channel_id=1, source_target_pairs={{0,1},{1,0},{2,3},{3,2},{4,5},{5,4},{6,7},{7,6},{8,9},{9,8},{10,11... | collective-permute-start | bytes 393224 | tf_op jit(solution)/shard_map/ppermute | solution.py:559
  46.1 0.8 collective-permute-start.9
  46.9 4.1 %collective-permute-start.11 = (f32[8,128]{1,0:T(8,128)S(1)}, f32[8,128]{1,0:T(8,128)S(1)}, u32[]{:S(2)}, u32[]{:S(2)}) collective-permute-start(f32[8,128]{1,0:T(8,128)S(1)} %get-tuple-element.111), channel_id=1, source_target_pairs={{0,1},{1,0},{2,3},{3,2},{4,5},{5,4},{6,7},{7,6},{8,9},{9,8},{10,11... | collective-permute-start | bytes 12296 | tf_op jit(solution)/shard_map/ppermute | solution.py:564
  51.0 0.9 %shard_map.135.refs_11_.refs_2_.refs_3_.refs_6_.refs_24_.refs_7_ = f32[12,64,128]{2,1,0:T(8,128)S(1)} custom-call(f32[4,64,128]{2,1,0:T(8,128)S(1)} %shard_map.130.refs_0_.refs_1_.refs_3_.refs_4_.refs_5_.refs_19_, f32[12,64,128]{2,1,0:T(8,128)S(1)} %get-tuple-element.90.refs_14_.refs_9_.refs_1_.refs_2_.refs_4_.refs_5_.refs_6_.refs_25_, ...), custom_call_target="tpu_custom_call" | custom-call | flops 120000 | bytes 12288 | tf_op jit(solution)/shard_map/pallas_call | solution.py:136
  52.0 0.3 shard_map.136.refs_0_.refs_1_.refs_4_.refs_5_.refs_18_
  52.4 0.9 %shard_map.137.refs_10_.refs_13_.refs_1_.refs_21_.refs_2_ = f32[12,64,128]{2,1,0:T(8,128)S(1)} custom-call(f32[4,64,128]{2,1,0:T(8,128)S(1)} %shard_map.136.refs_0_.refs_1_.refs_4_.refs_5_.refs_18_, f32[12,64,128]{2,1,0:T(8,128)S(1)} %shard_map.131.refs_12_.refs_7_.refs_10_.refs_1_.refs_2_.refs_5_.refs_23_.refs_6_, ...), custom_call_target="tpu_custom_call" | custom-call | flops 120000 | bytes 12288 | tf_op jit(solution)/shard_map/pallas_call | solution.py:136
  53.4 0.3 shard_map.138.refs_1_.refs_3_.refs_4_.refs_7_.refs_8_.refs_18_
  53.7 0.7 collective-permute-start.14
  54.4 1.6 %collective-permute-start.12 = (f32[16,64,128]{2,1,0:T(8,128)S(1)}, f32[16,64,128]{2,1,0:T(8,128)S(1)}, u32[]{:S(2)}, u32[]{:S(2)}) collective-permute-start(f32[16,64,128]{2,1,0:T(8,128)S(1)} %shard_map.139), channel_id=1, source_target_pairs={{0,16},{8,24},{16,0},{24,8},{1,17},{9,25},{17,1},{25,9},{2,18},{10... | collective-permute-start | bytes 1572872 | tf_op jit(solution)/shard_map/ppermute | solution.py:564
  56.0 4.7 %collective-permute-start.15 = (f32[8,128]{1,0:T(8,128)S(1)}, f32[8,128]{1,0:T(8,128)S(1)}, u32[]{:S(2)}, u32[]{:S(2)}) collective-permute-start(f32[8,128]{1,0:T(8,128)S(1)} %add.28), channel_id=1, source_target_pairs={{0,2},{1,3},{2,0},{3,1},{4,6},{5,7},{6,4},{7,5},{8,10},{9,11},{10,... | collective-permute-start | bytes 12296 | tf_op jit(solution)/shard_map/ppermute | solution.py:564
  60.7 0.9 %shard_map.140.refs_14_.refs_2_.refs_22_.refs_3_ = f32[12,64,128]{2,1,0:T(8,128)S(1)} custom-call(f32[4,64,128]{2,1,0:T(8,128)S(1)} %shard_map.136.refs_0_.refs_1_.refs_4_.refs_5_.refs_18_, f32[12,64,128]{2,1,0:T(8,128)S(1)} %shard_map.131.refs_12_.refs_7_.refs_10_.refs_1_.refs_2_.refs_5_.refs_23_.refs_6_, ...), custom_call_target="tpu_custom_call" | custom-call | flops 120000 | bytes 12288 | tf_op jit(solution)/shard_map/pallas_call | solution.py:136
  61.7 0.3 shard_map.141.refs_13_.refs_0_.refs_1_.refs_17_
  62.3 0.3 shard_map.142.refs_3_.refs_4_.refs_17_
  62.6 2.0 %shard_map.143 = (f32[12,64,128]{2,1,0:T(8,128)S(1)}, f32[12,64,128]{2,1,0:T(8,128)S(1)}) custom-call(f32[4,64,128]{2,1,0:T(8,128)S(1)} %shard_map.141.refs_13_.refs_0_.refs_1_.refs_17_, f32[12,64,128]{2,1,0:T(8,128)S(1)} %shard_map.137.refs_10_.refs_13_.refs_1_.refs_21_.refs_2_, f32[12,64,128]{2,1,0:T(8,128)S(1)} %shard_map.140.refs_14_.refs_2_.refs_22_.refs_3_, ...), custom_call_target="tpu_custom_call" | custom-call | flops 240000 | bytes 24576 | tf_op jit(solution)/shard_map/pallas_call | solution.py:136
  64.7 2.8 %collective-permute-start.20 = (f32[4,64,128]{2,1,0:T(8,128)S(1)}, f32[4,64,128]{2,1,0:T(8,128)S(1)}, u32[]{:S(2)}, u32[]{:S(2)}) collective-permute-start(f32[4,64,128]{2,1,0:T(8,128)S(1)} %shard_map.141.refs_13_.refs_0_.refs_1_.refs_17_), channel_id=1, source_target_pairs={{0,1},{1,0},{2,3},{3,2},{4,5},{5,4},{6,7},{7,6},{8,9},{9,8},{10,11... | collective-permute-start | bytes 393224 | tf_op jit(solution)/shard_map/ppermute | solution.py:559
  67.5 0.7 collective-permute-start.18
  68.3 0.6 collective-permute-start.17
  68.9 4.3 %collective-permute-start.19 = (f32[8,128]{1,0:T(8,128)S(1)}, f32[8,128]{1,0:T(8,128)S(1)}, u32[]{:S(2)}, u32[]{:S(2)}) collective-permute-start(f32[8,128]{1,0:T(8,128)S(1)} %add.29.refs_20_), channel_id=1, source_target_pairs={{0,4},{1,5},{2,6},{3,7},{4,0},{5,1},{6,2},{7,3},{8,12},{9,13},{10,... | collective-permute-start | bytes 12296 | tf_op jit(solution)/shard_map/ppermute | solution.py:564
  73.1 0.4 shard_map.145.refs_22_
  73.6 1.9 %collective-permute-done.19.refs_21_ = f32[8,128]{1,0:T(8,128)S(1)} collective-permute-done((f32[8,128]{1,0:T(8,128)S(1)}, f32[8,128]{1,0:T(8,128)S(1)}, u32[]{:S(2)}, u32[]{:S(2)}) %collective-permute-start.19) | collective-permute-done | bytes 4128 | tf_op jit(solution)/shard_map/ppermute | solution.py:564
  75.4 0.4 shard_map.146
  75.9 1.3 %collective-permute-done.21 = f32[264,128]{1,0:T(8,128)S(1)} collective-permute-done((f32[264,128]{1,0:T(8,128)S(1)}, f32[264,128]{1,0:T(8,128)S(1)}, u32[]{:S(2)}, u32[]{:S(2)}) %collective-permute-start.21) | collective-permute-done | bytes 135200 | tf_op jit(solution)/shard_map/ppermute | solution.py:564
  77.3 1.2 %collective-permute-start.22 = (f32[264,128]{1,0:T(8,128)S(1)}, f32[264,128]{1,0:T(8,128)S(1)}, u32[]{:S(2)}, u32[]{:S(2)}) collective-permute-start(f32[264,128]{1,0:T(8,128)S(1)} %add.30.rest_2_), channel_id=1, source_target_pairs={{0,16},{8,24},{16,0},{24,8},{1,17},{9,25},{17,1},{25,9},{2,18},{10... | collective-permute-start | bytes 405512 | tf_op jit(solution)/shard_map/ppermute | solution.py:564
  79.2 0.4 collective-permute-done.17.rest_1_
  79.5 3.4 %collective-permute-done.22.rest_3_ = f32[264,128]{1,0:T(8,128)S(1)} collective-permute-done((f32[264,128]{1,0:T(8,128)S(1)}, f32[264,128]{1,0:T(8,128)S(1)}, u32[]{:S(2)}, u32[]{:S(2)}) %collective-permute-start.22) | collective-permute-done | bytes 135200 | tf_op jit(solution)/shard_map/ppermute | solution.py:564
  83.0 0.8 shard_map.147.values_ref
  83.8 0.8 shard_map.148.refs_0_
  84.7 1.1 %collective-permute-done.23.values_ref = f32[16,64,128]{2,1,0:T(8,128)S(1)} collective-permute-done((f32[16,64,128]{2,1,0:T(8,128)S(1)}, f32[16,64,128]{2,1,0:T(8,128)S(1)}, u32[]{:S(2)}, u32[]{:S(2)}) %collective-permute-start.23) | collective-permute-done | bytes 524320 | tf_op jit(solution)/shard_map/ppermute | solution.py:564
  85.7 0.8 shard_map.149
  (50 shorter events, 2.2 us)
Async XLA Ops:
  0.0 5.1 %copy-start = (f32[1,32,64,128]{3,2,1,0:T(8,128)S(1)}, f32[1,32,64,128]{3,2,1,0:T(8,128)}, u32[]{:S(2)}) copy-start(f32[1,32,64,128]{3,2,1,0:T(8,128)} %param.12) | copy-start | bytes 3145732
  0.0 5.1 %copy-start.2 = (f32[1,32,64,128]{3,2,1,0:T(8,128)S(1)}, f32[1,32,64,128]{3,2,1,0:T(8,128)}, u32[]{:S(2)}) copy-start(f32[1,32,64,128]{3,2,1,0:T(8,128)} %param.11) | copy-start | bytes 3145732
  1.3 14.2 %collective-permute-start = (f32[8,64,128]{2,1,0:T(8,128)S(1)}, f32[8,64,128]{2,1,0:T(8,128)S(1)}, u32[]{:S(2)}, u32[]{:S(2)}) collective-permute-start(f32[8,64,128]{2,1,0:T(8,128)S(1)} %pad_maximum_fusion), channel_id=1, source_target_pairs={{0,1},{1,0},{2,3},{3,2},{4,5},{5,4},{6,7},{7,6},{8,9},{9,8},{10,11... | collective-permute-start | bytes 786440 | tf_op jit(solution)/shard_map/ppermute | solution.py:559
  4.4 14.9 %collective-permute-start.2 = (f32[8,64,128]{2,1,0:T(8,128)S(1)}, f32[8,64,128]{2,1,0:T(8,128)S(1)}, u32[]{:S(2)}, u32[]{:S(2)}) collective-permute-start(f32[8,64,128]{2,1,0:T(8,128)S(1)} %pad_maximum_fusion.1), channel_id=1, source_target_pairs={{1,2},{2,1},{3,4},{4,3},{5,6},{6,5},{9,10},{10,9},{11,12},{12,11},... | collective-permute-start | bytes 786440 | tf_op jit(solution)/shard_map/ppermute | solution.py:559
  5.1 1.2 %copy-start.3 = (f32[32,64,128]{2,1,0:T(8,128)S(1)}, f32[32,64,128]{2,1,0:T(8,128)}, u32[]{:S(2)}) copy-start(f32[32,64,128]{2,1,0:T(8,128)} %refs_2_.1) | copy-start | bytes 3145732
  7.6 0.7 copy-start.5
  7.6 0.7 copy-start.7
  7.6 0.7 copy-start.8
  15.9 6.4 %collective-permute-start.1 = (f32[4,64,128]{2,1,0:T(8,128)S(1)}, f32[4,64,128]{2,1,0:T(8,128)S(1)}, u32[]{:S(2)}, u32[]{:S(2)}) collective-permute-start(f32[4,64,128]{2,1,0:T(8,128)S(1)} %get-tuple-element.69.refs_0_.refs_1_.refs_3_.refs_4_.refs_5_.refs_9_), channel_id=1, source_target_pairs={{0,1},{1,0},{2,3},{3,2},{4,5},{5,4},{6,7},{7,6},{8,9},{9,8},{10,11... | collective-permute-start | bytes 393224 | tf_op jit(solution)/shard_map/ppermute | solution.py:559
  19.3 1.2 %copy-start.1 = (f32[1,32,64,128]{3,2,1,0:T(8,128)S(1)}, f32[1,32,64,128]{3,2,1,0:T(8,128)}, u32[]{:S(2)}) copy-start(f32[1,32,64,128]{3,2,1,0:T(8,128)} %param.13) | copy-start | bytes 3145732
  19.3 1.5 %copy-start.4 = (f32[1,32,64,128]{3,2,1,0:T(8,128)S(1)}, f32[1,32,64,128]{3,2,1,0:T(8,128)}, u32[]{:S(2)}) copy-start(f32[1,32,64,128]{3,2,1,0:T(8,128)} %param.14) | copy-start | bytes 3145732
  19.7 8.7 %collective-permute-start.4 = (f32[4,64,128]{2,1,0:T(8,128)S(1)}, f32[4,64,128]{2,1,0:T(8,128)S(1)}, u32[]{:S(2)}, u32[]{:S(2)}) collective-permute-start(f32[4,64,128]{2,1,0:T(8,128)S(1)} %get-tuple-element.72.refs_3_.refs_4_.refs_6_.refs_7_.refs_8_.refs_9_), channel_id=1, source_target_pairs={{1,2},{2,1},{3,4},{4,3},{5,6},{6,5},{9,10},{10,9},{11,12},{12,11},... | collective-permute-start | bytes 393224 | tf_op jit(solution)/shard_map/ppermute | solution.py:559
  22.6 7.8 %collective-permute-start.3 = (f32[4,64,128]{2,1,0:T(8,128)S(1)}, f32[4,64,128]{2,1,0:T(8,128)S(1)}, u32[]{:S(2)}, u32[]{:S(2)}) collective-permute-start(f32[4,64,128]{2,1,0:T(8,128)S(1)} %get-tuple-element.75.refs_0_.refs_1_.refs_3_.refs_4_.refs_5_.refs_9_), channel_id=1, source_target_pairs={{0,1},{1,0},{2,3},{3,2},{4,5},{5,4},{6,7},{7,6},{8,9},{9,8},{10,11... | collective-permute-start | bytes 393224 | tf_op jit(solution)/shard_map/ppermute | solution.py:559
  28.7 8.1 %collective-permute-start.6 = (f32[4,64,128]{2,1,0:T(8,128)S(1)}, f32[4,64,128]{2,1,0:T(8,128)S(1)}, u32[]{:S(2)}, u32[]{:S(2)}) collective-permute-start(f32[4,64,128]{2,1,0:T(8,128)S(1)} %get-tuple-element.80.refs_3_.refs_4_.refs_6_.refs_7_.refs_8_.refs_9_), channel_id=1, source_target_pairs={{1,2},{2,1},{3,4},{4,3},{5,6},{6,5},{9,10},{10,9},{11,12},{12,11},... | collective-permute-start | bytes 393224 | tf_op jit(solution)/shard_map/ppermute | solution.py:559
  30.7 8.3 %collective-permute-start.5 = (f32[4,64,128]{2,1,0:T(8,128)S(1)}, f32[4,64,128]{2,1,0:T(8,128)S(1)}, u32[]{:S(2)}, u32[]{:S(2)}) collective-permute-start(f32[4,64,128]{2,1,0:T(8,128)S(1)} %get-tuple-element.83.refs_0_.refs_1_.refs_6_), channel_id=1, source_target_pairs={{0,1},{1,0},{2,3},{3,2},{4,5},{5,4},{6,7},{7,6},{8,9},{9,8},{10,11... | collective-permute-start | bytes 393224 | tf_op jit(solution)/shard_map/ppermute | solution.py:559
  37.2 3.4 %collective-permute-start.7 = (f32[4,64,128]{2,1,0:T(8,128)S(1)}, f32[4,64,128]{2,1,0:T(8,128)S(1)}, u32[]{:S(2)}, u32[]{:S(2)}) collective-permute-start(f32[4,64,128]{2,1,0:T(8,128)S(1)} %get-tuple-element.86.refs_3_.refs_4_.refs_6_), channel_id=1, source_target_pairs={{1,2},{2,1},{3,4},{4,3},{5,6},{6,5},{9,10},{10,9},{11,12},{12,11},... | collective-permute-start | bytes 393224 | tf_op jit(solution)/shard_map/ppermute | solution.py:559
  41.6 12.8 %collective-permute-start.8 = (f32[16,64,128]{2,1,0:T(8,128)S(1)}, f32[16,64,128]{2,1,0:T(8,128)S(1)}, u32[]{:S(2)}, u32[]{:S(2)}) collective-permute-start(f32[16,64,128]{2,1,0:T(8,128)S(1)} %get-tuple-element.109), channel_id=1, source_target_pairs={{0,8},{8,0},{16,24},{24,16},{1,9},{9,1},{17,25},{25,17},{2,10},{10... | collective-permute-start | bytes 1572872 | tf_op jit(solution)/shard_map/ppermute | solution.py:564
  41.6 10.3 %collective-permute-start.10 = (f32[4,64,128]{2,1,0:T(8,128)S(1)}, f32[4,64,128]{2,1,0:T(8,128)S(1)}, u32[]{:S(2)}, u32[]{:S(2)}) collective-permute-start(f32[4,64,128]{2,1,0:T(8,128)S(1)} %shard_map.130.refs_0_.refs_1_.refs_3_.refs_4_.refs_5_.refs_19_), channel_id=1, source_target_pairs={{0,1},{1,0},{2,3},{3,2},{4,5},{5,4},{6,7},{7,6},{8,9},{9,8},{10,11... | collective-permute-start | bytes 393224 | tf_op jit(solution)/shard_map/ppermute | solution.py:559
  46.1 7.3 %collective-permute-start.9 = (f32[4,64,128]{2,1,0:T(8,128)S(1)}, f32[4,64,128]{2,1,0:T(8,128)S(1)}, u32[]{:S(2)}, u32[]{:S(2)}) collective-permute-start(f32[4,64,128]{2,1,0:T(8,128)S(1)} %shard_map.133.refs_16_.refs_3_.refs_4_.refs_6_.refs_7_.refs_8_.refs_19_), channel_id=1, source_target_pairs={{1,2},{2,1},{3,4},{4,3},{5,6},{6,5},{9,10},{10,9},{11,12},{12,11},... | collective-permute-start | bytes 393224 | tf_op jit(solution)/shard_map/ppermute | solution.py:559
  46.9 6.4 %collective-permute-start.11 = (f32[8,128]{1,0:T(8,128)S(1)}, f32[8,128]{1,0:T(8,128)S(1)}, u32[]{:S(2)}, u32[]{:S(2)}) collective-permute-start(f32[8,128]{1,0:T(8,128)S(1)} %get-tuple-element.111), channel_id=1, source_target_pairs={{0,1},{1,0},{2,3},{3,2},{4,5},{5,4},{6,7},{7,6},{8,9},{9,8},{10,11... | collective-permute-start | bytes 12296 | tf_op jit(solution)/shard_map/ppermute | solution.py:564
  52.3 9.4 %collective-permute-start.13 = (f32[4,64,128]{2,1,0:T(8,128)S(1)}, f32[4,64,128]{2,1,0:T(8,128)S(1)}, u32[]{:S(2)}, u32[]{:S(2)}) collective-permute-start(f32[4,64,128]{2,1,0:T(8,128)S(1)} %shard_map.136.refs_0_.refs_1_.refs_4_.refs_5_.refs_18_), channel_id=1, source_target_pairs={{0,1},{1,0},{2,3},{3,2},{4,5},{5,4},{6,7},{7,6},{8,9},{9,8},{10,11... | collective-permute-start | bytes 393224 | tf_op jit(solution)/shard_map/ppermute | solution.py:559
  53.7 8.6 %collective-permute-start.14 = (f32[4,64,128]{2,1,0:T(8,128)S(1)}, f32[4,64,128]{2,1,0:T(8,128)S(1)}, u32[]{:S(2)}, u32[]{:S(2)}) collective-permute-start(f32[4,64,128]{2,1,0:T(8,128)S(1)} %shard_map.138.refs_1_.refs_3_.refs_4_.refs_7_.refs_8_.refs_18_), channel_id=1, source_target_pairs={{1,2},{2,1},{3,4},{4,3},{5,6},{6,5},{9,10},{10,9},{11,12},{12,11},... | collective-permute-start | bytes 393224 | tf_op jit(solution)/shard_map/ppermute | solution.py:559
  54.4 19.1 %collective-permute-start.12 = (f32[16,64,128]{2,1,0:T(8,128)S(1)}, f32[16,64,128]{2,1,0:T(8,128)S(1)}, u32[]{:S(2)}, u32[]{:S(2)}) collective-permute-start(f32[16,64,128]{2,1,0:T(8,128)S(1)} %shard_map.139), channel_id=1, source_target_pairs={{0,16},{8,24},{16,0},{24,8},{1,17},{9,25},{17,1},{25,9},{2,18},{10... | collective-permute-start | bytes 1572872 | tf_op jit(solution)/shard_map/ppermute | solution.py:564
  56.0 6.3 %collective-permute-start.15 = (f32[8,128]{1,0:T(8,128)S(1)}, f32[8,128]{1,0:T(8,128)S(1)}, u32[]{:S(2)}, u32[]{:S(2)}) collective-permute-start(f32[8,128]{1,0:T(8,128)S(1)} %add.28), channel_id=1, source_target_pairs={{0,2},{1,3},{2,0},{3,1},{4,6},{5,7},{6,4},{7,5},{8,10},{9,11},{10,... | collective-permute-start | bytes 12296 | tf_op jit(solution)/shard_map/ppermute | solution.py:564
  64.6 3.6 %collective-permute-start.16 = (f32[12,64,128]{2,1,0:T(8,128)S(1)}, f32[12,64,128]{2,1,0:T(8,128)S(1)}, u32[]{:S(2)}, u32[]{:S(2)}) collective-permute-start(f32[12,64,128]{2,1,0:T(8,128)S(1)} %get-tuple-element.114), channel_id=1, source_target_pairs={{0,8},{8,0},{16,24},{24,16},{1,9},{9,1},{17,25},{25,17},{2,10},{10... | collective-permute-start | bytes 1179656 | tf_op jit(solution)/shard_map/ppermute | solution.py:564
  64.7 8.4 %collective-permute-start.20 = (f32[4,64,128]{2,1,0:T(8,128)S(1)}, f32[4,64,128]{2,1,0:T(8,128)S(1)}, u32[]{:S(2)}, u32[]{:S(2)}) collective-permute-start(f32[4,64,128]{2,1,0:T(8,128)S(1)} %shard_map.141.refs_13_.refs_0_.refs_1_.refs_17_), channel_id=1, source_target_pairs={{0,1},{1,0},{2,3},{3,2},{4,5},{5,4},{6,7},{7,6},{8,9},{9,8},{10,11... | collective-permute-start | bytes 393224 | tf_op jit(solution)/shard_map/ppermute | solution.py:559
  67.5 7.9 %collective-permute-start.18 = (f32[4,64,128]{2,1,0:T(8,128)S(1)}, f32[4,64,128]{2,1,0:T(8,128)S(1)}, u32[]{:S(2)}, u32[]{:S(2)}) collective-permute-start(f32[4,64,128]{2,1,0:T(8,128)S(1)} %shard_map.142.refs_3_.refs_4_.refs_17_), channel_id=1, source_target_pairs={{1,2},{2,1},{3,4},{4,3},{5,6},{6,5},{9,10},{10,9},{11,12},{12,11},... | collective-permute-start | bytes 393224 | tf_op jit(solution)/shard_map/ppermute | solution.py:559
  68.3 11.3 %collective-permute-start.17 = (f32[12,64,128]{2,1,0:T(8,128)S(1)}, f32[12,64,128]{2,1,0:T(8,128)S(1)}, u32[]{:S(2)}, u32[]{:S(2)}) collective-permute-start(f32[12,64,128]{2,1,0:T(8,128)S(1)} %shard_map.144.rest_0_), channel_id=1, source_target_pairs={{0,16},{8,24},{16,0},{24,8},{1,17},{9,25},{17,1},{25,9},{2,18},{10... | collective-permute-start | bytes 1179656 | tf_op jit(solution)/shard_map/ppermute | solution.py:564
  68.9 6.6 %collective-permute-start.19 = (f32[8,128]{1,0:T(8,128)S(1)}, f32[8,128]{1,0:T(8,128)S(1)}, u32[]{:S(2)}, u32[]{:S(2)}) collective-permute-start(f32[8,128]{1,0:T(8,128)S(1)} %add.29.refs_20_), channel_id=1, source_target_pairs={{0,4},{1,5},{2,6},{3,7},{4,0},{5,1},{6,2},{7,3},{8,12},{9,13},{10,... | collective-permute-start | bytes 12296 | tf_op jit(solution)/shard_map/ppermute | solution.py:564
  75.8 1.4 %collective-permute-start.21 = (f32[264,128]{1,0:T(8,128)S(1)}, f32[264,128]{1,0:T(8,128)S(1)}, u32[]{:S(2)}, u32[]{:S(2)}) collective-permute-start(f32[264,128]{1,0:T(8,128)S(1)} %get-tuple-element.116), channel_id=1, source_target_pairs={{0,8},{8,0},{16,24},{24,16},{1,9},{9,1},{17,25},{25,17},{2,10},{10... | collective-permute-start | bytes 405512 | tf_op jit(solution)/shard_map/ppermute | solution.py:564
  77.2 5.7 %copy-start.6 = (f32[64]{0:T(128)S(1)}, f32[64]{0:T(128)}, u32[]{:S(2)}) copy-start(f32[64]{0:T(128)} %table_ref.1) | copy-start | bytes 772
  77.3 5.7 %collective-permute-start.22 = (f32[264,128]{1,0:T(8,128)S(1)}, f32[264,128]{1,0:T(8,128)S(1)}, u32[]{:S(2)}, u32[]{:S(2)}) collective-permute-start(f32[264,128]{1,0:T(8,128)S(1)} %add.30.rest_2_), channel_id=1, source_target_pairs={{0,16},{8,24},{16,0},{24,8},{1,17},{9,25},{17,1},{25,9},{2,18},{10... | collective-permute-start | bytes 405512 | tf_op jit(solution)/shard_map/ppermute | solution.py:564
  83.8 2.0 %collective-permute-start.23 = (f32[16,64,128]{2,1,0:T(8,128)S(1)}, f32[16,64,128]{2,1,0:T(8,128)S(1)}, u32[]{:S(2)}, u32[]{:S(2)}) collective-permute-start(f32[16,64,128]{2,1,0:T(8,128)S(1)} %shard_map.147.values_ref), channel_id=1, source_target_pairs={{0,8},{8,0},{16,24},{24,16},{1,9},{9,1},{17,25},{25,17},{2,10},{10... | collective-permute-start | bytes 1572872 | tf_op jit(solution)/shard_map/ppermute | solution.py:564
